TPU v7x, 32 devices: a whole 2x2x4 slice. The times are simulated.
32 devices in a mesh: table: 8 (over z, core), row: 4 (over y, x).
Axes of the slice: x: 2, y: 2, z: 4, core: 2. Of those that a mesh axis runs over, the one named last changes fastest.
Arguments:
- dense_feat: bfloat16 [8192, 128], P(('table', 'row')), may hold values from -6 to 6
- pooled: bfloat16 [8192, 2048], P(('table', 'row')), may hold values from -6 to 6
- labels: int32 [8192], P(('table', 'row')), may hold values 0 or 1
- cross_down: bfloat16 [2176, 256], replicated, may hold values from -0.125 to 0.125
- cross_up: bfloat16 [256, 2176], replicated, may hold values from -0.375 to 0.375
- cross_bias: float32 [2176], replicated, may hold values from -3 to 3
- w_hidden1: bfloat16 [2176, 1024], replicated, may hold values from -0.125 to 0.125
- bias1: float32 [1024], replicated, may hold values from -3 to 3
- w_hidden2: bfloat16 [1024, 1024], replicated, may hold values from -0.1875 to 0.1875
- bias2: float32 [1024], replicated, may hold values from -3 to 3
- w_logit: float32 [1024], replicated, may hold values from -0.6 to 0.6
- lookup_slots: int32 [16, 8192, 4], P('table'), may hold values from 0 to 2047, as said below
Outputs:
- row_grads: float32 [16, 2048, 128], P('table', 'row')
- grad_cross_down: float32 [2176, 256], P('row')
- grad_cross_up: float32 [256, 2176], P('row')
- grad_cross_bias: float32 [2176], P('row')
- grad_hidden1: float32 [2176, 1024], P('row')
- grad_bias1: float32 [1024], P('row')
- grad_hidden2: float32 [1024, 1024], P('row')
- grad_bias2: float32 [1024], P('row')
- grad_logit: float32 [1024], P('row')
Inputs may be any that keep to these rules, and one draw needn't show every extreme that they name: `lookup_slots`: row shard r of a table owns the slots r * 512 to (r + 1) * 512 - 1; a lookup's slot is the deduplicated row that it reads.
All inputs are finite; a program needn't handle non-finite values. No bound on the sum of `labels` on one device may be relied on, other than what follows from the above.
Results may differ from a plain program's by a relative error of at most 0.015.
Values may be sent and summed in bfloat16 or wider, within the bound.
No kernel may reach another device: no remote copies, remote signals or barrier semaphores. Data moves between devices by JAX's collectives and lax.ppermute only.
A program may use at most 128 MiB of HBM per device.

v0:
```python
import jax
import jax.numpy as jnp
from jax import lax
from jax.sharding import PartitionSpec as P

loss_scale = 16.0


def swish_slope(value):
    sig = jax.nn.sigmoid(value)
    return sig * (1.0 + value * (1.0 - sig))


def dense_backward(
    dense_feat,
    pooled,
    labels,
    cross_down,
    cross_up,
    cross_bias,
    w_hidden1,
    bias1,
    w_hidden2,
    bias2,
    w_logit,
):
    stacked = jnp.concatenate([dense_feat, pooled], axis=1)
    stacked_wide = stacked.astype(jnp.float32)
    reduced = jnp.dot(stacked, cross_down, preferred_element_type=jnp.float32).astype(jnp.bfloat16)
    widened = jnp.dot(reduced, cross_up, preferred_element_type=jnp.float32) + cross_bias
    crossed = (stacked_wide * widened + stacked_wide).astype(jnp.bfloat16)
    pre_first = jnp.dot(crossed, w_hidden1, preferred_element_type=jnp.float32) + bias1
    act_first = jax.nn.silu(pre_first).astype(jnp.bfloat16)
    pre_second = jnp.dot(act_first, w_hidden2, preferred_element_type=jnp.float32) + bias2
    act_second = jax.nn.silu(pre_second).astype(jnp.bfloat16)
    act_wide = act_second.astype(jnp.float32)
    logits = jnp.sum(act_wide * w_logit, axis=1)
    delta_logit = loss_scale * (jax.nn.sigmoid(logits) - labels.astype(jnp.float32))
    delta_second = (delta_logit[:, None] * w_logit[None, :] * swish_slope(pre_second)).astype(
        jnp.bfloat16
    )
    grad_logit = jnp.sum(act_wide * delta_logit[:, None], axis=0)
    grad_hidden2 = jnp.dot(act_first.T, delta_second, preferred_element_type=jnp.float32)
    grad_bias2 = jnp.sum(delta_second.astype(jnp.float32), axis=0)
    back_first = jnp.dot(delta_second, w_hidden2.T, preferred_element_type=jnp.float32)
    delta_first = (back_first * swish_slope(pre_first)).astype(jnp.bfloat16)
    grad_hidden1 = jnp.dot(crossed.T, delta_first, preferred_element_type=jnp.float32)
    grad_bias1 = jnp.sum(delta_first.astype(jnp.float32), axis=0)
    delta_crossed = jnp.dot(delta_first, w_hidden1.T, preferred_element_type=jnp.float32)
    delta_widened = (delta_crossed * stacked_wide).astype(jnp.bfloat16)
    grad_cross_up = jnp.dot(reduced.T, delta_widened, preferred_element_type=jnp.float32)
    grad_cross_bias = jnp.sum(delta_widened.astype(jnp.float32), axis=0)
    delta_reduced = jnp.dot(delta_widened, cross_up.T, preferred_element_type=jnp.float32).astype(
        jnp.bfloat16
    )
    grad_cross_down = jnp.dot(stacked.T, delta_reduced, preferred_element_type=jnp.float32)
    delta_stacked = delta_crossed * (widened + 1.0) + jnp.dot(
        delta_reduced, cross_down.T, preferred_element_type=jnp.float32
    )
    grads = (
        grad_cross_down,
        grad_cross_up,
        grad_cross_bias,
        grad_hidden1,
        grad_bias1,
        grad_hidden2,
        grad_bias2,
        grad_logit,
    )
    return (grads, delta_stacked)


def local(
    dense_feat,
    pooled,
    labels,
    cross_down,
    cross_up,
    cross_bias,
    w_hidden1,
    bias1,
    w_hidden2,
    bias2,
    w_logit,
    lookup_slots,
):
    grads, delta_stacked = dense_backward(
        dense_feat,
        pooled,
        labels,
        cross_down,
        cross_up,
        cross_bias,
        w_hidden1,
        bias1,
        w_hidden2,
        bias2,
        w_logit,
    )
    width = dense_feat.shape[1]
    batch_dev = dense_feat.shape[0]
    n_table = lax.axis_size("table")
    n_row = lax.axis_size("row")
    tab_grp = lookup_slots.shape[0]
    hot_count = lookup_slots.shape[2]
    tables = tab_grp * n_table
    u_shard = batch_dev * n_table * hot_count // 16
    pooled_grad = delta_stacked[:, width:].astype(jnp.bfloat16).reshape(batch_dev, tables, width)
    received = lax.all_to_all(pooled_grad, "table", split_axis=1, concat_axis=0, tiled=True)
    row_pos = lax.axis_index("row")
    arranged = lookup_slots.reshape(tab_grp, n_table, n_row, batch_dev, hot_count)
    ordered = jnp.transpose(arranged, (0, 2, 1, 3, 4)).reshape(
        tab_grp, n_row * n_table * batch_dev, hot_count
    )
    in_shard = ordered - row_pos * u_shard
    in_shard = jnp.where((in_shard >= 0) & (in_shard < u_shard), in_shard, u_shard)
    initial = jnp.zeros((tab_grp, u_shard, width), jnp.float32)
    block_rows = lax.all_gather(received, "row", axis=0, tiled=True)
    parts = []
    for table_pos in range(tab_grp):
        values = block_rows[:, table_pos].astype(jnp.float32)
        current = initial[table_pos]
        for which in range(hot_count):
            current = current + jax.ops.segment_sum(
                values, in_shard[table_pos, :, which], num_segments=u_shard
            )
        parts.append(current)
    row_grads = jnp.stack(parts)
    g_down, g_up, g_cbias, g_first, g_bfirst, g_second, g_bsecond, g_logit = grads
    parted = (
        lax.psum_scatter(g_down, "row", scatter_dimension=0, tiled=True),
        lax.psum_scatter(g_up, "row", scatter_dimension=0, tiled=True),
        lax.psum_scatter(g_cbias, "row", scatter_dimension=0, tiled=True),
        lax.psum_scatter(g_first, "row", scatter_dimension=0, tiled=True),
        lax.psum_scatter(g_bfirst, "row", scatter_dimension=0, tiled=True),
        lax.psum_scatter(g_second, "row", scatter_dimension=0, tiled=True),
        lax.psum_scatter(g_bsecond, "row", scatter_dimension=0, tiled=True),
        lax.psum_scatter(g_logit, "row", scatter_dimension=0, tiled=True),
    )
    s_down, s_up, s_cbias, s_first, s_bfirst, s_second, s_bsecond, s_logit = parted
    totals = lax.psum(
        (s_down, s_up, s_cbias, s_first, s_bfirst, s_second, s_bsecond, s_logit), "table"
    )
    return (
        row_grads,
        totals[0],
        totals[1],
        totals[2],
        totals[3],
        totals[4],
        totals[5],
        totals[6],
        totals[7],
    )


def solution(mesh):
    in_specs = (
        P(("table", "row"), None),
        P(("table", "row"), None),
        P(("table", "row")),
        P(),
        P(),
        P(),
        P(),
        P(),
        P(),
        P(),
        P(),
        P("table", None, None),
    )
    out_specs = (
        P("table", "row", None),
        P("row", None),
        P("row", None),
        P("row"),
        P("row", None),
        P("row"),
        P("row", None),
        P("row"),
        P("row"),
    )
    return jax.shard_map(local, mesh=mesh, in_specs=in_specs, out_specs=out_specs, check_vma=False)
```

profile of v0, /device:TPU:0, one launch (start us, length us, event | category | flops | bytes accessed | tf_op | source)
XLA Modules:
  0.0 677.8 jit_solution(1060134400200022748)
XLA Ops:
  7.2 1.0 constant_dynamic-update-slice_fusion.1
  8.3 1.4 constant_dynamic-update-slice_fusion
  9.7 0.5 convolution_convert_fusion.1
  10.2 0.5 convolution_add_fusion
  10.7 1.3 copy-done.4
  12.0 1.5 convolution_add_fusion.2
  13.5 1.0 fusion.20
  14.6 0.6 convert_reduce_fusion.1
  15.2 0.9 convert_reduce_fusion.2
  16.1 2.8 convert_reduce_fusion
  19.0 1.0 copy-done.3
  20.0 1.9 fusion.38
  21.9 2.1 convolution_convert_fusion
  24.0 1.9 fusion.37
  26.0 4.1 fusion.33
  30.2 6.9 %fusion.30 = f32[2176,1024]{1,0:T(8,128)} fusion(bf16[256,1024]{1,0:T(8,128)(2,1)} %copy-done.9, f32[256,2176]{1,0:T(8,128)} %copy-done.1, bf16[256,2176]{1,0:T(8,128)(2,1)S(1)} %constant_dynamic-update-slice_fusion), kind=kOutput, calls=%fused_computation.71 | convolution fusion | flops 1143078912 | bytes 12779520 | tf_op jit(solution)/shard_map/dot_general | solution.py:47
  37.1 1.3 copy-done.7
  38.4 0.5 fusion.36
  38.9 1.3 copy-done.2
  40.1 2.0 copy_bitcast_fusion
  42.2 32.4 %all_to_all.18 = bf16[256,16,128]{2,0,1:T(8,128)(2,1)S(1)} all-to-all(bf16[256,16,128]{2,0,1:T(8,128)(2,1)S(1)} %copy_bitcast_fusion), channel_id=1, replica_groups=mesh['table'=8,'row'=4] {'table'}, dimensions={1} | all-to-all | bytes 2097152 | tf_op jit(solution)/shard_map/all_to_all | solution.py:109
  74.5 1.0 copy.26
  75.7 0.6 dynamic-slice
  77.6 0.2 sub.26
  77.9 0.1 sub.28
  78.0 16.1 %all-reduce.6 = (f32[2176]{0:T(1024)S(1)}, f32[1024]{0:T(1024)S(1)}, f32[1024]{0:T(1024)S(1)}, f32[1024]{0:T(1024)S(1)}) all-reduce(f32[2176]{0:T(1024)S(1)} %get-tuple-element.23, f32[1024]{0:T(1024)S(1)} %get-tuple-element.38, f32[1024]{0:T(1024)S(1)} %get-tuple-element.21, ...), channel_id=4, replica_groups=mesh['table'=8,'row'=4] {'row'}, use_global_device_ids=true, to_apply=%region_14.15.clone | all-reduce | flops 5248 | bytes 41984
  94.1 0.1 and_select_fusion
  94.3 6.5 reduce-scatter.5.cloned.1.call-done
  100.8 55.7 %reduce-scatter.11.cloned.1.call-done = f32[256,1024]{1,0:T(8,128)} async-done(((f32[1024,1024]{1,0:T(8,128)}), f32[256,1024]{1,0:T(8,128)}) %reduce-scatter.11.cloned.1.call-update) | async-done | bytes 1048592 | tf_op jit(solution)/shard_map/reduce_scatter | solution.py:136
  156.4 94.1 %reduce-scatter.9.cloned.1.call-done = f32[544,1024]{1,0:T(8,128)} async-done(((f32[2176,1024]{1,0:T(8,128)}), f32[544,1024]{1,0:T(8,128)}) %reduce-scatter.9.cloned.1.call-update) | async-done | bytes 2228240 | tf_op jit(solution)/shard_map/reduce_scatter | solution.py:134
  250.5 0.1 dynamic-slice.3
  250.8 17.3 %all-reduce.4 = (f32[544]{0:T(1024)}, f32[256]{0:T(256)}, f32[256]{0:T(256)}, f32[256]{0:T(256)}) all-reduce(f32[544]{0:T(1024)S(1)} %dynamic-slice.1, f32[256]{0:T(256)S(1)} %dynamic-slice.3, f32[256]{0:T(256)S(1)} %dynamic-slice.5, f32[256]{0:T(256)S(1)} %dynamic-slice.7), channel_id=1, replica_groups=mesh['table'=8,'row'=4] {'table'}, use_global_device_ids=true, to_apply=%region_15.16 | all-reduce | flops 1312 | bytes 10496 | tf_op jit(solution)/shard_map/psum | solution.py:141
  268.1 0.2 fusion.35
  268.3 37.4 %all-gather.2.cloned.1.call-done = bf16[8192,2,128]{2,0,1:T(8,128)(2,1)} async-done(((bf16[2048,2,128]{2,0,1:T(8,128)(2,1)}), bf16[8192,2,128]{2,0,1:T(8,128)(2,1)}) %all-gather.2.cloned.1.call-update) | async-done | bytes 4194320 | tf_op jit(solution)/shard_map/all_gather | solution.py:118
  305.7 44.6 %scatter_custom_fusion.5 = f32[512,128]{1,0:T(8,128)S(1)} fusion(s32[8192]{0:T(1024)S(1)} %bitcast.95, bf16[8192,2,128]{2,0,1:T(8,128)(2,1)} %all-gather.2.cloned.1.call-done, f32[]{:T(128)} %constant.6.clone.1), kind=kCustom, calls=%fused_computation.12 | custom fusion | flops 2097152 | bytes 2359808 | tf_op jit(solution)/shard_map/scatter-add | solution.py:124
  350.3 44.6 %scatter_custom_fusion.4 = f32[512,128]{1,0:T(8,128)S(1)} fusion(s32[8192]{0:T(1024)S(1)} %bitcast.94, bf16[8192,2,128]{2,0,1:T(8,128)(2,1)} %all-gather.2.cloned.1.call-done, f32[]{:T(128)} %constant.6.clone.1), kind=kCustom, calls=%fused_computation.14 | custom fusion | flops 2097152 | bytes 2359808 | tf_op jit(solution)/shard_map/scatter-add | solution.py:124
  395.0 44.6 %scatter_custom_fusion.1 = f32[512,128]{1,0:T(8,128)S(1)} fusion(s32[8192]{0:T(1024)S(1)} %bitcast.93, bf16[8192,2,128]{2,0,1:T(8,128)(2,1)} %all-gather.2.cloned.1.call-done, f32[]{:T(128)} %constant.6.clone.1), kind=kCustom, calls=%fused_computation.20 | custom fusion | flops 2097152 | bytes 2359808 | tf_op jit(solution)/shard_map/scatter-add | solution.py:124
  439.6 44.6 %scatter_custom_fusion = f32[512,128]{1,0:T(8,128)S(1)} fusion(s32[8192]{0:T(1024)S(1)} %bitcast.92, bf16[8192,2,128]{2,0,1:T(8,128)(2,1)} %all-gather.2.cloned.1.call-done, f32[]{:T(128)} %constant.6.clone.1), kind=kCustom, calls=%fused_computation.22 | custom fusion | flops 2097152 | bytes 2359808 | tf_op jit(solution)/shard_map/scatter-add | solution.py:124
  484.3 44.6 %scatter_custom_fusion.7 = f32[512,128]{1,0:T(8,128)S(1)} fusion(s32[8192]{0:T(1024)S(1)} %bitcast.91, bf16[8192,2,128]{2,0,1:T(8,128)(2,1)} %all-gather.2.cloned.1.call-done, f32[]{:T(128)} %constant.6.clone.1), kind=kCustom, calls=%fused_computation.8 | custom fusion | flops 2097152 | bytes 2359808 | tf_op jit(solution)/shard_map/scatter-add | solution.py:124
  528.9 44.6 %scatter_custom_fusion.3 = f32[512,128]{1,0:T(8,128)S(1)} fusion(s32[8192]{0:T(1024)S(1)} %bitcast.90, bf16[8192,2,128]{2,0,1:T(8,128)(2,1)} %all-gather.2.cloned.1.call-done, f32[]{:T(128)} %constant.6.clone.1), kind=kCustom, calls=%fused_computation.16 | custom fusion | flops 2097152 | bytes 2359808 | tf_op jit(solution)/shard_map/scatter-add | solution.py:124
  573.5 44.9 %scatter_custom_fusion.6 = f32[512,128]{1,0:T(8,128)S(1)} fusion(f32[512,128]{1,0:T(8,128)S(1)} %add.135, s32[8192]{0:T(1024)S(1)} %bitcast.89, bf16[8192,2,128]{2,0,1:T(8,128)(2,1)} %all-gather.2.cloned.1.call-done), kind=kCustom, calls=%fused_computation.10 | custom fusion | flops 2097152 | bytes 2359296 | tf_op jit(solution)/shard_map/scatter-add | solution.py:124
  618.5 44.7 %scatter_custom_fusion.2 = f32[512,128]{1,0:T(8,128)S(1)} fusion(f32[512,128]{1,0:T(8,128)S(1)} %add.133, s32[8192]{0:T(1024)S(1)} %bitcast.88, bf16[8192,2,128]{2,0,1:T(8,128)(2,1)} %all-gather.2.cloned.1.call-done), kind=kCustom, calls=%fused_computation.18 | custom fusion | flops 2097152 | bytes 2359296 | tf_op jit(solution)/shard_map/scatter-add | solution.py:124
  663.2 0.8 pad_maximum_fusion
  664.1 2.0 copy.38
  666.1 1.9 copy.39
  668.0 1.4 copy.40
  669.4 0.6 copy-done.10
  670.0 1.0 copy.41
  (58 shorter events, 0.9 us)
Async XLA Ops:
  7.2 6.3 copy-start
  7.2 87.1 %reduce-scatter.7.cloned.1.call-start = ((), (), s32[]{:S(2)}) async-start(), calls=%async_computation.7 | async-start | bytes 2785280 | tf_op jit(solution)/shard_map/reduce_scatter | solution.py:132
  7.2 2.4 copy-start.6
  8.3 1.9 copy-start.5
  8.3 1.9 copy-start.13
  9.7 2.3 copy-start.4
  10.2 1.8 copy-start.16
  12.0 1.5 copy-start.1
  12.0 1.5 copy-start.14
  12.0 1.5 copy-start.17
  13.5 1.7 copy-start.19
  13.5 1.0 copy-start.15
  15.2 1.0 copy-start.11
  16.1 2.8 copy-start.9
  19.0 1.0 copy-start.3
  21.9 78.9 %reduce-scatter.5.cloned.1.call-start = ((), (), s32[]{:S(2)}) async-start(), calls=%async_computation.6 | async-start | bytes 2785280 | tf_op jit(solution)/shard_map/reduce_scatter | solution.py:131
  25.9 130.5 %reduce-scatter.11.cloned.1.call-start = ((), (), s32[]{:S(2)}) async-start(), calls=%async_computation.9 | async-start | bytes 5242880 | tf_op jit(solution)/shard_map/reduce_scatter | solution.py:136
  30.1 220.4 %reduce-scatter.9.cloned.1.call-start = ((), (), s32[]{:S(2)}) async-start(), calls=%async_computation.8 | async-start | bytes 11141120 | tf_op jit(solution)/shard_map/reduce_scatter | solution.py:134
  37.0 1.3 copy-start.7
  37.1 268.6 %all-gather.2.cloned.1.call-start = ((), (), s32[]{:S(2)}) async-start(), calls=%async_computation.5 | async-start | bytes 5242880 | tf_op jit(solution)/shard_map/all_gather | solution.py:118
  38.4 1.8 copy-start.2
  42.1 33.5 %copy-start.18 = (u32[32]{0:T(128)S(1)}, u32[32]{0:T(128)}, u32[]{:S(2)}) copy-start(u32[32]{0:T(128)} %constant.24) | copy-start | bytes 388
  42.1 35.4 %copy-start.12 = (s32[2,8192,4]{1,2,0:T(4,128)S(1)}, s32[2,8192,4]{1,2,0:T(4,128)}, u32[]{:S(2)}) copy-start(s32[2,8192,4]{1,2,0:T(4,128)} %param.23) | copy-start | bytes 786436
  75.6 588.5 %all-reduce.9.cloned.1.call-start = ((), (), s32[]{:S(2)}) async-start(), calls=%async_computation.10 | async-start | bytes 8781824 | tf_op jit(solution)/shard_map/psum | solution.py:141
  664.1 3.9 copy-start.8
  668.0 2.0 copy-start.10
Sparse Core Ops, SparseCore 0:
  22.0 38.9 reduce-scatter.6
  64.0 36.6 reduce-scatter.4
  103.8 52.6 reduce-scatter.10
  159.8 90.7 reduce-scatter.8
  252.9 52.6 all-gather.1
  308.3 101.2 all-reduce.8
where the time goes:
time: 678 us
  other arithmetic  361 us (53%)
  waiting for transfers between devices  194 us (29%)
  blocking collectives  65.8 us (10%)
  matrix products  24.5 us (4%)
  local copies, waits for them, and re-layouts  16.7 us (2%)
  between operations  15.8 us (2%)
    scatter-add x8, other arithmetic, local(): jax.ops.segment_sum(values, in_shard[table_pos, :, which], num_segments=u...  357 us
    reduce_scatter x1, waiting for transfers between devices, local(): lax.psum_scatter(g_first, 'row', scatter_dimension=0, tiled=True)  94.1 us
    reduce_scatter x1, waiting for transfers between devices, local(): lax.psum_scatter(g_second, 'row', scatter_dimension=0, tiled=True)  55.7 us
    all_gather x1, waiting for transfers between devices, local(): block_rows = lax.all_gather(received, 'row', axis=0, tiled=True)  37.4 us
    all_to_all x1, blocking collectives, local(): lax.all_to_all(pooled_grad, 'table', split_axis=1, concat_axis=0, tiled=T...  32.4 us
    psum x1, blocking collectives, local(): lax.psum((s_down, s_up, s_cbias, s_first, s_bfirst, s_second, s_bsecond,...  17.3 us
    unnamed x1, blocking collectives  16.1 us
    unnamed x50, local copies, waits for them, and re-layouts  13.7 us
  transfers between devices with their start and end apart: 6, of which 4 were waited for; matrix products, arithmetic and copies ran while one was open for 56% of the time, Pallas kernels for 0%

commit v1 on v0

v1 whole, which is shorter than its diff:
```python
import functools

import jax
import jax.numpy as jnp
from jax import lax
from jax.experimental import pallas as pl
from jax.experimental.pallas import tpu as pltpu
from jax.sharding import PartitionSpec as P

loss_scale = 16.0
LANES = 128
VMEM_BYTES = 52 * 1024 * 1024
bf16 = jnp.bfloat16
f32 = jnp.float32


def round_up(value, unit):
    return -(-value // unit) * unit


def matmul(left, right):
    return jnp.dot(left, right, preferred_element_type=f32)


def matmul_rt(left, right):
    return lax.dot_general(left, right, (((1,), (1,)), ((), ())), preferred_element_type=f32)


def put_blocks(ref, offset, value, shards):
    rows = value.shape[0] // shards
    step = round_up(rows, 16)
    for shard in range(shards):
        for block in range(value.shape[1] // LANES):
            start = offset + block * step
            ref[shard, start : start + rows, :] = value[
                shard * rows : (shard + 1) * rows, block * LANES : (block + 1) * LANES
            ].astype(ref.dtype)


def put_rows(ref, offset, value):
    for block in range(value.shape[1] // LANES):
        ref[offset + block : offset + block + 1, :] = value[:, block * LANES : (block + 1) * LANES]


def front_kernel(
    shards,
    pos,
    dense_feat,
    pooled,
    labels,
    cross_down,
    cross_up,
    cross_bias,
    w_hidden1,
    bias1,
    w_hidden2,
    bias2,
    w_logit,
    send2,
    keep2,
    send1,
    keep1,
    delta_first_out,
    reduced_out,
    small,
    halves,
):
    core = pos[0]
    stacked = jnp.concatenate([dense_feat[...], pooled[...]], axis=1)
    reduced = matmul(stacked, cross_down[...]).astype(bf16)
    reduced_out[...] = reduced
    widened = matmul(reduced, cross_up[...]) + cross_bias[...]
    wide = stacked.astype(f32)
    crossed = (wide * widened + wide).astype(bf16)
    pre_first = matmul(crossed, w_hidden1[...]) + bias1[...]
    sig_first = jax.nn.sigmoid(pre_first)
    act_first = (pre_first * sig_first).astype(bf16)
    slope_first = sig_first * (1.0 + pre_first * (1.0 - sig_first))
    pre_second = matmul(act_first, w_hidden2[...]) + bias2[...]
    sig_second = jax.nn.sigmoid(pre_second)
    act_second = (pre_second * sig_second).astype(bf16).astype(f32)
    slope_second = sig_second * (1.0 + pre_second * (1.0 - sig_second))
    logits = jnp.sum(act_second * w_logit[...], axis=1, keepdims=True)
    count = labels.shape[1]
    same = lax.broadcasted_iota(jnp.int32, (count, count), 0) == lax.broadcasted_iota(
        jnp.int32, (count, count), 1
    )
    label_col = jnp.sum(jnp.where(same, labels[...].astype(f32), 0.0), axis=1, keepdims=True)
    delta_logit = loss_scale * (jax.nn.sigmoid(logits) - label_col)
    delta_second = (delta_logit * w_logit[...] * slope_second).astype(bf16)
    put_rows(small, 16, jnp.sum(act_second * delta_logit, axis=0, keepdims=True))
    put_rows(small, 8, jnp.sum(delta_second.astype(f32), axis=0, keepdims=True))
    half = halves.shape[2]
    halves[0] = delta_second[:, :half]
    halves[1] = delta_second[:, half:]
    act_t = act_first.T
    put_blocks(send2, 0, matmul(act_t, halves[1 - core]), shards)
    put_blocks(keep2, 0, matmul(act_t, halves[core]), shards)
    delta_first = (matmul_rt(delta_second, w_hidden2[...]) * slope_first).astype(bf16)
    delta_first_out[...] = delta_first
    put_rows(small, 0, jnp.sum(delta_first.astype(f32), axis=0, keepdims=True))
    halves[0] = delta_first[:, :half]
    halves[1] = delta_first[:, half:]
    crossed_t = crossed.T
    put_blocks(send1, 0, matmul(crossed_t, halves[1 - core]), shards)
    put_blocks(keep1, 0, matmul(crossed_t, halves[core]), shards)


def back_kernel(
    shards,
    groups,
    pos,
    dense_feat,
    pooled,
    cross_down,
    cross_up,
    cross_bias,
    w_hidden1,
    delta_first,
    reduced,
    small_in,
    send3,
    keep3,
    *rest,
):
    outs = rest[:groups]
    wide_delta, half_delta, by_group, small = rest[groups:]
    core = pos[0]
    table_pos = pos[2]
    width = dense_feat.shape[1]
    rank = cross_down.shape[1]
    feat = cross_up.shape[1]
    stacked = jnp.concatenate([dense_feat[...], pooled[...]], axis=1)
    wide = stacked.astype(f32)
    delta_crossed = matmul_rt(delta_first[...], w_hidden1[...])
    delta_widened = (delta_crossed * wide).astype(bf16)
    delta_reduced = matmul_rt(delta_widened, cross_up[...]).astype(bf16)
    widened = matmul(reduced[...], cross_up[...]) + cross_bias[...]
    delta_stacked = delta_crossed * (widened + 1.0) + matmul_rt(delta_reduced, cross_down[...])
    per_group = by_group.shape[1]
    for table in range(groups * per_group):
        by_group[table // per_group, table % per_group] = delta_stacked[
            :, width * (table + 1) : width * (table + 2)
        ].astype(bf16)
    for which in range(groups):
        outs[which][...] = by_group[table_pos ^ which]
    span = 9 * LANES
    wide_delta[...] = delta_widened
    half_delta[0] = delta_reduced[:, : rank // 2]
    half_delta[1] = delta_reduced[:, rank // 2 :]
    put_rows(small, 24, jnp.sum(delta_widened.astype(f32), axis=0, keepdims=True))
    small[0:24, :] = small_in[...]
    reduced_t = reduced[...].T
    stacked_t = stacked.T
    down_rows = (rank // 2 // LANES) * round_up(feat // shards, 16)
    up_rows = 9 * round_up(rank // shards, 16)
    for ref, who in ((send3, 1 - core), (keep3, core)):
        put_blocks(ref, 0, matmul(stacked_t, half_delta[who]), shards)
        start = pl.multiple_of(who * (feat - span), LANES)
        put_blocks(ref, down_rows, matmul(reduced_t, wide_delta[:, pl.ds(start, span)]), shards)
        for shard in range(shards):
            ref[shard, down_rows + up_rows : down_rows + up_rows + 48, :] = small[...].astype(bf16)
            if ref.shape[1] > down_rows + up_rows + 48:
                ref[shard, down_rows + up_rows + 48 :, :] = jnp.zeros(
                    (ref.shape[1] - down_rows - up_rows - 48, LANES), bf16
                )


def count_kernel(n_row, block, hot, n_src, pos, slots, *rest):
    values, out = rest[:n_src], rest[n_src]
    table = pl.program_id(0)
    base = pl.program_id(1) * block
    samples = values[0].shape[1]
    row_pos, table_pos = pos[1], pos[2]
    names = base + lax.broadcasted_iota(jnp.int32, (block, samples), 0)
    total = jnp.zeros((block, values[0].shape[2]), f32)
    for which in range(n_src):
        start = pl.multiple_of(((table_pos ^ which) * n_row + row_pos) * samples, LANES)
        counts = jnp.zeros((block, samples), f32)
        for look in range(hot):
            line = slots[table, look : look + 1, pl.ds(start, samples)]
            counts = counts + jnp.where(line == names, 1.0, 0.0)
        total = total + matmul(counts.astype(bf16), values[which][table])
    out[0] = total.astype(out.dtype)


def unpack_kernel(shards, pos, *refs):
    own, other = refs[0:3], refs[3:6]
    g_down, g_up, g_first, g_second, g_small = refs[6:11]
    held = refs[11:14]
    core = pos[0]
    z_pos = pos[2] // 2
    for mine, theirs, ref in zip(own, other, held):
        n_z, rows = mine.shape[0], mine.shape[1]
        for which in range(n_z):
            start = pl.multiple_of((z_pos ^ which) * rows, 16)
            ref[core, pl.ds(start, rows), :] = mine[which]
            ref[1 - core, pl.ds(start, rows), :] = theirs[which]
    second, first, third = held
    for out, ref, offset, spans in (
        (g_second, second, 0, None),
        (g_first, first, 0, None),
        (g_down, third, 0, None),
        (g_up, third, -1, 9),
    ):
        rows = out.shape[0]
        step = round_up(rows, 16)
        blocks = out.shape[1] // LANES
        if offset < 0:
            offset = round_up(g_down.shape[0], 16) * (g_down.shape[1] // 2 // LANES)
        for block in range(blocks):
            if spans is None:
                half, place = divmod(block, blocks // 2)
            else:
                half = 0 if block < spans else 1
                place = block - half * (blocks - spans)
            start = offset + place * step
            out[:, block * LANES : (block + 1) * LANES] = ref[
                half, start : start + rows, :
            ].astype(f32)
    start = round_up(g_down.shape[0], 16) * (g_down.shape[1] // 2 // LANES)
    start = start + 9 * round_up(g_up.shape[0], 16)
    g_small[...] = third[0, start : start + 48, :].astype(f32)


def whole(memory=pltpu.VMEM):
    return pl.BlockSpec(memory_space=memory)


def call(body, outs, scratch, n_in, name):
    return pl.pallas_call(
        body,
        out_shape=outs,
        in_specs=[whole(pltpu.SMEM)] + [whole()] * (n_in - 1),
        out_specs=[whole()] * len(outs),
        scratch_shapes=scratch,
        compiler_params=pltpu.CompilerParams(vmem_limit_bytes=VMEM_BYTES),
        name=name,
    )


def pick(value, index, axis):
    return lax.dynamic_index_in_dim(value, index, axis, keepdims=False)


def local(
    dense_feat,
    pooled,
    labels,
    cross_down,
    cross_up,
    cross_bias,
    w_hidden1,
    bias1,
    w_hidden2,
    bias2,
    w_logit,
    lookup_slots,
):
    n_table = lax.axis_size("table")
    n_row = lax.axis_size("row")
    n_z = n_table // 2
    bits = n_row.bit_length() - 1
    table_pos = lax.axis_index("table")
    row_pos = lax.axis_index("row")
    core = table_pos % 2
    z_pos = table_pos // 2
    pos = jnp.stack([core, row_pos, table_pos]).astype(jnp.int32)
    batch, width = dense_feat.shape
    feat, rank = cross_down.shape
    hid = w_hidden1.shape[1]
    tab_grp, _, hot = lookup_slots.shape
    u_shard = batch * n_table * hot // 16

    core_perm = [(at, at ^ 1) for at in range(n_table)]

    def z_perm(which):
        return [(at, at ^ (2 * which)) for at in range(n_table)]

    def row_perm(bit):
        return [(at, at ^ (1 << bit)) for at in range(n_row)]

    def packed(rows):
        return jax.ShapeDtypeStruct((n_row, rows, LANES), bf16)

    rows2 = (hid // 2 // LANES) * round_up(hid // n_row, 16)
    rows1 = (hid // 2 // LANES) * round_up(feat // n_row, 16)
    rows3 = (rank // 2 // LANES) * round_up(feat // n_row, 16) + 9 * round_up(rank // n_row, 16) + 48
    rows1, rows2, rows3 = (round_up(rows, 16 * n_z) for rows in (rows1, rows2, rows3))

    cbias = cross_bias.reshape(1, feat)
    send2, keep2, send1, keep1, delta_first, reduced, small = call(
        functools.partial(front_kernel, n_row),
        [
            packed(rows2),
            packed(rows2),
            packed(rows1),
            packed(rows1),
            jax.ShapeDtypeStruct((batch, hid), bf16),
            jax.ShapeDtypeStruct((batch, rank), bf16),
            jax.ShapeDtypeStruct((24, LANES), f32),
        ],
        [pltpu.VMEM((2, batch, hid // 2), bf16)],
        12,
        "front",
    )(
        pos,
        dense_feat,
        pooled,
        labels.reshape(1, batch),
        cross_down,
        cross_up,
        cbias,
        w_hidden1,
        bias1.reshape(1, hid),
        w_hidden2,
        bias2.reshape(1, hid),
        w_logit.reshape(1, hid),
    )
    got2 = lax.ppermute(send2, "table", core_perm)
    got1 = lax.ppermute(send1, "table", core_perm)

    outs = call(
        functools.partial(back_kernel, n_row, n_table),
        [packed(rows3), packed(rows3)]
        + [jax.ShapeDtypeStruct((tab_grp, batch, width), bf16)] * n_table,
        [
            pltpu.VMEM((batch, feat), bf16),
            pltpu.VMEM((2, batch, rank // 2), bf16),
            pltpu.VMEM((n_table, tab_grp, batch, width), bf16),
            pltpu.VMEM((48, LANES), f32),
        ],
        10,
        "back",
    )(pos, dense_feat, pooled, cross_down, cross_up, cbias, w_hidden1, delta_first, reduced, small)
    send3, keep3 = outs[:2]
    got3 = lax.ppermute(send3, "table", core_perm)
    values = [outs[2]]
    for which in range(1, n_table):
        perm = [(at, at ^ which) for at in range(n_table)]
        values.append(lax.ppermute(outs[2 + which], "table", perm))

    def halve(total, order):
        left = list(range(bits - 1, -1, -1))
        total = total.reshape((2,) * bits + total.shape[1:])
        for bit in order:
            axis = left.index(bit)
            left.remove(bit)
            mine = (row_pos >> bit) & 1
            sent = pick(total, 1 - mine, axis).astype(bf16)
            got = lax.ppermute(sent, "row", row_perm(bit))
            total = pick(total, mine, axis) + got.astype(f32)
        return total

    up_order = tuple(range(bits))
    down_order = up_order[::-1]

    def sum_z(total):
        parts = total.astype(bf16).reshape(n_z, total.shape[0] // n_z, LANES)
        result = pick(parts, z_pos, 0).astype(f32)
        for which in range(1, n_z):
            got = lax.ppermute(pick(parts, z_pos ^ which, 0), "table", z_perm(which))
            result = result + got.astype(f32)
        result = result.astype(bf16)
        pieces = [result]
        for which in range(1, n_z):
            pieces.append(lax.ppermute(result, "table", z_perm(which)))
        mine = jnp.stack(pieces)
        return mine, lax.ppermute(mine, "table", core_perm)

    streams = []
    for keep, got, order in (
        (keep2, got2, down_order),
        (keep1, got1, up_order),
        (keep3, got3, down_order),
    ):
        streams.append(sum_z(halve(keep.astype(f32) + got.astype(f32), order)))

    slots = jnp.transpose(lookup_slots, (0, 2, 1))
    n_slots = n_row * u_shard
    block = min(512, u_shard)
    sums = pl.pallas_call(
        functools.partial(count_kernel, n_row, block, hot, n_table),
        out_shape=jax.ShapeDtypeStruct((tab_grp, n_slots, width), bf16),
        grid=(tab_grp, n_slots // block),
        in_specs=[whole(pltpu.SMEM)] + [whole()] * (1 + n_table),
        out_specs=pl.BlockSpec((1, block, width), lambda table, at: (table, at, 0)),
        compiler_params=pltpu.CompilerParams(vmem_limit_bytes=VMEM_BYTES),
        name="counts",
    )(pos, slots, *values)
    row_grads = jnp.stack(
        [
            halve(
                sums[table].reshape(n_row, u_shard, width).astype(f32),
                down_order if table % 2 else up_order,
            )
            for table in range(tab_grp)
        ]
    )

    g_down, g_up, g_first, g_second, g_small = call(
        functools.partial(unpack_kernel, n_row),
        [
            jax.ShapeDtypeStruct((feat // n_row, rank), f32),
            jax.ShapeDtypeStruct((rank // n_row, feat), f32),
            jax.ShapeDtypeStruct((feat // n_row, hid), f32),
            jax.ShapeDtypeStruct((hid // n_row, hid), f32),
            jax.ShapeDtypeStruct((48, LANES), f32),
        ],
        [pltpu.VMEM((2, rows, LANES), bf16) for rows in (rows2, rows1, rows3)],
        7,
        "unpack",
    )(pos, *[mine for mine, _ in streams], *[theirs for _, theirs in streams])

    flat = g_small.reshape(-1)

    def part(start, length):
        share = length // n_row
        return lax.dynamic_slice(flat, (start * LANES + row_pos * share,), (share,))

    return (
        row_grads,
        g_down,
        g_up,
        part(24, feat),
        g_first,
        part(0, hid),
        g_second,
        part(8, hid),
        part(16, hid),
    )


def solution(mesh):
    in_specs = (
        P(("table", "row"), None),
        P(("table", "row"), None),
        P(("table", "row")),
        P(),
        P(),
        P(),
        P(),
        P(),
        P(),
        P(),
        P(),
        P("table", None, None),
    )
    out_specs = (
        P("table", "row", None),
        P("row", None),
        P("row", None),
        P("row"),
        P("row", None),
        P("row"),
        P("row", None),
        P("row"),
        P("row"),
    )
    return jax.shard_map(local, mesh=mesh, in_specs=in_specs, out_specs=out_specs, check_vma=False)
```

time: 678 us -> 192 us (0.28)
  other arithmetic: 361 us -> 7.52 us
  waiting for transfers between devices: 194 us -> 75.6 us
  blocking collectives: 65.8 us -> 0 us
  starting transfers between devices: 0.25 us -> 59.5 us
  Pallas kernels: 0 us -> 38.4 us
  matrix products: 24.5 us -> 0 us
  between operations: 15.8 us -> 0.99 us
  local copies, waits for them, and re-layouts: 16.7 us -> 8.41 us
    scatter-add x8 -> x0, other arithmetic: 357 us -> none  [local(): jax.ops.segment_sum(values, in_shard[table_pos, :, which], num_segments=u...]
    reduce_scatter x4 -> x0, waiting for transfers between devices: 156 us -> none  [the longest x1 94.1 us: local(): lax.psum_scatter(g_first, 'row', scatter_dimension=0, tiled=True)]
    ppermute x0 -> x41, waiting for transfers between devices: none -> 75.6 us  [the longest x10 35.3 us: halve(): got = lax.ppermute(sent, 'row', row_perm(bit))]
    ppermute x0 -> x41, starting transfers between devices: none -> 59.5 us  [the longest x9 22.6 us: sum_z(): got = lax.ppermute(pick(parts, z_pos ^ which, 0), 'table', z_perm(which))]
    pallas_call x0 -> x4, Pallas kernels: none -> 38.4 us  [the longest x1 15.3 us: local(): pl.pallas_call(functools.partial(count_kernel, n_row, block, hot, n_table...]
    all_gather x1 -> x0, waiting for transfers between devices: 37.4 us -> none  [local(): block_rows = lax.all_gather(received, 'row', axis=0, tiled=True)]
    all_to_all x1 -> x0, blocking collectives: 32.4 us -> none  [local(): lax.all_to_all(pooled_grad, 'table', split_axis=1, concat_axis=0, tiled=T...]
    dot_general x12 -> x0, matrix products: 24.5 us -> none  [the longest x1 6.86 us: dense_backward(): jnp.dot(crossed.T, delta_first, preferred_element_type=jnp.float32)]
  transfers between devices with their start and end apart: 6 -> 41, of which waited for: 4 -> 17; matrix products, arithmetic and copies ran while one was open for 56% -> 5% of each run, Pallas kernels for 0% -> 8%
where the time goes in v1:
time: 192 us; the launch traced here: 190 us
  waiting for transfers between devices  75.6 us (39%)
  starting transfers between devices  59.5 us (31%)
  Pallas kernels  38.4 us (20%)
  local copies, waits for them, and re-layouts  8.41 us (4%)
  other arithmetic  7.52 us (4%)
    ppermute x10, waiting for transfers between devices, halve(): got = lax.ppermute(sent, 'row', row_perm(bit))  35.3 us
    ppermute x9, starting transfers between devices, sum_z(): got = lax.ppermute(pick(parts, z_pos ^ which, 0), 'table', z_perm(which))  22.6 us
    ppermute x9, waiting for transfers between devices, sum_z(): got = lax.ppermute(pick(parts, z_pos ^ which, 0), 'table', z_perm(which))  17.1 us
    pallas_call x1, Pallas kernels, local(): pl.pallas_call(functools.partial(count_kernel, n_row, block, hot, n_table...  15.3 us
    ppermute x7, waiting for transfers between devices, local(): values.append(lax.ppermute(outs[2 + which], 'table', perm))  13.9 us
    ppermute x10, starting transfers between devices, halve(): got = lax.ppermute(sent, 'row', row_perm(bit))  13.8 us
    ppermute x9, starting transfers between devices, sum_z(): pieces.append(lax.ppermute(result, 'table', z_perm(which)))  13 us
    pallas_call x1, Pallas kernels, local(): call(functools.partial(front_kernel, n_row), [packed(rows2), packed(rows2...  11.7 us
  transfers between devices with their start and end apart: 41, of which 17 were waited for; matrix products, arithmetic and copies ran while one was open for 5% of the time, Pallas kernels for 8%

profile of v1, /device:TPU:0, one launch (start us, length us, event | category | flops | bytes accessed | tf_op | source)
XLA Modules:
  0.0 190.3 jit_solution(18399878894017511684)
XLA Ops:
  0.7 0.7 reshape.78.cross_bias
  1.4 0.8 copy-done
  5.0 11.7 %front.1 = (bf16[4,1024,128]{2,1,0:T(8,128)(2,1)S(1)}, bf16[4,1024,128]{2,1,0:T(8,128)(2,1)}, bf16[4,2176,128]{2,1,0:T(8,128)(2,1)}, bf16[4,2176,128]{2,1,0:T(8,...) custom-call(s32[3]{0:T(128)S(1)} %pad_add_fusion.pos, ...), custom_call_target="tpu_custom_call" | custom-call | tf_op jit(solution)/shard_map/front/pallas_call | solution.py:292
  16.7 8.2 %back.1 = (bf16[4,1216,128]{2,1,0:T(8,128)(2,1)}, bf16[4,1216,128]{2,1,0:T(8,128)(2,1)}, bf16[2,256,128]{2,1,0:T(8,128)(2,1)S(1)}, bf16[2,256,128]{2,1,0:T(8,128...) custom-call(s32[3]{0:T(128)S(1)} %pad_add_fusion.pos, ...), custom_call_target="tpu_custom_call" | custom-call | tf_op jit(solution)/shard_map/back/pallas_call | solution.py:323
  25.3 2.6 %collective-permute-start.1 = (bf16[2,256,128]{2,1,0:T(8,128)(2,1)S(1)}, bf16[2,256,128]{2,1,0:T(8,128)(2,1)S(1)}, u32[]{:S(2)}, u32[]{:S(2)}) collective-permute-start(bf16[2,256,128]{2,1,0:T(8,128)(2,1)S(1)} %get-tuple-element.36), channel_id=1, source_target_pairs={{0,8},{4,12},{8,0},{12,4},{16,24},{20,28},{24,16},{28,20},{1,9},{5... | collective-permute-start | bytes 393224 | tf_op jit(solution)/shard_map/ppermute | solution.py:341
  28.0 2.7 %collective-permute-start.3 = (bf16[2,256,128]{2,1,0:T(8,128)(2,1)S(1)}, bf16[2,256,128]{2,1,0:T(8,128)(2,1)S(1)}, u32[]{:S(2)}, u32[]{:S(2)}) collective-permute-start(bf16[2,256,128]{2,1,0:T(8,128)(2,1)S(1)} %get-tuple-element.38), channel_id=1, source_target_pairs={{0,16},{4,20},{8,24},{12,28},{16,0},{20,4},{24,8},{28,12},{1,17},{... | collective-permute-start | bytes 393224 | tf_op jit(solution)/shard_map/ppermute | solution.py:341
  30.7 3.5 %collective-permute-start.5 = (bf16[2,256,128]{2,1,0:T(8,128)(2,1)S(1)}, bf16[2,256,128]{2,1,0:T(8,128)(2,1)S(1)}, u32[]{:S(2)}, u32[]{:S(2)}) collective-permute-start(bf16[2,256,128]{2,1,0:T(8,128)(2,1)S(1)} %get-tuple-element.40), channel_id=1, source_target_pairs={{0,24},{4,28},{8,16},{12,20},{16,8},{20,12},{24,0},{28,4},{1,25},{... | collective-permute-start | bytes 393224 | tf_op jit(solution)/shard_map/ppermute | solution.py:341
  34.3 2.9 %collective-permute-done.1.rest_2_ = bf16[2,256,128]{2,1,0:T(8,128)(2,1)S(1)} collective-permute-done((bf16[2,256,128]{2,1,0:T(8,128)(2,1)S(1)}, bf16[2,256,128]{2,1,0:T(8,128)(2,1)S(1)}, u32[]{:S(2)}, u32[]{:S(2)}) %collective-permute-start.1) | collective-permute-done | bytes 131104 | tf_op jit(solution)/shard_map/ppermute | solution.py:341
  37.2 2.6 %collective-permute-done.2.rest_3_ = bf16[2,256,128]{2,1,0:T(8,128)(2,1)S(1)} collective-permute-done((bf16[2,256,128]{2,1,0:T(8,128)(2,1)S(1)}, bf16[2,256,128]{2,1,0:T(8,128)(2,1)S(1)}, u32[]{:S(2)}, u32[]{:S(2)}) %collective-permute-start.2) | collective-permute-done | bytes 131104 | tf_op jit(solution)/shard_map/ppermute | solution.py:341
  40.4 8.3 %collective-permute-done.4.rest_5_ = bf16[2,256,128]{2,1,0:T(8,128)(2,1)S(1)} collective-permute-done((bf16[2,256,128]{2,1,0:T(8,128)(2,1)S(1)}, bf16[2,256,128]{2,1,0:T(8,128)(2,1)S(1)}, u32[]{:S(2)}, u32[]{:S(2)}) %collective-permute-start.4) | collective-permute-done | bytes 131104 | tf_op jit(solution)/shard_map/ppermute | solution.py:341
  48.7 15.3 %counts.1 = bf16[2,2048,128]{2,1,0:T(8,128)(2,1)} custom-call(s32[3]{0:T(128)S(1)} %pad_add_fusion.pos, s32[2,4,8192]{2,1,0:T(4,128)S(1)} %bitcast.120, bf16[2,256,128]{2,1,0:T(8,128)(2,1)S(1)} %get-tuple-element.34.rest_0_, bf16[2,256,128]{2,1,0:T(8,128)(2,1)S(1)} %collective-permute-done.rest_1_, bf16[2,256,128]{2,1,0:T(8,128)(2,1)S(1)} %collective-permute-done.1.rest_2_, ...), custom_call_target="tpu_custom_call" | custom-call | tf_op jit(solution)/shard_map/counts/pallas_call | solution.py:382
  64.0 1.3 fusion.24
  65.4 1.6 collective-permute-start.9
  67.1 1.6 collective-permute-start.7
  68.7 5.1 %collective-permute-done.9 = bf16[2,512,128]{2,1,0:T(8,128)(2,1)S(1)} collective-permute-done((bf16[2,512,128]{2,1,0:T(8,128)(2,1)S(1)}, bf16[2,512,128]{2,1,0:T(8,128)(2,1)S(1)}, u32[]{:S(2)}, u32[]{:S(2)}) %collective-permute-start.9) | collective-permute-done | bytes 262176 | tf_op jit(solution)/shard_map/ppermute | solution.py:351
  73.9 1.6 collective-permute-start.10
  75.5 1.4 convert_add_fusion.2
  77.0 1.6 collective-permute-start.12
  79.3 12.0 %collective-permute-done.12 = bf16[2,1024,128]{2,1,0:T(8,128)(2,1)S(1)} collective-permute-done((bf16[2,1024,128]{2,1,0:T(8,128)(2,1)S(1)}, bf16[2,1024,128]{2,1,0:T(8,128)(2,1)S(1)}, u32[]{:S(2)}, u32[]{:S(2)}) %collective-permute-start.12) | collective-permute-done | bytes 524320 | tf_op jit(solution)/shard_map/ppermute | solution.py:351
  92.0 2.3 %convert_add_fusion = f32[4,2176,128]{2,1,0:T(8,128)S(1)} fusion(bf16[4,2176,128]{2,1,0:T(8,128)(2,1)} %collective-permute-done.20, bf16[4,2176,128]{2,1,0:T(8,128)(2,1)S(1)} %copy-done.6), kind=kLoop, calls=%fused_computation | loop fusion | flops 3342336 | bytes 8912896 | tf_op jit(solution)/shard_map/add | solution.py:377
  94.5 1.6 collective-permute-start.21
  96.1 1.5 convert_add_fusion.1
  97.8 1.6 collective-permute-start.30
  99.3 1.4 collective-permute-done.13
  100.8 5.7 %collective-permute-start.14 = (bf16[256,128]{1,0:T(8,128)(2,1)S(1)}, bf16[256,128]{1,0:T(8,128)(2,1)S(1)}, u32[]{:S(2)}, u32[]{:S(2)}) collective-permute-start(bf16[256,128]{1,0:T(8,128)(2,1)S(1)} %get-tuple-element.61), channel_id=1, source_target_pairs={{0,8},{4,12},{8,0},{12,4},{16,24},{20,28},{24,16},{28,20},{1,9},{5... | collective-permute-start | bytes 196616 | tf_op jit(solution)/shard_map/ppermute | solution.py:362
  106.5 4.1 %collective-permute-start.16 = (bf16[256,128]{1,0:T(8,128)(2,1)S(1)}, bf16[256,128]{1,0:T(8,128)(2,1)S(1)}, u32[]{:S(2)}, u32[]{:S(2)}) collective-permute-start(bf16[256,128]{1,0:T(8,128)(2,1)S(1)} %get-tuple-element.62), channel_id=1, source_target_pairs={{0,24},{4,28},{8,16},{12,20},{16,8},{20,12},{24,0},{28,4},{1,25},{... | collective-permute-start | bytes 196616 | tf_op jit(solution)/shard_map/ppermute | solution.py:362
  110.6 9.7 %collective-permute-done.21 = bf16[2,2176,128]{2,1,0:T(8,128)(2,1)S(1)} collective-permute-done((bf16[2,2176,128]{2,1,0:T(8,128)(2,1)S(1)}, bf16[2,2176,128]{2,1,0:T(8,128)(2,1)S(1)}, u32[]{:S(2)}, u32[]{:S(2)}) %collective-permute-start.21) | collective-permute-done | bytes 1114144 | tf_op jit(solution)/shard_map/ppermute | solution.py:351
  120.2 8.7 %collective-permute-start.15 = (bf16[256,128]{1,0:T(8,128)(2,1)S(1)}, bf16[256,128]{1,0:T(8,128)(2,1)S(1)}, u32[]{:S(2)}, u32[]{:S(2)}) collective-permute-start(bf16[256,128]{1,0:T(8,128)(2,1)S(1)} %get-tuple-element.63), channel_id=1, source_target_pairs={{0,16},{4,20},{8,24},{12,28},{16,0},{20,4},{24,8},{28,12},{1,17},{... | collective-permute-start | bytes 196616 | tf_op jit(solution)/shard_map/ppermute | solution.py:362
  129.3 1.6 collective-permute-start.22
  131.0 1.6 collective-permute-start.31
  132.7 7.2 %collective-permute-done.22 = bf16[2176,128]{1,0:T(8,128)(2,1)S(1)} collective-permute-done((bf16[2176,128]{1,0:T(8,128)(2,1)S(1)}, bf16[2176,128]{1,0:T(8,128)(2,1)S(1)}, u32[]{:S(2)}, u32[]{:S(2)}) %collective-permute-start.22) | collective-permute-done | bytes 557088 | tf_op jit(solution)/shard_map/ppermute | solution.py:351
  140.2 1.7 collective-permute-start.25
  141.9 1.7 collective-permute-start.24
  143.7 5.3 %collective-permute-done.23 = bf16[544,128]{1,0:T(8,128)(2,1)S(1)} collective-permute-done((bf16[544,128]{1,0:T(8,128)(2,1)S(1)}, bf16[544,128]{1,0:T(8,128)(2,1)S(1)}, u32[]{:S(2)}, u32[]{:S(2)}) %collective-permute-start.23) | collective-permute-done | bytes 139296 | tf_op jit(solution)/shard_map/ppermute | solution.py:362
  149.6 9.6 %collective-permute-done.24 = bf16[544,128]{1,0:T(8,128)(2,1)S(1)} collective-permute-done((bf16[544,128]{1,0:T(8,128)(2,1)S(1)}, bf16[544,128]{1,0:T(8,128)(2,1)S(1)}, u32[]{:S(2)}, u32[]{:S(2)}) %collective-permute-start.24) | collective-permute-done | bytes 139296 | tf_op jit(solution)/shard_map/ppermute | solution.py:362
  159.4 3.0 %collective-permute-start.27 = (bf16[544,128]{1,0:T(8,128)(2,1)S(1)}, bf16[544,128]{1,0:T(8,128)(2,1)S(1)}, u32[]{:S(2)}, u32[]{:S(2)}) collective-permute-start(bf16[544,128]{1,0:T(8,128)(2,1)S(1)} %fusion.10), channel_id=1, source_target_pairs={{0,16},{4,20},{8,24},{12,28},{16,0},{20,4},{24,8},{28,12},{1,17},{... | collective-permute-start | bytes 417800 | tf_op jit(solution)/shard_map/ppermute | solution.py:367
  162.4 2.2 %collective-permute-done.33 = bf16[304,128]{1,0:T(8,128)(2,1)S(1)} collective-permute-done((bf16[304,128]{1,0:T(8,128)(2,1)S(1)}, bf16[304,128]{1,0:T(8,128)(2,1)S(1)}, u32[]{:S(2)}, u32[]{:S(2)}) %collective-permute-start.33) | collective-permute-done | bytes 77856 | tf_op jit(solution)/shard_map/ppermute | solution.py:362
  164.6 3.0 %collective-permute-done.28 = bf16[544,128]{1,0:T(8,128)(2,1)S(1)} collective-permute-done((bf16[544,128]{1,0:T(8,128)(2,1)S(1)}, bf16[544,128]{1,0:T(8,128)(2,1)S(1)}, u32[]{:S(2)}, u32[]{:S(2)}) %collective-permute-start.28) | collective-permute-done | bytes 139296 | tf_op jit(solution)/shard_map/ppermute | solution.py:367
  167.6 5.4 %collective-permute-start.18 = (bf16[256,128]{1,0:T(8,128)(2,1)S(1)}, bf16[256,128]{1,0:T(8,128)(2,1)S(1)}, u32[]{:S(2)}, u32[]{:S(2)}) collective-permute-start(bf16[256,128]{1,0:T(8,128)(2,1)S(1)} %fusion.23), channel_id=1, source_target_pairs={{0,16},{4,20},{8,24},{12,28},{16,0},{20,4},{24,8},{28,12},{1,17},{... | collective-permute-start | bytes 196616 | tf_op jit(solution)/shard_map/ppermute | solution.py:367
  173.0 1.6 collective-permute-done.27
  174.6 1.7 collective-permute-start.37
  176.3 1.9 collective-permute-start.36
  178.2 0.9 collective-permute-start.35
  179.2 1.7 collective-permute-done.37
  180.9 2.2 %collective-permute-done.36 = bf16[304,128]{1,0:T(8,128)(2,1)S(1)} collective-permute-done((bf16[304,128]{1,0:T(8,128)(2,1)S(1)}, bf16[304,128]{1,0:T(8,128)(2,1)S(1)}, u32[]{:S(2)}, u32[]{:S(2)}) %collective-permute-start.36) | collective-permute-done | bytes 77856 | tf_op jit(solution)/shard_map/ppermute | solution.py:367
  183.4 0.8 pad_maximum_fusion.1
  184.9 0.8 copy-done.9
  185.7 3.3 %unpack.1 = (f32[544,256]{1,0:T(8,128)}, f32[64,2176]{1,0:T(8,128)}, f32[544,1024]{1,0:T(8,128)}, f32[256,1024]{1,0:T(8,128)}, f32[48,128]{1,0:T(8,128)S(1)}) custom-call(s32[3]{0:T(128)S(1)} %pad_add_fusion.pos, bf16[4,256,128]{2,1,0:T(8,128)(2,1)S(1)} %pad_maximum_fusion.3.refs_0_, bf16[4,544,128]{2,1,0:T(8,128)(2,1)S(1)} %pad_maximum_fusion.refs_1_, ...), custom_call_target="tpu_custom_call" | custom-call | tf_op jit(solution)/shard_map/unpack/pallas_call | solution.py:401
  (98 shorter events, 10.2 us)
Async XLA Ops:
  1.4 0.8 copy-start
  2.3 0.7 copy-start.2
  16.7 32.0 %copy-start.1 = (s32[2,8192,4]{1,2,0:T(4,128)S(1)}, s32[2,8192,4]{1,2,0:T(4,128)}, u32[]{:S(2)}) copy-start(s32[2,8192,4]{1,2,0:T(4,128)} %param.23) | copy-start | bytes 786436
  24.8 5.9 %collective-permute-start = (bf16[2,256,128]{2,1,0:T(8,128)(2,1)S(1)}, bf16[2,256,128]{2,1,0:T(8,128)(2,1)S(1)}, u32[]{:S(2)}, u32[]{:S(2)}) collective-permute-start(bf16[2,256,128]{2,1,0:T(8,128)(2,1)S(1)} %get-tuple-element.35), channel_id=1, source_target_pairs={{0,4},{4,0},{8,12},{12,8},{16,20},{20,16},{24,28},{28,24},{1,5},{5... | collective-permute-start | bytes 393224 | tf_op jit(solution)/shard_map/ppermute | solution.py:341
  25.3 11.9 %collective-permute-start.1 = (bf16[2,256,128]{2,1,0:T(8,128)(2,1)S(1)}, bf16[2,256,128]{2,1,0:T(8,128)(2,1)S(1)}, u32[]{:S(2)}, u32[]{:S(2)}) collective-permute-start(bf16[2,256,128]{2,1,0:T(8,128)(2,1)S(1)} %get-tuple-element.36), channel_id=1, source_target_pairs={{0,8},{4,12},{8,0},{12,4},{16,24},{20,28},{24,16},{28,20},{1,9},{5... | collective-permute-start | bytes 393224 | tf_op jit(solution)/shard_map/ppermute | solution.py:341
  27.9 12.0 %collective-permute-start.2 = (bf16[2,256,128]{2,1,0:T(8,128)(2,1)S(1)}, bf16[2,256,128]{2,1,0:T(8,128)(2,1)S(1)}, u32[]{:S(2)}, u32[]{:S(2)}) collective-permute-start(bf16[2,256,128]{2,1,0:T(8,128)(2,1)S(1)} %get-tuple-element.37), channel_id=1, source_target_pairs={{0,12},{4,8},{8,4},{12,0},{16,28},{20,24},{24,20},{28,16},{1,13},{... | collective-permute-start | bytes 393224 | tf_op jit(solution)/shard_map/ppermute | solution.py:341
  28.0 12.2 %collective-permute-start.3 = (bf16[2,256,128]{2,1,0:T(8,128)(2,1)S(1)}, bf16[2,256,128]{2,1,0:T(8,128)(2,1)S(1)}, u32[]{:S(2)}, u32[]{:S(2)}) collective-permute-start(bf16[2,256,128]{2,1,0:T(8,128)(2,1)S(1)} %get-tuple-element.38), channel_id=1, source_target_pairs={{0,16},{4,20},{8,24},{12,28},{16,0},{20,4},{24,8},{28,12},{1,17},{... | collective-permute-start | bytes 393224 | tf_op jit(solution)/shard_map/ppermute | solution.py:341
  30.7 17.9 %collective-permute-start.4 = (bf16[2,256,128]{2,1,0:T(8,128)(2,1)S(1)}, bf16[2,256,128]{2,1,0:T(8,128)(2,1)S(1)}, u32[]{:S(2)}, u32[]{:S(2)}) collective-permute-start(bf16[2,256,128]{2,1,0:T(8,128)(2,1)S(1)} %get-tuple-element.39), channel_id=1, source_target_pairs={{0,20},{4,16},{8,28},{12,24},{16,4},{20,0},{24,12},{28,8},{1,21},{... | collective-permute-start | bytes 393224 | tf_op jit(solution)/shard_map/ppermute | solution.py:341
  30.7 17.9 %collective-permute-start.5 = (bf16[2,256,128]{2,1,0:T(8,128)(2,1)S(1)}, bf16[2,256,128]{2,1,0:T(8,128)(2,1)S(1)}, u32[]{:S(2)}, u32[]{:S(2)}) collective-permute-start(bf16[2,256,128]{2,1,0:T(8,128)(2,1)S(1)} %get-tuple-element.40), channel_id=1, source_target_pairs={{0,24},{4,28},{8,16},{12,20},{16,8},{20,12},{24,0},{28,4},{1,25},{... | collective-permute-start | bytes 393224 | tf_op jit(solution)/shard_map/ppermute | solution.py:341
  37.2 11.4 %collective-permute-start.6 = (bf16[2,256,128]{2,1,0:T(8,128)(2,1)S(1)}, bf16[2,256,128]{2,1,0:T(8,128)(2,1)S(1)}, u32[]{:S(2)}, u32[]{:S(2)}) collective-permute-start(bf16[2,256,128]{2,1,0:T(8,128)(2,1)S(1)} %get-tuple-element.41), channel_id=1, source_target_pairs={{0,28},{4,24},{8,20},{12,16},{16,12},{20,8},{24,4},{28,0},{1,29},{... | collective-permute-start | bytes 393224 | tf_op jit(solution)/shard_map/ppermute | solution.py:341
  39.9 35.6 %collective-permute-start.11 = (bf16[4,1024,128]{2,1,0:T(8,128)(2,1)S(1)}, bf16[4,1024,128]{2,1,0:T(8,128)(2,1)}, u32[]{:S(2)}, u32[]{:S(2)}) collective-permute-start(bf16[4,1024,128]{2,1,0:T(8,128)(2,1)S(1)} %get-tuple-element.43), channel_id=1, source_target_pairs={{0,4},{4,0},{8,12},{12,8},{16,20},{20,16},{24,28},{28,24},{1,5},{5... | collective-permute-start | bytes 3145736 | tf_op jit(solution)/shard_map/ppermute | solution.py:320
  40.2 51.8 %collective-permute-start.20 = (bf16[4,2176,128]{2,1,0:T(8,128)(2,1)}, bf16[4,2176,128]{2,1,0:T(8,128)(2,1)}, u32[]{:S(2)}, u32[]{:S(2)}) collective-permute-start(bf16[4,2176,128]{2,1,0:T(8,128)(2,1)} %get-tuple-element.45), channel_id=1, source_target_pairs={{0,4},{4,0},{8,12},{12,8},{16,20},{20,16},{24,28},{28,24},{1,5},{5... | collective-permute-start | bytes 6684680 | tf_op jit(solution)/shard_map/ppermute | solution.py:321
  65.4 8.4 %collective-permute-start.9 = (bf16[2,512,128]{2,1,0:T(8,128)(2,1)S(1)}, bf16[2,512,128]{2,1,0:T(8,128)(2,1)S(1)}, u32[]{:S(2)}, u32[]{:S(2)}) collective-permute-start(bf16[2,512,128]{2,1,0:T(8,128)(2,1)S(1)} %fusion.11), channel_id=1, source_target_pairs={{0,2},{1,3},{2,0},{3,1},{4,6},{5,7},{6,4},{7,5},{8,10},{9,11},{10,... | collective-permute-start | bytes 786440 | tf_op jit(solution)/shard_map/ppermute | solution.py:351
  67.0 29.1 %collective-permute-start.29 = (bf16[4,1216,128]{2,1,0:T(8,128)(2,1)}, bf16[4,1216,128]{2,1,0:T(8,128)(2,1)}, u32[]{:S(2)}, u32[]{:S(2)}) collective-permute-start(bf16[4,1216,128]{2,1,0:T(8,128)(2,1)} %get-tuple-element.47), channel_id=1, source_target_pairs={{0,4},{4,0},{8,12},{12,8},{16,20},{20,16},{24,28},{28,24},{1,5},{5... | collective-permute-start | bytes 3735560 | tf_op jit(solution)/shard_map/ppermute | solution.py:337
  67.0 8.5 %copy-start.8 = (bf16[4,1024,128]{2,1,0:T(8,128)(2,1)S(1)}, bf16[4,1024,128]{2,1,0:T(8,128)(2,1)}, u32[]{:S(2)}) copy-start(bf16[4,1024,128]{2,1,0:T(8,128)(2,1)} %get-tuple-element.42) | copy-start | bytes 3145732
  67.1 11.4 %collective-permute-start.7 = (bf16[2,512,128]{2,1,0:T(8,128)(2,1)S(1)}, bf16[2,512,128]{2,1,0:T(8,128)(2,1)S(1)}, u32[]{:S(2)}, u32[]{:S(2)}) collective-permute-start(bf16[2,512,128]{2,1,0:T(8,128)(2,1)S(1)} %fusion.13), channel_id=1, source_target_pairs={{0,1},{1,0},{2,3},{3,2},{4,5},{5,4},{6,7},{7,6},{8,9},{9,8},{10,11... | collective-permute-start | bytes 786440 | tf_op jit(solution)/shard_map/ppermute | solution.py:351
  73.9 5.4 %collective-permute-start.10 = (bf16[512,128]{1,0:T(8,128)(2,1)S(1)}, bf16[512,128]{1,0:T(8,128)(2,1)S(1)}, u32[]{:S(2)}, u32[]{:S(2)}) collective-permute-start(bf16[512,128]{1,0:T(8,128)(2,1)S(1)} %fusion.20), channel_id=1, source_target_pairs={{0,1},{1,0},{2,3},{3,2},{4,5},{5,4},{6,7},{7,6},{8,9},{9,8},{10,11... | collective-permute-start | bytes 393224 | tf_op jit(solution)/shard_map/ppermute | solution.py:351
  77.0 14.3 %collective-permute-start.12 = (bf16[2,1024,128]{2,1,0:T(8,128)(2,1)S(1)}, bf16[2,1024,128]{2,1,0:T(8,128)(2,1)S(1)}, u32[]{:S(2)}, u32[]{:S(2)}) collective-permute-start(bf16[2,1024,128]{2,1,0:T(8,128)(2,1)S(1)} %fusion.5), channel_id=1, source_target_pairs={{0,2},{1,3},{2,0},{3,1},{4,6},{5,7},{6,4},{7,5},{8,10},{9,11},{10,... | collective-permute-start | bytes 1572872 | tf_op jit(solution)/shard_map/ppermute | solution.py:351
  78.6 13.4 %copy-start.6 = (bf16[4,2176,128]{2,1,0:T(8,128)(2,1)S(1)}, bf16[4,2176,128]{2,1,0:T(8,128)(2,1)}, u32[]{:S(2)}) copy-start(bf16[4,2176,128]{2,1,0:T(8,128)(2,1)} %get-tuple-element.44) | copy-start | bytes 6684676
  78.7 104.7 %collective-permute-start.8 = (bf16[512,128]{1,0:T(8,128)(2,1)S(1)}, bf16[512,128]{1,0:T(8,128)(2,1)S(1)}, u32[]{:S(2)}, u32[]{:S(2)}) collective-permute-start(bf16[512,128]{1,0:T(8,128)(2,1)S(1)} %fusion.19), channel_id=1, source_target_pairs={{0,2},{1,3},{2,0},{3,1},{4,6},{5,7},{6,4},{7,5},{8,10},{9,11},{10,... | collective-permute-start | bytes 393224 | tf_op jit(solution)/shard_map/ppermute | solution.py:351
  91.4 9.3 %collective-permute-start.13 = (bf16[1024,128]{1,0:T(8,128)(2,1)S(1)}, bf16[1024,128]{1,0:T(8,128)(2,1)S(1)}, u32[]{:S(2)}, u32[]{:S(2)}) collective-permute-start(bf16[1024,128]{1,0:T(8,128)(2,1)S(1)} %fusion.12), channel_id=1, source_target_pairs={{0,1},{1,0},{2,3},{3,2},{4,5},{5,4},{6,7},{7,6},{8,9},{9,8},{10,11... | collective-permute-start | bytes 786440 | tf_op jit(solution)/shard_map/ppermute | solution.py:351
  94.3 1.8 copy-start.7
  94.5 25.7 %collective-permute-start.21 = (bf16[2,2176,128]{2,1,0:T(8,128)(2,1)S(1)}, bf16[2,2176,128]{2,1,0:T(8,128)(2,1)S(1)}, u32[]{:S(2)}, u32[]{:S(2)}) collective-permute-start(bf16[2,2176,128]{2,1,0:T(8,128)(2,1)S(1)} %fusion), channel_id=1, source_target_pairs={{0,1},{1,0},{2,3},{3,2},{4,5},{5,4},{6,7},{7,6},{8,9},{9,8},{10,11... | collective-permute-start | bytes 3342344 | tf_op jit(solution)/shard_map/ppermute | solution.py:351
  97.8 31.6 %collective-permute-start.30 = (bf16[2,1216,128]{2,1,0:T(8,128)(2,1)S(1)}, bf16[2,1216,128]{2,1,0:T(8,128)(2,1)S(1)}, u32[]{:S(2)}, u32[]{:S(2)}) collective-permute-start(bf16[2,1216,128]{2,1,0:T(8,128)(2,1)S(1)} %fusion.2), channel_id=1, source_target_pairs={{0,2},{1,3},{2,0},{3,1},{4,6},{5,7},{6,4},{7,5},{8,10},{9,11},{10,... | collective-permute-start | bytes 1867784 | tf_op jit(solution)/shard_map/ppermute | solution.py:351
  100.8 30.2 %collective-permute-start.14 = (bf16[256,128]{1,0:T(8,128)(2,1)S(1)}, bf16[256,128]{1,0:T(8,128)(2,1)S(1)}, u32[]{:S(2)}, u32[]{:S(2)}) collective-permute-start(bf16[256,128]{1,0:T(8,128)(2,1)S(1)} %get-tuple-element.61), channel_id=1, source_target_pairs={{0,8},{4,12},{8,0},{12,4},{16,24},{20,28},{24,16},{28,20},{1,9},{5... | collective-permute-start | bytes 196616 | tf_op jit(solution)/shard_map/ppermute | solution.py:362
  106.5 26.1 %collective-permute-start.16 = (bf16[256,128]{1,0:T(8,128)(2,1)S(1)}, bf16[256,128]{1,0:T(8,128)(2,1)S(1)}, u32[]{:S(2)}, u32[]{:S(2)}) collective-permute-start(bf16[256,128]{1,0:T(8,128)(2,1)S(1)} %get-tuple-element.62), channel_id=1, source_target_pairs={{0,24},{4,28},{8,16},{12,20},{16,8},{20,12},{24,0},{28,4},{1,25},{... | collective-permute-start | bytes 196616 | tf_op jit(solution)/shard_map/ppermute | solution.py:362
  120.2 12.4 %collective-permute-start.15 = (bf16[256,128]{1,0:T(8,128)(2,1)S(1)}, bf16[256,128]{1,0:T(8,128)(2,1)S(1)}, u32[]{:S(2)}, u32[]{:S(2)}) collective-permute-start(bf16[256,128]{1,0:T(8,128)(2,1)S(1)} %get-tuple-element.63), channel_id=1, source_target_pairs={{0,16},{4,20},{8,24},{12,28},{16,0},{20,4},{24,8},{28,12},{1,17},{... | collective-permute-start | bytes 196616 | tf_op jit(solution)/shard_map/ppermute | solution.py:362
  129.3 10.6 %collective-permute-start.22 = (bf16[2176,128]{1,0:T(8,128)(2,1)S(1)}, bf16[2176,128]{1,0:T(8,128)(2,1)S(1)}, u32[]{:S(2)}, u32[]{:S(2)}) collective-permute-start(bf16[2176,128]{1,0:T(8,128)(2,1)S(1)} %fusion.4), channel_id=1, source_target_pairs={{0,2},{1,3},{2,0},{3,1},{4,6},{5,7},{6,4},{7,5},{8,10},{9,11},{10,... | collective-permute-start | bytes 1671176 | tf_op jit(solution)/shard_map/ppermute | solution.py:351
  131.0 10.8 %collective-permute-start.31 = (bf16[1216,128]{1,0:T(8,128)(2,1)S(1)}, bf16[1216,128]{1,0:T(8,128)(2,1)S(1)}, u32[]{:S(2)}, u32[]{:S(2)}) collective-permute-start(bf16[1216,128]{1,0:T(8,128)(2,1)S(1)} %fusion.7), channel_id=1, source_target_pairs={{0,1},{1,0},{2,3},{3,2},{4,5},{5,4},{6,7},{7,6},{8,9},{9,8},{10,11... | collective-permute-start | bytes 933896 | tf_op jit(solution)/shard_map/ppermute | solution.py:351
  132.7 43.7 %collective-permute-start.19 = (bf16[256,128]{1,0:T(8,128)(2,1)S(1)}, bf16[256,128]{1,0:T(8,128)(2,1)S(1)}, u32[]{:S(2)}, u32[]{:S(2)}) collective-permute-start(bf16[256,128]{1,0:T(8,128)(2,1)S(1)} %fusion.23), channel_id=1, source_target_pairs={{0,24},{4,28},{8,16},{12,20},{16,8},{20,12},{24,0},{28,4},{1,25},{... | collective-permute-start | bytes 196616 | tf_op jit(solution)/shard_map/ppermute | solution.py:367
  140.1 8.9 %collective-permute-start.23 = (bf16[544,128]{1,0:T(8,128)(2,1)S(1)}, bf16[544,128]{1,0:T(8,128)(2,1)S(1)}, u32[]{:S(2)}, u32[]{:S(2)}) collective-permute-start(bf16[544,128]{1,0:T(8,128)(2,1)S(1)} %get-tuple-element.55), channel_id=1, source_target_pairs={{0,8},{4,12},{8,0},{12,4},{16,24},{20,28},{24,16},{28,20},{1,9},{5... | collective-permute-start | bytes 417800 | tf_op jit(solution)/shard_map/ppermute | solution.py:362
  140.2 8.9 %collective-permute-start.25 = (bf16[544,128]{1,0:T(8,128)(2,1)S(1)}, bf16[544,128]{1,0:T(8,128)(2,1)S(1)}, u32[]{:S(2)}, u32[]{:S(2)}) collective-permute-start(bf16[544,128]{1,0:T(8,128)(2,1)S(1)} %get-tuple-element.56), channel_id=1, source_target_pairs={{0,24},{4,28},{8,16},{12,20},{16,8},{20,12},{24,0},{28,4},{1,25},{... | collective-permute-start | bytes 417800 | tf_op jit(solution)/shard_map/ppermute | solution.py:362
  141.9 17.3 %collective-permute-start.24 = (bf16[544,128]{1,0:T(8,128)(2,1)S(1)}, bf16[544,128]{1,0:T(8,128)(2,1)S(1)}, u32[]{:S(2)}, u32[]{:S(2)}) collective-permute-start(bf16[544,128]{1,0:T(8,128)(2,1)S(1)} %get-tuple-element.57), channel_id=1, source_target_pairs={{0,16},{4,20},{8,24},{12,28},{16,0},{20,4},{24,8},{28,12},{1,17},{... | collective-permute-start | bytes 417800 | tf_op jit(solution)/shard_map/ppermute | solution.py:362
  149.0 10.3 %collective-permute-start.32 = (bf16[304,128]{1,0:T(8,128)(2,1)S(1)}, bf16[304,128]{1,0:T(8,128)(2,1)S(1)}, u32[]{:S(2)}, u32[]{:S(2)}) collective-permute-start(bf16[304,128]{1,0:T(8,128)(2,1)S(1)} %get-tuple-element.58), channel_id=1, source_target_pairs={{0,8},{4,12},{8,0},{12,4},{16,24},{20,28},{24,16},{28,20},{1,9},{5... | collective-permute-start | bytes 233480 | tf_op jit(solution)/shard_map/ppermute | solution.py:362
  149.0 10.4 %collective-permute-start.34 = (bf16[304,128]{1,0:T(8,128)(2,1)S(1)}, bf16[304,128]{1,0:T(8,128)(2,1)S(1)}, u32[]{:S(2)}, u32[]{:S(2)}) collective-permute-start(bf16[304,128]{1,0:T(8,128)(2,1)S(1)} %get-tuple-element.59), channel_id=1, source_target_pairs={{0,24},{4,28},{8,16},{12,20},{16,8},{20,12},{24,0},{28,4},{1,25},{... | collective-permute-start | bytes 233480 | tf_op jit(solution)/shard_map/ppermute | solution.py:362
  159.2 5.3 %collective-permute-start.33 = (bf16[304,128]{1,0:T(8,128)(2,1)S(1)}, bf16[304,128]{1,0:T(8,128)(2,1)S(1)}, u32[]{:S(2)}, u32[]{:S(2)}) collective-permute-start(bf16[304,128]{1,0:T(8,128)(2,1)S(1)} %get-tuple-element.60), channel_id=1, source_target_pairs={{0,16},{4,20},{8,24},{12,28},{16,0},{20,4},{24,8},{28,12},{1,17},{... | collective-permute-start | bytes 233480 | tf_op jit(solution)/shard_map/ppermute | solution.py:362
  159.3 8.3 %collective-permute-start.28 = (bf16[544,128]{1,0:T(8,128)(2,1)S(1)}, bf16[544,128]{1,0:T(8,128)(2,1)S(1)}, u32[]{:S(2)}, u32[]{:S(2)}) collective-permute-start(bf16[544,128]{1,0:T(8,128)(2,1)S(1)} %fusion.10), channel_id=1, source_target_pairs={{0,24},{4,28},{8,16},{12,20},{16,8},{20,12},{24,0},{28,4},{1,25},{... | collective-permute-start | bytes 417800 | tf_op jit(solution)/shard_map/ppermute | solution.py:367
  159.4 15.2 %collective-permute-start.27 = (bf16[544,128]{1,0:T(8,128)(2,1)S(1)}, bf16[544,128]{1,0:T(8,128)(2,1)S(1)}, u32[]{:S(2)}, u32[]{:S(2)}) collective-permute-start(bf16[544,128]{1,0:T(8,128)(2,1)S(1)} %fusion.10), channel_id=1, source_target_pairs={{0,16},{4,20},{8,24},{12,28},{16,0},{20,4},{24,8},{28,12},{1,17},{... | collective-permute-start | bytes 417800 | tf_op jit(solution)/shard_map/ppermute | solution.py:367
  164.6 10.0 %collective-permute-start.26 = (bf16[544,128]{1,0:T(8,128)(2,1)S(1)}, bf16[544,128]{1,0:T(8,128)(2,1)S(1)}, u32[]{:S(2)}, u32[]{:S(2)}) collective-permute-start(bf16[544,128]{1,0:T(8,128)(2,1)S(1)} %fusion.10), channel_id=1, source_target_pairs={{0,8},{4,12},{8,0},{12,4},{16,24},{20,28},{24,16},{28,20},{1,9},{5... | collective-permute-start | bytes 417800 | tf_op jit(solution)/shard_map/ppermute | solution.py:367
  167.6 10.6 %collective-permute-start.18 = (bf16[256,128]{1,0:T(8,128)(2,1)S(1)}, bf16[256,128]{1,0:T(8,128)(2,1)S(1)}, u32[]{:S(2)}, u32[]{:S(2)}) collective-permute-start(bf16[256,128]{1,0:T(8,128)(2,1)S(1)} %fusion.23), channel_id=1, source_target_pairs={{0,16},{4,20},{8,24},{12,28},{16,0},{20,4},{24,8},{28,12},{1,17},{... | collective-permute-start | bytes 196616 | tf_op jit(solution)/shard_map/ppermute | solution.py:367
  174.6 4.6 %collective-permute-start.17 = (bf16[256,128]{1,0:T(8,128)(2,1)S(1)}, bf16[256,128]{1,0:T(8,128)(2,1)S(1)}, u32[]{:S(2)}, u32[]{:S(2)}) collective-permute-start(bf16[256,128]{1,0:T(8,128)(2,1)S(1)} %fusion.23), channel_id=1, source_target_pairs={{0,8},{4,12},{8,0},{12,4},{16,24},{20,28},{24,16},{28,20},{1,9},{5... | collective-permute-start | bytes 196616 | tf_op jit(solution)/shard_map/ppermute | solution.py:367
  174.6 6.3 %collective-permute-start.37 = (bf16[304,128]{1,0:T(8,128)(2,1)S(1)}, bf16[304,128]{1,0:T(8,128)(2,1)S(1)}, u32[]{:S(2)}, u32[]{:S(2)}) collective-permute-start(bf16[304,128]{1,0:T(8,128)(2,1)S(1)} %fusion.18), channel_id=1, source_target_pairs={{0,24},{4,28},{8,16},{12,20},{16,8},{20,12},{24,0},{28,4},{1,25},{... | collective-permute-start | bytes 233480 | tf_op jit(solution)/shard_map/ppermute | solution.py:367
  176.3 6.7 %collective-permute-start.36 = (bf16[304,128]{1,0:T(8,128)(2,1)S(1)}, bf16[304,128]{1,0:T(8,128)(2,1)S(1)}, u32[]{:S(2)}, u32[]{:S(2)}) collective-permute-start(bf16[304,128]{1,0:T(8,128)(2,1)S(1)} %fusion.18), channel_id=1, source_target_pairs={{0,16},{4,20},{8,24},{12,28},{16,0},{20,4},{24,8},{28,12},{1,17},{... | collective-permute-start | bytes 233480 | tf_op jit(solution)/shard_map/ppermute | solution.py:367
  178.2 5.0 %collective-permute-start.35 = (bf16[304,128]{1,0:T(8,128)(2,1)S(1)}, bf16[304,128]{1,0:T(8,128)(2,1)S(1)}, u32[]{:S(2)}, u32[]{:S(2)}) collective-permute-start(bf16[304,128]{1,0:T(8,128)(2,1)S(1)} %fusion.18), channel_id=1, source_target_pairs={{0,8},{4,12},{8,0},{12,4},{16,24},{20,28},{24,16},{28,20},{1,9},{5... | collective-permute-start | bytes 233480 | tf_op jit(solution)/shard_map/ppermute | solution.py:367
  179.1 5.8 %collective-permute-start.39 = (bf16[4,544,128]{2,1,0:T(8,128)(2,1)S(1)}, bf16[4,544,128]{2,1,0:T(8,128)(2,1)S(1)}, u32[]{:S(2)}, u32[]{:S(2)}) collective-permute-start(bf16[4,544,128]{2,1,0:T(8,128)(2,1)S(1)} %pad_maximum_fusion.refs_1_), channel_id=1, source_target_pairs={{0,4},{4,0},{8,12},{12,8},{16,20},{20,16},{24,28},{28,24},{1,5},{5... | collective-permute-start | bytes 1671176 | tf_op jit(solution)/shard_map/ppermute | solution.py:369
  180.9 3.3 %collective-permute-start.38 = (bf16[4,256,128]{2,1,0:T(8,128)(2,1)S(1)}, bf16[4,256,128]{2,1,0:T(8,128)(2,1)S(1)}, u32[]{:S(2)}, u32[]{:S(2)}) collective-permute-start(bf16[4,256,128]{2,1,0:T(8,128)(2,1)S(1)} %pad_maximum_fusion.3.refs_0_), channel_id=1, source_target_pairs={{0,4},{4,0},{8,12},{12,8},{16,20},{20,16},{24,28},{28,24},{1,5},{5... | collective-permute-start | bytes 786440 | tf_op jit(solution)/shard_map/ppermute | solution.py:369
  183.2 1.7 collective-permute-start.40
  184.9 0.8 copy-start.9
  (3 other events, 2.1 us)

commit v2 on v1

v2 whole, which is shorter than its diff:
```python
import functools

import jax
import jax.numpy as jnp
from jax import lax
from jax.experimental import pallas as pl
from jax.experimental.pallas import tpu as pltpu
from jax.sharding import PartitionSpec as P

loss_scale = 16.0
LANES = 128
VMEM_BYTES = 52 * 1024 * 1024
bf16 = jnp.bfloat16
f32 = jnp.float32


def round_up(value, unit):
    return -(-value // unit) * unit


def matmul(left, right):
    return jnp.dot(left, right, preferred_element_type=f32)


def matmul_rt(left, right):
    return lax.dot_general(left, right, (((1,), (1,)), ((), ())), preferred_element_type=f32)


def reverse_bits(value, bits):
    out = 0
    for bit in range(bits):
        out = out | (((value >> bit) & 1) << (bits - 1 - bit))
    return out


def places_of(z_pos, n_z):
    bits = n_z.bit_length() - 1
    return [reverse_bits(z_pos ^ quarter, bits) for quarter in range(n_z)]


def put_blocks(ref, row_pos, places, offset, value):
    shards, rows_q = ref.shape[0], ref.shape[2]
    rows = value.shape[0] // shards
    step = round_up(rows, 16)
    blocks = value.shape[1] // LANES
    for shard in range(shards):
        slot = shard ^ row_pos
        for block in range(blocks):
            done = 0
            while done < rows:
                quarter, at = divmod(offset + block * step + done, rows_q)
                length = min(rows - done, rows_q - at)
                ref[slot, places[quarter], at : at + length, :] = value[
                    shard * rows + done : shard * rows + done + length,
                    block * LANES : (block + 1) * LANES,
                ].astype(ref.dtype)
                done += length
    return offset + blocks * step


def put_rows(ref, offset, value):
    for block in range(value.shape[1] // LANES):
        ref[offset + block : offset + block + 1, :] = value[:, block * LANES : (block + 1) * LANES]


def front_kernel(
    pos,
    dense_feat,
    pooled,
    labels,
    cross_down,
    cross_up,
    cross_bias,
    w_hidden1,
    bias1,
    w_hidden2,
    bias2,
    w_logit,
    send,
    keep,
    delta_first_out,
    crossed_out,
    reduced_out,
    small,
    halves,
    quarters,
):
    row_pos = pos[1]
    places = places_of(pos[2] // 2, send.shape[1])
    core = pos[0]
    stacked = jnp.concatenate([dense_feat[...], pooled[...]], axis=1)
    reduced = matmul(stacked, cross_down[...]).astype(bf16)
    reduced_out[...] = reduced
    widened = matmul(reduced, cross_up[...]) + cross_bias[...]
    wide = stacked.astype(f32)
    crossed = (wide * widened + wide).astype(bf16)
    pre_first = matmul(crossed, w_hidden1[...]) + bias1[...]
    sig_first = jax.nn.sigmoid(pre_first)
    act_first = (pre_first * sig_first).astype(bf16)
    slope_first = sig_first * (1.0 + pre_first * (1.0 - sig_first))
    pre_second = matmul(act_first, w_hidden2[...]) + bias2[...]
    sig_second = jax.nn.sigmoid(pre_second)
    act_second = (pre_second * sig_second).astype(bf16).astype(f32)
    slope_second = sig_second * (1.0 + pre_second * (1.0 - sig_second))
    logits = jnp.sum(act_second * w_logit[...], axis=1, keepdims=True)
    count = labels.shape[1]
    same = lax.broadcasted_iota(jnp.int32, (count, count), 0) == lax.broadcasted_iota(
        jnp.int32, (count, count), 1
    )
    label_col = jnp.sum(jnp.where(same, labels[...].astype(f32), 0.0), axis=1, keepdims=True)
    delta_logit = loss_scale * (jax.nn.sigmoid(logits) - label_col)
    delta_second = (delta_logit * w_logit[...] * slope_second).astype(bf16)
    put_rows(small, 16, jnp.sum(act_second * delta_logit, axis=0, keepdims=True))
    put_rows(small, 8, jnp.sum(delta_second.astype(f32), axis=0, keepdims=True))
    half = halves.shape[2]
    halves[0] = delta_second[:, :half]
    halves[1] = delta_second[:, half:]
    act_t = act_first.T
    offset = put_blocks(send, row_pos, places, 0, matmul(act_t, halves[1 - core]))
    put_blocks(keep, row_pos, places, 0, matmul(act_t, halves[core]))
    delta_first = (matmul_rt(delta_second, w_hidden2[...]) * slope_first).astype(bf16)
    delta_first_out[...] = delta_first
    crossed_out[...] = crossed
    put_rows(small, 0, jnp.sum(delta_first.astype(f32), axis=0, keepdims=True))
    quarter = quarters.shape[2]
    quarters[0] = delta_first[:, :quarter]
    quarters[1] = delta_first[:, half : half + quarter]
    crossed_t = crossed.T
    put_blocks(send, row_pos, places, offset, matmul(crossed_t, quarters[1 - core]))
    put_blocks(keep, row_pos, places, offset, matmul(crossed_t, quarters[core]))


def back_kernel(
    n_z,
    pos,
    dense_feat,
    pooled,
    cross_down,
    cross_up,
    cross_bias,
    w_hidden1,
    delta_first,
    crossed,
    reduced,
    small_in,
    send,
    keep,
    *rest,
):
    outs = rest[:n_z]
    wide_delta, half_delta, quarters, by_group, small = rest[n_z:]
    core, row_pos, z_pos = pos[0], pos[1], pos[2] // 2
    places = places_of(z_pos, send.shape[1])
    width = dense_feat.shape[1]
    rank = cross_down.shape[1]
    feat = cross_up.shape[1]
    stacked = jnp.concatenate([dense_feat[...], pooled[...]], axis=1)
    wide = stacked.astype(f32)
    delta_crossed = matmul_rt(delta_first[...], w_hidden1[...])
    delta_widened = (delta_crossed * wide).astype(bf16)
    delta_reduced = matmul_rt(delta_widened, cross_up[...]).astype(bf16)
    widened = matmul(reduced[...], cross_up[...]) + cross_bias[...]
    delta_stacked = delta_crossed * (widened + 1.0) + matmul_rt(delta_reduced, cross_down[...])
    per_group = by_group.shape[2]
    for table in range(2 * n_z * per_group):
        group = table // per_group
        by_group[group // 2, group % 2, table % per_group] = delta_stacked[
            :, width * (table + 1) : width * (table + 2)
        ].astype(bf16)
    for which in range(n_z):
        outs[which][0] = by_group[z_pos ^ which, core]
        outs[which][1] = by_group[z_pos ^ which, 1 - core]
    span = 9 * LANES
    wide_delta[...] = delta_widened
    half_delta[0] = delta_reduced[:, : rank // 2]
    half_delta[1] = delta_reduced[:, rank // 2 :]
    hid = delta_first.shape[1]
    quarter = quarters.shape[2]
    quarters[0] = delta_first[:, quarter : hid // 2]
    quarters[1] = delta_first[:, hid // 2 + quarter :]
    put_rows(small, 24, jnp.sum(delta_widened.astype(f32), axis=0, keepdims=True))
    small[0:24, :] = small_in[...]
    small[41:48, :] = jnp.zeros((7, LANES), f32)
    reduced_t = reduced[...].T
    stacked_t = stacked.T
    crossed_t = crossed[...].T
    sums = small[...]
    for ref, who in ((send, 1 - core), (keep, core)):
        offset = put_blocks(ref, row_pos, places, 0, matmul(crossed_t, quarters[who]))
        offset = put_blocks(ref, row_pos, places, offset, matmul(stacked_t, half_delta[who]))
        start = pl.multiple_of(who * (feat - span), LANES)
        offset = put_blocks(
            ref, row_pos, places, offset, matmul(reduced_t, wide_delta[:, pl.ds(start, span)])
        )
        n_row = ref.shape[0]
        end = put_blocks(ref, row_pos, places, offset, jnp.concatenate([sums] * n_row, axis=0))
        tail = ref.shape[1] * ref.shape[2] - end
        if tail:
            put_blocks(ref, row_pos, places, end, jnp.zeros((n_row * tail, LANES), f32))


def count_kernel(n_row, table, hot, n_z, pos, slots, *rest):
    direct, crossed, out = rest[:n_z], rest[n_z : 2 * n_z], rest[2 * n_z]
    block = out.shape[1]
    samples = direct[0].shape[2]
    core, row_pos, z_pos = pos[0], pos[1], pos[2] // 2
    base = (pl.program_id(0) ^ row_pos) * block
    names = lax.broadcasted_iota(jnp.int16, (block, samples), 0)
    total = jnp.zeros((block, out.shape[2]), f32)
    one = jnp.ones((block, samples), bf16)
    zero = jnp.zeros((block, samples), bf16)
    for which in range(n_z):
        for held, who in ((direct[which][0, table], core), (crossed[which][table], 1 - core)):
            source = 2 * (z_pos ^ which) + who
            start = pl.multiple_of((source * n_row + row_pos) * samples, LANES)
            lines = slots[table, :, pl.ds(start, samples)] - base
            lines = jnp.where((lines >= 0) & (lines < block), lines, block).astype(jnp.int16)
            counts = zero
            for look in range(hot):
                line = jnp.broadcast_to(lines[look : look + 1, :], (block, samples))
                counts = counts + jnp.where(line == names, one, zero)
            total = total + matmul(counts, held)
    out[0] = total.astype(out.dtype)


def unpack_kernel(pos, *refs):
    parts = refs[0:8]
    g_down, g_up, g_first, g_second, g_small = refs[8:13]
    held = refs[13:15]
    core = pos[0]
    z_pos = pos[2] // 2
    for stream in range(2):
        lower, upper, lower_other, upper_other = parts[4 * stream : 4 * stream + 4]
        ref = held[stream]
        rows = lower.shape[1]
        n_z = 2 * lower.shape[0]
        z_bits = n_z.bit_length() - 1
        for who, pieces in ((core, (lower, upper)), (1 - core, (lower_other, upper_other))):
            for place in range(n_z):
                start = pl.multiple_of((reverse_bits(place, z_bits) ^ z_pos) * rows, 16)
                ref[who, pl.ds(start, rows), :] = pieces[place // (n_z // 2)][place % (n_z // 2)]
    front, back = held

    def take(ref, out, half, offset, columns):
        rows = out.shape[0]
        step = round_up(rows, 16)
        for column in columns:
            out[:, column * LANES : (column + 1) * LANES] = ref[
                half, offset : offset + rows, :
            ].astype(f32)
            offset += step
        return offset

    for half in range(2):
        blocks = g_second.shape[1] // LANES // 2
        offset = take(front, g_second, half, 0, range(half * blocks, (half + 1) * blocks))
        blocks = g_first.shape[1] // LANES // 4
        take(front, g_first, half, offset, range(2 * half * blocks, (2 * half + 1) * blocks))
        offset = take(
            back, g_first, half, 0, range((2 * half + 1) * blocks, (2 * half + 2) * blocks)
        )
        blocks = g_down.shape[1] // LANES // 2
        offset = take(back, g_down, half, offset, range(half * blocks, (half + 1) * blocks))
        blocks = g_up.shape[1] // LANES
        offset = take(back, g_up, half, offset, range(half * (blocks - 9), half * (blocks - 9) + 9))
    g_small[...] = back[0, offset : offset + 48, :].astype(f32)


def whole(memory=pltpu.VMEM):
    return pl.BlockSpec(memory_space=memory)


def cost(micros):
    return pl.CostEstimate(flops=int(micros * 1.0e9), transcendentals=0, bytes_accessed=int(micros * 3.0e6))


def call(body, outs, scratch, n_in, name, micros):
    return pl.pallas_call(
        body,
        out_shape=outs,
        in_specs=[whole(pltpu.SMEM)] + [whole()] * (n_in - 1),
        out_specs=[whole()] * len(outs),
        scratch_shapes=scratch,
        compiler_params=pltpu.CompilerParams(vmem_limit_bytes=VMEM_BYTES),
        cost_estimate=cost(micros),
        name=name,
    )


def add_terms(terms):
    total = terms[0].astype(f32)
    for term in terms[1:]:
        total = total + term.astype(f32)
    return total


def local(
    dense_feat,
    pooled,
    labels,
    cross_down,
    cross_up,
    cross_bias,
    w_hidden1,
    bias1,
    w_hidden2,
    bias2,
    w_logit,
    lookup_slots,
):
    n_table = lax.axis_size("table")
    n_row = lax.axis_size("row")
    n_z = n_table // 2
    row_bits = n_row.bit_length() - 1
    z_bits = n_z.bit_length() - 1
    table_pos = lax.axis_index("table")
    row_pos = lax.axis_index("row")
    pos = jnp.stack([table_pos % 2, row_pos, table_pos]).astype(jnp.int32)
    batch, width = dense_feat.shape
    feat, rank = cross_down.shape
    hid = w_hidden1.shape[1]
    tab_grp, _, hot = lookup_slots.shape
    u_shard = batch * n_table * hot // 16

    def swap_cores(value):
        return lax.ppermute(value, "table", [(at, at ^ 1) for at in range(n_table)])

    def swap_z(value, which):
        return lax.ppermute(value, "table", [(at, at ^ (2 * which)) for at in range(n_table)])

    def swap_row(value, bit):
        return lax.ppermute(value, "row", [(at, at ^ (1 << bit)) for at in range(n_row)])

    rows_front = (hid // 2 // LANES) * round_up(hid // n_row, 16)
    rows_front += (hid // 4 // LANES) * round_up(feat // n_row, 16)
    rows_back = (hid // 4 // LANES) * round_up(feat // n_row, 16)
    rows_back += (rank // 2 // LANES) * round_up(feat // n_row, 16)
    rows_back += 9 * round_up(rank // n_row, 16) + 48
    rows_front, rows_back = (round_up(rows, 16 * n_z) for rows in (rows_front, rows_back))

    def packed(rows):
        return jax.ShapeDtypeStruct((n_row, n_z, rows // n_z, LANES), bf16)

    cbias = cross_bias.reshape(1, feat)
    send_front, keep_front, delta_first, crossed, reduced, small = call(
        front_kernel,
        [
            packed(rows_front),
            packed(rows_front),
            jax.ShapeDtypeStruct((batch, hid), bf16),
            jax.ShapeDtypeStruct((batch, feat), bf16),
            jax.ShapeDtypeStruct((batch, rank), bf16),
            jax.ShapeDtypeStruct((24, LANES), f32),
        ],
        [pltpu.VMEM((2, batch, hid // 2), bf16), pltpu.VMEM((2, batch, hid // 4), bf16)],
        12,
        "front",
        10,
    )(
        pos,
        dense_feat,
        pooled,
        labels.reshape(1, batch),
        cross_down,
        cross_up,
        cbias,
        w_hidden1,
        bias1.reshape(1, hid),
        w_hidden2,
        bias2.reshape(1, hid),
        w_logit.reshape(1, hid),
    )
    got_front = swap_cores(send_front)

    outs = call(
        functools.partial(back_kernel, n_z),
        [packed(rows_back), packed(rows_back)]
        + [jax.ShapeDtypeStruct((2, tab_grp, batch, width), bf16)] * n_z,
        [
            pltpu.VMEM((batch, feat), bf16),
            pltpu.VMEM((2, batch, rank // 2), bf16),
            pltpu.VMEM((2, batch, hid // 4), bf16),
            pltpu.VMEM((n_z, 2, tab_grp, batch, width), bf16),
            pltpu.VMEM((48, LANES), f32),
        ],
        11,
        "back",
        10,
    )(pos, dense_feat, pooled, cross_down, cross_up, cbias, w_hidden1, delta_first, crossed, reduced, small)
    send_back, keep_back = outs[:2]
    got_back = swap_cores(send_back)
    pooled_out = outs[2:]

    def halve_row(terms, order):
        left = list(range(row_bits - 1, -1, -1))
        terms = [term.reshape((2,) * row_bits + term.shape[1:]) for term in terms]
        for bit in order:
            axis = left.index(bit)
            left.remove(bit)
            sent = add_terms([lax.index_in_dim(term, 1, axis, keepdims=False) for term in terms])
            got = swap_row(sent.astype(bf16), bit)
            terms = [lax.index_in_dim(term, 0, axis, keepdims=False) for term in terms] + [got]
        return terms

    low_first = tuple(range(row_bits))
    high_first = low_first[::-1]

    def sum_dense(terms):
        lower = halve_row([term[:, : n_z // 2] for term in terms], low_first)
        upper = halve_row([term[:, n_z // 2 :] for term in terms], high_first)
        got = swap_z(add_terms(upper).astype(bf16), 1)
        terms = lower + [got]
        for stage in range(1, z_bits):
            middle = n_z >> (stage + 1)
            got = swap_z(add_terms([term[middle:] for term in terms]).astype(bf16), 1 << stage)
            terms = [term[:middle] for term in terms] + [got]
        own = add_terms(terms).astype(bf16)
        for stage in range(z_bits - 1, 0, -1):
            own = jnp.concatenate([own, swap_z(own, 1 << stage)], axis=0)
        far = swap_z(own, 1)
        return [own, far, swap_cores(own), swap_cores(far)]

    streams = sum_dense([keep_front, got_front]) + sum_dense([keep_back, got_back])

    values = [pooled_out[0]] + [swap_z(pooled_out[which], which) for which in range(1, n_z)]
    values += [swap_cores(value[1]) for value in values]
    slots = jnp.transpose(lookup_slots, (0, 2, 1))
    shares = []
    for table in range(tab_grp):
        sums = pl.pallas_call(
            functools.partial(count_kernel, n_row, table, hot, n_z),
            out_shape=jax.ShapeDtypeStruct((n_row, u_shard, width), bf16),
            grid=(n_row,),
            in_specs=[whole(pltpu.SMEM)] + [whole()] * (1 + 2 * n_z),
            out_specs=pl.BlockSpec((1, u_shard, width), lambda at: (at, 0, 0)),
            compiler_params=pltpu.CompilerParams(vmem_limit_bytes=VMEM_BYTES),
            cost_estimate=cost(7),
            name="counts",
        )(pos, slots, *values)
        shares.append(add_terms(halve_row([sums], high_first if table % 2 else low_first)))
    row_grads = jnp.stack(shares)

    g_down, g_up, g_first, g_second, g_small = call(
        unpack_kernel,
        [
            jax.ShapeDtypeStruct((feat // n_row, rank), f32),
            jax.ShapeDtypeStruct((rank // n_row, feat), f32),
            jax.ShapeDtypeStruct((feat // n_row, hid), f32),
            jax.ShapeDtypeStruct((hid // n_row, hid), f32),
            jax.ShapeDtypeStruct((48, LANES), f32),
        ],
        [pltpu.VMEM((2, rows, LANES), bf16) for rows in (rows_front, rows_back)],
        9,
        "unpack",
        4,
    )(pos, *streams)

    flat = g_small.reshape(-1)

    def part(start, length):
        share = length // n_row
        return lax.dynamic_slice(flat, (start * LANES + row_pos * share,), (share,))

    return (
        row_grads,
        g_down,
        g_up,
        part(24, feat),
        g_first,
        part(0, hid),
        g_second,
        part(8, hid),
        part(16, hid),
    )


def solution(mesh):
    in_specs = (
        P(("table", "row"), None),
        P(("table", "row"), None),
        P(("table", "row")),
        P(),
        P(),
        P(),
        P(),
        P(),
        P(),
        P(),
        P(),
        P("table", None, None),
    )
    out_specs = (
        P("table", "row", None),
        P("row", None),
        P("row", None),
        P("row"),
        P("row", None),
        P("row"),
        P("row", None),
        P("row"),
        P("row"),
    )
    return jax.shard_map(local, mesh=mesh, in_specs=in_specs, out_specs=out_specs, check_vma=False)
```

time: 192 us -> 165 us (0.86)
  starting transfers between devices: 59.5 us -> 40 us
  waiting for transfers between devices: 75.6 us -> 65 us
  local copies, waits for them, and re-layouts: 8.41 us -> 14.2 us
  Pallas kernels: 38.4 us -> 35.6 us
    ppermute x41 -> x33, starting transfers between devices: 59.5 us -> 40 us  [the longest x11 23.7 us: swap_z(): lax.ppermute(value, 'table', [(at, at ^ 2 * which) for at in range(n_tabl...]
    ppermute x41 -> x33, waiting for transfers between devices: 75.6 us -> 65 us  [the longest x11 43.6 us: swap_z(): lax.ppermute(value, 'table', [(at, at ^ 2 * which) for at in range(n_tabl...]
    convert_element_type x8 -> x16, other arithmetic: 0.57 us -> 7.88 us  [the longest x10 5.17 us: halve_row(): got = swap_row(sent.astype(bf16), bit)]
    add x8 -> x0, other arithmetic: 5.85 us -> none  [the longest x3 5.31 us: local(): streams.append(sum_z(halve(keep.astype(f32) + got.astype(f32), order)))]
    slice x1 -> x5, local copies, waits for them, and re-layouts: 1.27 us -> 6.54 us  [the longest x4 6.52 us: sum_dense(): lower = halve_row([term[:, :n_z // 2] for term in terms], low_first)]
    pallas_call x4 -> x5, Pallas kernels: 38.4 us -> 35.6 us  [the longest x1 11.8 us: local(): call(front_kernel, [packed(rows_front), packed(rows_front), jax.ShapeDtyp...]
    unnamed x20 -> x26, local copies, waits for them, and re-layouts: 4.43 us -> 5.53 us
  transfers between devices with their start and end apart: 41 -> 33, of which waited for: 17 -> 14; matrix products, arithmetic and copies ran while one was open for 5% -> 9% of each run, Pallas kernels for 8% -> 7%
where the time goes in v2:
time: 165 us
  waiting for transfers between devices  65 us (39%)
  starting transfers between devices  40 us (24%)
  Pallas kernels  35.6 us (22%)
  local copies, waits for them, and re-layouts  14.2 us (9%)
  other arithmetic  8.94 us (5%)
    ppermute x11, waiting for transfers between devices, swap_z(): lax.ppermute(value, 'table', [(at, at ^ 2 * which) for at in range(n_tabl...  43.6 us
    ppermute x11, starting transfers between devices, swap_z(): lax.ppermute(value, 'table', [(at, at ^ 2 * which) for at in range(n_tabl...  23.7 us
    ppermute x12, waiting for transfers between devices, swap_row(): lax.ppermute(value, 'row', [(at, at ^ 1 << bit) for at in range(n_row)])  20.7 us
    ppermute x12, starting transfers between devices, swap_row(): lax.ppermute(value, 'row', [(at, at ^ 1 << bit) for at in range(n_row)])  14.8 us
    pallas_call x1, Pallas kernels, local(): call(front_kernel, [packed(rows_front), packed(rows_front), jax.ShapeDtyp...  11.8 us
    pallas_call x2, Pallas kernels, local(): pl.pallas_call(functools.partial(count_kernel, n_row, table, hot, n_z), o...  10.8 us
    pallas_call x1, Pallas kernels, local(): call(functools.partial(back_kernel, n_z), [packed(rows_back), packed(rows...  9.58 us
    slice x4, local copies, waits for them, and re-layouts, sum_dense(): lower = halve_row([term[:, :n_z // 2] for term in terms], low_first)  6.52 us
  transfers between devices with their start and end apart: 33, of which 14 were waited for; matrix products, arithmetic and copies ran while one was open for 9% of the time, Pallas kernels for 7%

profile of v2, /device:TPU:0, one launch (start us, length us, event | category | flops | bytes accessed | tf_op | source)
XLA Modules:
  0.0 164.6 jit_solution(7861802614349000897)
XLA Ops:
  0.7 0.7 reshape.369.cross_bias
  1.4 1.2 copy-done
  2.7 0.8 copy-done.2
  3.5 0.7 copy-done.3
  6.3 11.8 %front.1 = (bf16[4,4,528,128]{3,2,1,0:T(8,128)(2,1)}, bf16[4,4,528,128]{3,2,1,0:T(8,128)(2,1)}, bf16[256,1024]{1,0:T(8,128)(2,1)S(1)}, bf16[256,2176]{1,0:T(8,12...) custom-call(s32[3]{0:T(128)S(1)} %pad_add_fusion.pos, bf16[256,128]{1,0:T(8,128)(2,1)S(1)} %copy-done.2, ...), custom_call_target="tpu_custom_call" | custom-call | flops 10000000000 | bytes 30000000 | tf_op jit(solution)/shard_map/front/pallas_call | solution.py:345
  18.1 9.6 %back.1 = (bf16[4,4,576,128]{3,2,1,0:T(8,128)(2,1)}, bf16[4,4,576,128]{3,2,1,0:T(8,128)(2,1)}, bf16[2,2,256,128]{3,2,1,0:T(8,128)(2,1)S(1)}, bf16[2,2,256,128]{3...) custom-call(s32[3]{0:T(128)S(1)} %pad_add_fusion.pos, ...), custom_call_target="tpu_custom_call" | custom-call | flops 10000000000 | bytes 30000000 | tf_op jit(solution)/shard_map/back/pallas_call | solution.py:375
  27.7 3.0 %collective-permute-start = (bf16[2,2,256,128]{3,2,1,0:T(8,128)(2,1)S(1)}, bf16[2,2,256,128]{3,2,1,0:T(8,128)(2,1)S(1)}, u32[]{:S(2)}, u32[]{:S(2)}) collective-permute-start(bf16[2,2,256,128]{3,2,1,0:T(8,128)(2,1)S(1)} %get-tuple-element.31), channel_id=1, source_target_pairs={{0,8},{4,12},{8,0},{12,4},{16,24},{20,28},{24,16},{28,20},{1,9},{5... | collective-permute-start | bytes 786440 | tf_op jit(solution)/shard_map/ppermute | solution.py:329
  30.7 2.6 %collective-permute-start.1 = (bf16[2,2,256,128]{3,2,1,0:T(8,128)(2,1)S(1)}, bf16[2,2,256,128]{3,2,1,0:T(8,128)(2,1)S(1)}, u32[]{:S(2)}, u32[]{:S(2)}) collective-permute-start(bf16[2,2,256,128]{3,2,1,0:T(8,128)(2,1)S(1)} %get-tuple-element.32), channel_id=1, source_target_pairs={{0,16},{4,20},{8,24},{12,28},{16,0},{20,4},{24,8},{28,12},{1,17},{... | collective-permute-start | bytes 786440 | tf_op jit(solution)/shard_map/ppermute | solution.py:329
  33.8 7.8 %collective-permute-done.rest_1_ = bf16[2,2,256,128]{3,2,1,0:T(8,128)(2,1)S(1)} collective-permute-done((bf16[2,2,256,128]{3,2,1,0:T(8,128)(2,1)S(1)}, bf16[2,2,256,128]{3,2,1,0:T(8,128)(2,1)S(1)}, u32[]{:S(2)}, u32[]{:S(2)}) %collective-permute-start) | collective-permute-done | bytes 262176 | tf_op jit(solution)/shard_map/ppermute | solution.py:329
  41.6 10.4 %collective-permute-done.1.rest_2_ = bf16[2,2,256,128]{3,2,1,0:T(8,128)(2,1)S(1)} collective-permute-done((bf16[2,2,256,128]{3,2,1,0:T(8,128)(2,1)S(1)}, bf16[2,2,256,128]{3,2,1,0:T(8,128)(2,1)S(1)}, u32[]{:S(2)}, u32[]{:S(2)}) %collective-permute-start.1) | collective-permute-done | bytes 262176 | tf_op jit(solution)/shard_map/ppermute | solution.py:329
  52.7 2.3 %slice.303 = bf16[4,2,528,128]{3,2,1,0:T(8,128)(2,1)} slice(bf16[4,4,528,128]{3,2,1,0:T(8,128)(2,1)} %get-tuple-element.34), slice={[0:4], [0:2], [0:528], [0:128]} | slice | bytes 2162688 | tf_op jit(solution)/shard_map/slice | solution.py:409
  55.0 1.4 slice.328
  56.5 5.5 %counts.3 = bf16[4,512,128]{2,1,0:T(8,128)(2,1)} custom-call(s32[3]{0:T(128)S(1)} %pad_add_fusion.pos, s32[2,4,8192]{2,1,0:T(4,128)S(1)} %bitcast.114, bf16[2,2,256,128]{3,2,1,0:T(8,128)(2,1)S(1)} %get-tuple-element.30.rest_0_, bf16[2,2,256,128]{3,2,1,0:T(8,128)(2,1)S(1)} %collective-permute-done.rest_1_, ...), custom_call_target="tpu_custom_call" | custom-call | flops 7000000000 | bytes 21000000 | tf_op jit(solution)/shard_map/counts/pallas_call | solution.py:430
  62.0 5.3 %counts.2 = bf16[4,512,128]{2,1,0:T(8,128)(2,1)} custom-call(s32[3]{0:T(128)S(1)} %pad_add_fusion.pos, s32[2,4,8192]{2,1,0:T(4,128)S(1)} %bitcast.115, bf16[2,2,256,128]{3,2,1,0:T(8,128)(2,1)S(1)} %get-tuple-element.30.rest_0_, bf16[2,2,256,128]{3,2,1,0:T(8,128)(2,1)S(1)} %collective-permute-done.rest_1_, ...), custom_call_target="tpu_custom_call" | custom-call | flops 7000000000 | bytes 21000000 | tf_op jit(solution)/shard_map/counts/pallas_call | solution.py:430
  67.3 1.2 add_convert_fusion.2
  68.5 1.6 collective-permute-start.14
  70.1 1.5 slice.367
  71.7 1.6 collective-permute-start.12
  73.2 1.2 add_convert_fusion
  75.0 1.3 slice.388
  77.2 6.4 %collective-permute-done.14 = bf16[2,2,528,128]{3,2,1,0:T(8,128)(2,1)S(1)} collective-permute-done((bf16[2,2,528,128]{3,2,1,0:T(8,128)(2,1)S(1)}, bf16[2,2,528,128]{3,2,1,0:T(8,128)(2,1)S(1)}, u32[]{:S(2)}, u32[]{:S(2)}) %collective-permute-start.14) | collective-permute-done | bytes 540704 | tf_op jit(solution)/shard_map/ppermute | solution.py:332
  83.6 1.1 fusion.14
  84.7 1.6 collective-permute-start.15
  87.0 1.0 collective-permute-start.13
  87.9 8.3 %collective-permute-done.25 = bf16[2,2,576,128]{3,2,1,0:T(8,128)(2,1)S(1)} collective-permute-done((bf16[2,2,576,128]{3,2,1,0:T(8,128)(2,1)S(1)}, bf16[2,2,576,128]{3,2,1,0:T(8,128)(2,1)S(1)}, u32[]{:S(2)}, u32[]{:S(2)}) %collective-permute-start.25) | collective-permute-done | bytes 589856 | tf_op jit(solution)/shard_map/ppermute | solution.py:332
  96.2 1.1 fusion.6
  97.3 1.6 collective-permute-start.26
  99.6 1.0 collective-permute-start.24
  100.6 4.7 %collective-permute-done.15 = bf16[2,528,128]{2,1,0:T(8,128)(2,1)S(1)} collective-permute-done((bf16[2,528,128]{2,1,0:T(8,128)(2,1)S(1)}, bf16[2,528,128]{2,1,0:T(8,128)(2,1)S(1)}, u32[]{:S(2)}, u32[]{:S(2)}) %collective-permute-start.15) | collective-permute-done | bytes 270368 | tf_op jit(solution)/shard_map/ppermute | solution.py:332
  105.3 1.1 fusion.5
  106.4 5.8 %collective-permute-start.16 = (bf16[2,528,128]{2,1,0:T(8,128)(2,1)S(1)}, bf16[2,528,128]{2,1,0:T(8,128)(2,1)S(1)}, u32[]{:S(2)}, u32[]{:S(2)}) collective-permute-start(bf16[2,528,128]{2,1,0:T(8,128)(2,1)S(1)} %fusion.5), channel_id=1, source_target_pairs={{0,8},{4,12},{8,0},{12,4},{16,24},{20,28},{24,16},{28,20},{1,9},{5... | collective-permute-start | bytes 811016 | tf_op jit(solution)/shard_map/ppermute | solution.py:329
  112.2 1.1 fusion.2
  113.4 3.9 %collective-permute-start.27 = (bf16[2,576,128]{2,1,0:T(8,128)(2,1)S(1)}, bf16[2,576,128]{2,1,0:T(8,128)(2,1)S(1)}, u32[]{:S(2)}, u32[]{:S(2)}) collective-permute-start(bf16[2,576,128]{2,1,0:T(8,128)(2,1)S(1)} %fusion.2), channel_id=1, source_target_pairs={{0,8},{4,12},{8,0},{12,4},{16,24},{20,28},{24,16},{28,20},{1,9},{5... | collective-permute-start | bytes 884744 | tf_op jit(solution)/shard_map/ppermute | solution.py:329
  117.9 1.5 collective-permute-start.7
  119.5 1.1 collective-permute-start.17
  120.6 4.8 %collective-permute-done.27 = bf16[2,576,128]{2,1,0:T(8,128)(2,1)S(1)} collective-permute-done((bf16[2,576,128]{2,1,0:T(8,128)(2,1)S(1)}, bf16[2,576,128]{2,1,0:T(8,128)(2,1)S(1)}, u32[]{:S(2)}, u32[]{:S(2)}) %collective-permute-start.27) | collective-permute-done | bytes 294944 | tf_op jit(solution)/shard_map/ppermute | solution.py:329
  125.6 2.6 %collective-permute-start.28 = (bf16[1,576,128]{2,1,0:T(8,128)(2,1)S(1)}, bf16[1,576,128]{2,1,0:T(8,128)(2,1)S(1)}, u32[]{:S(2)}, u32[]{:S(2)}) collective-permute-start(bf16[1,576,128]{2,1,0:T(8,128)(2,1)S(1)} %fusion.9), channel_id=1, source_target_pairs={{0,16},{4,20},{8,24},{12,28},{16,0},{20,4},{24,8},{28,12},{1,17},{... | collective-permute-start | bytes 442376 | tf_op jit(solution)/shard_map/ppermute | solution.py:329
  128.4 1.9 %collective-permute-start.18 = (bf16[1,528,128]{2,1,0:T(8,128)(2,1)S(1)}, bf16[1,528,128]{2,1,0:T(8,128)(2,1)S(1)}, u32[]{:S(2)}, u32[]{:S(2)}) collective-permute-start(bf16[1,528,128]{2,1,0:T(8,128)(2,1)S(1)} %fusion.21), channel_id=1, source_target_pairs={{0,16},{4,20},{8,24},{12,28},{16,0},{20,4},{24,8},{28,12},{1,17},{... | collective-permute-start | bytes 405512 | tf_op jit(solution)/shard_map/ppermute | solution.py:329
  130.3 7.5 %collective-permute-done.28 = bf16[1,576,128]{2,1,0:T(8,128)(2,1)S(1)} collective-permute-done((bf16[1,576,128]{2,1,0:T(8,128)(2,1)S(1)}, bf16[1,576,128]{2,1,0:T(8,128)(2,1)S(1)}, u32[]{:S(2)}, u32[]{:S(2)}) %collective-permute-start.28) | collective-permute-done | bytes 147488 | tf_op jit(solution)/shard_map/ppermute | solution.py:329
  138.1 1.6 collective-permute-start.10
  140.2 2.3 %collective-permute-start.19 = (bf16[2,528,128]{2,1,0:T(8,128)(2,1)S(1)}, bf16[2,528,128]{2,1,0:T(8,128)(2,1)S(1)}, u32[]{:S(2)}, u32[]{:S(2)}) collective-permute-start(bf16[2,528,128]{2,1,0:T(8,128)(2,1)S(1)} %pad_maximum_fusion.2.refs_0_), channel_id=1, source_target_pairs={{0,8},{4,12},{8,0},{12,4},{16,24},{20,28},{24,16},{28,20},{1,9},{5... | collective-permute-start | bytes 811016 | tf_op jit(solution)/shard_map/ppermute | solution.py:329
  142.6 4.0 %collective-permute-done.29 = bf16[1,576,128]{2,1,0:T(8,128)(2,1)S(1)} collective-permute-done((bf16[1,576,128]{2,1,0:T(8,128)(2,1)S(1)}, bf16[1,576,128]{2,1,0:T(8,128)(2,1)S(1)}, u32[]{:S(2)}, u32[]{:S(2)}) %collective-permute-start.29) | collective-permute-done | bytes 147488 | tf_op jit(solution)/shard_map/ppermute | solution.py:329
  146.8 1.8 %collective-permute-start.8 = (bf16[512,128]{1,0:T(8,128)(2,1)S(1)}, bf16[512,128]{1,0:T(8,128)(2,1)S(1)}, u32[]{:S(2)}, u32[]{:S(2)}) collective-permute-start(bf16[512,128]{1,0:T(8,128)(2,1)S(1)} %fusion.22), channel_id=1, source_target_pairs={{0,2},{1,3},{2,0},{3,1},{4,6},{5,7},{6,4},{7,5},{8,10},{9,11},{10,... | collective-permute-start | bytes 393224 | tf_op jit(solution)/shard_map/ppermute | solution.py:332
  148.7 3.7 %collective-permute-done.19.refs_1_ = bf16[2,528,128]{2,1,0:T(8,128)(2,1)S(1)} collective-permute-done((bf16[2,528,128]{2,1,0:T(8,128)(2,1)S(1)}, bf16[2,528,128]{2,1,0:T(8,128)(2,1)S(1)}, u32[]{:S(2)}, u32[]{:S(2)}) %collective-permute-start.19) | collective-permute-done | bytes 270368 | tf_op jit(solution)/shard_map/ppermute | solution.py:329
  152.9 4.7 %collective-permute-done.30.refs_5_ = bf16[2,576,128]{2,1,0:T(8,128)(2,1)S(1)} collective-permute-done((bf16[2,576,128]{2,1,0:T(8,128)(2,1)S(1)}, bf16[2,576,128]{2,1,0:T(8,128)(2,1)S(1)}, u32[]{:S(2)}, u32[]{:S(2)}) %collective-permute-start.30) | collective-permute-done | bytes 294944 | tf_op jit(solution)/shard_map/ppermute | solution.py:329
  157.7 0.8 pad_maximum_fusion
  159.2 0.7 copy-done.12
  160.0 3.3 %unpack.1 = (f32[544,256]{1,0:T(8,128)}, f32[64,2176]{1,0:T(8,128)}, f32[544,1024]{1,0:T(8,128)}, f32[256,1024]{1,0:T(8,128)}, f32[48,128]{1,0:T(8,128)S(1)}) custom-call(s32[3]{0:T(128)S(1)} %pad_add_fusion.pos, bf16[2,528,128]{2,1,0:T(8,128)(2,1)S(1)} %pad_maximum_fusion.2.refs_0_, bf16[2,528,128]{2,1,0:T(8,128)(2,1)S(1)} %collective-permute-done.19.refs_1_, ...), custom_call_target="tpu_custom_call" | custom-call | flops 4000000000 | bytes 12000000 | tf_op jit(solution)/shard_map/unpack/pallas_call | solution.py:443
  (84 shorter events, 10.9 us)
Async XLA Ops:
  1.4 1.2 copy-start
  2.7 0.8 copy-start.2
  3.5 0.7 copy-start.3
  4.2 0.7 copy-start.4
  4.9 0.7 copy-start.5
  5.6 0.7 copy-start.6
  27.7 13.9 %collective-permute-start = (bf16[2,2,256,128]{3,2,1,0:T(8,128)(2,1)S(1)}, bf16[2,2,256,128]{3,2,1,0:T(8,128)(2,1)S(1)}, u32[]{:S(2)}, u32[]{:S(2)}) collective-permute-start(bf16[2,2,256,128]{3,2,1,0:T(8,128)(2,1)S(1)} %get-tuple-element.31), channel_id=1, source_target_pairs={{0,8},{4,12},{8,0},{12,4},{16,24},{20,28},{24,16},{28,20},{1,9},{5... | collective-permute-start | bytes 786440 | tf_op jit(solution)/shard_map/ppermute | solution.py:329
  30.7 36.6 %collective-permute-start.11 = (bf16[4,4,528,128]{3,2,1,0:T(8,128)(2,1)}, bf16[4,4,528,128]{3,2,1,0:T(8,128)(2,1)}, u32[]{:S(2)}, u32[]{:S(2)}) collective-permute-start(bf16[4,4,528,128]{3,2,1,0:T(8,128)(2,1)} %get-tuple-element.35), channel_id=1, source_target_pairs={{0,4},{4,0},{8,12},{12,8},{16,20},{20,16},{24,28},{28,24},{1,5},{5... | collective-permute-start | bytes 6488072 | tf_op jit(solution)/shard_map/ppermute | solution.py:326
  30.7 21.3 %collective-permute-start.1 = (bf16[2,2,256,128]{3,2,1,0:T(8,128)(2,1)S(1)}, bf16[2,2,256,128]{3,2,1,0:T(8,128)(2,1)S(1)}, u32[]{:S(2)}, u32[]{:S(2)}) collective-permute-start(bf16[2,2,256,128]{3,2,1,0:T(8,128)(2,1)S(1)} %get-tuple-element.32), channel_id=1, source_target_pairs={{0,16},{4,20},{8,24},{12,28},{16,0},{20,4},{24,8},{28,12},{1,17},{... | collective-permute-start | bytes 786440 | tf_op jit(solution)/shard_map/ppermute | solution.py:329
  33.3 19.3 %collective-permute-start.3 = (bf16[2,256,128]{2,1,0:T(8,128)(2,1)S(1)}, bf16[2,256,128]{2,1,0:T(8,128)(2,1)S(1)}, u32[]{:S(2)}, u32[]{:S(2)}) collective-permute-start(bf16[2,256,128]{2,1,0:T(8,128)(2,1)S(1)} %slice_bitcast_fusion.14), channel_id=1, source_target_pairs={{0,4},{4,0},{8,12},{12,8},{16,20},{20,16},{24,28},{28,24},{1,5},{5... | collective-permute-start | bytes 393224 | tf_op jit(solution)/shard_map/ppermute | solution.py:326
  33.6 18.4 %collective-permute-start.2 = (bf16[2,2,256,128]{3,2,1,0:T(8,128)(2,1)S(1)}, bf16[2,2,256,128]{3,2,1,0:T(8,128)(2,1)S(1)}, u32[]{:S(2)}, u32[]{:S(2)}) collective-permute-start(bf16[2,2,256,128]{3,2,1,0:T(8,128)(2,1)S(1)} %get-tuple-element.33), channel_id=1, source_target_pairs={{0,24},{4,28},{8,16},{12,20},{16,8},{20,12},{24,0},{28,4},{1,25},{... | collective-permute-start | bytes 786440 | tf_op jit(solution)/shard_map/ppermute | solution.py:329
  41.5 31.7 %collective-permute-start.22 = (bf16[4,4,576,128]{3,2,1,0:T(8,128)(2,1)}, bf16[4,4,576,128]{3,2,1,0:T(8,128)(2,1)}, u32[]{:S(2)}, u32[]{:S(2)}) collective-permute-start(bf16[4,4,576,128]{3,2,1,0:T(8,128)(2,1)} %get-tuple-element.37), channel_id=1, source_target_pairs={{0,4},{4,0},{8,12},{12,8},{16,20},{20,16},{24,28},{28,24},{1,5},{5... | collective-permute-start | bytes 7077896 | tf_op jit(solution)/shard_map/ppermute | solution.py:326
  52.0 4.4 %collective-permute-start.4 = (bf16[2,256,128]{2,1,0:T(8,128)(2,1)S(1)}, bf16[2,256,128]{2,1,0:T(8,128)(2,1)S(1)}, u32[]{:S(2)}, u32[]{:S(2)}) collective-permute-start(bf16[2,256,128]{2,1,0:T(8,128)(2,1)S(1)} %slice_bitcast_fusion.13), channel_id=1, source_target_pairs={{0,4},{4,0},{8,12},{12,8},{16,20},{20,16},{24,28},{28,24},{1,5},{5... | collective-permute-start | bytes 393224 | tf_op jit(solution)/shard_map/ppermute | solution.py:326
  52.0 4.4 %collective-permute-start.5 = (bf16[2,256,128]{2,1,0:T(8,128)(2,1)S(1)}, bf16[2,256,128]{2,1,0:T(8,128)(2,1)S(1)}, u32[]{:S(2)}, u32[]{:S(2)}) collective-permute-start(bf16[2,256,128]{2,1,0:T(8,128)(2,1)S(1)} %slice_bitcast_fusion.12), channel_id=1, source_target_pairs={{0,4},{4,0},{8,12},{12,8},{16,20},{20,16},{24,28},{28,24},{1,5},{5... | collective-permute-start | bytes 393224 | tf_op jit(solution)/shard_map/ppermute | solution.py:326
  52.6 3.8 %collective-permute-start.6 = (bf16[2,256,128]{2,1,0:T(8,128)(2,1)S(1)}, bf16[2,256,128]{2,1,0:T(8,128)(2,1)S(1)}, u32[]{:S(2)}, u32[]{:S(2)}) collective-permute-start(bf16[2,256,128]{2,1,0:T(8,128)(2,1)S(1)} %slice_bitcast_fusion.11), channel_id=1, source_target_pairs={{0,4},{4,0},{8,12},{12,8},{16,20},{20,16},{24,28},{28,24},{1,5},{5... | collective-permute-start | bytes 393224 | tf_op jit(solution)/shard_map/ppermute | solution.py:326
  55.0 1.4 copy-start.1
  62.0 5.3 %copy-start.9 = (bf16[4,4,528,128]{3,2,1,0:T(8,128)(2,1)S(1)}, bf16[4,4,528,128]{3,2,1,0:T(8,128)(2,1)}, u32[]{:S(2)}) copy-start(bf16[4,4,528,128]{3,2,1,0:T(8,128)(2,1)} %get-tuple-element.34) | copy-start | bytes 6488068
  68.5 3.1 %copy-start.7 = (bf16[4,2,528,128]{3,2,1,0:T(8,128)(2,1)S(1)}, bf16[4,2,528,128]{3,2,1,0:T(8,128)(2,1)}, u32[]{:S(2)}) copy-start(bf16[4,2,528,128]{3,2,1,0:T(8,128)(2,1)} %slice.303) | copy-start | bytes 3244036
  68.5 15.1 %collective-permute-start.14 = (bf16[2,2,528,128]{3,2,1,0:T(8,128)(2,1)S(1)}, bf16[2,2,528,128]{3,2,1,0:T(8,128)(2,1)S(1)}, u32[]{:S(2)}, u32[]{:S(2)}) collective-permute-start(bf16[2,2,528,128]{3,2,1,0:T(8,128)(2,1)S(1)} %add_convert_fusion.2), channel_id=1, source_target_pairs={{0,2},{1,3},{2,0},{3,1},{4,6},{5,7},{6,4},{7,5},{8,10},{9,11},{10,... | collective-permute-start | bytes 1622024 | tf_op jit(solution)/shard_map/ppermute | solution.py:332
  70.0 3.2 %copy-start.8 = (bf16[4,4,576,128]{3,2,1,0:T(8,128)(2,1)S(1)}, bf16[4,4,576,128]{3,2,1,0:T(8,128)(2,1)}, u32[]{:S(2)}) copy-start(bf16[4,4,576,128]{3,2,1,0:T(8,128)(2,1)} %get-tuple-element.36) | copy-start | bytes 7077892
  71.7 15.2 %collective-permute-start.12 = (bf16[2,2,528,128]{3,2,1,0:T(8,128)(2,1)S(1)}, bf16[2,2,528,128]{3,2,1,0:T(8,128)(2,1)S(1)}, u32[]{:S(2)}, u32[]{:S(2)}) collective-permute-start(bf16[2,2,528,128]{3,2,1,0:T(8,128)(2,1)S(1)} %fusion.3), channel_id=1, source_target_pairs={{0,1},{1,0},{2,3},{3,2},{4,5},{5,4},{6,7},{7,6},{8,9},{9,8},{10,11... | collective-permute-start | bytes 1622024 | tf_op jit(solution)/shard_map/ppermute | solution.py:332
  74.5 21.8 %collective-permute-start.25 = (bf16[2,2,576,128]{3,2,1,0:T(8,128)(2,1)S(1)}, bf16[2,2,576,128]{3,2,1,0:T(8,128)(2,1)S(1)}, u32[]{:S(2)}, u32[]{:S(2)}) collective-permute-start(bf16[2,2,576,128]{3,2,1,0:T(8,128)(2,1)S(1)} %add_convert_fusion), channel_id=1, source_target_pairs={{0,2},{1,3},{2,0},{3,1},{4,6},{5,7},{6,4},{7,5},{8,10},{9,11},{10,... | collective-permute-start | bytes 1769480 | tf_op jit(solution)/shard_map/ppermute | solution.py:332
  76.6 22.9 %collective-permute-start.23 = (bf16[2,2,576,128]{3,2,1,0:T(8,128)(2,1)S(1)}, bf16[2,2,576,128]{3,2,1,0:T(8,128)(2,1)S(1)}, u32[]{:S(2)}, u32[]{:S(2)}) collective-permute-start(bf16[2,2,576,128]{3,2,1,0:T(8,128)(2,1)S(1)} %fusion), channel_id=1, source_target_pairs={{0,1},{1,0},{2,3},{3,2},{4,5},{5,4},{6,7},{7,6},{8,9},{9,8},{10,11... | collective-permute-start | bytes 1769480 | tf_op jit(solution)/shard_map/ppermute | solution.py:332
  84.7 20.6 %collective-permute-start.15 = (bf16[2,528,128]{2,1,0:T(8,128)(2,1)S(1)}, bf16[2,528,128]{2,1,0:T(8,128)(2,1)S(1)}, u32[]{:S(2)}, u32[]{:S(2)}) collective-permute-start(bf16[2,528,128]{2,1,0:T(8,128)(2,1)S(1)} %fusion.14), channel_id=1, source_target_pairs={{0,1},{1,0},{2,3},{3,2},{4,5},{5,4},{6,7},{7,6},{8,9},{9,8},{10,11... | collective-permute-start | bytes 811016 | tf_op jit(solution)/shard_map/ppermute | solution.py:332
  87.0 31.0 %collective-permute-start.13 = (bf16[2,528,128]{2,1,0:T(8,128)(2,1)S(1)}, bf16[2,528,128]{2,1,0:T(8,128)(2,1)S(1)}, u32[]{:S(2)}, u32[]{:S(2)}) collective-permute-start(bf16[2,528,128]{2,1,0:T(8,128)(2,1)S(1)} %fusion.4), channel_id=1, source_target_pairs={{0,2},{1,3},{2,0},{3,1},{4,6},{5,7},{6,4},{7,5},{8,10},{9,11},{10,... | collective-permute-start | bytes 811016 | tf_op jit(solution)/shard_map/ppermute | solution.py:332
  97.3 14.9 %collective-permute-start.26 = (bf16[2,576,128]{2,1,0:T(8,128)(2,1)S(1)}, bf16[2,576,128]{2,1,0:T(8,128)(2,1)S(1)}, u32[]{:S(2)}, u32[]{:S(2)}) collective-permute-start(bf16[2,576,128]{2,1,0:T(8,128)(2,1)S(1)} %fusion.6), channel_id=1, source_target_pairs={{0,1},{1,0},{2,3},{3,2},{4,5},{5,4},{6,7},{7,6},{8,9},{9,8},{10,11... | collective-permute-start | bytes 884744 | tf_op jit(solution)/shard_map/ppermute | solution.py:332
  99.6 17.7 %copy-start.10 = (bf16[4,512,128]{2,1,0:T(8,128)(2,1)S(1)}, bf16[4,512,128]{2,1,0:T(8,128)(2,1)}, u32[]{:S(2)}) copy-start(bf16[4,512,128]{2,1,0:T(8,128)(2,1)} %counts.2) | copy-start | bytes 1572868
  99.6 21.0 %collective-permute-start.24 = (bf16[2,576,128]{2,1,0:T(8,128)(2,1)S(1)}, bf16[2,576,128]{2,1,0:T(8,128)(2,1)S(1)}, u32[]{:S(2)}, u32[]{:S(2)}) collective-permute-start(bf16[2,576,128]{2,1,0:T(8,128)(2,1)S(1)} %fusion.1), channel_id=1, source_target_pairs={{0,2},{1,3},{2,0},{3,1},{4,6},{5,7},{6,4},{7,5},{8,10},{9,11},{10,... | collective-permute-start | bytes 884744 | tf_op jit(solution)/shard_map/ppermute | solution.py:332
  106.4 10.9 %copy-start.11 = (bf16[4,512,128]{2,1,0:T(8,128)(2,1)S(1)}, bf16[4,512,128]{2,1,0:T(8,128)(2,1)}, u32[]{:S(2)}) copy-start(bf16[4,512,128]{2,1,0:T(8,128)(2,1)} %counts.3) | copy-start | bytes 1572868
  106.4 13.0 %collective-permute-start.16 = (bf16[2,528,128]{2,1,0:T(8,128)(2,1)S(1)}, bf16[2,528,128]{2,1,0:T(8,128)(2,1)S(1)}, u32[]{:S(2)}, u32[]{:S(2)}) collective-permute-start(bf16[2,528,128]{2,1,0:T(8,128)(2,1)S(1)} %fusion.5), channel_id=1, source_target_pairs={{0,8},{4,12},{8,0},{12,4},{16,24},{20,28},{24,16},{28,20},{1,9},{5... | collective-permute-start | bytes 811016 | tf_op jit(solution)/shard_map/ppermute | solution.py:329
  113.4 12.1 %collective-permute-start.27 = (bf16[2,576,128]{2,1,0:T(8,128)(2,1)S(1)}, bf16[2,576,128]{2,1,0:T(8,128)(2,1)S(1)}, u32[]{:S(2)}, u32[]{:S(2)}) collective-permute-start(bf16[2,576,128]{2,1,0:T(8,128)(2,1)S(1)} %fusion.2), channel_id=1, source_target_pairs={{0,8},{4,12},{8,0},{12,4},{16,24},{20,28},{24,16},{28,20},{1,9},{5... | collective-permute-start | bytes 884744 | tf_op jit(solution)/shard_map/ppermute | solution.py:329
  117.4 20.6 %collective-permute-start.9 = (bf16[2,512,128]{2,1,0:T(8,128)(2,1)S(1)}, bf16[2,512,128]{2,1,0:T(8,128)(2,1)S(1)}, u32[]{:S(2)}, u32[]{:S(2)}) collective-permute-start(bf16[2,512,128]{2,1,0:T(8,128)(2,1)S(1)} %slice.362), channel_id=1, source_target_pairs={{0,2},{1,3},{2,0},{3,1},{4,6},{5,7},{6,4},{7,5},{8,10},{9,11},{10,... | collective-permute-start | bytes 786440 | tf_op jit(solution)/shard_map/ppermute | solution.py:332
  117.9 28.8 %collective-permute-start.7 = (bf16[2,512,128]{2,1,0:T(8,128)(2,1)S(1)}, bf16[2,512,128]{2,1,0:T(8,128)(2,1)S(1)}, u32[]{:S(2)}, u32[]{:S(2)}) collective-permute-start(bf16[2,512,128]{2,1,0:T(8,128)(2,1)S(1)} %slice_bitcast_fusion.2), channel_id=1, source_target_pairs={{0,1},{1,0},{2,3},{3,2},{4,5},{5,4},{6,7},{7,6},{8,9},{9,8},{10,11... | collective-permute-start | bytes 786440 | tf_op jit(solution)/shard_map/ppermute | solution.py:332
  119.5 8.7 %collective-permute-start.17 = (bf16[1,528,128]{2,1,0:T(8,128)(2,1)S(1)}, bf16[1,528,128]{2,1,0:T(8,128)(2,1)S(1)}, u32[]{:S(2)}, u32[]{:S(2)}) collective-permute-start(bf16[1,528,128]{2,1,0:T(8,128)(2,1)S(1)} %fusion.17), channel_id=1, source_target_pairs={{0,16},{4,20},{8,24},{12,28},{16,0},{20,4},{24,8},{28,12},{1,17},{... | collective-permute-start | bytes 405512 | tf_op jit(solution)/shard_map/ppermute | solution.py:329
  125.6 12.2 %collective-permute-start.28 = (bf16[1,576,128]{2,1,0:T(8,128)(2,1)S(1)}, bf16[1,576,128]{2,1,0:T(8,128)(2,1)S(1)}, u32[]{:S(2)}, u32[]{:S(2)}) collective-permute-start(bf16[1,576,128]{2,1,0:T(8,128)(2,1)S(1)} %fusion.9), channel_id=1, source_target_pairs={{0,16},{4,20},{8,24},{12,28},{16,0},{20,4},{24,8},{28,12},{1,17},{... | collective-permute-start | bytes 442376 | tf_op jit(solution)/shard_map/ppermute | solution.py:329
  128.4 11.8 %collective-permute-start.18 = (bf16[1,528,128]{2,1,0:T(8,128)(2,1)S(1)}, bf16[1,528,128]{2,1,0:T(8,128)(2,1)S(1)}, u32[]{:S(2)}, u32[]{:S(2)}) collective-permute-start(bf16[1,528,128]{2,1,0:T(8,128)(2,1)S(1)} %fusion.21), channel_id=1, source_target_pairs={{0,16},{4,20},{8,24},{12,28},{16,0},{20,4},{24,8},{28,12},{1,17},{... | collective-permute-start | bytes 405512 | tf_op jit(solution)/shard_map/ppermute | solution.py:329
  137.9 8.7 %collective-permute-start.29 = (bf16[1,576,128]{2,1,0:T(8,128)(2,1)S(1)}, bf16[1,576,128]{2,1,0:T(8,128)(2,1)S(1)}, u32[]{:S(2)}, u32[]{:S(2)}) collective-permute-start(bf16[1,576,128]{2,1,0:T(8,128)(2,1)S(1)} %fusion.13), channel_id=1, source_target_pairs={{0,16},{4,20},{8,24},{12,28},{16,0},{20,4},{24,8},{28,12},{1,17},{... | collective-permute-start | bytes 442376 | tf_op jit(solution)/shard_map/ppermute | solution.py:329
  138.1 10.5 %collective-permute-start.10 = (bf16[512,128]{1,0:T(8,128)(2,1)S(1)}, bf16[512,128]{1,0:T(8,128)(2,1)S(1)}, u32[]{:S(2)}, u32[]{:S(2)}) collective-permute-start(bf16[512,128]{1,0:T(8,128)(2,1)S(1)} %fusion.26), channel_id=1, source_target_pairs={{0,1},{1,0},{2,3},{3,2},{4,5},{5,4},{6,7},{7,6},{8,9},{9,8},{10,11... | collective-permute-start | bytes 393224 | tf_op jit(solution)/shard_map/ppermute | solution.py:332
  140.2 12.2 %collective-permute-start.19 = (bf16[2,528,128]{2,1,0:T(8,128)(2,1)S(1)}, bf16[2,528,128]{2,1,0:T(8,128)(2,1)S(1)}, u32[]{:S(2)}, u32[]{:S(2)}) collective-permute-start(bf16[2,528,128]{2,1,0:T(8,128)(2,1)S(1)} %pad_maximum_fusion.2.refs_0_), channel_id=1, source_target_pairs={{0,8},{4,12},{8,0},{12,4},{16,24},{20,28},{24,16},{28,20},{1,9},{5... | collective-permute-start | bytes 811016 | tf_op jit(solution)/shard_map/ppermute | solution.py:329
  146.6 11.0 %collective-permute-start.30 = (bf16[2,576,128]{2,1,0:T(8,128)(2,1)S(1)}, bf16[2,576,128]{2,1,0:T(8,128)(2,1)S(1)}, u32[]{:S(2)}, u32[]{:S(2)}) collective-permute-start(bf16[2,576,128]{2,1,0:T(8,128)(2,1)S(1)} %pad_maximum_fusion.1.refs_4_), channel_id=1, source_target_pairs={{0,8},{4,12},{8,0},{12,4},{16,24},{20,28},{24,16},{28,20},{1,9},{5... | collective-permute-start | bytes 884744 | tf_op jit(solution)/shard_map/ppermute | solution.py:329
  146.8 10.9 %collective-permute-start.8 = (bf16[512,128]{1,0:T(8,128)(2,1)S(1)}, bf16[512,128]{1,0:T(8,128)(2,1)S(1)}, u32[]{:S(2)}, u32[]{:S(2)}) collective-permute-start(bf16[512,128]{1,0:T(8,128)(2,1)S(1)} %fusion.22), channel_id=1, source_target_pairs={{0,2},{1,3},{2,0},{3,1},{4,6},{5,7},{6,4},{7,5},{8,10},{9,11},{10,... | collective-permute-start | bytes 393224 | tf_op jit(solution)/shard_map/ppermute | solution.py:332
  148.6 9.9 %collective-permute-start.20 = (bf16[2,528,128]{2,1,0:T(8,128)(2,1)S(1)}, bf16[2,528,128]{2,1,0:T(8,128)(2,1)S(1)}, u32[]{:S(2)}, u32[]{:S(2)}) collective-permute-start(bf16[2,528,128]{2,1,0:T(8,128)(2,1)S(1)} %pad_maximum_fusion.2.refs_0_), channel_id=1, source_target_pairs={{0,4},{4,0},{8,12},{12,8},{16,20},{20,16},{24,28},{28,24},{1,5},{5... | collective-permute-start | bytes 811016 | tf_op jit(solution)/shard_map/ppermute | solution.py:326
  152.4 6.1 %collective-permute-start.21 = (bf16[2,528,128]{2,1,0:T(8,128)(2,1)S(1)}, bf16[2,528,128]{2,1,0:T(8,128)(2,1)S(1)}, u32[]{:S(2)}, u32[]{:S(2)}) collective-permute-start(bf16[2,528,128]{2,1,0:T(8,128)(2,1)S(1)} %collective-permute-done.19.refs_1_), channel_id=1, source_target_pairs={{0,4},{4,0},{8,12},{12,8},{16,20},{20,16},{24,28},{28,24},{1,5},{5... | collective-permute-start | bytes 811016 | tf_op jit(solution)/shard_map/ppermute | solution.py:326
  152.4 6.1 %collective-permute-start.31 = (bf16[2,576,128]{2,1,0:T(8,128)(2,1)S(1)}, bf16[2,576,128]{2,1,0:T(8,128)(2,1)S(1)}, u32[]{:S(2)}, u32[]{:S(2)}) collective-permute-start(bf16[2,576,128]{2,1,0:T(8,128)(2,1)S(1)} %pad_maximum_fusion.1.refs_4_), channel_id=1, source_target_pairs={{0,4},{4,0},{8,12},{12,8},{16,20},{20,16},{24,28},{28,24},{1,5},{5... | collective-permute-start | bytes 884744 | tf_op jit(solution)/shard_map/ppermute | solution.py:326
  157.7 1.6 collective-permute-start.32
  159.2 0.7 copy-start.12

commit v3 on v2

v3 whole, which is shorter than its diff:
```python
import functools

import jax
import jax.numpy as jnp
from jax import lax
from jax.experimental import pallas as pl
from jax.experimental.pallas import tpu as pltpu
from jax.sharding import PartitionSpec as P

loss_scale = 16.0
LANES = 128
SPAN = 9 * LANES
VMEM_BYTES = 52 * 1024 * 1024
bf16 = jnp.bfloat16
f32 = jnp.float32


def round_up(value, unit):
    return -(-value // unit) * unit


def matmul(left, right):
    return jnp.dot(left, right, preferred_element_type=f32)


def matmul_rt(left, right):
    return lax.dot_general(left, right, (((1,), (1,)), ((), ())), preferred_element_type=f32)


def reverse_bits(value, bits):
    out = 0
    for bit in range(bits):
        out = out | (((value >> bit) & 1) << (bits - 1 - bit))
    return out


def places_of(z_pos, n_z):
    bits = n_z.bit_length() - 1
    return [reverse_bits(z_pos ^ quarter, bits) for quarter in range(n_z)]


def put_blocks(ref, row_pos, places, offset, value):
    shards, rows_q = ref.shape[0], ref.shape[2]
    rows = value.shape[0] // shards
    step = round_up(rows, 16)
    blocks = value.shape[1] // LANES
    for shard in range(shards):
        slot = shard ^ row_pos
        for block in range(blocks):
            done = 0
            while done < rows:
                quarter, at = divmod(offset + block * step + done, rows_q)
                length = min(rows - done, rows_q - at)
                ref[slot, places[quarter], at : at + length, :] = value[
                    shard * rows + done : shard * rows + done + length,
                    block * LANES : (block + 1) * LANES,
                ].astype(ref.dtype)
                done += length
    return offset + blocks * step


def put_rows(ref, offset, value):
    for block in range(value.shape[1] // LANES):
        ref[offset + block : offset + block + 1, :] = value[:, block * LANES : (block + 1) * LANES]


def split_parts(pack, low, high):
    half = low.shape[1]
    low[...] = pack[:, :half]
    high[...] = pack[:, half:]


class Loads:
    def __init__(self, sources, targets, sems):
        self.copies = [
            pltpu.make_async_copy(source, target, sems.at[at])
            for at, (source, target) in enumerate(zip(sources, targets))
        ]
        self.targets = targets
        self.ready = set()
        for copy in self.copies:
            copy.start()

    def __call__(self, at):
        if at not in self.ready:
            self.copies[at].wait()
            self.ready.add(at)
        return self.targets[at][...]


def as_row(value):
    return value.reshape(1, value.shape[-1])


def front_kernel(pos, *refs):
    sources, outs, targets = refs[:11], refs[11:18], refs[18:29]
    halves, quarters, pack, sems = refs[29:]
    send_low, send_high, act_t_out, second_out, crossed_t_out, first_out, small = outs
    load = Loads(sources, targets, sems)
    core, row_pos = pos[0], pos[1]
    places = places_of(pos[2] // 2, pack.shape[1])
    stacked = jnp.concatenate([load(0), load(1)], axis=1)
    reduced = matmul(stacked, load(2)).astype(bf16)
    widened = matmul(reduced, load(3)) + as_row(load(4))
    wide = stacked.astype(f32)
    crossed = (wide * widened + wide).astype(bf16)
    pre_first = matmul(crossed, load(5)) + as_row(load(6))
    sig_first = jax.nn.sigmoid(pre_first)
    act_first = (pre_first * sig_first).astype(bf16)
    slope_first = sig_first * (1.0 + pre_first * (1.0 - sig_first))
    w_hidden2 = load(7)
    pre_second = matmul(act_first, w_hidden2) + as_row(load(8))
    sig_second = jax.nn.sigmoid(pre_second)
    act_second = (pre_second * sig_second).astype(bf16).astype(f32)
    slope_second = sig_second * (1.0 + pre_second * (1.0 - sig_second))
    w_logit = as_row(load(9))
    logits = jnp.sum(act_second * w_logit, axis=1, keepdims=True)
    labels = as_row(load(10))
    count = labels.shape[1]
    same = lax.broadcasted_iota(jnp.int32, (count, count), 0) == lax.broadcasted_iota(
        jnp.int32, (count, count), 1
    )
    label_col = jnp.sum(jnp.where(same, labels.astype(f32), 0.0), axis=1, keepdims=True)
    delta_logit = loss_scale * (jax.nn.sigmoid(logits) - label_col)
    delta_second = (delta_logit * w_logit * slope_second).astype(bf16)
    second_out[...] = delta_second
    put_rows(small, 16, jnp.sum(act_second * delta_logit, axis=0, keepdims=True))
    put_rows(small, 8, jnp.sum(delta_second.astype(f32), axis=0, keepdims=True))
    half = halves.shape[2]
    halves[0] = delta_second[:, :half]
    halves[1] = delta_second[:, half:]
    act_t = act_first.T
    act_t_out[...] = act_t
    offset = put_blocks(pack, row_pos, places, 0, matmul(act_t, halves[1 - core]))
    delta_first = (matmul_rt(delta_second, w_hidden2) * slope_first).astype(bf16)
    first_out[...] = delta_first
    put_rows(small, 0, jnp.sum(delta_first.astype(f32), axis=0, keepdims=True))
    quarter = quarters.shape[2]
    quarters[0] = delta_first[:, :quarter]
    quarters[1] = delta_first[:, half : half + quarter]
    crossed_t = crossed.T
    crossed_t_out[...] = crossed_t
    put_blocks(pack, row_pos, places, offset, matmul(crossed_t, quarters[1 - core]))
    split_parts(pack, send_low, send_high)


def middle_kernel(n_z, pos, *refs):
    sources, direct = refs[:6], refs[6:10]
    keep_low, keep_high, widened_out, reduced_out = refs[10:14]
    pooled_outs = refs[14 : 14 + n_z]
    rest = refs[14 + n_z :]
    targets = rest[:6]
    halves, quarters, pack, by_group, sems = rest[6:]
    act_t, delta_second, crossed_t, delta_first = direct
    load = Loads(sources, targets, sems)
    core, row_pos, z_pos = pos[0], pos[1], pos[2] // 2
    places = places_of(z_pos, pack.shape[1])
    half, quarter = halves.shape[2], quarters.shape[2]
    halves[0] = delta_second[:, :half]
    halves[1] = delta_second[:, half:]
    offset = put_blocks(pack, row_pos, places, 0, matmul(act_t[...], halves[core]))
    quarters[0] = delta_first[:, :quarter]
    quarters[1] = delta_first[:, half : half + quarter]
    put_blocks(pack, row_pos, places, offset, matmul(crossed_t[...], quarters[core]))
    split_parts(pack, keep_low, keep_high)
    delta_crossed = matmul_rt(delta_first[...], load(0))
    stacked = jnp.concatenate([load(1), load(2)], axis=1)
    delta_widened = (delta_crossed * stacked.astype(f32)).astype(bf16)
    widened_out[...] = delta_widened
    cross_up, cross_down = load(3), load(4)
    delta_reduced = matmul_rt(delta_widened, cross_up).astype(bf16)
    reduced_out[...] = delta_reduced
    reduced = matmul(stacked, cross_down).astype(bf16)
    widened = matmul(reduced, cross_up) + as_row(load(5))
    delta_stacked = delta_crossed * (widened + 1.0) + matmul_rt(delta_reduced, cross_down)
    width = targets[1].shape[1]
    per_group = by_group.shape[2]
    for table in range(2 * n_z * per_group):
        group = table // per_group
        by_group[group // 2, group % 2, table % per_group] = delta_stacked[
            :, width * (table + 1) : width * (table + 2)
        ].astype(bf16)
    for which in range(n_z):
        pooled_outs[which][0] = by_group[z_pos ^ which, core]
        pooled_outs[which][1] = by_group[z_pos ^ which, 1 - core]


def back_kernel(pos, *refs):
    dense_feat, pooled, cross_down, crossed_t, delta_first, delta_widened, delta_reduced = refs[:7]
    small_in = refs[7]
    send_low, send_high, keep_low, keep_high = refs[10:14]
    half_delta, quarters, pack, small = refs[14:]
    core, row_pos = pos[0], pos[1]
    n_row = pack.shape[0]
    places = places_of(pos[2] // 2, pack.shape[1])
    rank = delta_reduced.shape[1]
    feat = delta_widened.shape[1]
    hid = delta_first.shape[1]
    quarter = quarters.shape[2]
    half_delta[0] = delta_reduced[:, : rank // 2]
    half_delta[1] = delta_reduced[:, rank // 2 :]
    quarters[0] = delta_first[:, quarter : hid // 2]
    quarters[1] = delta_first[:, hid // 2 + quarter :]
    put_rows(small, 24, jnp.sum(delta_widened[...].astype(f32), axis=0, keepdims=True))
    small[0:24, :] = small_in[...]
    small[41:48, :] = jnp.zeros((7, LANES), f32)
    sums = jnp.concatenate([small[...]] * n_row, axis=0)
    stacked = jnp.concatenate([dense_feat[...], pooled[...]], axis=1)
    reduced_t = matmul(stacked, cross_down[...]).astype(bf16).T
    stacked_t = stacked.T
    for low, high, who in ((send_low, send_high, 1 - core), (keep_low, keep_high, core)):
        offset = put_blocks(pack, row_pos, places, 0, matmul(crossed_t[...], quarters[who]))
        offset = put_blocks(pack, row_pos, places, offset, matmul(stacked_t, half_delta[who]))
        start = pl.multiple_of(who * (feat - SPAN), LANES)
        offset = put_blocks(
            pack, row_pos, places, offset, matmul(reduced_t, delta_widened[:, pl.ds(start, SPAN)])
        )
        offset = put_blocks(pack, row_pos, places, offset, sums)
        tail = pack.shape[1] * pack.shape[2] - offset
        if tail:
            put_blocks(pack, row_pos, places, offset, jnp.zeros((n_row * tail, LANES), f32))
        split_parts(pack, low, high)


def select_kernel(n_z, *refs):
    out = refs[-1]
    for which in range(n_z):
        out[which] = refs[which][1]


def count_kernel(n_row, table, hot, n_z, pos, slots, *rest):
    direct, crossed, out = rest[:n_z], rest[n_z], rest[-1]
    block = out.shape[1]
    samples = crossed.shape[2]
    core, row_pos, z_pos = pos[0], pos[1], pos[2] // 2
    base = (pl.program_id(0) ^ row_pos) * block
    names = lax.broadcasted_iota(jnp.int16, (block, samples), 0)
    total = jnp.zeros((block, out.shape[2]), f32)
    one = jnp.ones((block, samples), bf16)
    zero = jnp.zeros((block, samples), bf16)
    for which in range(n_z):
        for held, who in ((direct[which][0, table], core), (crossed[which, table], 1 - core)):
            source = 2 * (z_pos ^ which) + who
            start = pl.multiple_of((source * n_row + row_pos) * samples, LANES)
            lines = slots[table, :, pl.ds(start, samples)] - base
            lines = jnp.where((lines >= 0) & (lines < block), lines, block).astype(jnp.int16)
            counts = zero
            for look in range(hot):
                line = jnp.broadcast_to(lines[look : look + 1, :], (block, samples))
                counts = counts + jnp.where(line == names, one, zero)
            total = total + matmul(counts, held)
    out[0] = total.astype(out.dtype)


def unpack_kernel(pos, *refs):
    parts = refs[0:8]
    g_down, g_up, g_first, g_second, g_small = refs[8:13]
    held = refs[13:15]
    core = pos[0]
    z_pos = pos[2] // 2
    for stream in range(2):
        lower, upper, lower_other, upper_other = parts[4 * stream : 4 * stream + 4]
        ref = held[stream]
        rows = lower.shape[1]
        n_z = 2 * lower.shape[0]
        z_bits = n_z.bit_length() - 1
        for who, pieces in ((core, (lower, upper)), (1 - core, (lower_other, upper_other))):
            for place in range(n_z):
                start = pl.multiple_of((reverse_bits(place, z_bits) ^ z_pos) * rows, 16)
                ref[who, pl.ds(start, rows), :] = pieces[place // (n_z // 2)][place % (n_z // 2)]
    front, back = held

    def take(ref, out, half, offset, columns):
        rows = out.shape[0]
        step = round_up(rows, 16)
        for column in columns:
            out[:, column * LANES : (column + 1) * LANES] = ref[
                half, offset : offset + rows, :
            ].astype(f32)
            offset += step
        return offset

    for half in range(2):
        blocks = g_second.shape[1] // LANES // 2
        offset = take(front, g_second, half, 0, range(half * blocks, (half + 1) * blocks))
        blocks = g_first.shape[1] // LANES // 4
        take(front, g_first, half, offset, range(2 * half * blocks, (2 * half + 1) * blocks))
        offset = take(
            back, g_first, half, 0, range((2 * half + 1) * blocks, (2 * half + 2) * blocks)
        )
        blocks = g_down.shape[1] // LANES // 2
        offset = take(back, g_down, half, offset, range(half * blocks, (half + 1) * blocks))
        blocks = g_up.shape[1] // LANES
        offset = take(back, g_up, half, offset, range(half * (blocks - 9), half * (blocks - 9) + 9))
    g_small[...] = back[0, offset : offset + 48, :].astype(f32)


def whole(memory=pltpu.VMEM):
    return pl.BlockSpec(memory_space=memory)


def cost(micros):
    return pl.CostEstimate(
        flops=int(micros * 1.0e9), transcendentals=0, bytes_accessed=int(micros * 3.0e6)
    )


def call(body, outs, scratch, in_specs, name, micros):
    return pl.pallas_call(
        body,
        out_shape=outs,
        in_specs=in_specs,
        out_specs=[whole()] * len(outs),
        scratch_shapes=scratch,
        compiler_params=pltpu.CompilerParams(vmem_limit_bytes=VMEM_BYTES),
        cost_estimate=cost(micros),
        name=name,
    )


def held_like(values):
    return [pltpu.VMEM(value.shape, value.dtype) for value in values]


def add_terms(terms):
    total = terms[0].astype(f32)
    for term in terms[1:]:
        total = total + term.astype(f32)
    return total


def local(
    dense_feat,
    pooled,
    labels,
    cross_down,
    cross_up,
    cross_bias,
    w_hidden1,
    bias1,
    w_hidden2,
    bias2,
    w_logit,
    lookup_slots,
):
    n_table = lax.axis_size("table")
    n_row = lax.axis_size("row")
    n_z = n_table // 2
    row_bits = n_row.bit_length() - 1
    z_bits = n_z.bit_length() - 1
    table_pos = lax.axis_index("table")
    row_pos = lax.axis_index("row")
    pos = jnp.stack([table_pos % 2, row_pos, table_pos]).astype(jnp.int32)
    batch, width = dense_feat.shape
    feat, rank = cross_down.shape
    hid = w_hidden1.shape[1]
    tab_grp, _, hot = lookup_slots.shape
    u_shard = batch * n_table * hot // 16

    def swap_cores(value):
        return lax.ppermute(value, "table", [(at, at ^ 1) for at in range(n_table)])

    def swap_z(value, which):
        return lax.ppermute(value, "table", [(at, at ^ (2 * which)) for at in range(n_table)])

    def swap_row(value, bit):
        return lax.ppermute(value, "row", [(at, at ^ (1 << bit)) for at in range(n_row)])

    rows_front = (hid // 2 // LANES) * round_up(hid // n_row, 16)
    rows_front += (hid // 4 // LANES) * round_up(feat // n_row, 16)
    rows_back = (hid // 4 // LANES) * round_up(feat // n_row, 16)
    rows_back += (rank // 2 // LANES) * round_up(feat // n_row, 16)
    rows_back += 9 * round_up(rank // n_row, 16) + 48
    rows_front, rows_back = (round_up(rows, 16 * n_z) for rows in (rows_front, rows_back))

    def half_pack(rows):
        return jax.ShapeDtypeStruct((n_row, n_z // 2, rows // n_z, LANES), bf16)

    def pack_scratch(rows):
        return pltpu.VMEM((n_row, n_z, rows // n_z, LANES), bf16)

    def wide(*shape):
        return jax.ShapeDtypeStruct(shape, bf16)

    smem, hbm, vmem, anywhere = whole(pltpu.SMEM), whole(pltpu.HBM), whole(), whole(pl.ANY)

    sources = (
        dense_feat,
        pooled,
        cross_down,
        cross_up,
        cross_bias,
        w_hidden1,
        bias1,
        w_hidden2,
        bias2,
        w_logit,
        labels,
    )
    send_low, send_high, act_t, delta_second, crossed_t, delta_first, small = call(
        front_kernel,
        [
            half_pack(rows_front),
            half_pack(rows_front),
            wide(hid, batch),
            wide(batch, hid),
            wide(feat, batch),
            wide(batch, hid),
            jax.ShapeDtypeStruct((24, LANES), f32),
        ],
        held_like(sources)
        + [
            pltpu.VMEM((2, batch, hid // 2), bf16),
            pltpu.VMEM((2, batch, hid // 4), bf16),
            pack_scratch(rows_front),
            pltpu.SemaphoreType.DMA((len(sources),)),
        ],
        [smem] + [hbm] * len(sources),
        "front",
        10,
    )(pos, *sources)
    got_low, got_high = swap_cores(send_low), swap_cores(send_high)

    sources = (w_hidden1, dense_feat, pooled, cross_up, cross_down, cross_bias)
    outs = call(
        functools.partial(middle_kernel, n_z),
        [half_pack(rows_front), half_pack(rows_front), wide(batch, feat), wide(batch, rank)]
        + [wide(2, tab_grp, batch, width)] * n_z,
        held_like(sources)
        + [
            pltpu.VMEM((2, batch, hid // 2), bf16),
            pltpu.VMEM((2, batch, hid // 4), bf16),
            pack_scratch(rows_front),
            pltpu.VMEM((n_z, 2, tab_grp, batch, width), bf16),
            pltpu.SemaphoreType.DMA((len(sources),)),
        ],
        [smem] + [hbm] * len(sources) + [vmem] * 4,
        "middle",
        8,
    )(pos, *sources, act_t, delta_second, crossed_t, delta_first)
    keep_low, keep_high, delta_widened, delta_reduced = outs[:4]
    pooled_out = outs[4:]

    low_first = tuple(range(row_bits))
    high_first = low_first[::-1]

    class Halving:
        def __init__(self, terms, order):
            self.terms = [term.reshape((2,) * row_bits + term.shape[1:]) for term in terms]
            self.order, self.left = order, list(range(row_bits - 1, -1, -1))
            self.sent = []

        def step(self, at):
            bit = self.order[at]
            axis = self.left.index(bit)
            self.left.remove(bit)
            far = [lax.index_in_dim(term, 1, axis, keepdims=False) for term in self.terms]
            sent = add_terms(far).astype(bf16)
            self.sent.append(sent)
            got = swap_row(sent, bit)
            near = [lax.index_in_dim(term, 0, axis, keepdims=False) for term in self.terms]
            self.terms = near + [got]
            return sent

    def sum_z(lower, upper):
        sents = [add_terms(upper).astype(bf16)]
        terms = lower + [swap_z(sents[0], 1)]
        for stage in range(1, z_bits):
            middle = n_z >> (stage + 1)
            sents.append(add_terms([term[middle:] for term in terms]).astype(bf16))
            terms = [term[:middle] for term in terms] + [swap_z(sents[-1], 1 << stage)]
        own = add_terms(terms).astype(bf16)
        for stage in range(z_bits - 1, 0, -1):
            own = jnp.concatenate([own, swap_z(own, 1 << stage)], axis=0)
        far = swap_z(own, 1)
        return sents, [own, far, swap_cores(own), swap_cores(far)]

    low1, high1 = Halving([keep_low, got_low], low_first), Halving([keep_high, got_high], high_first)
    ties = [low1.step(0), high1.step(0)]

    values = [pooled_out[0]] + [swap_z(pooled_out[which], which) for which in range(1, n_z)]

    send_low2, send_high2, keep_low2, keep_high2 = call(
        back_kernel,
        [half_pack(rows_back)] * 4,
        [
            pltpu.VMEM((2, batch, rank // 2), bf16),
            pltpu.VMEM((2, batch, hid // 4), bf16),
            pack_scratch(rows_back),
            pltpu.VMEM((48, LANES), f32),
        ],
        [smem] + [vmem] * 8 + [anywhere] * 2,
        "back",
        6,
    )(
        pos,
        dense_feat,
        pooled,
        cross_down,
        crossed_t,
        delta_first,
        delta_widened,
        delta_reduced,
        small,
        *ties,
    )
    got_low2, got_high2 = swap_cores(send_low2), swap_cores(send_high2)
    low2 = Halving([keep_low2, got_low2], low_first)
    high2 = Halving([keep_high2, got_high2], high_first)
    ties = [low2.step(0), high2.step(0)]
    for at in range(1, row_bits):
        ties += [low1.step(at), high1.step(at)]

    far_values = call(
        functools.partial(select_kernel, n_z),
        [wide(n_z, tab_grp, batch, width)],
        [],
        [vmem] * n_z + [anywhere] * len(ties),
        "select",
        1,
    )(*values, *ties)[0]
    values.append(swap_cores(far_values))

    for at in range(1, row_bits):
        low2.step(at), high2.step(at)
    sents1, stream1 = sum_z(low1.terms, high1.terms)
    sents2, stream2 = sum_z(low2.terms, high2.terms)

    slots = jnp.transpose(lookup_slots, (0, 2, 1))
    shares = []
    for table in range(tab_grp):
        sums = pl.pallas_call(
            functools.partial(count_kernel, n_row, table, hot, n_z),
            out_shape=wide(n_row, u_shard, width),
            grid=(n_row,),
            in_specs=[smem] + [vmem] * (2 + n_z) + [anywhere],
            out_specs=pl.BlockSpec((1, u_shard, width), lambda at: (at, 0, 0)),
            compiler_params=pltpu.CompilerParams(vmem_limit_bytes=VMEM_BYTES),
            cost_estimate=cost(6),
            name="counts",
        )(pos, slots, *values, sents1[min(table, len(sents1) - 1)])
        share = Halving([sums], high_first if table % 2 else low_first)
        for at in range(row_bits):
            share.step(at)
        shares.append(add_terms(share.terms))
    row_grads = jnp.stack(shares)

    g_down, g_up, g_first, g_second, g_small = call(
        unpack_kernel,
        [
            jax.ShapeDtypeStruct((feat // n_row, rank), f32),
            jax.ShapeDtypeStruct((rank // n_row, feat), f32),
            jax.ShapeDtypeStruct((feat // n_row, hid), f32),
            jax.ShapeDtypeStruct((hid // n_row, hid), f32),
            jax.ShapeDtypeStruct((48, LANES), f32),
        ],
        [pltpu.VMEM((2, rows, LANES), bf16) for rows in (rows_front, rows_back)],
        [smem] + [vmem] * 8,
        "unpack",
        4,
    )(pos, *stream1, *stream2)

    flat = g_small.reshape(-1)

    def part(start, length):
        share = length // n_row
        return lax.dynamic_slice(flat, (start * LANES + row_pos * share,), (share,))

    return (
        row_grads,
        g_down,
        g_up,
        part(24, feat),
        g_first,
        part(0, hid),
        g_second,
        part(8, hid),
        part(16, hid),
    )


def solution(mesh):
    in_specs = (
        P(("table", "row"), None),
        P(("table", "row"), None),
        P(("table", "row")),
        P(),
        P(),
        P(),
        P(),
        P(),
        P(),
        P(),
        P(),
        P("table", None, None),
    )
    out_specs = (
        P("table", "row", None),
        P("row", None),
        P("row", None),
        P("row"),
        P("row", None),
        P("row"),
        P("row", None),
        P("row"),
        P("row"),
    )
    return jax.shard_map(local, mesh=mesh, in_specs=in_specs, out_specs=out_specs, check_vma=False)
```

time: 165 us -> 165 us (level)
  starting transfers between devices: 40 us -> 30.6 us
  waiting for transfers between devices: 65 us -> 73.4 us
  Pallas kernels: 35.6 us -> 41.6 us
  local copies, waits for them, and re-layouts: 14.2 us -> 8.92 us
    ppermute x11, waiting for transfers between devices: 43.6 us -> 54.8 us  [swap_z(): lax.ppermute(value, 'table', [(at, at ^ 2 * which) for at in range(n_tabl...]
    ppermute x11, starting transfers between devices: 23.7 us -> 14.8 us  [swap_z(): lax.ppermute(value, 'table', [(at, at ^ 2 * which) for at in range(n_tabl...]
    slice x5 -> x1, local copies, waits for them, and re-layouts: 6.54 us -> 0.02 us  [step(): lax.index_in_dim(term, 1, axis, keepdims=False)]
    pallas_call x2 -> x4, Pallas kernels: 21.4 us -> 27.2 us  [the longest x1 10.9 us: local(): call(front_kernel, [half_pack(rows_front), half_pack(rows_front), wide(hi...]
    ppermute x12, waiting for transfers between devices: 20.7 us -> 17.9 us  [swap_row(): lax.ppermute(value, 'row', [(at, at ^ 1 << bit) for at in range(n_row)])]
    unnamed x26 -> x40, local copies, waits for them, and re-layouts: 5.53 us -> 6.62 us
  transfers between devices with their start and end apart: 33 -> 32, of which waited for: 14 -> 14; matrix products, arithmetic and copies ran while one was open for 9% -> 6% of each run, Pallas kernels for 7% -> 17%
where the time goes in v3:
time: 165 us
  waiting for transfers between devices  73.4 us (44%)
  Pallas kernels  41.6 us (25%)
  starting transfers between devices  30.6 us (19%)
  other arithmetic  9.12 us (6%)
  local copies, waits for them, and re-layouts  8.92 us (5%)
    ppermute x11, waiting for transfers between devices, swap_z(): lax.ppermute(value, 'table', [(at, at ^ 2 * which) for at in range(n_tabl...  54.8 us
    ppermute x12, waiting for transfers between devices, swap_row(): lax.ppermute(value, 'row', [(at, at ^ 1 << bit) for at in range(n_row)])  17.9 us
    ppermute x12, starting transfers between devices, swap_row(): lax.ppermute(value, 'row', [(at, at ^ 1 << bit) for at in range(n_row)])  15 us
    ppermute x11, starting transfers between devices, swap_z(): lax.ppermute(value, 'table', [(at, at ^ 2 * which) for at in range(n_tabl...  14.8 us
    pallas_call x2, Pallas kernels, local(): pl.pallas_call(functools.partial(count_kernel, n_row, table, hot, n_z), o...  11 us
    pallas_call x1, Pallas kernels, local(): call(front_kernel, [half_pack(rows_front), half_pack(rows_front), wide(hi...  10.9 us
    pallas_call x1, Pallas kernels, local(): call(functools.partial(middle_kernel, n_z), [half_pack(rows_front), half_...  8.54 us
    pallas_call x1, Pallas kernels, local(): call(back_kernel, [half_pack(rows_back)] * 4, [pltpu.VMEM((2, batch, rank...  6.93 us
  transfers between devices with their start and end apart: 32, of which 14 were waited for; matrix products, arithmetic and copies ran while one was open for 6% of the time, Pallas kernels for 17%

profile of v3, /device:TPU:0, one launch (start us, length us, event | category | flops | bytes accessed | tf_op | source)
XLA Modules:
  0.0 164.6 jit_solution(4026365106822043973)
XLA Ops:
  0.7 0.8 copy-done.1
  1.6 0.7 copy-done.2
  2.3 0.7 copy-done.3
  5.0 10.9 %front.1 = (bf16[4,2,528,128]{3,2,1,0:T(8,128)(2,1)}, bf16[4,2,528,128]{3,2,1,0:T(8,128)(2,1)}, bf16[1024,256]{1,0:T(8,128)(2,1)S(1)}, bf16[256,1024]{1,0:T(8,12...) custom-call(s32[3]{0:T(128)S(1)} %pad_add_fusion.pos, ...), custom_call_target="tpu_custom_call" | custom-call | flops 10000000000 | bytes 30000000 | tf_op jit(solution)/shard_map/front/pallas_call | solution.py:400
  16.0 0.8 copy-done.7
  16.8 0.8 copy-done.9
  18.1 8.5 %middle.1 = (bf16[4,2,528,128]{3,2,1,0:T(8,128)(2,1)}, bf16[4,2,528,128]{3,2,1,0:T(8,128)(2,1)}, bf16[256,2176]{1,0:T(8,128)(2,1)}, bf16[256,256]{1,0:T(8,128)(2...) custom-call(s32[3]{0:T(128)S(1)} %pad_add_fusion.pos, ...), custom_call_target="tpu_custom_call" | custom-call | flops 8000000000 | bytes 24000000 | tf_op jit(solution)/shard_map/middle/pallas_call | solution.py:425
  26.6 1.3 add_convert_fusion.2.refs_9_
  28.0 3.0 %collective-permute-start.8 = (bf16[2,2,528,128]{3,2,1,0:T(8,128)(2,1)S(1)}, bf16[2,2,528,128]{3,2,1,0:T(8,128)(2,1)S(1)}, u32[]{:S(2)}, u32[]{:S(2)}) collective-permute-start(bf16[2,2,528,128]{3,2,1,0:T(8,128)(2,1)S(1)} %add_convert_fusion.2.refs_9_), channel_id=1, source_target_pairs={{0,2},{1,3},{2,0},{3,1},{4,6},{5,7},{6,4},{7,5},{8,10},{9,11},{10,... | collective-permute-start | bytes 1622024 | tf_op jit(solution)/shard_map/ppermute | solution.py:367
  31.1 1.6 collective-permute-start.7
  32.7 6.9 %back.1 = (bf16[4,2,576,128]{3,2,1,0:T(8,128)(2,1)}, bf16[4,2,576,128]{3,2,1,0:T(8,128)(2,1)}, bf16[4,2,576,128]{3,2,1,0:T(8,128)(2,1)}, bf16[4,2,576,128]{3,2,1,0:T(8,128)(2,1)}) custom-call(s32[3]{0:T(128)S(1)} %pad_add_fusion.pos, bf16[256,128]{1,0:T(8,128)(2,1)S(1)} %copy-done.1, bf16[256,2048]{1,0:T(8,128)(2,1)} %refs_1_.5, bf16[2176,256]{1,0:T(8,128)(2,1)} %refs_2_.5, ...), custom_call_target="tpu_custom_call" | custom-call | flops 6000000000 | bytes 18000000 | tf_op jit(solution)/shard_map/back/pallas_call | solution.py:483
  39.6 3.8 %collective-permute-done.8 = bf16[2,2,528,128]{3,2,1,0:T(8,128)(2,1)S(1)} collective-permute-done((bf16[2,2,528,128]{3,2,1,0:T(8,128)(2,1)S(1)}, bf16[2,2,528,128]{3,2,1,0:T(8,128)(2,1)S(1)}, u32[]{:S(2)}, u32[]{:S(2)}) %collective-permute-start.8) | collective-permute-done | bytes 540704 | tf_op jit(solution)/shard_map/ppermute | solution.py:367
  43.6 1.8 %collective-permute-start.10 = (bf16[2,528,128]{2,1,0:T(8,128)(2,1)S(1)}, bf16[2,528,128]{2,1,0:T(8,128)(2,1)S(1)}, u32[]{:S(2)}, u32[]{:S(2)}) collective-permute-start(bf16[2,528,128]{2,1,0:T(8,128)(2,1)S(1)} %fusion.14.refs_7_), channel_id=1, source_target_pairs={{0,1},{1,0},{2,3},{3,2},{4,5},{5,4},{6,7},{7,6},{8,9},{9,8},{10,11... | collective-permute-start | bytes 811016 | tf_op jit(solution)/shard_map/ppermute | solution.py:367
  45.5 1.6 collective-permute-start.13
  47.1 4.4 %collective-permute-done.10 = bf16[2,528,128]{2,1,0:T(8,128)(2,1)S(1)} collective-permute-done((bf16[2,528,128]{2,1,0:T(8,128)(2,1)S(1)}, bf16[2,528,128]{2,1,0:T(8,128)(2,1)S(1)}, u32[]{:S(2)}, u32[]{:S(2)}) %collective-permute-start.10) | collective-permute-done | bytes 270368 | tf_op jit(solution)/shard_map/ppermute | solution.py:367
  51.6 1.6 collective-permute-start.14
  53.7 0.7 collective-permute-done.13
  54.5 2.6 %collective-permute-start.1 = (bf16[2,2,256,128]{3,2,1,0:T(8,128)(2,1)S(1)}, bf16[2,2,256,128]{3,2,1,0:T(8,128)(2,1)S(1)}, u32[]{:S(2)}, u32[]{:S(2)}) collective-permute-start(bf16[2,2,256,128]{3,2,1,0:T(8,128)(2,1)S(1)} %get-tuple-element.39), channel_id=1, source_target_pairs={{0,16},{4,20},{8,24},{12,28},{16,0},{20,4},{24,8},{28,12},{1,17},{... | collective-permute-start | bytes 786440 | tf_op jit(solution)/shard_map/ppermute | solution.py:364
  57.1 9.7 %collective-permute-done.14 = bf16[2,528,128]{2,1,0:T(8,128)(2,1)S(1)} collective-permute-done((bf16[2,528,128]{2,1,0:T(8,128)(2,1)S(1)}, bf16[2,528,128]{2,1,0:T(8,128)(2,1)S(1)}, u32[]{:S(2)}, u32[]{:S(2)}) %collective-permute-start.14) | collective-permute-done | bytes 270368 | tf_op jit(solution)/shard_map/ppermute | solution.py:364
  66.7 2.9 %collective-permute-start.2 = (bf16[2,2,256,128]{3,2,1,0:T(8,128)(2,1)S(1)}, bf16[2,2,256,128]{3,2,1,0:T(8,128)(2,1)S(1)}, u32[]{:S(2)}, u32[]{:S(2)}) collective-permute-start(bf16[2,2,256,128]{3,2,1,0:T(8,128)(2,1)S(1)} %get-tuple-element.40), channel_id=1, source_target_pairs={{0,24},{4,28},{8,16},{12,20},{16,8},{20,12},{24,0},{28,4},{1,25},{... | collective-permute-start | bytes 786440 | tf_op jit(solution)/shard_map/ppermute | solution.py:364
  69.9 1.0 add_convert_fusion.refs_5_
  70.9 15.1 %collective-permute-done.17 = bf16[1,528,128]{2,1,0:T(8,128)(2,1)S(1)} collective-permute-done((bf16[1,528,128]{2,1,0:T(8,128)(2,1)S(1)}, bf16[1,528,128]{2,1,0:T(8,128)(2,1)S(1)}, u32[]{:S(2)}, u32[]{:S(2)}) %collective-permute-start.17) | collective-permute-done | bytes 135200 | tf_op jit(solution)/shard_map/ppermute | solution.py:364
  86.0 1.5 collective-permute-start.24
  87.5 1.0 fusion.18
  88.7 1.1 fusion.refs_4_
  89.8 4.8 %collective-permute-done.18 = bf16[1,528,128]{2,1,0:T(8,128)(2,1)S(1)} collective-permute-done((bf16[1,528,128]{2,1,0:T(8,128)(2,1)S(1)}, bf16[1,528,128]{2,1,0:T(8,128)(2,1)S(1)}, u32[]{:S(2)}, u32[]{:S(2)}) %collective-permute-start.18) | collective-permute-done | bytes 135200 | tf_op jit(solution)/shard_map/ppermute | solution.py:364
  94.6 2.7 %collective-permute-start.19 = (bf16[2,528,128]{2,1,0:T(8,128)(2,1)S(1)}, bf16[2,528,128]{2,1,0:T(8,128)(2,1)S(1)}, u32[]{:S(2)}, u32[]{:S(2)}) collective-permute-start(bf16[2,528,128]{2,1,0:T(8,128)(2,1)S(1)} %pad_maximum_fusion.2.refs_0_), channel_id=1, source_target_pairs={{0,8},{4,12},{8,0},{12,4},{16,24},{20,28},{24,16},{28,20},{1,9},{5... | collective-permute-start | bytes 811016 | tf_op jit(solution)/shard_map/ppermute | solution.py:364
  97.4 0.8 select.3
  98.2 0.8 collective-permute-start.22
  99.2 2.6 %collective-permute-done.19.refs_1_ = bf16[2,528,128]{2,1,0:T(8,128)(2,1)S(1)} collective-permute-done((bf16[2,528,128]{2,1,0:T(8,128)(2,1)S(1)}, bf16[2,528,128]{2,1,0:T(8,128)(2,1)S(1)}, u32[]{:S(2)}, u32[]{:S(2)}) %collective-permute-start.19) | collective-permute-done | bytes 270368 | tf_op jit(solution)/shard_map/ppermute | solution.py:364
  101.8 1.3 fusion.6
  103.0 2.8 %collective-permute-start.25 = (bf16[2,576,128]{2,1,0:T(8,128)(2,1)S(1)}, bf16[2,576,128]{2,1,0:T(8,128)(2,1)S(1)}, u32[]{:S(2)}, u32[]{:S(2)}) collective-permute-start(bf16[2,576,128]{2,1,0:T(8,128)(2,1)S(1)} %fusion.6), channel_id=1, source_target_pairs={{0,1},{1,0},{2,3},{3,2},{4,5},{5,4},{6,7},{7,6},{8,9},{9,8},{10,11... | collective-permute-start | bytes 884744 | tf_op jit(solution)/shard_map/ppermute | solution.py:367
  105.9 5.2 %counts.3 = bf16[4,512,128]{2,1,0:T(8,128)(2,1)S(1)} custom-call(s32[3]{0:T(128)S(1)} %pad_add_fusion.pos, s32[2,4,8192]{2,1,0:T(4,128)S(1)} %bitcast.102, bf16[2,2,256,128]{3,2,1,0:T(8,128)(2,1)S(1)} %get-tuple-element.37.refs_0_.rest_0_, bf16[2,2,256,128]{3,2,1,0:T(8,128)(2,1)S(1)} %collective-permute-done.refs_1_.rest_1_, ...), custom_call_target="tpu_custom_call" | custom-call | flops 6000000000 | bytes 18000000 | tf_op jit(solution)/shard_map/counts/pallas_call | solution.py:532
  111.3 3.2 %collective-permute-done.22 = bf16[2,2,576,128]{3,2,1,0:T(8,128)(2,1)S(1)} collective-permute-done((bf16[2,2,576,128]{3,2,1,0:T(8,128)(2,1)}, bf16[2,2,576,128]{3,2,1,0:T(8,128)(2,1)S(1)}, u32[]{:S(2)}, u32[]{:S(2)}) %collective-permute-start.22) | collective-permute-done | bytes 589856 | tf_op jit(solution)/shard_map/ppermute | solution.py:367
  114.7 5.7 %collective-permute-done.25 = bf16[2,576,128]{2,1,0:T(8,128)(2,1)S(1)} collective-permute-done((bf16[2,576,128]{2,1,0:T(8,128)(2,1)S(1)}, bf16[2,576,128]{2,1,0:T(8,128)(2,1)S(1)}, u32[]{:S(2)}, u32[]{:S(2)}) %collective-permute-start.25) | collective-permute-done | bytes 294944 | tf_op jit(solution)/shard_map/ppermute | solution.py:367
  120.5 1.3 fusion.2
  121.8 1.1 collective-permute-start.26
  122.9 5.8 %counts.2 = bf16[4,512,128]{2,1,0:T(8,128)(2,1)} custom-call(s32[3]{0:T(128)S(1)} %pad_add_fusion.pos, s32[2,4,8192]{2,1,0:T(4,128)S(1)} %bitcast.103, bf16[2,2,256,128]{3,2,1,0:T(8,128)(2,1)S(1)} %get-tuple-element.37.refs_0_.rest_0_, bf16[2,2,256,128]{3,2,1,0:T(8,128)(2,1)S(1)} %collective-permute-done.refs_1_.rest_1_, ...), custom_call_target="tpu_custom_call" | custom-call | flops 6000000000 | bytes 18000000 | tf_op jit(solution)/shard_map/counts/pallas_call | solution.py:532
  128.7 1.8 %collective-permute-done.26 = bf16[2,576,128]{2,1,0:T(8,128)(2,1)S(1)} collective-permute-done((bf16[2,576,128]{2,1,0:T(8,128)(2,1)S(1)}, bf16[2,576,128]{2,1,0:T(8,128)(2,1)S(1)}, u32[]{:S(2)}, u32[]{:S(2)}) %collective-permute-start.26) | collective-permute-done | bytes 294944 | tf_op jit(solution)/shard_map/ppermute | solution.py:364
  130.6 3.0 %collective-permute-start.27 = (bf16[1,576,128]{2,1,0:T(8,128)(2,1)S(1)}, bf16[1,576,128]{2,1,0:T(8,128)(2,1)S(1)}, u32[]{:S(2)}, u32[]{:S(2)}) collective-permute-start(bf16[1,576,128]{2,1,0:T(8,128)(2,1)S(1)} %fusion.9), channel_id=1, source_target_pairs={{0,16},{4,20},{8,24},{12,28},{16,0},{20,4},{24,8},{28,12},{1,17},{... | collective-permute-start | bytes 442376 | tf_op jit(solution)/shard_map/ppermute | solution.py:364
  133.6 1.0 slice_bitcast_fusion.2
  135.1 4.4 %collective-permute-done.27 = bf16[1,576,128]{2,1,0:T(8,128)(2,1)S(1)} collective-permute-done((bf16[1,576,128]{2,1,0:T(8,128)(2,1)S(1)}, bf16[1,576,128]{2,1,0:T(8,128)(2,1)S(1)}, u32[]{:S(2)}, u32[]{:S(2)}) %collective-permute-start.27) | collective-permute-done | bytes 147488 | tf_op jit(solution)/shard_map/ppermute | solution.py:364
  140.0 1.0 collective-permute-start.16
  140.9 7.7 %collective-permute-done.28 = bf16[1,576,128]{2,1,0:T(8,128)(2,1)S(1)} collective-permute-done((bf16[1,576,128]{2,1,0:T(8,128)(2,1)S(1)}, bf16[1,576,128]{2,1,0:T(8,128)(2,1)S(1)}, u32[]{:S(2)}, u32[]{:S(2)}) %collective-permute-start.28) | collective-permute-done | bytes 147488 | tf_op jit(solution)/shard_map/ppermute | solution.py:364
  149.1 8.6 %collective-permute-done.29.refs_5_ = bf16[2,576,128]{2,1,0:T(8,128)(2,1)S(1)} collective-permute-done((bf16[2,576,128]{2,1,0:T(8,128)(2,1)S(1)}, bf16[2,576,128]{2,1,0:T(8,128)(2,1)S(1)}, u32[]{:S(2)}, u32[]{:S(2)}) %collective-permute-start.29) | collective-permute-done | bytes 294944 | tf_op jit(solution)/shard_map/ppermute | solution.py:364
  157.8 0.8 pad_maximum_fusion
  159.3 0.7 copy-done.19
  160.0 3.3 %unpack.1 = (f32[544,256]{1,0:T(8,128)}, f32[64,2176]{1,0:T(8,128)}, f32[544,1024]{1,0:T(8,128)}, f32[256,1024]{1,0:T(8,128)}, f32[48,128]{1,0:T(8,128)S(1)}) custom-call(s32[3]{0:T(128)S(1)} %pad_add_fusion.pos, bf16[2,528,128]{2,1,0:T(8,128)(2,1)S(1)} %pad_maximum_fusion.2.refs_0_, bf16[2,528,128]{2,1,0:T(8,128)(2,1)S(1)} %collective-permute-done.19.refs_1_, ...), custom_call_target="tpu_custom_call" | custom-call | flops 4000000000 | bytes 12000000 | tf_op jit(solution)/shard_map/unpack/pallas_call | solution.py:548
  (89 shorter events, 8.1 us)
Async XLA Ops:
  0.7 0.8 copy-start.1
  1.6 0.7 copy-start.2
  16.0 0.8 copy-start.7
  16.8 0.8 copy-start.9
  17.6 9.1 %collective-permute-start.4 = (bf16[4,2,528,128]{3,2,1,0:T(8,128)(2,1)}, bf16[4,2,528,128]{3,2,1,0:T(8,128)(2,1)S(1)}, u32[]{:S(2)}, u32[]{:S(2)}) collective-permute-start(bf16[4,2,528,128]{3,2,1,0:T(8,128)(2,1)} %get-tuple-element.47), channel_id=1, source_target_pairs={{0,4},{4,0},{8,12},{12,8},{16,20},{20,16},{24,28},{28,24},{1,5},{5... | collective-permute-start | bytes 3244040 | tf_op jit(solution)/shard_map/ppermute | solution.py:361
  18.0 13.0 %collective-permute-start.3 = (bf16[4,2,528,128]{3,2,1,0:T(8,128)(2,1)}, bf16[4,2,528,128]{3,2,1,0:T(8,128)(2,1)S(1)}, u32[]{:S(2)}, u32[]{:S(2)}) collective-permute-start(bf16[4,2,528,128]{3,2,1,0:T(8,128)(2,1)} %get-tuple-element.45), channel_id=1, source_target_pairs={{0,4},{4,0},{8,12},{12,8},{16,20},{20,16},{24,28},{28,24},{1,5},{5... | collective-permute-start | bytes 3244040 | tf_op jit(solution)/shard_map/ppermute | solution.py:361
  26.6 4.4 %copy-start.15 = (bf16[4,2,528,128]{3,2,1,0:T(8,128)(2,1)S(1)}, bf16[4,2,528,128]{3,2,1,0:T(8,128)(2,1)}, u32[]{:S(2)}) copy-start(bf16[4,2,528,128]{3,2,1,0:T(8,128)(2,1)} %get-tuple-element.44) | copy-start | bytes 3244036
  28.0 4.8 %copy-start.8 = (bf16[256,1024]{1,0:T(8,128)(2,1)S(1)}, bf16[256,1024]{1,0:T(8,128)(2,1)}, u32[]{:S(2)}) copy-start(bf16[256,1024]{1,0:T(8,128)(2,1)} %copy-done.7) | copy-start | bytes 1572868
  28.0 15.5 %collective-permute-start.8 = (bf16[2,2,528,128]{3,2,1,0:T(8,128)(2,1)S(1)}, bf16[2,2,528,128]{3,2,1,0:T(8,128)(2,1)S(1)}, u32[]{:S(2)}, u32[]{:S(2)}) collective-permute-start(bf16[2,2,528,128]{3,2,1,0:T(8,128)(2,1)S(1)} %add_convert_fusion.2.refs_9_), channel_id=1, source_target_pairs={{0,2},{1,3},{2,0},{3,1},{4,6},{5,7},{6,4},{7,5},{8,10},{9,11},{10,... | collective-permute-start | bytes 1622024 | tf_op jit(solution)/shard_map/ppermute | solution.py:367
  31.1 14.2 %collective-permute-start.7 = (bf16[2,2,528,128]{3,2,1,0:T(8,128)(2,1)S(1)}, bf16[2,2,528,128]{3,2,1,0:T(8,128)(2,1)S(1)}, u32[]{:S(2)}, u32[]{:S(2)}) collective-permute-start(bf16[2,2,528,128]{3,2,1,0:T(8,128)(2,1)S(1)} %fusion.3.refs_8_), channel_id=1, source_target_pairs={{0,1},{1,0},{2,3},{3,2},{4,5},{5,4},{6,7},{7,6},{8,9},{9,8},{10,11... | collective-permute-start | bytes 1622024 | tf_op jit(solution)/shard_map/ppermute | solution.py:367
  32.7 10.7 %copy-start.16 = (bf16[4,2,528,128]{3,2,1,0:T(8,128)(2,1)S(1)}, bf16[4,2,528,128]{3,2,1,0:T(8,128)(2,1)}, u32[]{:S(2)}) copy-start(bf16[4,2,528,128]{3,2,1,0:T(8,128)(2,1)} %get-tuple-element.46) | copy-start | bytes 3244036
  39.6 30.1 %collective-permute-start.6 = (bf16[4,2,576,128]{3,2,1,0:T(8,128)(2,1)}, bf16[4,2,576,128]{3,2,1,0:T(8,128)(2,1)S(1)}, u32[]{:S(2)}, u32[]{:S(2)}) collective-permute-start(bf16[4,2,576,128]{3,2,1,0:T(8,128)(2,1)} %get-tuple-element.51), channel_id=1, source_target_pairs={{0,4},{4,0},{8,12},{12,8},{16,20},{20,16},{24,28},{28,24},{1,5},{5... | collective-permute-start | bytes 3538952 | tf_op jit(solution)/shard_map/ppermute | solution.py:361
  43.6 7.9 %collective-permute-start.10 = (bf16[2,528,128]{2,1,0:T(8,128)(2,1)S(1)}, bf16[2,528,128]{2,1,0:T(8,128)(2,1)S(1)}, u32[]{:S(2)}, u32[]{:S(2)}) collective-permute-start(bf16[2,528,128]{2,1,0:T(8,128)(2,1)S(1)} %fusion.14.refs_7_), channel_id=1, source_target_pairs={{0,1},{1,0},{2,3},{3,2},{4,5},{5,4},{6,7},{7,6},{8,9},{9,8},{10,11... | collective-permute-start | bytes 811016 | tf_op jit(solution)/shard_map/ppermute | solution.py:367
  45.3 43.2 %collective-permute-start.5 = (bf16[4,2,576,128]{3,2,1,0:T(8,128)(2,1)}, bf16[4,2,576,128]{3,2,1,0:T(8,128)(2,1)S(1)}, u32[]{:S(2)}, u32[]{:S(2)}) collective-permute-start(bf16[4,2,576,128]{3,2,1,0:T(8,128)(2,1)} %get-tuple-element.49), channel_id=1, source_target_pairs={{0,4},{4,0},{8,12},{12,8},{16,20},{20,16},{24,28},{28,24},{1,5},{5... | collective-permute-start | bytes 3538952 | tf_op jit(solution)/shard_map/ppermute | solution.py:361
  45.3 24.3 %copy-start.17 = (bf16[2,2,528,128]{3,2,1,0:T(8,128)(2,1)}, bf16[2,2,528,128]{3,2,1,0:T(8,128)(2,1)S(1)}, u32[]{:S(2)}) copy-start(bf16[2,2,528,128]{3,2,1,0:T(8,128)(2,1)S(1)} %collective-permute-done.7) | copy-start | bytes 1622020
  45.5 24.4 %copy-start.13 = (bf16[4,2,576,128]{3,2,1,0:T(8,128)(2,1)S(1)}, bf16[4,2,576,128]{3,2,1,0:T(8,128)(2,1)}, u32[]{:S(2)}) copy-start(bf16[4,2,576,128]{3,2,1,0:T(8,128)(2,1)} %get-tuple-element.50) | copy-start | bytes 3538948
  45.5 9.0 %collective-permute-start.13 = (bf16[2,528,128]{2,1,0:T(8,128)(2,1)S(1)}, bf16[2,528,128]{2,1,0:T(8,128)(2,1)S(1)}, u32[]{:S(2)}, u32[]{:S(2)}) collective-permute-start(bf16[2,528,128]{2,1,0:T(8,128)(2,1)S(1)} %fusion.4.refs_6_), channel_id=1, source_target_pairs={{0,2},{1,3},{2,0},{3,1},{4,6},{5,7},{6,4},{7,5},{8,10},{9,11},{10,... | collective-permute-start | bytes 811016 | tf_op jit(solution)/shard_map/ppermute | solution.py:367
  51.6 15.1 %collective-permute-start.14 = (bf16[2,528,128]{2,1,0:T(8,128)(2,1)S(1)}, bf16[2,528,128]{2,1,0:T(8,128)(2,1)S(1)}, u32[]{:S(2)}, u32[]{:S(2)}) collective-permute-start(bf16[2,528,128]{2,1,0:T(8,128)(2,1)S(1)} %fusion.5.rest_5_), channel_id=1, source_target_pairs={{0,8},{4,12},{8,0},{12,4},{16,24},{20,28},{24,16},{28,20},{1,9},{5... | collective-permute-start | bytes 811016 | tf_op jit(solution)/shard_map/ppermute | solution.py:364
  53.2 44.2 %collective-permute-start = (bf16[2,2,256,128]{3,2,1,0:T(8,128)(2,1)S(1)}, bf16[2,2,256,128]{3,2,1,0:T(8,128)(2,1)S(1)}, u32[]{:S(2)}, u32[]{:S(2)}) collective-permute-start(bf16[2,2,256,128]{3,2,1,0:T(8,128)(2,1)S(1)} %get-tuple-element.38), channel_id=1, source_target_pairs={{0,8},{4,12},{8,0},{12,4},{16,24},{20,28},{24,16},{28,20},{1,9},{5... | collective-permute-start | bytes 786440 | tf_op jit(solution)/shard_map/ppermute | solution.py:364
  54.5 42.9 %collective-permute-start.1 = (bf16[2,2,256,128]{3,2,1,0:T(8,128)(2,1)S(1)}, bf16[2,2,256,128]{3,2,1,0:T(8,128)(2,1)S(1)}, u32[]{:S(2)}, u32[]{:S(2)}) collective-permute-start(bf16[2,2,256,128]{3,2,1,0:T(8,128)(2,1)S(1)} %get-tuple-element.39), channel_id=1, source_target_pairs={{0,16},{4,20},{8,24},{12,28},{16,0},{20,4},{24,8},{28,12},{1,17},{... | collective-permute-start | bytes 786440 | tf_op jit(solution)/shard_map/ppermute | solution.py:364
  66.7 30.6 %collective-permute-start.2 = (bf16[2,2,256,128]{3,2,1,0:T(8,128)(2,1)S(1)}, bf16[2,2,256,128]{3,2,1,0:T(8,128)(2,1)S(1)}, u32[]{:S(2)}, u32[]{:S(2)}) collective-permute-start(bf16[2,2,256,128]{3,2,1,0:T(8,128)(2,1)S(1)} %get-tuple-element.40), channel_id=1, source_target_pairs={{0,24},{4,28},{8,16},{12,20},{16,8},{20,12},{24,0},{28,4},{1,25},{... | collective-permute-start | bytes 786440 | tf_op jit(solution)/shard_map/ppermute | solution.py:364
  69.8 18.8 %copy-start.14 = (bf16[4,2,576,128]{3,2,1,0:T(8,128)(2,1)}, bf16[4,2,576,128]{3,2,1,0:T(8,128)(2,1)S(1)}, u32[]{:S(2)}) copy-start(bf16[4,2,576,128]{3,2,1,0:T(8,128)(2,1)S(1)} %collective-permute-done.6) | copy-start | bytes 3538948
  69.8 16.2 %collective-permute-start.17 = (bf16[1,528,128]{2,1,0:T(8,128)(2,1)S(1)}, bf16[1,528,128]{2,1,0:T(8,128)(2,1)S(1)}, u32[]{:S(2)}, u32[]{:S(2)}) collective-permute-start(bf16[1,528,128]{2,1,0:T(8,128)(2,1)S(1)} %fusion.21.rest_5_), channel_id=1, source_target_pairs={{0,16},{4,20},{8,24},{12,28},{16,0},{20,4},{24,8},{28,12},{1,17},{... | collective-permute-start | bytes 405512 | tf_op jit(solution)/shard_map/ppermute | solution.py:364
  69.9 18.8 %copy-start.10 = (bf16[4,2,576,128]{3,2,1,0:T(8,128)(2,1)S(1)}, bf16[4,2,576,128]{3,2,1,0:T(8,128)(2,1)}, u32[]{:S(2)}) copy-start(bf16[4,2,576,128]{3,2,1,0:T(8,128)(2,1)} %get-tuple-element.48) | copy-start | bytes 3538948
  86.0 15.8 %collective-permute-start.24 = (bf16[2,2,576,128]{3,2,1,0:T(8,128)(2,1)}, bf16[2,2,576,128]{3,2,1,0:T(8,128)(2,1)}, u32[]{:S(2)}, u32[]{:S(2)}) collective-permute-start(bf16[2,2,576,128]{3,2,1,0:T(8,128)(2,1)} %add_convert_fusion.refs_5_), channel_id=1, source_target_pairs={{0,2},{1,3},{2,0},{3,1},{4,6},{5,7},{6,4},{7,5},{8,10},{9,11},{10,... | collective-permute-start | bytes 1769480 | tf_op jit(solution)/shard_map/ppermute | solution.py:367
  88.6 6.1 %copy-start.11 = (bf16[4,2,576,128]{3,2,1,0:T(8,128)(2,1)}, bf16[4,2,576,128]{3,2,1,0:T(8,128)(2,1)S(1)}, u32[]{:S(2)}) copy-start(bf16[4,2,576,128]{3,2,1,0:T(8,128)(2,1)S(1)} %collective-permute-done.5) | copy-start | bytes 3538948
  88.6 6.0 %collective-permute-start.18 = (bf16[1,528,128]{2,1,0:T(8,128)(2,1)S(1)}, bf16[1,528,128]{2,1,0:T(8,128)(2,1)S(1)}, u32[]{:S(2)}, u32[]{:S(2)}) collective-permute-start(bf16[1,528,128]{2,1,0:T(8,128)(2,1)S(1)} %fusion.18), channel_id=1, source_target_pairs={{0,16},{4,20},{8,24},{12,28},{16,0},{20,4},{24,8},{28,12},{1,17},{... | collective-permute-start | bytes 405512 | tf_op jit(solution)/shard_map/ppermute | solution.py:364
  94.6 7.2 %collective-permute-start.19 = (bf16[2,528,128]{2,1,0:T(8,128)(2,1)S(1)}, bf16[2,528,128]{2,1,0:T(8,128)(2,1)S(1)}, u32[]{:S(2)}, u32[]{:S(2)}) collective-permute-start(bf16[2,528,128]{2,1,0:T(8,128)(2,1)S(1)} %pad_maximum_fusion.2.refs_0_), channel_id=1, source_target_pairs={{0,8},{4,12},{8,0},{12,4},{16,24},{20,28},{24,16},{28,20},{1,9},{5... | collective-permute-start | bytes 811016 | tf_op jit(solution)/shard_map/ppermute | solution.py:364
  98.2 7.7 %copy-start = (s32[2,8192,4]{1,2,0:T(4,128)S(1)}, s32[2,8192,4]{1,2,0:T(4,128)}, u32[]{:S(2)}) copy-start(s32[2,8192,4]{1,2,0:T(4,128)} %param.23) | copy-start | bytes 786436
  98.2 7.7 %collective-permute-start.9 = (bf16[4,2,256,128]{3,2,1,0:T(8,128)(2,1)}, bf16[4,2,256,128]{3,2,1,0:T(8,128)(2,1)}, u32[]{:S(2)}, u32[]{:S(2)}) collective-permute-start(bf16[4,2,256,128]{3,2,1,0:T(8,128)(2,1)} %select.3), channel_id=1, source_target_pairs={{0,4},{4,0},{8,12},{12,8},{16,20},{20,16},{24,28},{28,24},{1,5},{5... | collective-permute-start | bytes 1572872 | tf_op jit(solution)/shard_map/ppermute | solution.py:361
  98.2 16.3 %collective-permute-start.22 = (bf16[2,2,576,128]{3,2,1,0:T(8,128)(2,1)}, bf16[2,2,576,128]{3,2,1,0:T(8,128)(2,1)S(1)}, u32[]{:S(2)}, u32[]{:S(2)}) collective-permute-start(bf16[2,2,576,128]{3,2,1,0:T(8,128)(2,1)} %fusion.refs_4_), channel_id=1, source_target_pairs={{0,1},{1,0},{2,3},{3,2},{4,5},{5,4},{6,7},{7,6},{8,9},{9,8},{10,11... | collective-permute-start | bytes 1769480 | tf_op jit(solution)/shard_map/ppermute | solution.py:367
  99.0 59.6 %collective-permute-start.20 = (bf16[2,528,128]{2,1,0:T(8,128)(2,1)S(1)}, bf16[2,528,128]{2,1,0:T(8,128)(2,1)S(1)}, u32[]{:S(2)}, u32[]{:S(2)}) collective-permute-start(bf16[2,528,128]{2,1,0:T(8,128)(2,1)S(1)} %pad_maximum_fusion.2.refs_0_), channel_id=1, source_target_pairs={{0,4},{4,0},{8,12},{12,8},{16,20},{20,16},{24,28},{28,24},{1,5},{5... | collective-permute-start | bytes 811016 | tf_op jit(solution)/shard_map/ppermute | solution.py:361
  101.8 56.8 %collective-permute-start.21 = (bf16[2,528,128]{2,1,0:T(8,128)(2,1)S(1)}, bf16[2,528,128]{2,1,0:T(8,128)(2,1)S(1)}, u32[]{:S(2)}, u32[]{:S(2)}) collective-permute-start(bf16[2,528,128]{2,1,0:T(8,128)(2,1)S(1)} %collective-permute-done.19.refs_1_), channel_id=1, source_target_pairs={{0,4},{4,0},{8,12},{12,8},{16,20},{20,16},{24,28},{28,24},{1,5},{5... | collective-permute-start | bytes 811016 | tf_op jit(solution)/shard_map/ppermute | solution.py:361
  103.0 17.4 %collective-permute-start.25 = (bf16[2,576,128]{2,1,0:T(8,128)(2,1)S(1)}, bf16[2,576,128]{2,1,0:T(8,128)(2,1)S(1)}, u32[]{:S(2)}, u32[]{:S(2)}) collective-permute-start(bf16[2,576,128]{2,1,0:T(8,128)(2,1)S(1)} %fusion.6), channel_id=1, source_target_pairs={{0,1},{1,0},{2,3},{3,2},{4,5},{5,4},{6,7},{7,6},{8,9},{9,8},{10,11... | collective-permute-start | bytes 884744 | tf_op jit(solution)/shard_map/ppermute | solution.py:367
  105.9 8.6 %copy-start.12 = (bf16[4,2,576,128]{3,2,1,0:T(8,128)(2,1)S(1)}, bf16[4,2,576,128]{3,2,1,0:T(8,128)(2,1)}, u32[]{:S(2)}) copy-start(bf16[4,2,576,128]{3,2,1,0:T(8,128)(2,1)} %copy-done.11) | copy-start | bytes 3538948
  111.1 28.8 %collective-permute-start.15 = (bf16[2,512,128]{2,1,0:T(8,128)(2,1)S(1)}, bf16[2,512,128]{2,1,0:T(8,128)(2,1)S(1)}, u32[]{:S(2)}, u32[]{:S(2)}) collective-permute-start(bf16[2,512,128]{2,1,0:T(8,128)(2,1)S(1)} %slice.333), channel_id=1, source_target_pairs={{0,2},{1,3},{2,0},{3,1},{4,6},{5,7},{6,4},{7,5},{8,10},{9,11},{10,... | collective-permute-start | bytes 786440 | tf_op jit(solution)/shard_map/ppermute | solution.py:367
  114.6 14.0 %collective-permute-start.23 = (bf16[2,576,128]{2,1,0:T(8,128)(2,1)S(1)}, bf16[2,576,128]{2,1,0:T(8,128)(2,1)S(1)}, u32[]{:S(2)}, u32[]{:S(2)}) collective-permute-start(bf16[2,576,128]{2,1,0:T(8,128)(2,1)S(1)} %fusion.1), channel_id=1, source_target_pairs={{0,2},{1,3},{2,0},{3,1},{4,6},{5,7},{6,4},{7,5},{8,10},{9,11},{10,... | collective-permute-start | bytes 884744 | tf_op jit(solution)/shard_map/ppermute | solution.py:367
  121.8 8.7 %collective-permute-start.26 = (bf16[2,576,128]{2,1,0:T(8,128)(2,1)S(1)}, bf16[2,576,128]{2,1,0:T(8,128)(2,1)S(1)}, u32[]{:S(2)}, u32[]{:S(2)}) collective-permute-start(bf16[2,576,128]{2,1,0:T(8,128)(2,1)S(1)} %fusion.2), channel_id=1, source_target_pairs={{0,8},{4,12},{8,0},{12,4},{16,24},{20,28},{24,16},{28,20},{1,9},{5... | collective-permute-start | bytes 884744 | tf_op jit(solution)/shard_map/ppermute | solution.py:364
  130.6 9.0 %collective-permute-start.27 = (bf16[1,576,128]{2,1,0:T(8,128)(2,1)S(1)}, bf16[1,576,128]{2,1,0:T(8,128)(2,1)S(1)}, u32[]{:S(2)}, u32[]{:S(2)}) collective-permute-start(bf16[1,576,128]{2,1,0:T(8,128)(2,1)S(1)} %fusion.9), channel_id=1, source_target_pairs={{0,16},{4,20},{8,24},{12,28},{16,0},{20,4},{24,8},{28,12},{1,17},{... | collective-permute-start | bytes 442376 | tf_op jit(solution)/shard_map/ppermute | solution.py:364
  134.6 14.2 %copy-start.18 = (bf16[4,512,128]{2,1,0:T(8,128)(2,1)S(1)}, bf16[4,512,128]{2,1,0:T(8,128)(2,1)}, u32[]{:S(2)}) copy-start(bf16[4,512,128]{2,1,0:T(8,128)(2,1)} %counts.2) | copy-start | bytes 1572868
  134.6 14.2 %collective-permute-start.11 = (bf16[2,512,128]{2,1,0:T(8,128)(2,1)S(1)}, bf16[2,512,128]{2,1,0:T(8,128)(2,1)S(1)}, u32[]{:S(2)}, u32[]{:S(2)}) collective-permute-start(bf16[2,512,128]{2,1,0:T(8,128)(2,1)S(1)} %slice_bitcast_fusion.2), channel_id=1, source_target_pairs={{0,1},{1,0},{2,3},{3,2},{4,5},{5,4},{6,7},{7,6},{8,9},{9,8},{10,11... | collective-permute-start | bytes 786440 | tf_op jit(solution)/shard_map/ppermute | solution.py:367
  139.7 9.0 %collective-permute-start.28 = (bf16[1,576,128]{2,1,0:T(8,128)(2,1)S(1)}, bf16[1,576,128]{2,1,0:T(8,128)(2,1)S(1)}, u32[]{:S(2)}, u32[]{:S(2)}) collective-permute-start(bf16[1,576,128]{2,1,0:T(8,128)(2,1)S(1)} %fusion.13), channel_id=1, source_target_pairs={{0,16},{4,20},{8,24},{12,28},{16,0},{20,4},{24,8},{28,12},{1,17},{... | collective-permute-start | bytes 442376 | tf_op jit(solution)/shard_map/ppermute | solution.py:364
  140.0 9.0 %collective-permute-start.16 = (bf16[512,128]{1,0:T(8,128)(2,1)S(1)}, bf16[512,128]{1,0:T(8,128)(2,1)S(1)}, u32[]{:S(2)}, u32[]{:S(2)}) collective-permute-start(bf16[512,128]{1,0:T(8,128)(2,1)S(1)} %fusion.26), channel_id=1, source_target_pairs={{0,1},{1,0},{2,3},{3,2},{4,5},{5,4},{6,7},{7,6},{8,9},{9,8},{10,11... | collective-permute-start | bytes 393224 | tf_op jit(solution)/shard_map/ppermute | solution.py:367
  148.7 9.0 %collective-permute-start.29 = (bf16[2,576,128]{2,1,0:T(8,128)(2,1)S(1)}, bf16[2,576,128]{2,1,0:T(8,128)(2,1)S(1)}, u32[]{:S(2)}, u32[]{:S(2)}) collective-permute-start(bf16[2,576,128]{2,1,0:T(8,128)(2,1)S(1)} %pad_maximum_fusion.1.refs_4_), channel_id=1, source_target_pairs={{0,8},{4,12},{8,0},{12,4},{16,24},{20,28},{24,16},{28,20},{1,9},{5... | collective-permute-start | bytes 884744 | tf_op jit(solution)/shard_map/ppermute | solution.py:364
  148.8 8.9 %collective-permute-start.12 = (bf16[512,128]{1,0:T(8,128)(2,1)S(1)}, bf16[512,128]{1,0:T(8,128)(2,1)S(1)}, u32[]{:S(2)}, u32[]{:S(2)}) collective-permute-start(bf16[512,128]{1,0:T(8,128)(2,1)S(1)} %fusion.22), channel_id=1, source_target_pairs={{0,2},{1,3},{2,0},{3,1},{4,6},{5,7},{6,4},{7,5},{8,10},{9,11},{10,... | collective-permute-start | bytes 393224 | tf_op jit(solution)/shard_map/ppermute | solution.py:367
  149.0 9.6 %collective-permute-start.30 = (bf16[2,576,128]{2,1,0:T(8,128)(2,1)S(1)}, bf16[2,576,128]{2,1,0:T(8,128)(2,1)S(1)}, u32[]{:S(2)}, u32[]{:S(2)}) collective-permute-start(bf16[2,576,128]{2,1,0:T(8,128)(2,1)S(1)} %pad_maximum_fusion.1.refs_4_), channel_id=1, source_target_pairs={{0,4},{4,0},{8,12},{12,8},{16,20},{20,16},{24,28},{28,24},{1,5},{5... | collective-permute-start | bytes 884744 | tf_op jit(solution)/shard_map/ppermute | solution.py:361
  157.7 1.6 collective-permute-start.31
  159.3 0.7 copy-start.19
  (4 other events, 2.7 us)

commit v4 on v3

--- a/solution.py
+++ b/solution.py
@@ -10,7 +10,7 @@
 loss_scale = 16.0
 LANES = 128
 SPAN = 9 * LANES
-VMEM_BYTES = 52 * 1024 * 1024
+MIB = 1024 * 1024
 bf16 = jnp.bfloat16
 f32 = jnp.float32
 
@@ -94,8 +94,8 @@
 
 def front_kernel(pos, *refs):
     sources, outs, targets = refs[:11], refs[11:18], refs[18:29]
-    halves, quarters, pack, sems = refs[29:]
-    send_low, send_high, act_t_out, second_out, crossed_t_out, first_out, small = outs
+    halves, thirds, pack, sems = refs[29:]
+    send_low, send_high, keep_low, keep_high, crossed_t_out, first_out, small = outs
     load = Loads(sources, targets, sems)
     core, row_pos = pos[0], pos[1]
     places = places_of(pos[2] // 2, pack.shape[1])
@@ -123,57 +123,46 @@
     label_col = jnp.sum(jnp.where(same, labels.astype(f32), 0.0), axis=1, keepdims=True)
     delta_logit = loss_scale * (jax.nn.sigmoid(logits) - label_col)
     delta_second = (delta_logit * w_logit * slope_second).astype(bf16)
-    second_out[...] = delta_second
     put_rows(small, 16, jnp.sum(act_second * delta_logit, axis=0, keepdims=True))
     put_rows(small, 8, jnp.sum(delta_second.astype(f32), axis=0, keepdims=True))
     half = halves.shape[2]
     halves[0] = delta_second[:, :half]
     halves[1] = delta_second[:, half:]
-    act_t = act_first.T
-    act_t_out[...] = act_t
-    offset = put_blocks(pack, row_pos, places, 0, matmul(act_t, halves[1 - core]))
     delta_first = (matmul_rt(delta_second, w_hidden2) * slope_first).astype(bf16)
     first_out[...] = delta_first
     put_rows(small, 0, jnp.sum(delta_first.astype(f32), axis=0, keepdims=True))
-    quarter = quarters.shape[2]
-    quarters[0] = delta_first[:, :quarter]
-    quarters[1] = delta_first[:, half : half + quarter]
+    part = thirds.shape[2]
+    thirds[0] = delta_first[:, :part]
+    thirds[1] = delta_first[:, half : half + part]
+    act_t = act_first.T
     crossed_t = crossed.T
     crossed_t_out[...] = crossed_t
-    put_blocks(pack, row_pos, places, offset, matmul(crossed_t, quarters[1 - core]))
-    split_parts(pack, send_low, send_high)
+    for low, high, who in ((send_low, send_high, 1 - core), (keep_low, keep_high, core)):
+        offset = put_blocks(pack, row_pos, places, 0, matmul(act_t, halves[who]))
+        put_blocks(pack, row_pos, places, offset, matmul(crossed_t, thirds[who]))
+        split_parts(pack, low, high)
 
 
 def middle_kernel(n_z, pos, *refs):
-    sources, direct = refs[:6], refs[6:10]
-    keep_low, keep_high, widened_out, reduced_out = refs[10:14]
-    pooled_outs = refs[14 : 14 + n_z]
-    rest = refs[14 + n_z :]
+    sources, delta_first = refs[:6], refs[6]
+    widened_out, reduced_out = refs[7:9]
+    pooled_outs = refs[9 : 9 + n_z]
+    rest = refs[9 + n_z :]
     targets = rest[:6]
-    halves, quarters, pack, by_group, sems = rest[6:]
-    act_t, delta_second, crossed_t, delta_first = direct
+    by_group, sems = rest[6:]
     load = Loads(sources, targets, sems)
-    core, row_pos, z_pos = pos[0], pos[1], pos[2] // 2
-    places = places_of(z_pos, pack.shape[1])
-    half, quarter = halves.shape[2], quarters.shape[2]
-    halves[0] = delta_second[:, :half]
-    halves[1] = delta_second[:, half:]
-    offset = put_blocks(pack, row_pos, places, 0, matmul(act_t[...], halves[core]))
-    quarters[0] = delta_first[:, :quarter]
-    quarters[1] = delta_first[:, half : half + quarter]
-    put_blocks(pack, row_pos, places, offset, matmul(crossed_t[...], quarters[core]))
-    split_parts(pack, keep_low, keep_high)
-    delta_crossed = matmul_rt(delta_first[...], load(0))
-    stacked = jnp.concatenate([load(1), load(2)], axis=1)
+    core, z_pos = pos[0], pos[2] // 2
+    stacked = jnp.concatenate([load(0), load(1)], axis=1)
+    cross_down, cross_up = load(2), load(3)
+    reduced = matmul(stacked, cross_down).astype(bf16)
+    widened = matmul(reduced, cross_up) + as_row(load(4))
+    delta_crossed = matmul_rt(delta_first[...], load(5))
     delta_widened = (delta_crossed * stacked.astype(f32)).astype(bf16)
     widened_out[...] = delta_widened
-    cross_up, cross_down = load(3), load(4)
     delta_reduced = matmul_rt(delta_widened, cross_up).astype(bf16)
     reduced_out[...] = delta_reduced
-    reduced = matmul(stacked, cross_down).astype(bf16)
-    widened = matmul(reduced, cross_up) + as_row(load(5))
     delta_stacked = delta_crossed * (widened + 1.0) + matmul_rt(delta_reduced, cross_down)
-    width = targets[1].shape[1]
+    width = targets[0].shape[1]
     per_group = by_group.shape[2]
     for table in range(2 * n_z * per_group):
         group = table // per_group
@@ -189,18 +178,18 @@
     dense_feat, pooled, cross_down, crossed_t, delta_first, delta_widened, delta_reduced = refs[:7]
     small_in = refs[7]
     send_low, send_high, keep_low, keep_high = refs[10:14]
-    half_delta, quarters, pack, small = refs[14:]
+    half_delta, sixths, pack, small = refs[14:]
     core, row_pos = pos[0], pos[1]
     n_row = pack.shape[0]
     places = places_of(pos[2] // 2, pack.shape[1])
     rank = delta_reduced.shape[1]
     feat = delta_widened.shape[1]
     hid = delta_first.shape[1]
-    quarter = quarters.shape[2]
+    part = hid // 2 - sixths.shape[2]
     half_delta[0] = delta_reduced[:, : rank // 2]
     half_delta[1] = delta_reduced[:, rank // 2 :]
-    quarters[0] = delta_first[:, quarter : hid // 2]
-    quarters[1] = delta_first[:, hid // 2 + quarter :]
+    sixths[0] = delta_first[:, part : hid // 2]
+    sixths[1] = delta_first[:, hid // 2 + part :]
     put_rows(small, 24, jnp.sum(delta_widened[...].astype(f32), axis=0, keepdims=True))
     small[0:24, :] = small_in[...]
     small[41:48, :] = jnp.zeros((7, LANES), f32)
@@ -209,7 +198,7 @@
     reduced_t = matmul(stacked, cross_down[...]).astype(bf16).T
     stacked_t = stacked.T
     for low, high, who in ((send_low, send_high, 1 - core), (keep_low, keep_high, core)):
-        offset = put_blocks(pack, row_pos, places, 0, matmul(crossed_t[...], quarters[who]))
+        offset = put_blocks(pack, row_pos, places, 0, matmul(crossed_t[...], sixths[who]))
         offset = put_blocks(pack, row_pos, places, offset, matmul(stacked_t, half_delta[who]))
         start = pl.multiple_of(who * (feat - SPAN), LANES)
         offset = put_blocks(
@@ -283,11 +272,10 @@
     for half in range(2):
         blocks = g_second.shape[1] // LANES // 2
         offset = take(front, g_second, half, 0, range(half * blocks, (half + 1) * blocks))
-        blocks = g_first.shape[1] // LANES // 4
-        take(front, g_first, half, offset, range(2 * half * blocks, (2 * half + 1) * blocks))
-        offset = take(
-            back, g_first, half, 0, range((2 * half + 1) * blocks, (2 * half + 2) * blocks)
-        )
+        blocks = g_first.shape[1] // LANES // 2
+        early = blocks - blocks // 4
+        take(front, g_first, half, offset, range(half * blocks, half * blocks + early))
+        offset = take(back, g_first, half, 0, range(half * blocks + early, (half + 1) * blocks))
         blocks = g_down.shape[1] // LANES // 2
         offset = take(back, g_down, half, offset, range(half * blocks, (half + 1) * blocks))
         blocks = g_up.shape[1] // LANES
@@ -305,17 +293,21 @@
     )
 
 
-def call(body, outs, scratch, in_specs, name, micros):
+def call(body, outs, scratch, in_specs, name, micros, mib):
     return pl.pallas_call(
         body,
         out_shape=outs,
         in_specs=in_specs,
         out_specs=[whole()] * len(outs),
         scratch_shapes=scratch,
-        compiler_params=pltpu.CompilerParams(vmem_limit_bytes=VMEM_BYTES),
+        compiler_params=pltpu.CompilerParams(vmem_limit_bytes=mib * MIB),
         cost_estimate=cost(micros),
         name=name,
     )
+
+
+def after(values, deps):
+    return list(lax.optimization_barrier(tuple(values) + tuple(deps))[: len(values)])
 
 
 def held_like(values):
@@ -366,9 +358,11 @@
     def swap_row(value, bit):
         return lax.ppermute(value, "row", [(at, at ^ (1 << bit)) for at in range(n_row)])
 
+    late = hid // 8
+    early = hid // 2 - late
     rows_front = (hid // 2 // LANES) * round_up(hid // n_row, 16)
-    rows_front += (hid // 4 // LANES) * round_up(feat // n_row, 16)
-    rows_back = (hid // 4 // LANES) * round_up(feat // n_row, 16)
+    rows_front += (early // LANES) * round_up(feat // n_row, 16)
+    rows_back = (late // LANES) * round_up(feat // n_row, 16)
     rows_back += (rank // 2 // LANES) * round_up(feat // n_row, 16)
     rows_back += 9 * round_up(rank // n_row, 16) + 48
     rows_front, rows_back = (round_up(rows, 16 * n_z) for rows in (rows_front, rows_back))
@@ -397,101 +391,133 @@
         w_logit,
         labels,
     )
-    send_low, send_high, act_t, delta_second, crossed_t, delta_first, small = call(
+    send_low, send_high, keep_low, keep_high, crossed_t, delta_first, small = call(
         front_kernel,
-        [
-            half_pack(rows_front),
-            half_pack(rows_front),
-            wide(hid, batch),
-            wide(batch, hid),
-            wide(feat, batch),
-            wide(batch, hid),
-            jax.ShapeDtypeStruct((24, LANES), f32),
-        ],
+        [half_pack(rows_front)] * 4
+        + [wide(feat, batch), wide(batch, hid), jax.ShapeDtypeStruct((24, LANES), f32)],
         held_like(sources)
         + [
             pltpu.VMEM((2, batch, hid // 2), bf16),
-            pltpu.VMEM((2, batch, hid // 4), bf16),
+            pltpu.VMEM((2, batch, early), bf16),
             pack_scratch(rows_front),
             pltpu.SemaphoreType.DMA((len(sources),)),
         ],
         [smem] + [hbm] * len(sources),
         "front",
         10,
+        60,
     )(pos, *sources)
     got_low, got_high = swap_cores(send_low), swap_cores(send_high)
 
-    sources = (w_hidden1, dense_feat, pooled, cross_up, cross_down, cross_bias)
+    sources = (dense_feat, pooled, cross_down, cross_up, cross_bias, w_hidden1)
     outs = call(
         functools.partial(middle_kernel, n_z),
-        [half_pack(rows_front), half_pack(rows_front), wide(batch, feat), wide(batch, rank)]
-        + [wide(2, tab_grp, batch, width)] * n_z,
+        [wide(batch, feat), wide(batch, rank)] + [wide(2, tab_grp, batch, width)] * n_z,
         held_like(sources)
         + [
-            pltpu.VMEM((2, batch, hid // 2), bf16),
-            pltpu.VMEM((2, batch, hid // 4), bf16),
-            pack_scratch(rows_front),
             pltpu.VMEM((n_z, 2, tab_grp, batch, width), bf16),
             pltpu.SemaphoreType.DMA((len(sources),)),
         ],
-        [smem] + [hbm] * len(sources) + [vmem] * 4,
+        [smem] + [hbm] * len(sources) + [vmem],
         "middle",
-        8,
-    )(pos, *sources, act_t, delta_second, crossed_t, delta_first)
-    keep_low, keep_high, delta_widened, delta_reduced = outs[:4]
-    pooled_out = outs[4:]
+        7,
+        40,
+    )(pos, *sources, delta_first)
+    delta_widened, delta_reduced = outs[:2]
+    pooled_out = outs[2:]
 
     low_first = tuple(range(row_bits))
     high_first = low_first[::-1]
 
-    class Halving:
-        def __init__(self, terms, order):
-            self.terms = [term.reshape((2,) * row_bits + term.shape[1:]) for term in terms]
+    class Terms:
+        def __init__(self, arrays):
+            self.items = [(array, ()) for array in arrays]
+
+        def tie(self, deps):
+            arrays = after([array for array, _ in self.items], deps)
+            self.items = [(array, path) for array, (_, path) in zip(arrays, self.items)]
+
+        def total(self, *extra):
+            parts = []
+            for array, path in self.items:
+                for pick in path + extra:
+                    array = pick(array)
+                parts.append(array)
+            return add_terms(parts)
+
+        def narrow(self, pick, got):
+            self.items = [(array, path + (pick,)) for array, path in self.items] + [(got, ())]
+
+    def index_of(index, axis):
+        return lambda array: lax.index_in_dim(array, index, axis, keepdims=False)
+
+    def rows_of(start, stop):
+        return lambda array: array[start:stop]
+
+    class Halving(Terms):
+        def __init__(self, arrays, order):
+            super().__init__([array.reshape((2,) * row_bits + array.shape[1:]) for array in arrays])
             self.order, self.left = order, list(range(row_bits - 1, -1, -1))
-            self.sent = []
-
-        def step(self, at):
+
+        def step(self, at, deps=()):
             bit = self.order[at]
             axis = self.left.index(bit)
             self.left.remove(bit)
-            far = [lax.index_in_dim(term, 1, axis, keepdims=False) for term in self.terms]
-            sent = add_terms(far).astype(bf16)
-            self.sent.append(sent)
-            got = swap_row(sent, bit)
-            near = [lax.index_in_dim(term, 0, axis, keepdims=False) for term in self.terms]
-            self.terms = near + [got]
+            if deps:
+                self.tie(deps)
+            sent = self.total(index_of(1, axis)).astype(bf16)
+            self.narrow(index_of(0, axis), swap_row(sent, bit))
             return sent
 
-    def sum_z(lower, upper):
-        sents = [add_terms(upper).astype(bf16)]
-        terms = lower + [swap_z(sents[0], 1)]
-        for stage in range(1, z_bits):
-            middle = n_z >> (stage + 1)
-            sents.append(add_terms([term[middle:] for term in terms]).astype(bf16))
-            terms = [term[:middle] for term in terms] + [swap_z(sents[-1], 1 << stage)]
-        own = add_terms(terms).astype(bf16)
-        for stage in range(z_bits - 1, 0, -1):
-            own = jnp.concatenate([own, swap_z(own, 1 << stage)], axis=0)
-        far = swap_z(own, 1)
-        return sents, [own, far, swap_cores(own), swap_cores(far)]
-
-    low1, high1 = Halving([keep_low, got_low], low_first), Halving([keep_high, got_high], high_first)
-    ties = [low1.step(0), high1.step(0)]
+    class Dense:
+        def __init__(self, keep_low, got_low, keep_high, got_high):
+            self.low = Halving([keep_low, got_low], low_first)
+            self.high = Halving([keep_high, got_high], high_first)
+
+        def row_step(self, at, deps=()):
+            sent = self.low.step(at, deps)
+            return [sent, self.high.step(at, deps)]
+
+        def z_step(self, stage, deps):
+            if stage == 0:
+                self.high.tie(deps)
+                sent = self.high.total().astype(bf16)
+                self.low.items.append((swap_z(sent, 1), ()))
+            else:
+                middle = n_z >> (stage + 1)
+                self.low.tie(deps)
+                sent = self.low.total(rows_of(middle, None)).astype(bf16)
+                self.low.narrow(rows_of(0, middle), swap_z(sent, 1 << stage))
+            return [sent]
+
+        def z_back(self, deps):
+            self.low.tie(deps)
+            own = self.low.total().astype(bf16)
+            first = own
+            for stage in range(z_bits - 1, 0, -1):
+                own = jnp.concatenate([own, swap_z(own, 1 << stage)], axis=0)
+            far = swap_z(own, 1)
+            self.pieces = [own, far, swap_cores(own), swap_cores(far)]
+            return [first]
+
+    one = Dense(keep_low, got_low, keep_high, got_high)
+    sent = one.row_step(0)
 
     values = [pooled_out[0]] + [swap_z(pooled_out[which], which) for which in range(1, n_z)]
 
-    send_low2, send_high2, keep_low2, keep_high2 = call(
+    send_low, send_high, keep_low, keep_high = call(
         back_kernel,
         [half_pack(rows_back)] * 4,
         [
             pltpu.VMEM((2, batch, rank // 2), bf16),
-            pltpu.VMEM((2, batch, hid // 4), bf16),
+            pltpu.VMEM((2, batch, late), bf16),
             pack_scratch(rows_back),
             pltpu.VMEM((48, LANES), f32),
         ],
         [smem] + [vmem] * 8 + [anywhere] * 2,
         "back",
         6,
+        36,
     )(
         pos,
         dense_feat,
@@ -502,29 +528,25 @@
         delta_widened,
         delta_reduced,
         small,
-        *ties,
-    )
-    got_low2, got_high2 = swap_cores(send_low2), swap_cores(send_high2)
-    low2 = Halving([keep_low2, got_low2], low_first)
-    high2 = Halving([keep_high2, got_high2], high_first)
-    ties = [low2.step(0), high2.step(0)]
+        *sent,
+    )
+    two = Dense(keep_low, swap_cores(send_low), keep_high, swap_cores(send_high))
+    last = [send_low]
     for at in range(1, row_bits):
-        ties += [low1.step(at), high1.step(at)]
+        last = one.row_step(at, last)
 
     far_values = call(
         functools.partial(select_kernel, n_z),
         [wide(n_z, tab_grp, batch, width)],
         [],
-        [vmem] * n_z + [anywhere] * len(ties),
+        [vmem] * n_z + [anywhere] * len(last),
         "select",
         1,
-    )(*values, *ties)[0]
+        8,
+    )(*values, *last)[0]
     values.append(swap_cores(far_values))
-
-    for at in range(1, row_bits):
-        low2.step(at), high2.step(at)
-    sents1, stream1 = sum_z(low1.terms, high1.terms)
-    sents2, stream2 = sum_z(low2.terms, high2.terms)
+    last = two.row_step(0, [far_values])
+    last = one.z_step(0, last)
 
     slots = jnp.transpose(lookup_slots, (0, 2, 1))
     shares = []
@@ -535,15 +557,28 @@
             grid=(n_row,),
             in_specs=[smem] + [vmem] * (2 + n_z) + [anywhere],
             out_specs=pl.BlockSpec((1, u_shard, width), lambda at: (at, 0, 0)),
-            compiler_params=pltpu.CompilerParams(vmem_limit_bytes=VMEM_BYTES),
+            compiler_params=pltpu.CompilerParams(vmem_limit_bytes=16 * MIB),
             cost_estimate=cost(6),
             name="counts",
-        )(pos, slots, *values, sents1[min(table, len(sents1) - 1)])
-        share = Halving([sums], high_first if table % 2 else low_first)
-        for at in range(row_bits):
-            share.step(at)
-        shares.append(add_terms(share.terms))
-    row_grads = jnp.stack(shares)
+        )(pos, slots, *values, last[0])
+        last = [sums]
+        shares.append(Halving([sums], high_first if table % 2 else low_first))
+        if table == 0:
+            for stage in range(1, z_bits):
+                last = one.z_step(stage, last)
+            for at in range(1, row_bits):
+                last = two.row_step(at, last)
+    for share in shares:
+        share.step(0, last)
+    last = one.z_back(last)
+    last = two.z_step(0, last)
+    for share in shares:
+        for at in range(1, row_bits):
+            share.step(at, last)
+    row_grads = jnp.stack([share.total() for share in shares])
+    for stage in range(1, z_bits):
+        last = two.z_step(stage, last)
+    two.z_back(last)
 
     g_down, g_up, g_first, g_second, g_small = call(
         unpack_kernel,
@@ -558,7 +593,8 @@
         [smem] + [vmem] * 8,
         "unpack",
         4,
-    )(pos, *stream1, *stream2)
+        24,
+    )(pos, *one.pieces, *two.pieces)
 
     flat = g_small.reshape(-1)
 

time: 165 us -> 142 us (0.86)
  waiting for transfers between devices: 73.4 us -> 47.4 us
  starting transfers between devices: 30.6 us -> 36.8 us
  other arithmetic: 9.12 us -> 15 us
  Pallas kernels: 41.6 us -> 36.3 us
  local copies, waits for them, and re-layouts: 8.92 us -> 4.74 us
    ppermute x11, waiting for transfers between devices: 54.8 us -> 37.6 us  [swap_z(): lax.ppermute(value, 'table', [(at, at ^ 2 * which) for at in range(n_tabl...]
    ppermute x12, waiting for transfers between devices: 17.9 us -> 9.22 us  [swap_row(): lax.ppermute(value, 'row', [(at, at ^ 1 << bit) for at in range(n_row)])]
    ppermute x11, starting transfers between devices: 14.8 us -> 20.5 us  [swap_z(): lax.ppermute(value, 'table', [(at, at ^ 2 * which) for at in range(n_tabl...]
    convert_element_type x16 -> x15, other arithmetic: 8.06 us -> 13.4 us  [the longest x9 6.58 us: step(): sent = self.total(index_of(1, axis)).astype(bf16)]
    unnamed x40 -> x42, local copies, waits for them, and re-layouts: 6.62 us -> 3.39 us
    pallas_call x1, Pallas kernels: 6.93 us -> 3.98 us  [local(): call(back_kernel, [half_pack(rows_back)] * 4, [pltpu.VMEM((2, batch, rank...]
  transfers between devices with their start and end apart: 32 -> 32, of which waited for: 14 -> 10; matrix products, arithmetic and copies ran while one was open for 6% -> 10% of each run, Pallas kernels for 17% -> 14%
where the time goes in v4:
time: 142 us; the launch traced here: 141 us
  waiting for transfers between devices  47.4 us (33%)
  starting transfers between devices  36.8 us (26%)
  Pallas kernels  36.3 us (26%)
  other arithmetic  15 us (11%)
  local copies, waits for them, and re-layouts  4.74 us (3%)
    ppermute x11, waiting for transfers between devices, swap_z(): lax.ppermute(value, 'table', [(at, at ^ 2 * which) for at in range(n_tabl...  37.6 us
    ppermute x11, starting transfers between devices, swap_z(): lax.ppermute(value, 'table', [(at, at ^ 2 * which) for at in range(n_tabl...  20.5 us
    ppermute x12, starting transfers between devices, swap_row(): lax.ppermute(value, 'row', [(at, at ^ 1 << bit) for at in range(n_row)])  15.1 us
    pallas_call x1, Pallas kernels, local(): call(front_kernel, [half_pack(rows_front)] * 4 + [wide(feat, batch), wide...  13.5 us
    pallas_call x2, Pallas kernels, local(): pl.pallas_call(functools.partial(count_kernel, n_row, table, hot, n_z), o...  9.39 us
    ppermute x12, waiting for transfers between devices, swap_row(): lax.ppermute(value, 'row', [(at, at ^ 1 << bit) for at in range(n_row)])  9.22 us
    convert_element_type x9, other arithmetic, step(): sent = self.total(index_of(1, axis)).astype(bf16)  6.58 us
    pallas_call x1, Pallas kernels, local(): call(functools.partial(middle_kernel, n_z), [wide(batch, feat), wide(batc...  6.52 us
  transfers between devices with their start and end apart: 32, of which 10 were waited for; matrix products, arithmetic and copies ran while one was open for 10% of the time, Pallas kernels for 14%

profile of v4, /device:TPU:0, one launch (start us, length us, event | category | flops | bytes accessed | tf_op | source)
XLA Modules:
  0.0 141.2 jit_solution(144393738984436183)
XLA Ops:
  1.3 13.5 %front.1 = (bf16[4,2,672,128]{3,2,1,0:T(8,128)(2,1)}, bf16[4,2,672,128]{3,2,1,0:T(8,128)(2,1)}, bf16[4,2,672,128]{3,2,1,0:T(8,128)(2,1)}, bf16[4,2,672,128]{3,2,...) custom-call(s32[3]{0:T(128)} %pad_add_fusion.pos, ...), custom_call_target="tpu_custom_call" | custom-call | flops 10000000000 | bytes 30000000 | tf_op jit(solution)/shard_map/front/pallas_call | solution.py:394
  15.4 2.3 %copy-done.1 = bf16[2176,1024]{1,0:T(8,128)(2,1)S(1)} copy-done((bf16[2176,1024]{1,0:T(8,128)(2,1)S(1)}, bf16[2176,1024]{1,0:T(8,128)(2,1)}, u32[]{:S(2)}) %copy-start.1) | copy-done | bytes 4456472
  17.7 1.0 copy-done.15
  18.7 6.5 %middle.1 = (bf16[256,2176]{1,0:T(8,128)(2,1)S(1)}, bf16[256,256]{1,0:T(8,128)(2,1)S(1)}, bf16[2,2,256,128]{3,2,1,0:T(8,128)(2,1)S(1)}, bf16[2,2,256,128]{3,2,1,...) custom-call(s32[3]{0:T(128)S(1)} %copy-done, ...), custom_call_target="tpu_custom_call" | custom-call | flops 7000000000 | bytes 21000000 | tf_op jit(solution)/shard_map/middle/pallas_call | solution.py:413
  25.5 3.0 %collective-permute-start.4 = (bf16[2,2,672,128]{3,2,1,0:T(8,128)(2,1)S(1)}, bf16[2,2,672,128]{3,2,1,0:T(8,128)(2,1)}, u32[]{:S(2)}, u32[]{:S(2)}) collective-permute-start(bf16[2,2,672,128]{3,2,1,0:T(8,128)(2,1)S(1)} %fusion.refs_8_), channel_id=1, source_target_pairs={{0,1},{1,0},{2,3},{3,2},{4,5},{5,4},{6,7},{7,6},{8,9},{9,8},{10,11... | collective-permute-start | bytes 2064392 | tf_op jit(solution)/shard_map/ppermute | solution.py:359
  28.8 1.6 %collective-permute-start.6 = (bf16[2,2,672,128]{3,2,1,0:T(8,128)(2,1)S(1)}, bf16[2,2,672,128]{3,2,1,0:T(8,128)(2,1)}, u32[]{:S(2)}, u32[]{:S(2)}) collective-permute-start(bf16[2,2,672,128]{3,2,1,0:T(8,128)(2,1)S(1)} %add_convert_fusion.refs_9_), channel_id=1, source_target_pairs={{0,2},{1,3},{2,0},{3,1},{4,6},{5,7},{6,4},{7,5},{8,10},{9,11},{10,... | collective-permute-start | bytes 2064392 | tf_op jit(solution)/shard_map/ppermute | solution.py:359
  30.3 4.0 %back.1 = (bf16[4,2,432,128]{3,2,1,0:T(8,128)(2,1)}, bf16[4,2,432,128]{3,2,1,0:T(8,128)(2,1)}, bf16[4,2,432,128]{3,2,1,0:T(8,128)(2,1)S(1)}, bf16[4,2,432,128]{3,2,1,0:T(8,128)(2,1)S(1)}) custom-call(s32[3]{0:T(128)S(1)} %copy-done, bf16[256,128]{1,0:T(8,128)(2,1)S(1)} %copy-done.10, bf16[256,2048]{1,0:T(8,128)(2,1)S(1)} %copy-done.6, ...), custom_call_target="tpu_custom_call" | custom-call | flops 6000000000 | bytes 18000000 | tf_op jit(solution)/shard_map/back/pallas_call | solution.py:508
  34.8 1.6 %collective-permute-start = (bf16[2,2,256,128]{3,2,1,0:T(8,128)(2,1)}, bf16[2,2,256,128]{3,2,1,0:T(8,128)(2,1)S(1)}, u32[]{:S(2)}, u32[]{:S(2)}) collective-permute-start(bf16[2,2,256,128]{3,2,1,0:T(8,128)(2,1)} %get-tuple-element.85), channel_id=1, source_target_pairs={{0,8},{4,12},{8,0},{12,4},{16,24},{20,28},{24,16},{28,20},{1,9},{5... | collective-permute-start | bytes 786440 | tf_op jit(solution)/shard_map/ppermute | solution.py:356
  36.4 7.9 %collective-permute-done.4 = bf16[2,2,672,128]{3,2,1,0:T(8,128)(2,1)} collective-permute-done((bf16[2,2,672,128]{3,2,1,0:T(8,128)(2,1)S(1)}, bf16[2,2,672,128]{3,2,1,0:T(8,128)(2,1)}, u32[]{:S(2)}, u32[]{:S(2)}) %collective-permute-start.4) | collective-permute-done | bytes 688160 | tf_op jit(solution)/shard_map/ppermute | solution.py:359
  44.3 2.8 %collective-permute-start.1 = (bf16[2,2,256,128]{3,2,1,0:T(8,128)(2,1)}, bf16[2,2,256,128]{3,2,1,0:T(8,128)(2,1)S(1)}, u32[]{:S(2)}, u32[]{:S(2)}) collective-permute-start(bf16[2,2,256,128]{3,2,1,0:T(8,128)(2,1)} %copy-done.9), channel_id=1, source_target_pairs={{0,16},{4,20},{8,24},{12,28},{16,0},{20,4},{24,8},{28,12},{1,17},{... | collective-permute-start | bytes 786440 | tf_op jit(solution)/shard_map/ppermute | solution.py:356
  47.1 2.5 %collective-permute-start.2 = (bf16[2,2,256,128]{3,2,1,0:T(8,128)(2,1)}, bf16[2,2,256,128]{3,2,1,0:T(8,128)(2,1)S(1)}, u32[]{:S(2)}, u32[]{:S(2)}) collective-permute-start(bf16[2,2,256,128]{3,2,1,0:T(8,128)(2,1)} %copy-done.8), channel_id=1, source_target_pairs={{0,24},{4,28},{8,16},{12,20},{16,8},{20,12},{24,0},{28,4},{1,25},{... | collective-permute-start | bytes 786440 | tf_op jit(solution)/shard_map/ppermute | solution.py:356
  49.7 1.8 %fusion.3 = (bf16[2,672,128]{2,1,0:T(8,128)(2,1)S(1)}, bf16[2,672,128]{2,1,0:T(8,128)(2,1)S(1)}) fusion(bf16[2,2,672,128]{3,2,1,0:T(8,128)(2,1)} %collective-permute-done.6, bf16[2,2,2,672,128]{4,3,2,1,0:T(8,128)(2,1)} %bitcast.130, bf16[2,2,2,672,128]{4,3,2,1,0:T(8,128)(2,1)} %bitcast.128, bf16[2,2,672,128]{3,2,1,0:T(8,128)(2,1)} %collective-permute-done.4, ...), kind=kLoop, calls=%fused_computation.9 | loop fusion | flops 2064384 | bytes 2752512 | tf_op jit(solution)/shard_map/convert_element_type | solution.py:468
  51.5 0.6 collective-permute-start.8
  52.1 13.4 %collective-permute-done.1.refs_2_.rest_2_ = bf16[2,2,256,128]{3,2,1,0:T(8,128)(2,1)S(1)} collective-permute-done((bf16[2,2,256,128]{3,2,1,0:T(8,128)(2,1)}, bf16[2,2,256,128]{3,2,1,0:T(8,128)(2,1)S(1)}, u32[]{:S(2)}, u32[]{:S(2)}) %collective-permute-start.1) | collective-permute-done | bytes 262176 | tf_op jit(solution)/shard_map/ppermute | solution.py:356
  65.5 1.5 %collective-permute-start.12 = (bf16[2,672,128]{2,1,0:T(8,128)(2,1)S(1)}, bf16[2,672,128]{2,1,0:T(8,128)(2,1)S(1)}, u32[]{:S(2)}, u32[]{:S(2)}) collective-permute-start(bf16[2,672,128]{2,1,0:T(8,128)(2,1)S(1)} %get-tuple-element.161.refs_4_), channel_id=1, source_target_pairs={{0,2},{1,3},{2,0},{3,1},{4,6},{5,7},{6,4},{7,5},{8,10},{9,11},{10,... | collective-permute-start | bytes 1032200 | tf_op jit(solution)/shard_map/ppermute | solution.py:359
  67.2 1.1 fusion.5
  68.3 1.6 %collective-permute-start.11 = (bf16[2,2,432,128]{3,2,1,0:T(8,128)(2,1)S(1)}, bf16[2,2,432,128]{3,2,1,0:T(8,128)(2,1)S(1)}, u32[]{:S(2)}, u32[]{:S(2)}) collective-permute-start(bf16[2,2,432,128]{3,2,1,0:T(8,128)(2,1)S(1)} %fusion.5), channel_id=1, source_target_pairs={{0,1},{1,0},{2,3},{3,2},{4,5},{5,4},{6,7},{7,6},{8,9},{9,8},{10,11... | collective-permute-start | bytes 1327112 | tf_op jit(solution)/shard_map/ppermute | solution.py:359
  69.9 1.1 fusion.6
  71.6 1.4 fusion.2.rest_5_
  73.0 4.8 %collective-permute-start.13 = (bf16[2,672,128]{2,1,0:T(8,128)(2,1)S(1)}, bf16[2,672,128]{2,1,0:T(8,128)(2,1)S(1)}, u32[]{:S(2)}, u32[]{:S(2)}) collective-permute-start(bf16[2,672,128]{2,1,0:T(8,128)(2,1)S(1)} %fusion.2.rest_5_), channel_id=1, source_target_pairs={{0,8},{4,12},{8,0},{12,4},{16,24},{20,28},{24,16},{28,20},{1,9},{5... | collective-permute-start | bytes 1032200 | tf_op jit(solution)/shard_map/ppermute | solution.py:356
  77.8 4.6 %counts.2 = bf16[4,512,128]{2,1,0:T(8,128)(2,1)S(1)} custom-call(s32[3]{0:T(128)S(1)} %copy-done, s32[2,4,8192]{2,1,0:T(4,128)S(1)} %bitcast.118, bf16[2,2,256,128]{3,2,1,0:T(8,128)(2,1)S(1)} %copy-done.13, bf16[2,2,256,128]{3,2,1,0:T(8,128)(2,1)S(1)} %collective-permute-done.refs_1_.rest_1_, ...), custom_call_target="tpu_custom_call" | custom-call | flops 6000000000 | bytes 18000000 | tf_op jit(solution)/shard_map/counts/pallas_call | solution.py:554
  82.4 3.5 %collective-permute-done.13 = bf16[2,672,128]{2,1,0:T(8,128)(2,1)S(1)} collective-permute-done((bf16[2,672,128]{2,1,0:T(8,128)(2,1)S(1)}, bf16[2,672,128]{2,1,0:T(8,128)(2,1)S(1)}, u32[]{:S(2)}, u32[]{:S(2)}) %collective-permute-start.13) | collective-permute-done | bytes 344096 | tf_op jit(solution)/shard_map/ppermute | solution.py:356
  85.9 1.2 fusion.17
  87.1 3.6 %collective-permute-start.17 = (bf16[1,672,128]{2,1,0:T(8,128)(2,1)S(1)}, bf16[1,672,128]{2,1,0:T(8,128)(2,1)S(1)}, u32[]{:S(2)}, u32[]{:S(2)}) collective-permute-start(bf16[1,672,128]{2,1,0:T(8,128)(2,1)S(1)} %fusion.17), channel_id=1, source_target_pairs={{0,16},{4,20},{8,24},{12,28},{16,0},{20,4},{24,8},{28,12},{1,17},{... | collective-permute-start | bytes 516104 | tf_op jit(solution)/shard_map/ppermute | solution.py:356
  90.7 1.0 fusion.9
  91.8 0.6 collective-permute-start.16
  92.4 1.0 fusion.10.rest_5_
  94.0 4.8 %counts.3 = bf16[4,512,128]{2,1,0:T(8,128)(2,1)S(1)} custom-call(s32[3]{0:T(128)S(1)} %copy-done, s32[2,4,8192]{2,1,0:T(4,128)S(1)} %bitcast.119, bf16[2,2,256,128]{3,2,1,0:T(8,128)(2,1)S(1)} %copy-done.13, bf16[2,2,256,128]{3,2,1,0:T(8,128)(2,1)S(1)} %collective-permute-done.refs_1_.rest_1_, ...), custom_call_target="tpu_custom_call" | custom-call | flops 6000000000 | bytes 18000000 | tf_op jit(solution)/shard_map/counts/pallas_call | solution.py:554
  98.8 1.6 %collective-permute-start.14 = (bf16[2,512,128]{2,1,0:T(8,128)(2,1)S(1)}, bf16[2,512,128]{2,1,0:T(8,128)(2,1)S(1)}, u32[]{:S(2)}, u32[]{:S(2)}) collective-permute-start(bf16[2,512,128]{2,1,0:T(8,128)(2,1)S(1)} %slice_bitcast_fusion.1), channel_id=1, source_target_pairs={{0,1},{1,0},{2,3},{3,2},{4,5},{5,4},{6,7},{7,6},{8,9},{9,8},{10,11... | collective-permute-start | bytes 786440 | tf_op jit(solution)/shard_map/ppermute | solution.py:359
  100.4 1.6 %collective-permute-start.19 = (bf16[2,512,128]{2,1,0:T(8,128)(2,1)S(1)}, bf16[2,512,128]{2,1,0:T(8,128)(2,1)S(1)}, u32[]{:S(2)}, u32[]{:S(2)}) collective-permute-start(bf16[2,512,128]{2,1,0:T(8,128)(2,1)S(1)} %slice_bitcast_fusion), channel_id=1, source_target_pairs={{0,2},{1,3},{2,0},{3,1},{4,6},{5,7},{6,4},{7,5},{8,10},{9,11},{10,... | collective-permute-start | bytes 786440 | tf_op jit(solution)/shard_map/ppermute | solution.py:359
  102.0 1.2 fusion.14
  103.3 1.1 fusion.8
  104.4 1.1 collective-permute-start.26
  105.6 1.4 collective-permute-start.18
  106.9 1.3 collective-permute-done.19
  108.2 4.7 %collective-permute-done.26 = bf16[2,432,128]{2,1,0:T(8,128)(2,1)S(1)} collective-permute-done((bf16[2,432,128]{2,1,0:T(8,128)(2,1)S(1)}, bf16[2,432,128]{2,1,0:T(8,128)(2,1)S(1)}, u32[]{:S(2)}, u32[]{:S(2)}) %collective-permute-start.26) | collective-permute-done | bytes 221216 | tf_op jit(solution)/shard_map/ppermute | solution.py:356
  113.0 1.0 fusion.30
  113.9 1.0 collective-permute-start.27
  115.6 5.0 %collective-permute-done.27 = bf16[1,432,128]{2,1,0:T(8,128)(2,1)S(1)} collective-permute-done((bf16[1,432,128]{2,1,0:T(8,128)(2,1)S(1)}, bf16[1,432,128]{2,1,0:T(8,128)(2,1)S(1)}, u32[]{:S(2)}, u32[]{:S(2)}) %collective-permute-start.27) | collective-permute-done | bytes 110624 | tf_op jit(solution)/shard_map/ppermute | solution.py:356
  120.6 1.0 fusion.27
  121.8 2.6 %collective-permute-start.22 = (bf16[2,672,128]{2,1,0:T(8,128)(2,1)S(1)}, bf16[2,672,128]{2,1,0:T(8,128)(2,1)S(1)}, u32[]{:S(2)}, u32[]{:S(2)}) collective-permute-start(bf16[2,672,128]{2,1,0:T(8,128)(2,1)S(1)} %pad_maximum_fusion.1.refs_0_), channel_id=1, source_target_pairs={{0,8},{4,12},{8,0},{12,4},{16,24},{20,28},{24,16},{28,20},{1,9},{5... | collective-permute-start | bytes 1032200 | tf_op jit(solution)/shard_map/ppermute | solution.py:356
  124.4 3.7 %collective-permute-done.28 = bf16[1,432,128]{2,1,0:T(8,128)(2,1)S(1)} collective-permute-done((bf16[1,432,128]{2,1,0:T(8,128)(2,1)S(1)}, bf16[1,432,128]{2,1,0:T(8,128)(2,1)S(1)}, u32[]{:S(2)}, u32[]{:S(2)}) %collective-permute-start.28) | collective-permute-done | bytes 110624 | tf_op jit(solution)/shard_map/ppermute | solution.py:356
  128.4 4.8 %collective-permute-done.22.refs_1_ = bf16[2,672,128]{2,1,0:T(8,128)(2,1)S(1)} collective-permute-done((bf16[2,672,128]{2,1,0:T(8,128)(2,1)S(1)}, bf16[2,672,128]{2,1,0:T(8,128)(2,1)S(1)}, u32[]{:S(2)}, u32[]{:S(2)}) %collective-permute-start.22) | collective-permute-done | bytes 344096 | tf_op jit(solution)/shard_map/ppermute | solution.py:356
  133.2 2.4 %collective-permute-done.29.refs_5_ = bf16[2,432,128]{2,1,0:T(8,128)(2,1)S(1)} collective-permute-done((bf16[2,432,128]{2,1,0:T(8,128)(2,1)S(1)}, bf16[2,432,128]{2,1,0:T(8,128)(2,1)S(1)}, u32[]{:S(2)}, u32[]{:S(2)}) %collective-permute-start.29) | collective-permute-done | bytes 221216 | tf_op jit(solution)/shard_map/ppermute | solution.py:356
  135.6 0.8 pad_maximum_fusion
  137.0 2.9 %unpack.1 = (f32[544,256]{1,0:T(8,128)}, f32[64,2176]{1,0:T(8,128)}, f32[544,1024]{1,0:T(8,128)}, f32[256,1024]{1,0:T(8,128)}, f32[48,128]{1,0:T(8,128)S(1)}) custom-call(s32[3]{0:T(128)S(1)} %copy-done, bf16[2,672,128]{2,1,0:T(8,128)(2,1)S(1)} %pad_maximum_fusion.1.refs_0_, bf16[2,672,128]{2,1,0:T(8,128)(2,1)S(1)} %collective-permute-done.22.refs_1_, ...), custom_call_target="tpu_custom_call" | custom-call | flops 4000000000 | bytes 12000000 | tf_op jit(solution)/shard_map/unpack/pallas_call | solution.py:583
  139.9 0.7 dynamic_slice.12
  140.6 0.6 fusion.31
  (90 shorter events, 5.4 us)
Async XLA Ops:
  1.2 14.1 %copy-start = (s32[3]{0:T(128)S(1)}, s32[3]{0:T(128)}, u32[]{:S(2)}) copy-start(s32[3]{0:T(128)} %pad_add_fusion.pos) | copy-start | bytes 40
  1.2 14.1 %copy-start.2 = (bf16[256,2176]{1,0:T(8,128)(2,1)S(1)}, bf16[256,2176]{1,0:T(8,128)(2,1)}, u32[]{:S(2)}) copy-start(bf16[256,2176]{1,0:T(8,128)(2,1)} %refs_3_.3) | copy-start | bytes 3342340
  1.2 14.1 %copy-start.3 = (bf16[2176,256]{1,0:T(8,128)(2,1)S(1)}, bf16[2176,256]{1,0:T(8,128)(2,1)}, u32[]{:S(2)}) copy-start(bf16[2176,256]{1,0:T(8,128)(2,1)} %refs_2_.5) | copy-start | bytes 3342340
  1.2 14.1 %copy-start.5 = (bf16[256,2048]{1,0:T(8,128)(2,1)S(1)}, bf16[256,2048]{1,0:T(8,128)(2,1)}, u32[]{:S(2)}) copy-start(bf16[256,2048]{1,0:T(8,128)(2,1)} %refs_1_.5) | copy-start | bytes 3145732
  1.3 14.1 %copy-start.10 = (bf16[256,128]{1,0:T(8,128)(2,1)S(1)}, bf16[256,128]{1,0:T(8,128)(2,1)}, u32[]{:S(2)}) copy-start(bf16[256,128]{1,0:T(8,128)(2,1)} %refs_0_.5) | copy-start | bytes 196612
  1.3 14.1 %copy-start.11 = (f32[2176]{0:T(1024)S(1)}, f32[2176]{0:T(1024)}, u32[]{:S(2)}) copy-start(f32[2176]{0:T(1024)} %refs_4_.3) | copy-start | bytes 26116
  14.8 10.5 %collective-permute-start.3 = (bf16[4,2,672,128]{3,2,1,0:T(8,128)(2,1)}, bf16[4,2,672,128]{3,2,1,0:T(8,128)(2,1)S(1)}, u32[]{:S(2)}, u32[]{:S(2)}) collective-permute-start(bf16[4,2,672,128]{3,2,1,0:T(8,128)(2,1)} %get-tuple-element.89), channel_id=1, source_target_pairs={{0,4},{4,0},{8,12},{12,8},{16,20},{20,16},{24,28},{28,24},{1,5},{5... | collective-permute-start | bytes 4128776 | tf_op jit(solution)/shard_map/ppermute | solution.py:353
  15.3 13.2 %collective-permute-start.5 = (bf16[4,2,672,128]{3,2,1,0:T(8,128)(2,1)}, bf16[4,2,672,128]{3,2,1,0:T(8,128)(2,1)S(1)}, u32[]{:S(2)}, u32[]{:S(2)}) collective-permute-start(bf16[4,2,672,128]{3,2,1,0:T(8,128)(2,1)} %get-tuple-element.95), channel_id=1, source_target_pairs={{0,4},{4,0},{8,12},{12,8},{16,20},{20,16},{24,28},{28,24},{1,5},{5... | collective-permute-start | bytes 4128776 | tf_op jit(solution)/shard_map/ppermute | solution.py:353
  18.7 6.6 %copy-start.17 = (bf16[4,2,672,128]{3,2,1,0:T(8,128)(2,1)S(1)}, bf16[4,2,672,128]{3,2,1,0:T(8,128)(2,1)}, u32[]{:S(2)}) copy-start(bf16[4,2,672,128]{3,2,1,0:T(8,128)(2,1)} %get-tuple-element.88) | copy-start | bytes 4128772
  18.7 9.8 %copy-start.19 = (bf16[4,2,672,128]{3,2,1,0:T(8,128)(2,1)S(1)}, bf16[4,2,672,128]{3,2,1,0:T(8,128)(2,1)}, u32[]{:S(2)}) copy-start(bf16[4,2,672,128]{3,2,1,0:T(8,128)(2,1)} %get-tuple-element.94) | copy-start | bytes 4128772
  25.3 9.0 %copy-start.18 = (bf16[4,2,672,128]{3,2,1,0:T(8,128)(2,1)}, bf16[4,2,672,128]{3,2,1,0:T(8,128)(2,1)S(1)}, u32[]{:S(2)}) copy-start(bf16[4,2,672,128]{3,2,1,0:T(8,128)(2,1)S(1)} %collective-permute-done.3) | copy-start | bytes 4128772
  25.3 5.0 %copy-start.6 = (bf16[256,2048]{1,0:T(8,128)(2,1)S(1)}, bf16[256,2048]{1,0:T(8,128)(2,1)}, u32[]{:S(2)}) copy-start(bf16[256,2048]{1,0:T(8,128)(2,1)} %refs_1_.5) | copy-start | bytes 3145732
  25.3 5.0 %copy-start.14 = (bf16[2176,256]{1,0:T(8,128)(2,1)S(1)}, bf16[2176,256]{1,0:T(8,128)(2,1)}, u32[]{:S(2)}) copy-start(bf16[2176,256]{1,0:T(8,128)(2,1)} %get-tuple-element.90.refs_3_) | copy-start | bytes 3342340
  25.5 4.8 %copy-start.4 = (bf16[2176,256]{1,0:T(8,128)(2,1)S(1)}, bf16[2176,256]{1,0:T(8,128)(2,1)}, u32[]{:S(2)}) copy-start(bf16[2176,256]{1,0:T(8,128)(2,1)} %refs_2_.5) | copy-start | bytes 3342340
  25.5 4.8 %copy-start.16 = (f32[24,128]{1,0:T(8,128)S(1)}, f32[24,128]{1,0:T(8,128)}, u32[]{:S(2)}) copy-start(f32[24,128]{1,0:T(8,128)} %get-tuple-element.93.refs_7_) | copy-start | bytes 36868
  25.5 18.8 %collective-permute-start.4 = (bf16[2,2,672,128]{3,2,1,0:T(8,128)(2,1)S(1)}, bf16[2,2,672,128]{3,2,1,0:T(8,128)(2,1)}, u32[]{:S(2)}, u32[]{:S(2)}) collective-permute-start(bf16[2,2,672,128]{3,2,1,0:T(8,128)(2,1)S(1)} %fusion.refs_8_), channel_id=1, source_target_pairs={{0,1},{1,0},{2,3},{3,2},{4,5},{5,4},{6,7},{7,6},{8,9},{9,8},{10,11... | collective-permute-start | bytes 2064392 | tf_op jit(solution)/shard_map/ppermute | solution.py:359
  28.5 5.8 %copy-start.20 = (bf16[4,2,672,128]{3,2,1,0:T(8,128)(2,1)}, bf16[4,2,672,128]{3,2,1,0:T(8,128)(2,1)S(1)}, u32[]{:S(2)}) copy-start(bf16[4,2,672,128]{3,2,1,0:T(8,128)(2,1)S(1)} %collective-permute-done.5) | copy-start | bytes 4128772
  28.8 18.4 %collective-permute-start.6 = (bf16[2,2,672,128]{3,2,1,0:T(8,128)(2,1)S(1)}, bf16[2,2,672,128]{3,2,1,0:T(8,128)(2,1)}, u32[]{:S(2)}, u32[]{:S(2)}) collective-permute-start(bf16[2,2,672,128]{3,2,1,0:T(8,128)(2,1)S(1)} %add_convert_fusion.refs_9_), channel_id=1, source_target_pairs={{0,2},{1,3},{2,0},{3,1},{4,6},{5,7},{6,4},{7,5},{8,10},{9,11},{10,... | collective-permute-start | bytes 2064392 | tf_op jit(solution)/shard_map/ppermute | solution.py:359
  34.3 32.8 %collective-permute-start.9 = (bf16[4,2,432,128]{3,2,1,0:T(8,128)(2,1)}, bf16[4,2,432,128]{3,2,1,0:T(8,128)(2,1)}, u32[]{:S(2)}, u32[]{:S(2)}) collective-permute-start(bf16[4,2,432,128]{3,2,1,0:T(8,128)(2,1)} %get-tuple-element.96), channel_id=1, source_target_pairs={{0,4},{4,0},{8,12},{12,8},{16,20},{20,16},{24,28},{28,24},{1,5},{5... | collective-permute-start | bytes 2654216 | tf_op jit(solution)/shard_map/ppermute | solution.py:353
  34.3 34.0 %collective-permute-start.10 = (bf16[4,2,432,128]{3,2,1,0:T(8,128)(2,1)}, bf16[4,2,432,128]{3,2,1,0:T(8,128)(2,1)}, u32[]{:S(2)}, u32[]{:S(2)}) collective-permute-start(bf16[4,2,432,128]{3,2,1,0:T(8,128)(2,1)} %get-tuple-element.107), channel_id=1, source_target_pairs={{0,4},{4,0},{8,12},{12,8},{16,20},{20,16},{24,28},{28,24},{1,5},{5... | collective-permute-start | bytes 2654216 | tf_op jit(solution)/shard_map/ppermute | solution.py:353
  34.8 16.6 %collective-permute-start = (bf16[2,2,256,128]{3,2,1,0:T(8,128)(2,1)}, bf16[2,2,256,128]{3,2,1,0:T(8,128)(2,1)S(1)}, u32[]{:S(2)}, u32[]{:S(2)}) collective-permute-start(bf16[2,2,256,128]{3,2,1,0:T(8,128)(2,1)} %get-tuple-element.85), channel_id=1, source_target_pairs={{0,8},{4,12},{8,0},{12,4},{16,24},{20,28},{24,16},{28,20},{1,9},{5... | collective-permute-start | bytes 786440 | tf_op jit(solution)/shard_map/ppermute | solution.py:356
  44.3 21.2 %collective-permute-start.1 = (bf16[2,2,256,128]{3,2,1,0:T(8,128)(2,1)}, bf16[2,2,256,128]{3,2,1,0:T(8,128)(2,1)S(1)}, u32[]{:S(2)}, u32[]{:S(2)}) collective-permute-start(bf16[2,2,256,128]{3,2,1,0:T(8,128)(2,1)} %copy-done.9), channel_id=1, source_target_pairs={{0,16},{4,20},{8,24},{12,28},{16,0},{20,4},{24,8},{28,12},{1,17},{... | collective-permute-start | bytes 786440 | tf_op jit(solution)/shard_map/ppermute | solution.py:356
  47.1 19.9 %collective-permute-start.2 = (bf16[2,2,256,128]{3,2,1,0:T(8,128)(2,1)}, bf16[2,2,256,128]{3,2,1,0:T(8,128)(2,1)S(1)}, u32[]{:S(2)}, u32[]{:S(2)}) collective-permute-start(bf16[2,2,256,128]{3,2,1,0:T(8,128)(2,1)} %copy-done.8), channel_id=1, source_target_pairs={{0,24},{4,28},{8,16},{12,20},{16,8},{20,12},{24,0},{28,4},{1,25},{... | collective-permute-start | bytes 786440 | tf_op jit(solution)/shard_map/ppermute | solution.py:356
  49.7 17.4 %copy-start.13 = (bf16[2,2,256,128]{3,2,1,0:T(8,128)(2,1)S(1)}, bf16[2,2,256,128]{3,2,1,0:T(8,128)(2,1)}, u32[]{:S(2)}) copy-start(bf16[2,2,256,128]{3,2,1,0:T(8,128)(2,1)} %copy-done.12) | copy-start | bytes 786436
  51.5 20.1 %collective-permute-start.8 = (bf16[2,672,128]{2,1,0:T(8,128)(2,1)S(1)}, bf16[2,672,128]{2,1,0:T(8,128)(2,1)S(1)}, u32[]{:S(2)}, u32[]{:S(2)}) collective-permute-start(bf16[2,672,128]{2,1,0:T(8,128)(2,1)S(1)} %get-tuple-element.160.refs_5_), channel_id=1, source_target_pairs={{0,1},{1,0},{2,3},{3,2},{4,5},{5,4},{6,7},{7,6},{8,9},{9,8},{10,11... | collective-permute-start | bytes 1032200 | tf_op jit(solution)/shard_map/ppermute | solution.py:359
  65.5 16.9 %collective-permute-start.12 = (bf16[2,672,128]{2,1,0:T(8,128)(2,1)S(1)}, bf16[2,672,128]{2,1,0:T(8,128)(2,1)S(1)}, u32[]{:S(2)}, u32[]{:S(2)}) collective-permute-start(bf16[2,672,128]{2,1,0:T(8,128)(2,1)S(1)} %get-tuple-element.161.refs_4_), channel_id=1, source_target_pairs={{0,2},{1,3},{2,0},{3,1},{4,6},{5,7},{6,4},{7,5},{8,10},{9,11},{10,... | collective-permute-start | bytes 1032200 | tf_op jit(solution)/shard_map/ppermute | solution.py:359
  67.1 10.7 %collective-permute-start.7 = (bf16[4,2,256,128]{3,2,1,0:T(8,128)(2,1)S(1)}, bf16[4,2,256,128]{3,2,1,0:T(8,128)(2,1)S(1)}, u32[]{:S(2)}, u32[]{:S(2)}) collective-permute-start(bf16[4,2,256,128]{3,2,1,0:T(8,128)(2,1)S(1)} %select.3), channel_id=1, source_target_pairs={{0,4},{4,0},{8,12},{12,8},{16,20},{20,16},{24,28},{28,24},{1,5},{5... | collective-permute-start | bytes 1572872 | tf_op jit(solution)/shard_map/ppermute | solution.py:353
  68.3 9.4 %copy-start.7 = (s32[2,8192,4]{1,2,0:T(4,128)S(1)}, s32[2,8192,4]{1,2,0:T(4,128)}, u32[]{:S(2)}) copy-start(s32[2,8192,4]{1,2,0:T(4,128)} %param.23) | copy-start | bytes 786436
  68.3 22.4 %collective-permute-start.11 = (bf16[2,2,432,128]{3,2,1,0:T(8,128)(2,1)S(1)}, bf16[2,2,432,128]{3,2,1,0:T(8,128)(2,1)S(1)}, u32[]{:S(2)}, u32[]{:S(2)}) collective-permute-start(bf16[2,2,432,128]{3,2,1,0:T(8,128)(2,1)S(1)} %fusion.5), channel_id=1, source_target_pairs={{0,1},{1,0},{2,3},{3,2},{4,5},{5,4},{6,7},{7,6},{8,9},{9,8},{10,11... | collective-permute-start | bytes 1327112 | tf_op jit(solution)/shard_map/ppermute | solution.py:359
  71.0 19.7 %collective-permute-start.15 = (bf16[2,2,432,128]{3,2,1,0:T(8,128)(2,1)S(1)}, bf16[2,2,432,128]{3,2,1,0:T(8,128)(2,1)S(1)}, u32[]{:S(2)}, u32[]{:S(2)}) collective-permute-start(bf16[2,2,432,128]{3,2,1,0:T(8,128)(2,1)S(1)} %fusion.6), channel_id=1, source_target_pairs={{0,2},{1,3},{2,0},{3,1},{4,6},{5,7},{6,4},{7,5},{8,10},{9,11},{10,... | collective-permute-start | bytes 1327112 | tf_op jit(solution)/shard_map/ppermute | solution.py:359
  73.0 12.9 %collective-permute-start.13 = (bf16[2,672,128]{2,1,0:T(8,128)(2,1)S(1)}, bf16[2,672,128]{2,1,0:T(8,128)(2,1)S(1)}, u32[]{:S(2)}, u32[]{:S(2)}) collective-permute-start(bf16[2,672,128]{2,1,0:T(8,128)(2,1)S(1)} %fusion.2.rest_5_), channel_id=1, source_target_pairs={{0,8},{4,12},{8,0},{12,4},{16,24},{20,28},{24,16},{28,20},{1,9},{5... | collective-permute-start | bytes 1032200 | tf_op jit(solution)/shard_map/ppermute | solution.py:356
  87.1 14.9 %collective-permute-start.17 = (bf16[1,672,128]{2,1,0:T(8,128)(2,1)S(1)}, bf16[1,672,128]{2,1,0:T(8,128)(2,1)S(1)}, u32[]{:S(2)}, u32[]{:S(2)}) collective-permute-start(bf16[1,672,128]{2,1,0:T(8,128)(2,1)S(1)} %fusion.17), channel_id=1, source_target_pairs={{0,16},{4,20},{8,24},{12,28},{16,0},{20,4},{24,8},{28,12},{1,17},{... | collective-permute-start | bytes 516104 | tf_op jit(solution)/shard_map/ppermute | solution.py:356
  91.8 11.5 %collective-permute-start.16 = (bf16[2,432,128]{2,1,0:T(8,128)(2,1)S(1)}, bf16[2,432,128]{2,1,0:T(8,128)(2,1)S(1)}, u32[]{:S(2)}, u32[]{:S(2)}) collective-permute-start(bf16[2,432,128]{2,1,0:T(8,128)(2,1)S(1)} %fusion.9), channel_id=1, source_target_pairs={{0,1},{1,0},{2,3},{3,2},{4,5},{5,4},{6,7},{7,6},{8,9},{9,8},{10,11... | collective-permute-start | bytes 663560 | tf_op jit(solution)/shard_map/ppermute | solution.py:359
  93.4 14.8 %collective-permute-start.25 = (bf16[2,432,128]{2,1,0:T(8,128)(2,1)S(1)}, bf16[2,432,128]{2,1,0:T(8,128)(2,1)S(1)}, u32[]{:S(2)}, u32[]{:S(2)}) collective-permute-start(bf16[2,432,128]{2,1,0:T(8,128)(2,1)S(1)} %fusion.10.rest_5_), channel_id=1, source_target_pairs={{0,2},{1,3},{2,0},{3,1},{4,6},{5,7},{6,4},{7,5},{8,10},{9,11},{10,... | collective-permute-start | bytes 663560 | tf_op jit(solution)/shard_map/ppermute | solution.py:359
  98.8 6.7 %collective-permute-start.14 = (bf16[2,512,128]{2,1,0:T(8,128)(2,1)S(1)}, bf16[2,512,128]{2,1,0:T(8,128)(2,1)S(1)}, u32[]{:S(2)}, u32[]{:S(2)}) collective-permute-start(bf16[2,512,128]{2,1,0:T(8,128)(2,1)S(1)} %slice_bitcast_fusion.1), channel_id=1, source_target_pairs={{0,1},{1,0},{2,3},{3,2},{4,5},{5,4},{6,7},{7,6},{8,9},{9,8},{10,11... | collective-permute-start | bytes 786440 | tf_op jit(solution)/shard_map/ppermute | solution.py:359
  100.4 7.8 %collective-permute-start.19 = (bf16[2,512,128]{2,1,0:T(8,128)(2,1)S(1)}, bf16[2,512,128]{2,1,0:T(8,128)(2,1)S(1)}, u32[]{:S(2)}, u32[]{:S(2)}) collective-permute-start(bf16[2,512,128]{2,1,0:T(8,128)(2,1)S(1)} %slice_bitcast_fusion), channel_id=1, source_target_pairs={{0,2},{1,3},{2,0},{3,1},{4,6},{5,7},{6,4},{7,5},{8,10},{9,11},{10,... | collective-permute-start | bytes 786440 | tf_op jit(solution)/shard_map/ppermute | solution.py:359
  103.2 18.5 %collective-permute-start.21 = (bf16[1,672,128]{2,1,0:T(8,128)(2,1)S(1)}, bf16[1,672,128]{2,1,0:T(8,128)(2,1)S(1)}, u32[]{:S(2)}, u32[]{:S(2)}) collective-permute-start(bf16[1,672,128]{2,1,0:T(8,128)(2,1)S(1)} %fusion.14), channel_id=1, source_target_pairs={{0,16},{4,20},{8,24},{12,28},{16,0},{20,4},{24,8},{28,12},{1,17},{... | collective-permute-start | bytes 516104 | tf_op jit(solution)/shard_map/ppermute | solution.py:356
  104.4 8.6 %collective-permute-start.26 = (bf16[2,432,128]{2,1,0:T(8,128)(2,1)S(1)}, bf16[2,432,128]{2,1,0:T(8,128)(2,1)S(1)}, u32[]{:S(2)}, u32[]{:S(2)}) collective-permute-start(bf16[2,432,128]{2,1,0:T(8,128)(2,1)S(1)} %fusion.8), channel_id=1, source_target_pairs={{0,8},{4,12},{8,0},{12,4},{16,24},{20,28},{24,16},{28,20},{1,9},{5... | collective-permute-start | bytes 663560 | tf_op jit(solution)/shard_map/ppermute | solution.py:356
  105.6 22.7 %collective-permute-start.18 = (bf16[512,128]{1,0:T(8,128)(2,1)S(1)}, bf16[512,128]{1,0:T(8,128)(2,1)S(1)}, u32[]{:S(2)}, u32[]{:S(2)}) collective-permute-start(bf16[512,128]{1,0:T(8,128)(2,1)S(1)} %fusion.21), channel_id=1, source_target_pairs={{0,2},{1,3},{2,0},{3,1},{4,6},{5,7},{6,4},{7,5},{8,10},{9,11},{10,... | collective-permute-start | bytes 393224 | tf_op jit(solution)/shard_map/ppermute | solution.py:359
  113.9 6.6 %collective-permute-start.27 = (bf16[1,432,128]{2,1,0:T(8,128)(2,1)S(1)}, bf16[1,432,128]{2,1,0:T(8,128)(2,1)S(1)}, u32[]{:S(2)}, u32[]{:S(2)}) collective-permute-start(bf16[1,432,128]{2,1,0:T(8,128)(2,1)S(1)} %fusion.30), channel_id=1, source_target_pairs={{0,16},{4,20},{8,24},{12,28},{16,0},{20,4},{24,8},{28,12},{1,17},{... | collective-permute-start | bytes 331784 | tf_op jit(solution)/shard_map/ppermute | solution.py:356
  115.0 20.6 %collective-permute-start.20 = (bf16[512,128]{1,0:T(8,128)(2,1)S(1)}, bf16[512,128]{1,0:T(8,128)(2,1)S(1)}, u32[]{:S(2)}, u32[]{:S(2)}) collective-permute-start(bf16[512,128]{1,0:T(8,128)(2,1)S(1)} %fusion.18), channel_id=1, source_target_pairs={{0,1},{1,0},{2,3},{3,2},{4,5},{5,4},{6,7},{7,6},{8,9},{9,8},{10,11... | collective-permute-start | bytes 393224 | tf_op jit(solution)/shard_map/ppermute | solution.py:359
  121.5 6.6 %collective-permute-start.28 = (bf16[1,432,128]{2,1,0:T(8,128)(2,1)S(1)}, bf16[1,432,128]{2,1,0:T(8,128)(2,1)S(1)}, u32[]{:S(2)}, u32[]{:S(2)}) collective-permute-start(bf16[1,432,128]{2,1,0:T(8,128)(2,1)S(1)} %fusion.27), channel_id=1, source_target_pairs={{0,16},{4,20},{8,24},{12,28},{16,0},{20,4},{24,8},{28,12},{1,17},{... | collective-permute-start | bytes 331784 | tf_op jit(solution)/shard_map/ppermute | solution.py:356
  121.8 11.4 %collective-permute-start.22 = (bf16[2,672,128]{2,1,0:T(8,128)(2,1)S(1)}, bf16[2,672,128]{2,1,0:T(8,128)(2,1)S(1)}, u32[]{:S(2)}, u32[]{:S(2)}) collective-permute-start(bf16[2,672,128]{2,1,0:T(8,128)(2,1)S(1)} %pad_maximum_fusion.1.refs_0_), channel_id=1, source_target_pairs={{0,8},{4,12},{8,0},{12,4},{16,24},{20,28},{24,16},{28,20},{1,9},{5... | collective-permute-start | bytes 1032200 | tf_op jit(solution)/shard_map/ppermute | solution.py:356
  124.4 12.0 %collective-permute-start.23 = (bf16[2,672,128]{2,1,0:T(8,128)(2,1)S(1)}, bf16[2,672,128]{2,1,0:T(8,128)(2,1)S(1)}, u32[]{:S(2)}, u32[]{:S(2)}) collective-permute-start(bf16[2,672,128]{2,1,0:T(8,128)(2,1)S(1)} %pad_maximum_fusion.1.refs_0_), channel_id=1, source_target_pairs={{0,4},{4,0},{8,12},{12,8},{16,20},{20,16},{24,28},{28,24},{1,5},{5... | collective-permute-start | bytes 1032200 | tf_op jit(solution)/shard_map/ppermute | solution.py:353
  128.2 7.4 %collective-permute-start.29 = (bf16[2,432,128]{2,1,0:T(8,128)(2,1)S(1)}, bf16[2,432,128]{2,1,0:T(8,128)(2,1)S(1)}, u32[]{:S(2)}, u32[]{:S(2)}) collective-permute-start(bf16[2,432,128]{2,1,0:T(8,128)(2,1)S(1)} %pad_maximum_fusion.2.refs_4_), channel_id=1, source_target_pairs={{0,8},{4,12},{8,0},{12,4},{16,24},{20,28},{24,16},{28,20},{1,9},{5... | collective-permute-start | bytes 663560 | tf_op jit(solution)/shard_map/ppermute | solution.py:356
  128.3 8.1 %collective-permute-start.30 = (bf16[2,432,128]{2,1,0:T(8,128)(2,1)S(1)}, bf16[2,432,128]{2,1,0:T(8,128)(2,1)S(1)}, u32[]{:S(2)}, u32[]{:S(2)}) collective-permute-start(bf16[2,432,128]{2,1,0:T(8,128)(2,1)S(1)} %pad_maximum_fusion.2.refs_4_), channel_id=1, source_target_pairs={{0,4},{4,0},{8,12},{12,8},{16,20},{20,16},{24,28},{28,24},{1,5},{5... | collective-permute-start | bytes 663560 | tf_op jit(solution)/shard_map/ppermute | solution.py:353
  133.2 3.3 %collective-permute-start.24 = (bf16[2,672,128]{2,1,0:T(8,128)(2,1)S(1)}, bf16[2,672,128]{2,1,0:T(8,128)(2,1)S(1)}, u32[]{:S(2)}, u32[]{:S(2)}) collective-permute-start(bf16[2,672,128]{2,1,0:T(8,128)(2,1)S(1)} %collective-permute-done.22.refs_1_), channel_id=1, source_target_pairs={{0,4},{4,0},{8,12},{12,8},{16,20},{20,16},{24,28},{28,24},{1,5},{5... | collective-permute-start | bytes 1032200 | tf_op jit(solution)/shard_map/ppermute | solution.py:353
  135.6 1.5 %collective-permute-start.31 = (bf16[2,432,128]{2,1,0:T(8,128)(2,1)S(1)}, bf16[2,432,128]{2,1,0:T(8,128)(2,1)S(1)}, u32[]{:S(2)}, u32[]{:S(2)}) collective-permute-start(bf16[2,432,128]{2,1,0:T(8,128)(2,1)S(1)} %collective-permute-done.29.refs_5_), channel_id=1, source_target_pairs={{0,4},{4,0},{8,12},{12,8},{16,20},{20,16},{24,28},{28,24},{1,5},{5... | collective-permute-start | bytes 663560 | tf_op jit(solution)/shard_map/ppermute | solution.py:353
  (5 other events, 13.7 us)

commit v5 on v4

--- a/solution.py
+++ b/solution.py
@@ -40,7 +40,7 @@
 
 
 def put_blocks(ref, row_pos, places, offset, value):
-    shards, rows_q = ref.shape[0], ref.shape[2]
+    shards, n_half, rows_q = ref.shape[1], ref.shape[2], ref.shape[3]
     rows = value.shape[0] // shards
     step = round_up(rows, 16)
     blocks = value.shape[1] // LANES
@@ -51,7 +51,8 @@
             while done < rows:
                 quarter, at = divmod(offset + block * step + done, rows_q)
                 length = min(rows - done, rows_q - at)
-                ref[slot, places[quarter], at : at + length, :] = value[
+                place = places[quarter]
+                ref[lax.div(place, n_half), slot, lax.rem(place, n_half), at : at + length, :] = value[
                     shard * rows + done : shard * rows + done + length,
                     block * LANES : (block + 1) * LANES,
                 ].astype(ref.dtype)
@@ -64,10 +65,9 @@
         ref[offset + block : offset + block + 1, :] = value[:, block * LANES : (block + 1) * LANES]
 
 
-def split_parts(pack, low, high):
-    half = low.shape[1]
-    low[...] = pack[:, :half]
-    high[...] = pack[:, half:]
+def position():
+    table_pos = lax.axis_index("table")
+    return lax.rem(table_pos, 2), lax.axis_index("row"), table_pos
 
 
 class Loads:
@@ -92,13 +92,13 @@
     return value.reshape(1, value.shape[-1])
 
 
-def front_kernel(pos, *refs):
-    sources, outs, targets = refs[:11], refs[11:18], refs[18:29]
-    halves, thirds, pack, sems = refs[29:]
-    send_low, send_high, keep_low, keep_high, crossed_t_out, first_out, small = outs
+def front_kernel(*refs):
+    sources, outs, targets = refs[:11], refs[11:16], refs[16:27]
+    halves, thirds, sems = refs[27:]
+    send, keep, crossed_t_out, first_out, small = outs
     load = Loads(sources, targets, sems)
-    core, row_pos = pos[0], pos[1]
-    places = places_of(pos[2] // 2, pack.shape[1])
+    core, row_pos, table_pos = position()
+    places = places_of(lax.div(table_pos, 2), 2 * send.shape[2])
     stacked = jnp.concatenate([load(0), load(1)], axis=1)
     reduced = matmul(stacked, load(2)).astype(bf16)
     widened = matmul(reduced, load(3)) + as_row(load(4))
@@ -137,13 +137,12 @@
     act_t = act_first.T
     crossed_t = crossed.T
     crossed_t_out[...] = crossed_t
-    for low, high, who in ((send_low, send_high, 1 - core), (keep_low, keep_high, core)):
-        offset = put_blocks(pack, row_pos, places, 0, matmul(act_t, halves[who]))
-        put_blocks(pack, row_pos, places, offset, matmul(crossed_t, thirds[who]))
-        split_parts(pack, low, high)
-
-
-def middle_kernel(n_z, pos, *refs):
+    for ref, who in ((send, 1 - core), (keep, core)):
+        offset = put_blocks(ref, row_pos, places, 0, matmul(act_t, halves[who]))
+        put_blocks(ref, row_pos, places, offset, matmul(crossed_t, thirds[who]))
+
+
+def middle_kernel(n_z, *refs):
     sources, delta_first = refs[:6], refs[6]
     widened_out, reduced_out = refs[7:9]
     pooled_outs = refs[9 : 9 + n_z]
@@ -151,7 +150,8 @@
     targets = rest[:6]
     by_group, sems = rest[6:]
     load = Loads(sources, targets, sems)
-    core, z_pos = pos[0], pos[2] // 2
+    core, _, table_pos = position()
+    z_pos = lax.div(table_pos, 2)
     stacked = jnp.concatenate([load(0), load(1)], axis=1)
     cross_down, cross_up = load(2), load(3)
     reduced = matmul(stacked, cross_down).astype(bf16)
@@ -174,14 +174,14 @@
         pooled_outs[which][1] = by_group[z_pos ^ which, 1 - core]
 
 
-def back_kernel(pos, *refs):
+def back_kernel(*refs):
     dense_feat, pooled, cross_down, crossed_t, delta_first, delta_widened, delta_reduced = refs[:7]
     small_in = refs[7]
-    send_low, send_high, keep_low, keep_high = refs[10:14]
-    half_delta, sixths, pack, small = refs[14:]
-    core, row_pos = pos[0], pos[1]
-    n_row = pack.shape[0]
-    places = places_of(pos[2] // 2, pack.shape[1])
+    send, keep = refs[10:12]
+    half_delta, sixths, small = refs[12:]
+    core, row_pos, table_pos = position()
+    n_row = send.shape[1]
+    places = places_of(lax.div(table_pos, 2), 2 * send.shape[2])
     rank = delta_reduced.shape[1]
     feat = delta_widened.shape[1]
     hid = delta_first.shape[1]
@@ -197,18 +197,17 @@
     stacked = jnp.concatenate([dense_feat[...], pooled[...]], axis=1)
     reduced_t = matmul(stacked, cross_down[...]).astype(bf16).T
     stacked_t = stacked.T
-    for low, high, who in ((send_low, send_high, 1 - core), (keep_low, keep_high, core)):
-        offset = put_blocks(pack, row_pos, places, 0, matmul(crossed_t[...], sixths[who]))
-        offset = put_blocks(pack, row_pos, places, offset, matmul(stacked_t, half_delta[who]))
+    for ref, who in ((send, 1 - core), (keep, core)):
+        offset = put_blocks(ref, row_pos, places, 0, matmul(crossed_t[...], sixths[who]))
+        offset = put_blocks(ref, row_pos, places, offset, matmul(stacked_t, half_delta[who]))
         start = pl.multiple_of(who * (feat - SPAN), LANES)
         offset = put_blocks(
-            pack, row_pos, places, offset, matmul(reduced_t, delta_widened[:, pl.ds(start, SPAN)])
+            ref, row_pos, places, offset, matmul(reduced_t, delta_widened[:, pl.ds(start, SPAN)])
         )
-        offset = put_blocks(pack, row_pos, places, offset, sums)
-        tail = pack.shape[1] * pack.shape[2] - offset
+        offset = put_blocks(ref, row_pos, places, offset, sums)
+        tail = 2 * ref.shape[2] * ref.shape[3] - offset
         if tail:
-            put_blocks(pack, row_pos, places, offset, jnp.zeros((n_row * tail, LANES), f32))
-        split_parts(pack, low, high)
+            put_blocks(ref, row_pos, places, offset, jnp.zeros((n_row * tail, LANES), f32))
 
 
 def select_kernel(n_z, *refs):
@@ -217,11 +216,12 @@
         out[which] = refs[which][1]
 
 
-def count_kernel(n_row, table, hot, n_z, pos, slots, *rest):
+def count_kernel(n_row, table, hot, n_z, slots, *rest):
     direct, crossed, out = rest[:n_z], rest[n_z], rest[-1]
     block = out.shape[1]
     samples = crossed.shape[2]
-    core, row_pos, z_pos = pos[0], pos[1], pos[2] // 2
+    core, row_pos, table_pos = position()
+    z_pos = lax.div(table_pos, 2)
     base = (pl.program_id(0) ^ row_pos) * block
     names = lax.broadcasted_iota(jnp.int16, (block, samples), 0)
     total = jnp.zeros((block, out.shape[2]), f32)
@@ -241,12 +241,13 @@
     out[0] = total.astype(out.dtype)
 
 
-def unpack_kernel(pos, *refs):
+def unpack_kernel(*refs):
     parts = refs[0:8]
-    g_down, g_up, g_first, g_second, g_small = refs[8:13]
-    held = refs[13:15]
-    core = pos[0]
-    z_pos = pos[2] // 2
+    g_down, g_up, g_first, g_second = refs[8:12]
+    small_outs = refs[12:16]
+    held, small = refs[16:18], refs[18]
+    core, row_pos, table_pos = position()
+    z_pos = lax.div(table_pos, 2)
     for stream in range(2):
         lower, upper, lower_other, upper_other = parts[4 * stream : 4 * stream + 4]
         ref = held[stream]
@@ -280,20 +281,31 @@
         offset = take(back, g_down, half, offset, range(half * blocks, (half + 1) * blocks))
         blocks = g_up.shape[1] // LANES
         offset = take(back, g_up, half, offset, range(half * (blocks - 9), half * (blocks - 9) + 9))
-    g_small[...] = back[0, offset : offset + 48, :].astype(f32)
+    small[0:48, :] = back[0, offset : offset + 48, :].astype(f32)
+    small[48:, :] = jnp.zeros((small.shape[0] - 48, LANES), f32)
+    for out, first in zip(small_outs, (24, 0, 8, 16)):
+        share = out.shape[0]
+        begin = row_pos * share
+        row, lane = lax.div(begin, LANES), lax.rem(begin, LANES)
+        lanes = lax.broadcasted_iota(jnp.int32, (1, LANES), 1)
+        for start in range(0, share, LANES):
+            length = min(LANES, share - start)
+            this = small[pl.ds(first + row + start // LANES, 1), :]
+            later = small[pl.ds(first + row + start // LANES + 1, 1), :]
+            both = jnp.where(lanes < lane, later, this)
+            turned = pltpu.roll(both, lax.rem(LANES - lane, LANES), 1)
+            out[start : start + length] = turned.reshape(LANES)[:length]
 
 
 def whole(memory=pltpu.VMEM):
     return pl.BlockSpec(memory_space=memory)
 
 
-def cost(micros):
-    return pl.CostEstimate(
-        flops=int(micros * 1.0e9), transcendentals=0, bytes_accessed=int(micros * 3.0e6)
-    )
-
-
-def call(body, outs, scratch, in_specs, name, micros, mib):
+def no_cost():
+    return pl.CostEstimate(flops=0, transcendentals=0, bytes_accessed=0)
+
+
+def call(body, outs, scratch, in_specs, name, mib):
     return pl.pallas_call(
         body,
         out_shape=outs,
@@ -301,7 +313,7 @@
         out_specs=[whole()] * len(outs),
         scratch_shapes=scratch,
         compiler_params=pltpu.CompilerParams(vmem_limit_bytes=mib * MIB),
-        cost_estimate=cost(micros),
+        cost_estimate=no_cost(),
         name=name,
     )
 
@@ -340,9 +352,6 @@
     n_z = n_table // 2
     row_bits = n_row.bit_length() - 1
     z_bits = n_z.bit_length() - 1
-    table_pos = lax.axis_index("table")
-    row_pos = lax.axis_index("row")
-    pos = jnp.stack([table_pos % 2, row_pos, table_pos]).astype(jnp.int32)
     batch, width = dense_feat.shape
     feat, rank = cross_down.shape
     hid = w_hidden1.shape[1]
@@ -367,16 +376,13 @@
     rows_back += 9 * round_up(rank // n_row, 16) + 48
     rows_front, rows_back = (round_up(rows, 16 * n_z) for rows in (rows_front, rows_back))
 
-    def half_pack(rows):
-        return jax.ShapeDtypeStruct((n_row, n_z // 2, rows // n_z, LANES), bf16)
-
-    def pack_scratch(rows):
-        return pltpu.VMEM((n_row, n_z, rows // n_z, LANES), bf16)
+    def packed(rows):
+        return jax.ShapeDtypeStruct((2, n_row, n_z // 2, rows // n_z, LANES), bf16)
 
     def wide(*shape):
         return jax.ShapeDtypeStruct(shape, bf16)
 
-    smem, hbm, vmem, anywhere = whole(pltpu.SMEM), whole(pltpu.HBM), whole(), whole(pl.ANY)
+    hbm, vmem, anywhere = whole(pltpu.HBM), whole(), whole(pl.ANY)
 
     sources = (
         dense_feat,
@@ -391,23 +397,21 @@
         w_logit,
         labels,
     )
-    send_low, send_high, keep_low, keep_high, crossed_t, delta_first, small = call(
+    send, keep, crossed_t, delta_first, small = call(
         front_kernel,
-        [half_pack(rows_front)] * 4
+        [packed(rows_front)] * 2
         + [wide(feat, batch), wide(batch, hid), jax.ShapeDtypeStruct((24, LANES), f32)],
         held_like(sources)
         + [
             pltpu.VMEM((2, batch, hid // 2), bf16),
             pltpu.VMEM((2, batch, early), bf16),
-            pack_scratch(rows_front),
             pltpu.SemaphoreType.DMA((len(sources),)),
         ],
-        [smem] + [hbm] * len(sources),
+        [hbm] * len(sources),
         "front",
-        10,
         60,
-    )(pos, *sources)
-    got_low, got_high = swap_cores(send_low), swap_cores(send_high)
+    )(*sources)
+    got = swap_cores(send)
 
     sources = (dense_feat, pooled, cross_down, cross_up, cross_bias, w_hidden1)
     outs = call(
@@ -418,11 +422,10 @@
             pltpu.VMEM((n_z, 2, tab_grp, batch, width), bf16),
             pltpu.SemaphoreType.DMA((len(sources),)),
         ],
-        [smem] + [hbm] * len(sources) + [vmem],
+        [hbm] * len(sources) + [vmem],
         "middle",
-        7,
-        40,
-    )(pos, *sources, delta_first)
+        60,
+    )(*sources, delta_first)
     delta_widened, delta_reduced = outs[:2]
     pooled_out = outs[2:]
 
@@ -455,8 +458,16 @@
         return lambda array: array[start:stop]
 
     class Halving(Terms):
-        def __init__(self, arrays, order):
-            super().__init__([array.reshape((2,) * row_bits + array.shape[1:]) for array in arrays])
+        def __init__(self, arrays, order, half=None):
+            dims = 0 if half is None else 1
+            super().__init__(
+                [
+                    array.reshape(array.shape[:dims] + (2,) * row_bits + array.shape[dims + 1 :])
+                    for array in arrays
+                ]
+            )
+            if half is not None:
+                self.items = [(array, (index_of(half, 0),)) for array, _ in self.items]
             self.order, self.left = order, list(range(row_bits - 1, -1, -1))
 
         def step(self, at, deps=()):
@@ -470,9 +481,9 @@
             return sent
 
     class Dense:
-        def __init__(self, keep_low, got_low, keep_high, got_high):
-            self.low = Halving([keep_low, got_low], low_first)
-            self.high = Halving([keep_high, got_high], high_first)
+        def __init__(self, keep, got):
+            self.low = Halving([keep, got], low_first, 0)
+            self.high = Halving([keep, got], high_first, 1)
 
         def row_step(self, at, deps=()):
             sent = self.low.step(at, deps)
@@ -500,26 +511,22 @@
             self.pieces = [own, far, swap_cores(own), swap_cores(far)]
             return [first]
 
-    one = Dense(keep_low, got_low, keep_high, got_high)
+    one = Dense(keep, got)
     sent = one.row_step(0)
-
     values = [pooled_out[0]] + [swap_z(pooled_out[which], which) for which in range(1, n_z)]
 
-    send_low, send_high, keep_low, keep_high = call(
+    send, keep = call(
         back_kernel,
-        [half_pack(rows_back)] * 4,
+        [packed(rows_back)] * 2,
         [
             pltpu.VMEM((2, batch, rank // 2), bf16),
             pltpu.VMEM((2, batch, late), bf16),
-            pack_scratch(rows_back),
             pltpu.VMEM((48, LANES), f32),
         ],
-        [smem] + [vmem] * 8 + [anywhere] * 2,
+        [vmem] * 8 + [anywhere] * 2,
         "back",
-        6,
         36,
     )(
-        pos,
         dense_feat,
         pooled,
         cross_down,
@@ -530,23 +537,21 @@
         small,
         *sent,
     )
-    two = Dense(keep_low, swap_cores(send_low), keep_high, swap_cores(send_high))
-    last = [send_low]
-    for at in range(1, row_bits):
-        last = one.row_step(at, last)
+    two = Dense(keep, swap_cores(send))
 
     far_values = call(
         functools.partial(select_kernel, n_z),
         [wide(n_z, tab_grp, batch, width)],
         [],
-        [vmem] * n_z + [anywhere] * len(last),
+        [vmem] * n_z + [anywhere],
         "select",
-        1,
         8,
-    )(*values, *last)[0]
+    )(*values, keep)[0]
     values.append(swap_cores(far_values))
-    last = two.row_step(0, [far_values])
-    last = one.z_step(0, last)
+    last = [far_values]
+    for at in range(1, row_bits):
+        last = one.row_step(at, last)
+    last = two.row_step(0, last)
 
     slots = jnp.transpose(lookup_slots, (0, 2, 1))
     shares = []
@@ -555,64 +560,51 @@
             functools.partial(count_kernel, n_row, table, hot, n_z),
             out_shape=wide(n_row, u_shard, width),
             grid=(n_row,),
-            in_specs=[smem] + [vmem] * (2 + n_z) + [anywhere],
+            in_specs=[vmem] * (2 + n_z) + [anywhere],
             out_specs=pl.BlockSpec((1, u_shard, width), lambda at: (at, 0, 0)),
             compiler_params=pltpu.CompilerParams(vmem_limit_bytes=16 * MIB),
-            cost_estimate=cost(6),
+            cost_estimate=no_cost(),
             name="counts",
-        )(pos, slots, *values, last[0])
+        )(slots, *values, last[0])
+        shares.append(Halving([sums], high_first if table % 2 else low_first))
         last = [sums]
-        shares.append(Halving([sums], high_first if table % 2 else low_first))
         if table == 0:
-            for stage in range(1, z_bits):
-                last = one.z_step(stage, last)
-            for at in range(1, row_bits):
-                last = two.row_step(at, last)
+            last = one.z_step(0, last)
+    for at in range(1, row_bits):
+        last = two.row_step(at, last)
+    for stage in range(1, z_bits):
+        last = one.z_step(stage, last)
     for share in shares:
         share.step(0, last)
+    last = two.z_step(0, last)
     last = one.z_back(last)
-    last = two.z_step(0, last)
     for share in shares:
         for at in range(1, row_bits):
             share.step(at, last)
-    row_grads = jnp.stack([share.total() for share in shares])
     for stage in range(1, z_bits):
         last = two.z_step(stage, last)
-    two.z_back(last)
-
-    g_down, g_up, g_first, g_second, g_small = call(
+    for share in shares:
+        share.tie(last)
+    row_grads = jnp.stack([share.total() for share in shares])
+    two.z_back([row_grads])
+
+    g_down, g_up, g_first, g_second, g_cbias, g_bias1, g_bias2, g_logit = call(
         unpack_kernel,
         [
             jax.ShapeDtypeStruct((feat // n_row, rank), f32),
             jax.ShapeDtypeStruct((rank // n_row, feat), f32),
             jax.ShapeDtypeStruct((feat // n_row, hid), f32),
             jax.ShapeDtypeStruct((hid // n_row, hid), f32),
-            jax.ShapeDtypeStruct((48, LANES), f32),
-        ],
-        [pltpu.VMEM((2, rows, LANES), bf16) for rows in (rows_front, rows_back)],
-        [smem] + [vmem] * 8,
+            jax.ShapeDtypeStruct((feat // n_row,), f32),
+        ]
+        + [jax.ShapeDtypeStruct((hid // n_row,), f32)] * 3,
+        [pltpu.VMEM((2, rows, LANES), bf16) for rows in (rows_front, rows_back)]
+        + [pltpu.VMEM((56, LANES), f32)],
+        [vmem] * 8,
         "unpack",
-        4,
         24,
-    )(pos, *one.pieces, *two.pieces)
-
-    flat = g_small.reshape(-1)
-
-    def part(start, length):
-        share = length // n_row
-        return lax.dynamic_slice(flat, (start * LANES + row_pos * share,), (share,))
-
-    return (
-        row_grads,
-        g_down,
-        g_up,
-        part(24, feat),
-        g_first,
-        part(0, hid),
-        g_second,
-        part(8, hid),
-        part(16, hid),
-    )
+    )(*one.pieces, *two.pieces)
+    return (row_grads, g_down, g_up, g_cbias, g_first, g_bias1, g_second, g_bias2, g_logit)
 
 
 def solution(mesh):

time: 142 us -> 134 us (0.944)
  other arithmetic: 15 us -> 6.09 us
  local copies, waits for them, and re-layouts: 4.74 us -> 8.64 us
  Pallas kernels: 36.3 us -> 33 us
  starting transfers between devices: 36.8 us -> 39 us
  waiting for transfers between devices: 47.4 us -> 45.8 us
    ppermute x12, waiting for transfers between devices: 9.22 us -> 0.59 us  [swap_row(): lax.ppermute(value, 'row', [(at, at ^ 1 << bit) for at in range(n_row)])]
    ppermute x11, waiting for transfers between devices: 37.6 us -> 43.7 us  [swap_z(): lax.ppermute(value, 'table', [(at, at ^ 2 * which) for at in range(n_tabl...]
    squeeze x2 -> x15, local copies, waits for them, and re-layouts: 0.04 us -> 5.08 us  [index_of(): return lambda array: lax.index_in_dim(array, index, axis, keepdims=False)]
    convert_element_type x9 -> x10, other arithmetic: 6.58 us -> 3.38 us  [step(): sent = self.total(index_of(1, axis)).astype(bf16)]
    pallas_call x2, Pallas kernels: 17.5 us -> 14.5 us  [the longest x1 11.9 us: local(): call(front_kernel, [packed(rows_front)] * 2 + [wide(feat, batch), wide(ba...]
    slice x0 -> x2, local copies, waits for them, and re-layouts: none -> 2.95 us  [index_of(): return lambda array: lax.index_in_dim(array, index, axis, keepdims=False)]
    unnamed x42 -> x28, local copies, waits for them, and re-layouts: 3.39 us -> 0.62 us
    ppermute x11, starting transfers between devices: 20.5 us -> 23 us  [swap_z(): lax.ppermute(value, 'table', [(at, at ^ 2 * which) for at in range(n_tabl...]
  transfers between devices with their start and end apart: 32 -> 30, of which waited for: 10 -> 10; matrix products, arithmetic and copies ran while one was open for 10% -> 8% of each run, Pallas kernels for 14% -> 12%
where the time goes in v5:
time: 134 us
  waiting for transfers between devices  45.8 us (34%)
  starting transfers between devices  39 us (29%)
  Pallas kernels  33 us (25%)
  local copies, waits for them, and re-layouts  8.64 us (6%)
  other arithmetic  6.09 us (5%)
    ppermute x11, waiting for transfers between devices, swap_z(): lax.ppermute(value, 'table', [(at, at ^ 2 * which) for at in range(n_tabl...  43.7 us
    ppermute x11, starting transfers between devices, swap_z(): lax.ppermute(value, 'table', [(at, at ^ 2 * which) for at in range(n_tabl...  23 us
    ppermute x12, starting transfers between devices, swap_row(): lax.ppermute(value, 'row', [(at, at ^ 1 << bit) for at in range(n_row)])  14.6 us
    pallas_call x1, Pallas kernels, local(): call(front_kernel, [packed(rows_front)] * 2 + [wide(feat, batch), wide(ba...  11.9 us
    pallas_call x1, Pallas kernels, local(): call(functools.partial(middle_kernel, n_z), [wide(batch, feat), wide(batc...  8.21 us
    pallas_call x2, Pallas kernels, local(): pl.pallas_call(functools.partial(count_kernel, n_row, table, hot, n_z), o...  8.03 us
    squeeze x15, local copies, waits for them, and re-layouts, index_of(): return lambda array: lax.index_in_dim(array, index, axis, keepdims=False)  5.08 us
    convert_element_type x10, other arithmetic, step(): sent = self.total(index_of(1, axis)).astype(bf16)  3.38 us
  transfers between devices with their start and end apart: 30, of which 10 were waited for; matrix products, arithmetic and copies ran while one was open for 8% of the time, Pallas kernels for 12%

profile of v5, /device:TPU:0, one launch (start us, length us, event | category | flops | bytes accessed | tf_op | source)
XLA Modules:
  0.0 133.6 jit_solution(83164892689604682)
XLA Ops:
  0.6 11.9 %front.1 = (bf16[2,4,2,672,128]{4,3,2,1,0:T(8,128)(2,1)}, bf16[2,4,2,672,128]{4,3,2,1,0:T(8,128)(2,1)}, bf16[2176,256]{1,0:T(8,128)(2,1)}, bf16[256,1024]{1,0:T(8,128)(2,1)}, f32[24,128]{1,0:T(8,128)}) custom-call(bf16[256,128]{1,0:T(8,128)(2,1)} %refs_0_.5, bf16[256,2048]{1,0:T(8,128)(2,1)} %refs_1_.5, bf16[2176,256]{1,0:T(8,128)(2,1)} %refs_2_.5, ...), custom_call_target="tpu_custom_call" | custom-call | tf_op jit(solution)/shard_map/front/pallas_call | solution.py:400
  12.5 0.5 collective-permute-start.3
  13.0 1.4 %slice.364 = bf16[1,4,2,672,128]{4,3,2,1,0:T(8,128)(2,1)S(1)} slice(bf16[2,4,2,672,128]{4,3,2,1,0:T(8,128)(2,1)} %get-tuple-element.95), slice={[0:1], [0:4], [0:2], [0:672], [0:128]} | slice | bytes 2752512 | tf_op jit(solution)/shard_map/slice | solution.py:455
  14.5 8.2 %middle.1 = (bf16[256,2176]{1,0:T(8,128)(2,1)}, bf16[256,256]{1,0:T(8,128)(2,1)}, bf16[2,2,256,128]{3,2,1,0:T(8,128)(2,1)}, bf16[2,2,256,128]{3,2,1,0:T(8,128)(2...) custom-call(bf16[256,128]{1,0:T(8,128)(2,1)} %refs_0_.5, bf16[256,2048]{1,0:T(8,128)(2,1)} %refs_1_.5, ...), custom_call_target="tpu_custom_call" | custom-call | tf_op jit(solution)/shard_map/middle/pallas_call | solution.py:417
  22.7 1.5 %slice.437 = bf16[1,4,2,672,128]{4,3,2,1,0:T(8,128)(2,1)S(1)} slice(bf16[2,4,2,672,128]{4,3,2,1,0:T(8,128)(2,1)} %collective-permute-done.3), slice={[0:1], [0:4], [0:2], [0:672], [0:128]} | slice | bytes 2752512 | tf_op jit(solution)/shard_map/slice | solution.py:455
  24.5 1.4 %fusion.1.refs_9_ = bf16[2,2,672,128]{3,2,1,0:T(8,128)(2,1)S(1)} fusion(bf16[2,4,2,672,128]{4,3,2,1,0:T(8,128)(2,1)} %collective-permute-done.3, bf16[2,4,2,672,128]{4,3,2,1,0:T(8,128)(2,1)S(1)} %copy-done.10), kind=kLoop, calls=%fused_computation.19 | loop fusion | flops 1376256 | bytes 2064384 | tf_op jit(solution)/shard_map/convert_element_type | solution.py:479
  26.2 0.4 copy-done.4
  26.6 2.6 %back.1 = (bf16[2,4,2,432,128]{4,3,2,1,0:T(8,128)(2,1)S(1)}, bf16[2,4,2,432,128]{4,3,2,1,0:T(8,128)(2,1)S(1)}) custom-call(bf16[256,128]{1,0:T(8,128)(2,1)S(1)} %copy-done.7, bf16[256,2048]{1,0:T(8,128)(2,1)S(1)} %copy-done.1, bf16[2176,256]{1,0:T(8,128)(2,1)S(1)} %copy-done, bf16[2176,256]{1,0:T(8,128)(2,1)S(1)} %copy-done.4, ...), custom_call_target="tpu_custom_call" | custom-call | tf_op jit(solution)/shard_map/back/pallas_call | solution.py:518
  29.3 2.9 %collective-permute-start.6 = (bf16[2,2,672,128]{3,2,1,0:T(8,128)(2,1)S(1)}, bf16[2,2,672,128]{3,2,1,0:T(8,128)(2,1)S(1)}, u32[]{:S(2)}, u32[]{:S(2)}) collective-permute-start(bf16[2,2,672,128]{3,2,1,0:T(8,128)(2,1)S(1)} %fusion.refs_8_), channel_id=1, source_target_pairs={{0,1},{1,0},{2,3},{3,2},{4,5},{5,4},{6,7},{7,6},{8,9},{9,8},{10,11... | collective-permute-start | bytes 2064392 | tf_op jit(solution)/shard_map/ppermute | solution.py:368
  32.3 1.5 %collective-permute-start.7 = (bf16[2,2,672,128]{3,2,1,0:T(8,128)(2,1)S(1)}, bf16[2,2,672,128]{3,2,1,0:T(8,128)(2,1)S(1)}, u32[]{:S(2)}, u32[]{:S(2)}) collective-permute-start(bf16[2,2,672,128]{3,2,1,0:T(8,128)(2,1)S(1)} %fusion.1.refs_9_), channel_id=1, source_target_pairs={{0,2},{1,3},{2,0},{3,1},{4,6},{5,7},{6,4},{7,5},{8,10},{9,11},{10,... | collective-permute-start | bytes 2064392 | tf_op jit(solution)/shard_map/ppermute | solution.py:368
  33.8 1.6 %collective-permute-start = (bf16[2,2,256,128]{3,2,1,0:T(8,128)(2,1)S(1)}, bf16[2,2,256,128]{3,2,1,0:T(8,128)(2,1)S(1)}, u32[]{:S(2)}, u32[]{:S(2)}) collective-permute-start(bf16[2,2,256,128]{3,2,1,0:T(8,128)(2,1)S(1)} %copy-done.13), channel_id=1, source_target_pairs={{0,8},{4,12},{8,0},{12,4},{16,24},{20,28},{24,16},{28,20},{1,9},{5... | collective-permute-start | bytes 786440 | tf_op jit(solution)/shard_map/ppermute | solution.py:365
  35.4 2.6 %collective-permute-start.1 = (bf16[2,2,256,128]{3,2,1,0:T(8,128)(2,1)S(1)}, bf16[2,2,256,128]{3,2,1,0:T(8,128)(2,1)S(1)}, u32[]{:S(2)}, u32[]{:S(2)}) collective-permute-start(bf16[2,2,256,128]{3,2,1,0:T(8,128)(2,1)S(1)} %copy-done.12), channel_id=1, source_target_pairs={{0,16},{4,20},{8,24},{12,28},{16,0},{20,4},{24,8},{28,12},{1,17},{... | collective-permute-start | bytes 786440 | tf_op jit(solution)/shard_map/ppermute | solution.py:365
  38.0 9.1 %collective-permute-done.refs_1_.rest_1_ = bf16[2,2,256,128]{3,2,1,0:T(8,128)(2,1)S(1)} collective-permute-done((bf16[2,2,256,128]{3,2,1,0:T(8,128)(2,1)S(1)}, bf16[2,2,256,128]{3,2,1,0:T(8,128)(2,1)S(1)}, u32[]{:S(2)}, u32[]{:S(2)}) %collective-permute-start) | collective-permute-done | bytes 262176 | tf_op jit(solution)/shard_map/ppermute | solution.py:365
  47.0 2.4 %collective-permute-start.2 = (bf16[2,2,256,128]{3,2,1,0:T(8,128)(2,1)S(1)}, bf16[2,2,256,128]{3,2,1,0:T(8,128)(2,1)S(1)}, u32[]{:S(2)}, u32[]{:S(2)}) collective-permute-start(bf16[2,2,256,128]{3,2,1,0:T(8,128)(2,1)S(1)} %copy-done.11), channel_id=1, source_target_pairs={{0,24},{4,28},{8,16},{12,20},{16,8},{20,12},{24,0},{28,4},{1,25},{... | collective-permute-start | bytes 786440 | tf_op jit(solution)/shard_map/ppermute | solution.py:365
  49.5 6.3 %collective-permute-done.2.refs_3_.rest_3_ = bf16[2,2,256,128]{3,2,1,0:T(8,128)(2,1)S(1)} collective-permute-done((bf16[2,2,256,128]{3,2,1,0:T(8,128)(2,1)S(1)}, bf16[2,2,256,128]{3,2,1,0:T(8,128)(2,1)S(1)}, u32[]{:S(2)}, u32[]{:S(2)}) %collective-permute-start.2) | collective-permute-done | bytes 262176 | tf_op jit(solution)/shard_map/ppermute | solution.py:365
  55.9 1.1 fusion.4
  57.0 0.6 collective-permute-start.9
  57.6 1.5 %slice_bitcast_fusion.4 = (bf16[2,2,2,672,128]{4,3,2,1,0:T(8,128)(2,1)S(1)}, bf16[2,2,2,672,128]{4,3,2,1,0:T(8,128)(2,1)S(1)}) fusion(bf16[2,2,2,2,672,128]{5,4,3,2,1,0:T(8,128)(2,1)} %bitcast.8, bf16[2,2,2,2,672,128]{5,4,3,2,1,0:T(8,128)(2,1)S(1)} %bitcast.151), kind=kLoop, calls=%fused_computation.4 | loop fusion | bytes 5505024 | tf_op jit(solution)/shard_map/squeeze | solution.py:455
  59.6 0.7 collective-permute-start.12
  60.4 1.4 %collective-permute-start.11 = (bf16[2,2,432,128]{3,2,1,0:T(8,128)(2,1)S(1)}, bf16[2,2,432,128]{3,2,1,0:T(8,128)(2,1)S(1)}, u32[]{:S(2)}, u32[]{:S(2)}) collective-permute-start(bf16[2,2,432,128]{3,2,1,0:T(8,128)(2,1)S(1)} %fusion.6.rest_5_), channel_id=1, source_target_pairs={{0,1},{1,0},{2,3},{3,2},{4,5},{5,4},{6,7},{7,6},{8,9},{9,8},{10,11... | collective-permute-start | bytes 1327112 | tf_op jit(solution)/shard_map/ppermute | solution.py:368
  61.8 1.6 %collective-permute-start.8 = (bf16[2,672,128]{2,1,0:T(8,128)(2,1)S(1)}, bf16[2,672,128]{2,1,0:T(8,128)(2,1)S(1)}, u32[]{:S(2)}, u32[]{:S(2)}) collective-permute-start(bf16[2,672,128]{2,1,0:T(8,128)(2,1)S(1)} %fusion.5), channel_id=1, source_target_pairs={{0,2},{1,3},{2,0},{3,1},{4,6},{5,7},{6,4},{7,5},{8,10},{9,11},{10,... | collective-permute-start | bytes 1032200 | tf_op jit(solution)/shard_map/ppermute | solution.py:368
  63.4 4.0 %counts.2 = bf16[4,512,128]{2,1,0:T(8,128)(2,1)S(1)} custom-call(s32[2,4,8192]{2,1,0:T(4,128)S(1)} %bitcast.148, bf16[2,2,256,128]{3,2,1,0:T(8,128)(2,1)S(1)} %copy-done.2, bf16[2,2,256,128]{3,2,1,0:T(8,128)(2,1)S(1)} %collective-permute-done.refs_1_.rest_1_, bf16[2,2,256,128]{3,2,1,0:T(8,128)(2,1)S(1)} %collective-permute-done.1.refs_2_.rest_2_, ...), custom_call_target="tpu_custom_call" | custom-call | tf_op jit(solution)/shard_map/counts/pallas_call | solution.py:559
  67.4 0.6 collective-permute-done.9
  68.0 1.2 fusion.3.rest_5_
  69.1 5.5 %collective-permute-start.10 = (bf16[2,672,128]{2,1,0:T(8,128)(2,1)S(1)}, bf16[2,672,128]{2,1,0:T(8,128)(2,1)S(1)}, u32[]{:S(2)}, u32[]{:S(2)}) collective-permute-start(bf16[2,672,128]{2,1,0:T(8,128)(2,1)S(1)} %fusion.3.rest_5_), channel_id=1, source_target_pairs={{0,8},{4,12},{8,0},{12,4},{16,24},{20,28},{24,16},{28,20},{1,9},{5... | collective-permute-start | bytes 1032200 | tf_op jit(solution)/shard_map/ppermute | solution.py:365
  74.6 4.0 %counts.3 = bf16[4,512,128]{2,1,0:T(8,128)(2,1)S(1)} custom-call(s32[2,4,8192]{2,1,0:T(4,128)S(1)} %bitcast.149, bf16[2,2,256,128]{3,2,1,0:T(8,128)(2,1)S(1)} %copy-done.2, bf16[2,2,256,128]{3,2,1,0:T(8,128)(2,1)S(1)} %collective-permute-done.refs_1_.rest_1_, bf16[2,2,256,128]{3,2,1,0:T(8,128)(2,1)S(1)} %collective-permute-done.1.refs_2_.rest_2_, ...), custom_call_target="tpu_custom_call" | custom-call | tf_op jit(solution)/shard_map/counts/pallas_call | solution.py:559
  78.9 0.6 collective-permute-start.15
  79.6 0.6 collective-permute-start.17
  80.2 1.9 %collective-permute-done.10 = bf16[2,672,128]{2,1,0:T(8,128)(2,1)S(1)} collective-permute-done((bf16[2,672,128]{2,1,0:T(8,128)(2,1)S(1)}, bf16[2,672,128]{2,1,0:T(8,128)(2,1)S(1)}, u32[]{:S(2)}, u32[]{:S(2)}) %collective-permute-start.10) | collective-permute-done | bytes 344096 | tf_op jit(solution)/shard_map/ppermute | solution.py:365
  82.1 1.4 %slice_bitcast_fusion.2 = bf16[2,2,2,672,128]{4,3,2,1,0:T(8,128)(2,1)S(1)} fusion(bf16[2,2,2,2,672,128]{5,4,3,2,1,0:T(8,128)(2,1)} %bitcast.8), kind=kLoop, calls=%fused_computation.2 | loop fusion | bytes 2752512 | tf_op jit(solution)/shard_map/squeeze | solution.py:455
  83.7 3.7 %collective-permute-start.14 = (bf16[1,672,128]{2,1,0:T(8,128)(2,1)S(1)}, bf16[1,672,128]{2,1,0:T(8,128)(2,1)S(1)}, u32[]{:S(2)}, u32[]{:S(2)}) collective-permute-start(bf16[1,672,128]{2,1,0:T(8,128)(2,1)S(1)} %fusion.18), channel_id=1, source_target_pairs={{0,16},{4,20},{8,24},{12,28},{16,0},{20,4},{24,8},{28,12},{1,17},{... | collective-permute-start | bytes 516104 | tf_op jit(solution)/shard_map/ppermute | solution.py:365
  87.5 1.6 %collective-permute-start.13 = (bf16[2,512,128]{2,1,0:T(8,128)(2,1)S(1)}, bf16[2,512,128]{2,1,0:T(8,128)(2,1)S(1)}, u32[]{:S(2)}, u32[]{:S(2)}) collective-permute-start(bf16[2,512,128]{2,1,0:T(8,128)(2,1)S(1)} %slice_bitcast_fusion.17), channel_id=1, source_target_pairs={{0,1},{1,0},{2,3},{3,2},{4,5},{5,4},{6,7},{7,6},{8,9},{9,8},{10,11... | collective-permute-start | bytes 786440 | tf_op jit(solution)/shard_map/ppermute | solution.py:368
  89.1 0.8 collective-permute-start.19
  90.0 1.1 collective-permute-start.18
  91.1 4.1 %collective-permute-done.14 = bf16[1,672,128]{2,1,0:T(8,128)(2,1)S(1)} collective-permute-done((bf16[1,672,128]{2,1,0:T(8,128)(2,1)S(1)}, bf16[1,672,128]{2,1,0:T(8,128)(2,1)S(1)}, u32[]{:S(2)}, u32[]{:S(2)}) %collective-permute-start.14) | collective-permute-done | bytes 172064 | tf_op jit(solution)/shard_map/ppermute | solution.py:365
  95.2 1.4 %slice_bitcast_fusion = bf16[2,2,2,672,128]{4,3,2,1,0:T(8,128)(2,1)S(1)} fusion(bf16[2,2,2,2,672,128]{5,4,3,2,1,0:T(8,128)(2,1)} %bitcast.8), kind=kLoop, calls=%fused_computation | loop fusion | bytes 2752512 | tf_op jit(solution)/shard_map/squeeze | solution.py:455
  96.9 0.6 collective-permute-start.21
  97.6 2.3 %collective-permute-start.20 = (bf16[512,128]{1,0:T(8,128)(2,1)S(1)}, bf16[512,128]{1,0:T(8,128)(2,1)S(1)}, u32[]{:S(2)}, u32[]{:S(2)}) collective-permute-start(bf16[512,128]{1,0:T(8,128)(2,1)S(1)} %fusion.21), channel_id=1, source_target_pairs={{0,1},{1,0},{2,3},{3,2},{4,5},{5,4},{6,7},{7,6},{8,9},{9,8},{10,11... | collective-permute-start | bytes 393224 | tf_op jit(solution)/shard_map/ppermute | solution.py:368
  99.9 5.0 %collective-permute-done.21 = bf16[1,672,128]{2,1,0:T(8,128)(2,1)S(1)} collective-permute-done((bf16[1,672,128]{2,1,0:T(8,128)(2,1)S(1)}, bf16[1,672,128]{2,1,0:T(8,128)(2,1)S(1)}, u32[]{:S(2)}, u32[]{:S(2)}) %collective-permute-start.21) | collective-permute-done | bytes 172064 | tf_op jit(solution)/shard_map/ppermute | solution.py:365
  105.2 1.9 %collective-permute-start.25 = (bf16[1,432,128]{2,1,0:T(8,128)(2,1)S(1)}, bf16[1,432,128]{2,1,0:T(8,128)(2,1)S(1)}, u32[]{:S(2)}, u32[]{:S(2)}) collective-permute-start(bf16[1,432,128]{2,1,0:T(8,128)(2,1)S(1)} %fusion.31), channel_id=1, source_target_pairs={{0,16},{4,20},{8,24},{12,28},{16,0},{20,4},{24,8},{28,12},{1,17},{... | collective-permute-start | bytes 331784 | tf_op jit(solution)/shard_map/ppermute | solution.py:365
  107.2 0.8 pad_maximum_fusion
  108.0 7.0 %collective-permute-done.25 = bf16[1,432,128]{2,1,0:T(8,128)(2,1)S(1)} collective-permute-done((bf16[1,432,128]{2,1,0:T(8,128)(2,1)S(1)}, bf16[1,432,128]{2,1,0:T(8,128)(2,1)S(1)}, u32[]{:S(2)}, u32[]{:S(2)}) %collective-permute-start.25) | collective-permute-done | bytes 110624 | tf_op jit(solution)/shard_map/ppermute | solution.py:365
  115.2 3.5 %collective-permute-start.26 = (bf16[1,432,128]{2,1,0:T(8,128)(2,1)S(1)}, bf16[1,432,128]{2,1,0:T(8,128)(2,1)S(1)}, u32[]{:S(2)}, u32[]{:S(2)}) collective-permute-start(bf16[1,432,128]{2,1,0:T(8,128)(2,1)S(1)} %fusion.28), channel_id=1, source_target_pairs={{0,16},{4,20},{8,24},{12,28},{16,0},{20,4},{24,8},{28,12},{1,17},{... | collective-permute-start | bytes 331784 | tf_op jit(solution)/shard_map/ppermute | solution.py:365
  118.7 4.4 %collective-permute-done.26 = bf16[1,432,128]{2,1,0:T(8,128)(2,1)S(1)} collective-permute-done((bf16[1,432,128]{2,1,0:T(8,128)(2,1)S(1)}, bf16[1,432,128]{2,1,0:T(8,128)(2,1)S(1)}, u32[]{:S(2)}, u32[]{:S(2)}) %collective-permute-start.26) | collective-permute-done | bytes 110624 | tf_op jit(solution)/shard_map/ppermute | solution.py:365
  123.3 0.5 collective-permute-start.24
  123.9 6.0 %collective-permute-done.27.refs_5_ = bf16[2,432,128]{2,1,0:T(8,128)(2,1)S(1)} collective-permute-done((bf16[2,432,128]{2,1,0:T(8,128)(2,1)S(1)}, bf16[2,432,128]{2,1,0:T(8,128)(2,1)S(1)}, u32[]{:S(2)}, u32[]{:S(2)}) %collective-permute-start.27) | collective-permute-done | bytes 221216 | tf_op jit(solution)/shard_map/ppermute | solution.py:365
  129.9 1.5 %collective-permute-done.29.refs_7_ = bf16[2,432,128]{2,1,0:T(8,128)(2,1)S(1)} collective-permute-done((bf16[2,432,128]{2,1,0:T(8,128)(2,1)S(1)}, bf16[2,432,128]{2,1,0:T(8,128)(2,1)S(1)}, u32[]{:S(2)}, u32[]{:S(2)}) %collective-permute-start.29) | collective-permute-done | bytes 221216 | tf_op jit(solution)/shard_map/ppermute | solution.py:362
  131.4 2.2 %unpack.1 = (f32[544,256]{1,0:T(8,128)}, f32[64,2176]{1,0:T(8,128)}, f32[544,1024]{1,0:T(8,128)}, f32[256,1024]{1,0:T(8,128)}, f32[544]{0:T(1024)}, /*index=5*/f32[256]{0:T(256)}, f32[256]{0:T(256)}, f32[256]{0:T(256)}) custom-call(bf16[2,672,128]{2,1,0:T(8,128)(2,1)S(1)} %pad_maximum_fusion.1.refs_0_, ...), custom_call_target="tpu_custom_call" | custom-call | tf_op jit(solution)/shard_map/unpack/pallas_call | solution.py:591
  (85 shorter events, 3.2 us)
Async XLA Ops:
  12.5 10.2 %collective-permute-start.3 = (bf16[2,4,2,672,128]{4,3,2,1,0:T(8,128)(2,1)}, bf16[2,4,2,672,128]{4,3,2,1,0:T(8,128)(2,1)}, u32[]{:S(2)}, u32[]{:S(2)}) collective-permute-start(bf16[2,4,2,672,128]{4,3,2,1,0:T(8,128)(2,1)} %get-tuple-element.96), channel_id=1, source_target_pairs={{0,4},{4,0},{8,12},{12,8},{16,20},{20,16},{24,28},{28,24},{1,5},{5... | collective-permute-start | bytes 8257544 | tf_op jit(solution)/shard_map/ppermute | solution.py:362
  14.5 10.0 %copy-start.10 = (bf16[2,4,2,672,128]{4,3,2,1,0:T(8,128)(2,1)S(1)}, bf16[2,4,2,672,128]{4,3,2,1,0:T(8,128)(2,1)}, u32[]{:S(2)}) copy-start(bf16[2,4,2,672,128]{4,3,2,1,0:T(8,128)(2,1)} %get-tuple-element.95) | copy-start | bytes 8257540
  22.7 3.3 %copy-start.5 = (bf16[256,2176]{1,0:T(8,128)(2,1)S(1)}, bf16[256,2176]{1,0:T(8,128)(2,1)}, u32[]{:S(2)}) copy-start(bf16[256,2176]{1,0:T(8,128)(2,1)} %get-tuple-element.92.refs_5_) | copy-start | bytes 3342340
  24.2 1.7 %copy-start = (bf16[2176,256]{1,0:T(8,128)(2,1)S(1)}, bf16[2176,256]{1,0:T(8,128)(2,1)}, u32[]{:S(2)}) copy-start(bf16[2176,256]{1,0:T(8,128)(2,1)} %refs_2_.5) | copy-start | bytes 3342340
  24.3 1.8 %copy-start.1 = (bf16[256,2048]{1,0:T(8,128)(2,1)S(1)}, bf16[256,2048]{1,0:T(8,128)(2,1)}, u32[]{:S(2)}) copy-start(bf16[256,2048]{1,0:T(8,128)(2,1)} %refs_1_.5) | copy-start | bytes 3145732
  24.3 1.9 %copy-start.3 = (bf16[256,1024]{1,0:T(8,128)(2,1)S(1)}, bf16[256,1024]{1,0:T(8,128)(2,1)}, u32[]{:S(2)}) copy-start(bf16[256,1024]{1,0:T(8,128)(2,1)} %get-tuple-element.86.refs_6_.refs_4_) | copy-start | bytes 1572868
  24.3 2.3 %copy-start.4 = (bf16[2176,256]{1,0:T(8,128)(2,1)S(1)}, bf16[2176,256]{1,0:T(8,128)(2,1)}, u32[]{:S(2)}) copy-start(bf16[2176,256]{1,0:T(8,128)(2,1)} %get-tuple-element.91.refs_3_) | copy-start | bytes 3342340
  24.3 2.2 %copy-start.7 = (bf16[256,128]{1,0:T(8,128)(2,1)S(1)}, bf16[256,128]{1,0:T(8,128)(2,1)}, u32[]{:S(2)}) copy-start(bf16[256,128]{1,0:T(8,128)(2,1)} %refs_0_.5) | copy-start | bytes 196612
  24.3 2.2 %copy-start.8 = (bf16[256,256]{1,0:T(8,128)(2,1)S(1)}, bf16[256,256]{1,0:T(8,128)(2,1)}, u32[]{:S(2)}) copy-start(bf16[256,256]{1,0:T(8,128)(2,1)} %get-tuple-element.93.refs_6_) | copy-start | bytes 393220
  24.3 2.2 %copy-start.9 = (f32[24,128]{1,0:T(8,128)S(1)}, f32[24,128]{1,0:T(8,128)}, u32[]{:S(2)}) copy-start(f32[24,128]{1,0:T(8,128)} %get-tuple-element.94.refs_7_) | copy-start | bytes 36868
  26.5 7.3 %copy-start.13 = (bf16[2,2,256,128]{3,2,1,0:T(8,128)(2,1)S(1)}, bf16[2,2,256,128]{3,2,1,0:T(8,128)(2,1)}, u32[]{:S(2)}) copy-start(bf16[2,2,256,128]{3,2,1,0:T(8,128)(2,1)} %get-tuple-element.88) | copy-start | bytes 786436
  26.5 8.8 %copy-start.12 = (bf16[2,2,256,128]{3,2,1,0:T(8,128)(2,1)S(1)}, bf16[2,2,256,128]{3,2,1,0:T(8,128)(2,1)}, u32[]{:S(2)}) copy-start(bf16[2,2,256,128]{3,2,1,0:T(8,128)(2,1)} %get-tuple-element.89) | copy-start | bytes 786436
  26.6 20.5 %copy-start.11 = (bf16[2,2,256,128]{3,2,1,0:T(8,128)(2,1)S(1)}, bf16[2,2,256,128]{3,2,1,0:T(8,128)(2,1)}, u32[]{:S(2)}) copy-start(bf16[2,2,256,128]{3,2,1,0:T(8,128)(2,1)} %get-tuple-element.90) | copy-start | bytes 786436
  26.6 29.2 %copy-start.2 = (bf16[2,2,256,128]{3,2,1,0:T(8,128)(2,1)S(1)}, bf16[2,2,256,128]{3,2,1,0:T(8,128)(2,1)}, u32[]{:S(2)}) copy-start(bf16[2,2,256,128]{3,2,1,0:T(8,128)(2,1)} %get-tuple-element.87.refs_0_.rest_0_) | copy-start | bytes 786436
  29.2 30.1 %collective-permute-start.5 = (bf16[2,4,2,432,128]{4,3,2,1,0:T(8,128)(2,1)S(1)}, bf16[2,4,2,432,128]{4,3,2,1,0:T(8,128)(2,1)S(1)}, u32[]{:S(2)}, u32[]{:S(2)}) collective-permute-start(bf16[2,4,2,432,128]{4,3,2,1,0:T(8,128)(2,1)S(1)} %get-tuple-element.98), channel_id=1, source_target_pairs={{0,4},{4,0},{8,12},{12,8},{16,20},{20,16},{24,28},{28,24},{1,5},{5... | collective-permute-start | bytes 5308424 | tf_op jit(solution)/shard_map/ppermute | solution.py:362
  29.3 26.6 %collective-permute-start.6 = (bf16[2,2,672,128]{3,2,1,0:T(8,128)(2,1)S(1)}, bf16[2,2,672,128]{3,2,1,0:T(8,128)(2,1)S(1)}, u32[]{:S(2)}, u32[]{:S(2)}) collective-permute-start(bf16[2,2,672,128]{3,2,1,0:T(8,128)(2,1)S(1)} %fusion.refs_8_), channel_id=1, source_target_pairs={{0,1},{1,0},{2,3},{3,2},{4,5},{5,4},{6,7},{7,6},{8,9},{9,8},{10,11... | collective-permute-start | bytes 2064392 | tf_op jit(solution)/shard_map/ppermute | solution.py:368
  32.3 23.6 %collective-permute-start.7 = (bf16[2,2,672,128]{3,2,1,0:T(8,128)(2,1)S(1)}, bf16[2,2,672,128]{3,2,1,0:T(8,128)(2,1)S(1)}, u32[]{:S(2)}, u32[]{:S(2)}) collective-permute-start(bf16[2,2,672,128]{3,2,1,0:T(8,128)(2,1)S(1)} %fusion.1.refs_9_), channel_id=1, source_target_pairs={{0,2},{1,3},{2,0},{3,1},{4,6},{5,7},{6,4},{7,5},{8,10},{9,11},{10,... | collective-permute-start | bytes 2064392 | tf_op jit(solution)/shard_map/ppermute | solution.py:368
  33.8 13.2 %collective-permute-start = (bf16[2,2,256,128]{3,2,1,0:T(8,128)(2,1)S(1)}, bf16[2,2,256,128]{3,2,1,0:T(8,128)(2,1)S(1)}, u32[]{:S(2)}, u32[]{:S(2)}) collective-permute-start(bf16[2,2,256,128]{3,2,1,0:T(8,128)(2,1)S(1)} %copy-done.13), channel_id=1, source_target_pairs={{0,8},{4,12},{8,0},{12,4},{16,24},{20,28},{24,16},{28,20},{1,9},{5... | collective-permute-start | bytes 786440 | tf_op jit(solution)/shard_map/ppermute | solution.py:365
  35.4 14.1 %collective-permute-start.1 = (bf16[2,2,256,128]{3,2,1,0:T(8,128)(2,1)S(1)}, bf16[2,2,256,128]{3,2,1,0:T(8,128)(2,1)S(1)}, u32[]{:S(2)}, u32[]{:S(2)}) collective-permute-start(bf16[2,2,256,128]{3,2,1,0:T(8,128)(2,1)S(1)} %copy-done.12), channel_id=1, source_target_pairs={{0,16},{4,20},{8,24},{12,28},{16,0},{20,4},{24,8},{28,12},{1,17},{... | collective-permute-start | bytes 786440 | tf_op jit(solution)/shard_map/ppermute | solution.py:365
  47.0 8.7 %collective-permute-start.2 = (bf16[2,2,256,128]{3,2,1,0:T(8,128)(2,1)S(1)}, bf16[2,2,256,128]{3,2,1,0:T(8,128)(2,1)S(1)}, u32[]{:S(2)}, u32[]{:S(2)}) collective-permute-start(bf16[2,2,256,128]{3,2,1,0:T(8,128)(2,1)S(1)} %copy-done.11), channel_id=1, source_target_pairs={{0,24},{4,28},{8,16},{12,20},{16,8},{20,12},{24,0},{28,4},{1,25},{... | collective-permute-start | bytes 786440 | tf_op jit(solution)/shard_map/ppermute | solution.py:365
  55.8 7.6 %collective-permute-start.4 = (bf16[4,2,256,128]{3,2,1,0:T(8,128)(2,1)S(1)}, bf16[4,2,256,128]{3,2,1,0:T(8,128)(2,1)S(1)}, u32[]{:S(2)}, u32[]{:S(2)}) collective-permute-start(bf16[4,2,256,128]{3,2,1,0:T(8,128)(2,1)S(1)} %select.1), channel_id=1, source_target_pairs={{0,4},{4,0},{8,12},{12,8},{16,20},{20,16},{24,28},{28,24},{1,5},{5... | collective-permute-start | bytes 1572872 | tf_op jit(solution)/shard_map/ppermute | solution.py:362
  57.0 10.9 %collective-permute-start.9 = (bf16[2,672,128]{2,1,0:T(8,128)(2,1)S(1)}, bf16[2,672,128]{2,1,0:T(8,128)(2,1)S(1)}, u32[]{:S(2)}, u32[]{:S(2)}) collective-permute-start(bf16[2,672,128]{2,1,0:T(8,128)(2,1)S(1)} %fusion.4), channel_id=1, source_target_pairs={{0,1},{1,0},{2,3},{3,2},{4,5},{5,4},{6,7},{7,6},{8,9},{9,8},{10,11... | collective-permute-start | bytes 1032200 | tf_op jit(solution)/shard_map/ppermute | solution.py:368
  59.4 3.9 %copy-start.6 = (s32[2,8192,4]{1,2,0:T(4,128)S(1)}, s32[2,8192,4]{1,2,0:T(4,128)}, u32[]{:S(2)}) copy-start(s32[2,8192,4]{1,2,0:T(4,128)} %param.23) | copy-start | bytes 786436
  59.6 19.0 %collective-permute-start.12 = (bf16[2,2,432,128]{3,2,1,0:T(8,128)(2,1)S(1)}, bf16[2,2,432,128]{3,2,1,0:T(8,128)(2,1)S(1)}, u32[]{:S(2)}, u32[]{:S(2)}) collective-permute-start(bf16[2,2,432,128]{3,2,1,0:T(8,128)(2,1)S(1)} %fusion.7), channel_id=1, source_target_pairs={{0,2},{1,3},{2,0},{3,1},{4,6},{5,7},{6,4},{7,5},{8,10},{9,11},{10,... | collective-permute-start | bytes 1327112 | tf_op jit(solution)/shard_map/ppermute | solution.py:368
  60.4 18.2 %collective-permute-start.11 = (bf16[2,2,432,128]{3,2,1,0:T(8,128)(2,1)S(1)}, bf16[2,2,432,128]{3,2,1,0:T(8,128)(2,1)S(1)}, u32[]{:S(2)}, u32[]{:S(2)}) collective-permute-start(bf16[2,2,432,128]{3,2,1,0:T(8,128)(2,1)S(1)} %fusion.6.rest_5_), channel_id=1, source_target_pairs={{0,1},{1,0},{2,3},{3,2},{4,5},{5,4},{6,7},{7,6},{8,9},{9,8},{10,11... | collective-permute-start | bytes 1327112 | tf_op jit(solution)/shard_map/ppermute | solution.py:368
  61.8 18.4 %collective-permute-start.8 = (bf16[2,672,128]{2,1,0:T(8,128)(2,1)S(1)}, bf16[2,672,128]{2,1,0:T(8,128)(2,1)S(1)}, u32[]{:S(2)}, u32[]{:S(2)}) collective-permute-start(bf16[2,672,128]{2,1,0:T(8,128)(2,1)S(1)} %fusion.5), channel_id=1, source_target_pairs={{0,2},{1,3},{2,0},{3,1},{4,6},{5,7},{6,4},{7,5},{8,10},{9,11},{10,... | collective-permute-start | bytes 1032200 | tf_op jit(solution)/shard_map/ppermute | solution.py:368
  69.1 13.0 %collective-permute-start.10 = (bf16[2,672,128]{2,1,0:T(8,128)(2,1)S(1)}, bf16[2,672,128]{2,1,0:T(8,128)(2,1)S(1)}, u32[]{:S(2)}, u32[]{:S(2)}) collective-permute-start(bf16[2,672,128]{2,1,0:T(8,128)(2,1)S(1)} %fusion.3.rest_5_), channel_id=1, source_target_pairs={{0,8},{4,12},{8,0},{12,4},{16,24},{20,28},{24,16},{28,20},{1,9},{5... | collective-permute-start | bytes 1032200 | tf_op jit(solution)/shard_map/ppermute | solution.py:365
  78.9 11.0 %collective-permute-start.15 = (bf16[2,432,128]{2,1,0:T(8,128)(2,1)S(1)}, bf16[2,432,128]{2,1,0:T(8,128)(2,1)S(1)}, u32[]{:S(2)}, u32[]{:S(2)}) collective-permute-start(bf16[2,432,128]{2,1,0:T(8,128)(2,1)S(1)} %fusion.10), channel_id=1, source_target_pairs={{0,1},{1,0},{2,3},{3,2},{4,5},{5,4},{6,7},{7,6},{8,9},{9,8},{10,11... | collective-permute-start | bytes 663560 | tf_op jit(solution)/shard_map/ppermute | solution.py:368
  79.6 25.4 %collective-permute-start.17 = (bf16[2,432,128]{2,1,0:T(8,128)(2,1)S(1)}, bf16[2,432,128]{2,1,0:T(8,128)(2,1)S(1)}, u32[]{:S(2)}, u32[]{:S(2)}) collective-permute-start(bf16[2,432,128]{2,1,0:T(8,128)(2,1)S(1)} %fusion.11), channel_id=1, source_target_pairs={{0,2},{1,3},{2,0},{3,1},{4,6},{5,7},{6,4},{7,5},{8,10},{9,11},{10,... | collective-permute-start | bytes 663560 | tf_op jit(solution)/shard_map/ppermute | solution.py:368
  83.7 11.4 %collective-permute-start.14 = (bf16[1,672,128]{2,1,0:T(8,128)(2,1)S(1)}, bf16[1,672,128]{2,1,0:T(8,128)(2,1)S(1)}, u32[]{:S(2)}, u32[]{:S(2)}) collective-permute-start(bf16[1,672,128]{2,1,0:T(8,128)(2,1)S(1)} %fusion.18), channel_id=1, source_target_pairs={{0,16},{4,20},{8,24},{12,28},{16,0},{20,4},{24,8},{28,12},{1,17},{... | collective-permute-start | bytes 516104 | tf_op jit(solution)/shard_map/ppermute | solution.py:365
  87.5 9.9 %collective-permute-start.13 = (bf16[2,512,128]{2,1,0:T(8,128)(2,1)S(1)}, bf16[2,512,128]{2,1,0:T(8,128)(2,1)S(1)}, u32[]{:S(2)}, u32[]{:S(2)}) collective-permute-start(bf16[2,512,128]{2,1,0:T(8,128)(2,1)S(1)} %slice_bitcast_fusion.17), channel_id=1, source_target_pairs={{0,1},{1,0},{2,3},{3,2},{4,5},{5,4},{6,7},{7,6},{8,9},{9,8},{10,11... | collective-permute-start | bytes 786440 | tf_op jit(solution)/shard_map/ppermute | solution.py:368
  89.1 8.5 %collective-permute-start.19 = (bf16[2,512,128]{2,1,0:T(8,128)(2,1)S(1)}, bf16[2,512,128]{2,1,0:T(8,128)(2,1)S(1)}, u32[]{:S(2)}, u32[]{:S(2)}) collective-permute-start(bf16[2,512,128]{2,1,0:T(8,128)(2,1)S(1)} %slice_bitcast_fusion.16), channel_id=1, source_target_pairs={{0,2},{1,3},{2,0},{3,1},{4,6},{5,7},{6,4},{7,5},{8,10},{9,11},{10,... | collective-permute-start | bytes 786440 | tf_op jit(solution)/shard_map/ppermute | solution.py:368
  90.0 15.0 %collective-permute-start.18 = (bf16[2,432,128]{2,1,0:T(8,128)(2,1)S(1)}, bf16[2,432,128]{2,1,0:T(8,128)(2,1)S(1)}, u32[]{:S(2)}, u32[]{:S(2)}) collective-permute-start(bf16[2,432,128]{2,1,0:T(8,128)(2,1)S(1)} %fusion.9), channel_id=1, source_target_pairs={{0,8},{4,12},{8,0},{12,4},{16,24},{20,28},{24,16},{28,20},{1,9},{5... | collective-permute-start | bytes 663560 | tf_op jit(solution)/shard_map/ppermute | solution.py:365
  96.9 8.0 %collective-permute-start.21 = (bf16[1,672,128]{2,1,0:T(8,128)(2,1)S(1)}, bf16[1,672,128]{2,1,0:T(8,128)(2,1)S(1)}, u32[]{:S(2)}, u32[]{:S(2)}) collective-permute-start(bf16[1,672,128]{2,1,0:T(8,128)(2,1)S(1)} %fusion.15), channel_id=1, source_target_pairs={{0,16},{4,20},{8,24},{12,28},{16,0},{20,4},{24,8},{28,12},{1,17},{... | collective-permute-start | bytes 516104 | tf_op jit(solution)/shard_map/ppermute | solution.py:365
  97.5 9.6 %collective-permute-start.16 = (bf16[512,128]{1,0:T(8,128)(2,1)S(1)}, bf16[512,128]{1,0:T(8,128)(2,1)S(1)}, u32[]{:S(2)}, u32[]{:S(2)}) collective-permute-start(bf16[512,128]{1,0:T(8,128)(2,1)S(1)} %fusion.24), channel_id=1, source_target_pairs={{0,2},{1,3},{2,0},{3,1},{4,6},{5,7},{6,4},{7,5},{8,10},{9,11},{10,... | collective-permute-start | bytes 393224 | tf_op jit(solution)/shard_map/ppermute | solution.py:368
  97.6 9.5 %collective-permute-start.20 = (bf16[512,128]{1,0:T(8,128)(2,1)S(1)}, bf16[512,128]{1,0:T(8,128)(2,1)S(1)}, u32[]{:S(2)}, u32[]{:S(2)}) collective-permute-start(bf16[512,128]{1,0:T(8,128)(2,1)S(1)} %fusion.21), channel_id=1, source_target_pairs={{0,1},{1,0},{2,3},{3,2},{4,5},{5,4},{6,7},{7,6},{8,9},{9,8},{10,11... | collective-permute-start | bytes 393224 | tf_op jit(solution)/shard_map/ppermute | solution.py:368
  104.9 18.4 %collective-permute-start.22 = (bf16[2,672,128]{2,1,0:T(8,128)(2,1)S(1)}, bf16[2,672,128]{2,1,0:T(8,128)(2,1)S(1)}, u32[]{:S(2)}, u32[]{:S(2)}) collective-permute-start(bf16[2,672,128]{2,1,0:T(8,128)(2,1)S(1)} %pad_maximum_fusion.1.refs_0_), channel_id=1, source_target_pairs={{0,8},{4,12},{8,0},{12,4},{16,24},{20,28},{24,16},{28,20},{1,9},{5... | collective-permute-start | bytes 1032200 | tf_op jit(solution)/shard_map/ppermute | solution.py:365
  105.2 9.8 %collective-permute-start.25 = (bf16[1,432,128]{2,1,0:T(8,128)(2,1)S(1)}, bf16[1,432,128]{2,1,0:T(8,128)(2,1)S(1)}, u32[]{:S(2)}, u32[]{:S(2)}) collective-permute-start(bf16[1,432,128]{2,1,0:T(8,128)(2,1)S(1)} %fusion.31), channel_id=1, source_target_pairs={{0,16},{4,20},{8,24},{12,28},{16,0},{20,4},{24,8},{28,12},{1,17},{... | collective-permute-start | bytes 331784 | tf_op jit(solution)/shard_map/ppermute | solution.py:365
  115.2 7.9 %collective-permute-start.26 = (bf16[1,432,128]{2,1,0:T(8,128)(2,1)S(1)}, bf16[1,432,128]{2,1,0:T(8,128)(2,1)S(1)}, u32[]{:S(2)}, u32[]{:S(2)}) collective-permute-start(bf16[1,432,128]{2,1,0:T(8,128)(2,1)S(1)} %fusion.28), channel_id=1, source_target_pairs={{0,16},{4,20},{8,24},{12,28},{16,0},{20,4},{24,8},{28,12},{1,17},{... | collective-permute-start | bytes 331784 | tf_op jit(solution)/shard_map/ppermute | solution.py:365
  123.2 6.8 %collective-permute-start.27 = (bf16[2,432,128]{2,1,0:T(8,128)(2,1)S(1)}, bf16[2,432,128]{2,1,0:T(8,128)(2,1)S(1)}, u32[]{:S(2)}, u32[]{:S(2)}) collective-permute-start(bf16[2,432,128]{2,1,0:T(8,128)(2,1)S(1)} %pad_maximum_fusion.2.refs_4_), channel_id=1, source_target_pairs={{0,8},{4,12},{8,0},{12,4},{16,24},{20,28},{24,16},{28,20},{1,9},{5... | collective-permute-start | bytes 663560 | tf_op jit(solution)/shard_map/ppermute | solution.py:365
  123.2 6.7 %collective-permute-start.23 = (bf16[2,672,128]{2,1,0:T(8,128)(2,1)S(1)}, bf16[2,672,128]{2,1,0:T(8,128)(2,1)S(1)}, u32[]{:S(2)}, u32[]{:S(2)}) collective-permute-start(bf16[2,672,128]{2,1,0:T(8,128)(2,1)S(1)} %pad_maximum_fusion.1.refs_0_), channel_id=1, source_target_pairs={{0,4},{4,0},{8,12},{12,8},{16,20},{20,16},{24,28},{28,24},{1,5},{5... | collective-permute-start | bytes 1032200 | tf_op jit(solution)/shard_map/ppermute | solution.py:362
  123.3 6.6 %collective-permute-start.24 = (bf16[2,672,128]{2,1,0:T(8,128)(2,1)S(1)}, bf16[2,672,128]{2,1,0:T(8,128)(2,1)S(1)}, u32[]{:S(2)}, u32[]{:S(2)}) collective-permute-start(bf16[2,672,128]{2,1,0:T(8,128)(2,1)S(1)} %collective-permute-done.22.refs_1_), channel_id=1, source_target_pairs={{0,4},{4,0},{8,12},{12,8},{16,20},{20,16},{24,28},{28,24},{1,5},{5... | collective-permute-start | bytes 1032200 | tf_op jit(solution)/shard_map/ppermute | solution.py:362
  123.8 6.1 %collective-permute-start.28 = (bf16[2,432,128]{2,1,0:T(8,128)(2,1)S(1)}, bf16[2,432,128]{2,1,0:T(8,128)(2,1)S(1)}, u32[]{:S(2)}, u32[]{:S(2)}) collective-permute-start(bf16[2,432,128]{2,1,0:T(8,128)(2,1)S(1)} %pad_maximum_fusion.2.refs_4_), channel_id=1, source_target_pairs={{0,4},{4,0},{8,12},{12,8},{16,20},{20,16},{24,28},{28,24},{1,5},{5... | collective-permute-start | bytes 663560 | tf_op jit(solution)/shard_map/ppermute | solution.py:362
  129.9 1.5 %collective-permute-start.29 = (bf16[2,432,128]{2,1,0:T(8,128)(2,1)S(1)}, bf16[2,432,128]{2,1,0:T(8,128)(2,1)S(1)}, u32[]{:S(2)}, u32[]{:S(2)}) collective-permute-start(bf16[2,432,128]{2,1,0:T(8,128)(2,1)S(1)} %collective-permute-done.27.refs_5_), channel_id=1, source_target_pairs={{0,4},{4,0},{8,12},{12,8},{16,20},{20,16},{24,28},{28,24},{1,5},{5... | collective-permute-start | bytes 663560 | tf_op jit(solution)/shard_map/ppermute | solution.py:362

commit v6 on v5

--- a/solution.py
+++ b/solution.py
@@ -1,4 +1,5 @@
 import functools
+import itertools
 
 import jax
 import jax.numpy as jnp
@@ -177,8 +178,8 @@
 def back_kernel(*refs):
     dense_feat, pooled, cross_down, crossed_t, delta_first, delta_widened, delta_reduced = refs[:7]
     small_in = refs[7]
-    send, keep = refs[10:12]
-    half_delta, sixths, small = refs[12:]
+    send, keep = refs[8:10]
+    half_delta, sixths, small = refs[10:]
     core, row_pos, table_pos = position()
     n_row = send.shape[1]
     places = places_of(lax.div(table_pos, 2), 2 * send.shape[2])
@@ -211,15 +212,16 @@
 
 
 def select_kernel(n_z, *refs):
-    out = refs[-1]
     for which in range(n_z):
-        out[which] = refs[which][1]
+        out = refs[len(refs) - 2 + which // (n_z // 2)]
+        out[which % (n_z // 2)] = refs[which][1]
 
 
 def count_kernel(n_row, table, hot, n_z, slots, *rest):
-    direct, crossed, out = rest[:n_z], rest[n_z], rest[-1]
+    direct, crossed, out = rest[:n_z], rest[n_z : n_z + 2], rest[-1]
+    near = n_z // 2
     block = out.shape[1]
-    samples = crossed.shape[2]
+    samples = crossed[0].shape[2]
     core, row_pos, table_pos = position()
     z_pos = lax.div(table_pos, 2)
     base = (pl.program_id(0) ^ row_pos) * block
@@ -228,7 +230,8 @@
     one = jnp.ones((block, samples), bf16)
     zero = jnp.zeros((block, samples), bf16)
     for which in range(n_z):
-        for held, who in ((direct[which][0, table], core), (crossed[which, table], 1 - core)):
+        far = crossed[which // near]
+        for held, who in ((direct[which][0, table], core), (far[which % near, table], 1 - core)):
             source = 2 * (z_pos ^ which) + who
             start = pl.multiple_of((source * n_row + row_pos) * samples, LANES)
             lines = slots[table, :, pl.ds(start, samples)] - base
@@ -326,11 +329,75 @@
     return [pltpu.VMEM(value.shape, value.dtype) for value in values]
 
 
-def add_terms(terms):
-    total = terms[0].astype(f32)
-    for term in terms[1:]:
-        total = total + term.astype(f32)
-    return total
+def sum_rows_kernel(plan, *refs):
+    out = refs[-1]
+    for table, terms in enumerate(plan):
+        total = None
+        for which, picks in terms:
+            part = refs[which][picks].astype(f32)
+            total = part if total is None else total + part
+        out[table] = total
+
+
+def sum_rows(groups, deps):
+    arrays = [array for items in groups for array, _ in items]
+    plan, count = [], 0
+    for items in groups:
+        plan.append([(count + at, tuple(picks)) for at, (_, picks) in enumerate(items)])
+        count += len(items)
+    kept = [pick.stop - pick.start for pick in groups[0][0][1] if isinstance(pick, slice)]
+    return call(
+        functools.partial(sum_rows_kernel, plan),
+        [jax.ShapeDtypeStruct((len(groups), *kept), f32)],
+        [],
+        [whole()] * len(arrays) + [whole(pl.ANY)] * len(deps),
+        "rows",
+        24,
+    )(*arrays, *deps)[0]
+
+
+def sum_kernel(plan, n_in, *refs):
+    outs = refs[len(refs) - len(plan) :]
+    for out, terms in zip(outs, plan):
+        rows = out.shape[-2]
+        chunk = next(size for size in (64, 48, 80, 32, 16, 8, rows) if rows % size == 0)
+
+        def one_chunk(at, carry, out=out, terms=terms, chunk=chunk):
+            window = pl.ds(pl.multiple_of(at * chunk, chunk), chunk)
+            for lead in itertools.product(*[range(size) for size in out.shape[:-2]]):
+                total = None
+                for which, picks in terms:
+                    axes, place = iter(lead), []
+                    for pick in picks[:-2]:
+                        place.append(pick.start + next(axes) if isinstance(pick, slice) else pick)
+                    part = refs[which][(*place, window, slice(None))].astype(f32)
+                    total = part if total is None else total + part
+                out[(*lead, window, slice(None))] = total.astype(out.dtype)
+            return carry
+
+        lax.fori_loop(0, rows // chunk, one_chunk, 0)
+
+
+def take_sums(groups, deps, dtype=bf16):
+    arrays, plan, shapes = [], [], []
+    for items in groups:
+        terms = []
+        for array, picks in items:
+            found = [at for at, known in enumerate(arrays) if known is array]
+            if not found:
+                arrays.append(array)
+            terms.append((found[0] if found else len(arrays) - 1, tuple(picks)))
+        plan.append(terms)
+        kept = [pick.stop - pick.start for pick in items[0][1] if isinstance(pick, slice)]
+        shapes.append(jax.ShapeDtypeStruct(tuple(kept), dtype))
+    return call(
+        functools.partial(sum_kernel, plan, len(arrays)),
+        shapes,
+        [],
+        [whole()] * len(arrays) + [whole(pl.ANY)] * len(deps),
+        "sums",
+        24,
+    )(*arrays, *deps)
 
 
 def local(
@@ -397,7 +464,7 @@
         w_logit,
         labels,
     )
-    send, keep, crossed_t, delta_first, small = call(
+    send1, keep1, crossed_t, delta_first, small = call(
         front_kernel,
         [packed(rows_front)] * 2
         + [wide(feat, batch), wide(batch, hid), jax.ShapeDtypeStruct((24, LANES), f32)],
@@ -411,7 +478,7 @@
         "front",
         60,
     )(*sources)
-    got = swap_cores(send)
+    got1 = swap_cores(send1)
 
     sources = (dense_feat, pooled, cross_down, cross_up, cross_bias, w_hidden1)
     outs = call(
@@ -433,89 +500,82 @@
     high_first = low_first[::-1]
 
     class Terms:
-        def __init__(self, arrays):
-            self.items = [(array, ()) for array in arrays]
-
-        def tie(self, deps):
-            arrays = after([array for array, _ in self.items], deps)
-            self.items = [(array, path) for array, (_, path) in zip(arrays, self.items)]
-
-        def total(self, *extra):
-            parts = []
-            for array, path in self.items:
-                for pick in path + extra:
-                    array = pick(array)
-                parts.append(array)
-            return add_terms(parts)
-
-        def narrow(self, pick, got):
-            self.items = [(array, path + (pick,)) for array, path in self.items] + [(got, ())]
-
-    def index_of(index, axis):
-        return lambda array: lax.index_in_dim(array, index, axis, keepdims=False)
-
-    def rows_of(start, stop):
-        return lambda array: array[start:stop]
+        def __init__(self, arrays, picks):
+            self.items = []
+            for array in arrays:
+                self.add(array, picks)
+
+        def add(self, array, picks=()):
+            whole_axes = [slice(0, size) for size in array.shape[len(picks) :]]
+            self.items.append((array, list(picks) + whole_axes))
+
+        def narrowed(self, axis, what):
+            items = []
+            for array, picks in self.items:
+                at = [number for number, pick in enumerate(picks) if isinstance(pick, slice)][axis]
+                items.append((array, picks[:at] + [what] + picks[at + 1 :]))
+            return items
+
+        def far_near(self, axis, near, far):
+            sent = self.narrowed(axis, far)
+            self.items = self.narrowed(axis, near)
+            return sent
 
     class Halving(Terms):
-        def __init__(self, arrays, order, half=None):
-            dims = 0 if half is None else 1
-            super().__init__(
-                [
-                    array.reshape(array.shape[:dims] + (2,) * row_bits + array.shape[dims + 1 :])
-                    for array in arrays
-                ]
-            )
-            if half is not None:
-                self.items = [(array, (index_of(half, 0),)) for array, _ in self.items]
+        def __init__(self, arrays, order, picks=()):
+            dims = len(picks)
+            arrays = [
+                array.reshape(array.shape[:dims] + (2,) * row_bits + array.shape[dims + 1 :])
+                for array in arrays
+            ]
+            super().__init__(arrays, picks)
             self.order, self.left = order, list(range(row_bits - 1, -1, -1))
 
-        def step(self, at, deps=()):
-            bit = self.order[at]
-            axis = self.left.index(bit)
-            self.left.remove(bit)
-            if deps:
-                self.tie(deps)
-            sent = self.total(index_of(1, axis)).astype(bf16)
-            self.narrow(index_of(0, axis), swap_row(sent, bit))
-            return sent
+        def part(self, at):
+            axis = self.left.index(self.order[at])
+            self.left.remove(self.order[at])
+            return self.far_near(axis, 0, 1)
+
+    def row_step(streams, at, deps):
+        sent = take_sums([stream.part(at) for stream in streams], deps)
+        for stream, value in zip(streams, sent):
+            stream.add(swap_row(value, stream.order[at]))
+        return list(sent)
 
     class Dense:
         def __init__(self, keep, got):
-            self.low = Halving([keep, got], low_first, 0)
-            self.high = Halving([keep, got], high_first, 1)
-
-        def row_step(self, at, deps=()):
-            sent = self.low.step(at, deps)
-            return [sent, self.high.step(at, deps)]
+            self.low = Halving([keep, got], low_first, [0])
+            self.high = Halving([keep, got], high_first, [1])
+
+        def row_step(self, at, deps):
+            deps = [*deps, self.low.items[-1][0], self.high.items[-1][0]]
+            return row_step((self.low, self.high), at, deps)
 
         def z_step(self, stage, deps):
-            if stage == 0:
-                self.high.tie(deps)
-                sent = self.high.total().astype(bf16)
-                self.low.items.append((swap_z(sent, 1), ()))
-            else:
-                middle = n_z >> (stage + 1)
-                self.low.tie(deps)
-                sent = self.low.total(rows_of(middle, None)).astype(bf16)
-                self.low.narrow(rows_of(0, middle), swap_z(sent, 1 << stage))
+            middle = n_z >> (stage + 1)
+            items, deps = self.high.items, [*deps, self.low.items[-1][0]]
+            if stage > 0:
+                items = self.low.far_near(0, slice(0, middle), slice(middle, 2 * middle))
+            (sent,) = take_sums([items], deps)
+            self.low.add(swap_z(sent, 1 << stage))
             return [sent]
 
+        def z_own(self, deps):
+            (self.own,) = take_sums([self.low.items], deps)
+            self.back = swap_z(self.own, 1 << (z_bits - 1)) if z_bits > 1 else None
+            return [self.own]
+
         def z_back(self, deps):
-            self.low.tie(deps)
-            own = self.low.total().astype(bf16)
-            first = own
             for stage in range(z_bits - 1, 0, -1):
-                own = jnp.concatenate([own, swap_z(own, 1 << stage)], axis=0)
-            far = swap_z(own, 1)
-            self.pieces = [own, far, swap_cores(own), swap_cores(far)]
-            return [first]
-
-    one = Dense(keep, got)
-    sent = one.row_step(0)
-    values = [pooled_out[0]] + [swap_z(pooled_out[which], which) for which in range(1, n_z)]
-
-    send, keep = call(
+                if stage < z_bits - 1:
+                    self.back = swap_z(self.own, 1 << stage)
+                (back,) = after([self.back], deps)
+                self.own = jnp.concatenate([self.own, back], axis=0)
+            far = swap_z(self.own, 1)
+            self.pieces = [self.own, far, swap_cores(self.own), swap_cores(far)]
+            return [self.own]
+
+    send2, keep2 = call(
         back_kernel,
         [packed(rows_back)] * 2,
         [
@@ -523,7 +583,7 @@
             pltpu.VMEM((2, batch, late), bf16),
             pltpu.VMEM((48, LANES), f32),
         ],
-        [vmem] * 8 + [anywhere] * 2,
+        [vmem] * 8,
         "back",
         36,
     )(
@@ -535,32 +595,45 @@
         delta_widened,
         delta_reduced,
         small,
-        *sent,
     )
-    two = Dense(keep, swap_cores(send))
-
+
+    got2 = swap_cores(send2)
+
+    one, two = Dense(keep1, got1), Dense(keep2, got2)
+    last = one.row_step(0, [keep2])
+    two.row_step(0, last)
+    values, chain = {0: pooled_out[0]}, [n_z // 2]
+    chain += [which for which in range(n_z - 1, 0, -1) if which != n_z // 2]
+    for at, which in enumerate(chain):
+        moved = pooled_out[which]
+        if at > 0:
+            (moved,) = after([moved], [values[chain[at - 1]]])
+        values[which] = swap_z(moved, which)
+    last = [values[chain[0]]]
+    for at in range(1, row_bits):
+        last = one.row_step(at, last)
+    last = [*last, values[chain[min(1, len(chain) - 1)]]]
+    for at in range(1, row_bits):
+        last = two.row_step(at, last)
+    last = one.z_step(0, last)
+    values = [values[which] for which in range(n_z)]
     far_values = call(
         functools.partial(select_kernel, n_z),
-        [wide(n_z, tab_grp, batch, width)],
+        [wide(n_z // 2, tab_grp, batch, width)] * 2,
         [],
         [vmem] * n_z + [anywhere],
         "select",
         8,
-    )(*values, keep)[0]
-    values.append(swap_cores(far_values))
-    last = [far_values]
-    for at in range(1, row_bits):
-        last = one.row_step(at, last)
-    last = two.row_step(0, last)
-
+    )(*values, last[0])
+    values += [swap_cores(value) for value in far_values]
     slots = jnp.transpose(lookup_slots, (0, 2, 1))
-    shares = []
+    last, shares = [far_values[0]], []
     for table in range(tab_grp):
         sums = pl.pallas_call(
             functools.partial(count_kernel, n_row, table, hot, n_z),
             out_shape=wide(n_row, u_shard, width),
             grid=(n_row,),
-            in_specs=[vmem] * (2 + n_z) + [anywhere],
+            in_specs=[vmem] * (3 + n_z) + [anywhere],
             out_specs=pl.BlockSpec((1, u_shard, width), lambda at: (at, 0, 0)),
             compiler_params=pltpu.CompilerParams(vmem_limit_bytes=16 * MIB),
             cost_estimate=no_cost(),
@@ -569,23 +642,18 @@
         shares.append(Halving([sums], high_first if table % 2 else low_first))
         last = [sums]
         if table == 0:
-            last = one.z_step(0, last)
-    for at in range(1, row_bits):
-        last = two.row_step(at, last)
-    for stage in range(1, z_bits):
-        last = one.z_step(stage, last)
-    for share in shares:
-        share.step(0, last)
-    last = two.z_step(0, last)
-    last = one.z_back(last)
-    for share in shares:
-        for at in range(1, row_bits):
-            share.step(at, last)
+            for stage in range(1, z_bits):
+                last = one.z_step(stage, last)
+            last = two.z_step(0, last)
     for stage in range(1, z_bits):
         last = two.z_step(stage, last)
-    for share in shares:
-        share.tie(last)
-    row_grads = jnp.stack([share.total() for share in shares])
+    last = one.z_own(last)
+    last = row_step(shares, 0, last)
+    last = two.z_own(last)
+    last = one.z_back(last)
+    for at in range(1, row_bits):
+        last = row_step(shares, at, last)
+    row_grads = sum_rows([share.items for share in shares], last)
     two.z_back([row_grads])
 
     g_down, g_up, g_first, g_second, g_cbias, g_bias1, g_bias2, g_logit = call(

time: 134 us -> 128 us (0.955)
  other arithmetic: 6.09 us -> 0.06 us
  starting transfers between devices: 39 us -> 33.3 us
  waiting for transfers between devices: 45.8 us -> 50.2 us
  Pallas kernels: 33 us -> 36.7 us
  local copies, waits for them, and re-layouts: 8.64 us -> 6.28 us
    ppermute x12, waiting for transfers between devices: 0.59 us -> 11.4 us  [swap_row(): lax.ppermute(value, 'row', [(at, at ^ 1 << bit) for at in range(n_row)])]
    ppermute x11, waiting for transfers between devices: 43.7 us -> 37.3 us  [swap_z(): lax.ppermute(value, 'table', [(at, at ^ 2 * which) for at in range(n_tabl...]
    unnamed x28, local copies, waits for them, and re-layouts: 0.62 us -> 6.28 us
    convert_element_type x16 -> x0, other arithmetic: 5.11 us -> none  [the longest x10 3.38 us: step(): sent = self.total(index_of(1, axis)).astype(bf16)]
    squeeze x15 -> x0, local copies, waits for them, and re-layouts: 5.08 us -> none  [index_of(): return lambda array: lax.index_in_dim(array, index, axis, keepdims=False)]
    ppermute x11, starting transfers between devices: 23 us -> 18.4 us  [swap_z(): lax.ppermute(value, 'table', [(at, at ^ 2 * which) for at in range(n_tabl...]
    pallas_call x1 -> x14, Pallas kernels: 0.03 us -> 3.78 us  [the longest x12 2.87 us: take_sums(): call(functools.partial(sum_kernel, plan, len(arrays)), shapes, [], [whole...]
    slice x2 -> x0, local copies, waits for them, and re-layouts: 2.95 us -> none  [index_of(): return lambda array: lax.index_in_dim(array, index, axis, keepdims=False)]
  transfers between devices with their start and end apart: 30 -> 31, of which waited for: 10 -> 16; matrix products, arithmetic and copies ran while one was open for 8% -> 0% of each run, Pallas kernels for 12% -> 17%
where the time goes in v6:
time: 128 us; the launch traced here: 127 us
  waiting for transfers between devices  50.2 us (39%)
  Pallas kernels  36.7 us (29%)
  starting transfers between devices  33.3 us (26%)
  local copies, waits for them, and re-layouts  6.28 us (5%)
    ppermute x11, waiting for transfers between devices, swap_z(): lax.ppermute(value, 'table', [(at, at ^ 2 * which) for at in range(n_tabl...  37.3 us
    ppermute x11, starting transfers between devices, swap_z(): lax.ppermute(value, 'table', [(at, at ^ 2 * which) for at in range(n_tabl...  18.4 us
    ppermute x12, starting transfers between devices, swap_row(): lax.ppermute(value, 'row', [(at, at ^ 1 << bit) for at in range(n_row)])  13.1 us
    pallas_call x1, Pallas kernels, local(): call(front_kernel, [packed(rows_front)] * 2 + [wide(feat, batch), wide(ba...  11.9 us
    ppermute x12, waiting for transfers between devices, swap_row(): lax.ppermute(value, 'row', [(at, at ^ 1 << bit) for at in range(n_row)])  11.4 us
    pallas_call x1, Pallas kernels, local(): call(functools.partial(middle_kernel, n_z), [wide(batch, feat), wide(batc...  8.14 us
    pallas_call x2, Pallas kernels, local(): pl.pallas_call(functools.partial(count_kernel, n_row, table, hot, n_z), o...  8.04 us
    unnamed x28, local copies, waits for them, and re-layouts  6.28 us
  transfers between devices with their start and end apart: 31, of which 16 were waited for; matrix products, arithmetic and copies ran while one was open for 0% of the time, Pallas kernels for 17%

profile of v6, /device:TPU:0, one launch (start us, length us, event | category | flops | bytes accessed | tf_op | source)
XLA Modules:
  0.0 127.4 jit_solution(1715892820753599756)
XLA Ops:
  0.6 11.9 %front.1 = (bf16[2,4,2,672,128]{4,3,2,1,0:T(8,128)(2,1)}, bf16[2,4,2,672,128]{4,3,2,1,0:T(8,128)(2,1)}, bf16[2176,256]{1,0:T(8,128)(2,1)}, bf16[256,1024]{1,0:T(8,128)(2,1)}, f32[24,128]{1,0:T(8,128)}) custom-call(bf16[256,128]{1,0:T(8,128)(2,1)} %refs_0_.5, bf16[256,2048]{1,0:T(8,128)(2,1)} %refs_1_.5, bf16[2176,256]{1,0:T(8,128)(2,1)} %refs_2_.5, ...), custom_call_target="tpu_custom_call" | custom-call | tf_op jit(solution)/shard_map/front/pallas_call | solution.py:467
  12.5 0.5 collective-permute-start.3
  13.0 8.1 %middle.1 = (bf16[256,2176]{1,0:T(8,128)(2,1)}, bf16[256,256]{1,0:T(8,128)(2,1)}, bf16[2,2,256,128]{3,2,1,0:T(8,128)(2,1)}, bf16[2,2,256,128]{3,2,1,0:T(8,128)(2...) custom-call(bf16[256,128]{1,0:T(8,128)(2,1)} %refs_0_.5, bf16[256,2048]{1,0:T(8,128)(2,1)} %refs_1_.5, ...), custom_call_target="tpu_custom_call" | custom-call | tf_op jit(solution)/shard_map/middle/pallas_call | solution.py:484
  21.2 1.2 copy-done.2
  22.5 1.0 copy-done.4
  23.5 1.2 copy-done.5
  24.7 1.2 copy-done.6
  26.0 0.9 copy-done.9
  26.9 2.6 %back.1 = (bf16[2,4,2,432,128]{4,3,2,1,0:T(8,128)(2,1)S(1)}, bf16[2,4,2,432,128]{4,3,2,1,0:T(8,128)(2,1)S(1)}) custom-call(bf16[256,128]{1,0:T(8,128)(2,1)S(1)} %copy-done.8, bf16[256,2048]{1,0:T(8,128)(2,1)S(1)} %copy-done.2, bf16[2176,256]{1,0:T(8,128)(2,1)S(1)} %copy-done.1, bf16[2176,256]{1,0:T(8,128)(2,1)S(1)} %copy-done.5, ...), custom_call_target="tpu_custom_call" | custom-call | tf_op jit(solution)/shard_map/back/pallas_call | solution.py:578
  30.1 3.0 %collective-permute-start.5 = (bf16[2,2,672,128]{3,2,1,0:T(8,128)(2,1)S(1)}, bf16[2,2,672,128]{3,2,1,0:T(8,128)(2,1)S(1)}, u32[]{:S(2)}, u32[]{:S(2)}) collective-permute-start(bf16[2,2,672,128]{3,2,1,0:T(8,128)(2,1)S(1)} %get-tuple-element.63.refs_4_), channel_id=1, source_target_pairs={{0,1},{1,0},{2,3},{3,2},{4,5},{5,4},{6,7},{7,6},{8,9},{9,8},{10,11... | collective-permute-start | bytes 2064392 | tf_op jit(solution)/shard_map/ppermute | solution.py:435
  33.1 1.5 %collective-permute-start.4 = (bf16[2,2,672,128]{3,2,1,0:T(8,128)(2,1)S(1)}, bf16[2,2,672,128]{3,2,1,0:T(8,128)(2,1)S(1)}, u32[]{:S(2)}, u32[]{:S(2)}) collective-permute-start(bf16[2,2,672,128]{3,2,1,0:T(8,128)(2,1)S(1)} %get-tuple-element.62.refs_5_), channel_id=1, source_target_pairs={{0,2},{1,3},{2,0},{3,1},{4,6},{5,7},{6,4},{7,5},{8,10},{9,11},{10,... | collective-permute-start | bytes 2064392 | tf_op jit(solution)/shard_map/ppermute | solution.py:435
  34.7 2.6 %collective-permute-start = (bf16[2,2,256,128]{3,2,1,0:T(8,128)(2,1)S(1)}, bf16[2,2,256,128]{3,2,1,0:T(8,128)(2,1)S(1)}, u32[]{:S(2)}, u32[]{:S(2)}) collective-permute-start(bf16[2,2,256,128]{3,2,1,0:T(8,128)(2,1)S(1)} %copy-done.13), channel_id=1, source_target_pairs={{0,16},{4,20},{8,24},{12,28},{16,0},{20,4},{24,8},{28,12},{1,17},{... | collective-permute-start | bytes 786440 | tf_op jit(solution)/shard_map/ppermute | solution.py:432
  37.3 11.6 %collective-permute-done.refs_6_.refs_2_.rest_2_ = bf16[2,2,256,128]{3,2,1,0:T(8,128)(2,1)S(1)} collective-permute-done((bf16[2,2,256,128]{3,2,1,0:T(8,128)(2,1)S(1)}, bf16[2,2,256,128]{3,2,1,0:T(8,128)(2,1)S(1)}, u32[]{:S(2)}, u32[]{:S(2)}) %collective-permute-start) | collective-permute-done | bytes 262176 | tf_op jit(solution)/shard_map/ppermute | solution.py:432
  48.9 3.5 %collective-permute-start.1 = (bf16[2,2,256,128]{3,2,1,0:T(8,128)(2,1)S(1)}, bf16[2,2,256,128]{3,2,1,0:T(8,128)(2,1)S(1)}, u32[]{:S(2)}, u32[]{:S(2)}) collective-permute-start(bf16[2,2,256,128]{3,2,1,0:T(8,128)(2,1)S(1)} %copy-done.12), channel_id=1, source_target_pairs={{0,24},{4,28},{8,16},{12,20},{16,8},{20,12},{24,0},{28,4},{1,25},{... | collective-permute-start | bytes 786440 | tf_op jit(solution)/shard_map/ppermute | solution.py:432
  52.7 0.6 collective-permute-start.8
  54.2 1.6 %collective-permute-start.10 = (bf16[2,672,128]{2,1,0:T(8,128)(2,1)S(1)}, bf16[2,672,128]{2,1,0:T(8,128)(2,1)S(1)}, u32[]{:S(2)}, u32[]{:S(2)}) collective-permute-start(bf16[2,672,128]{2,1,0:T(8,128)(2,1)S(1)} %get-tuple-element.68.refs_6_), channel_id=1, source_target_pairs={{0,2},{1,3},{2,0},{3,1},{4,6},{5,7},{6,4},{7,5},{8,10},{9,11},{10,... | collective-permute-start | bytes 1032200 | tf_op jit(solution)/shard_map/ppermute | solution.py:435
  55.8 1.5 %collective-permute-start.6 = (bf16[2,672,128]{2,1,0:T(8,128)(2,1)S(1)}, bf16[2,672,128]{2,1,0:T(8,128)(2,1)S(1)}, u32[]{:S(2)}, u32[]{:S(2)}) collective-permute-start(bf16[2,672,128]{2,1,0:T(8,128)(2,1)S(1)} %get-tuple-element.64.refs_7_), channel_id=1, source_target_pairs={{0,1},{1,0},{2,3},{3,2},{4,5},{5,4},{6,7},{7,6},{8,9},{9,8},{10,11... | collective-permute-start | bytes 1032200 | tf_op jit(solution)/shard_map/ppermute | solution.py:435
  57.3 1.7 %collective-permute-done.1.refs_8_.refs_3_.rest_3_ = bf16[2,2,256,128]{3,2,1,0:T(8,128)(2,1)S(1)} collective-permute-done((bf16[2,2,256,128]{3,2,1,0:T(8,128)(2,1)S(1)}, bf16[2,2,256,128]{3,2,1,0:T(8,128)(2,1)S(1)}, u32[]{:S(2)}, u32[]{:S(2)}) %collective-permute-start.1) | collective-permute-done | bytes 262176 | tf_op jit(solution)/shard_map/ppermute | solution.py:432
  59.0 4.4 %collective-permute-start.2 = (bf16[2,2,256,128]{3,2,1,0:T(8,128)(2,1)S(1)}, bf16[2,2,256,128]{3,2,1,0:T(8,128)(2,1)S(1)}, u32[]{:S(2)}, u32[]{:S(2)}) collective-permute-start(bf16[2,2,256,128]{3,2,1,0:T(8,128)(2,1)S(1)} %copy-done.11), channel_id=1, source_target_pairs={{0,8},{4,12},{8,0},{12,4},{16,24},{20,28},{24,16},{28,20},{1,9},{5... | collective-permute-start | bytes 786440 | tf_op jit(solution)/shard_map/ppermute | solution.py:432
  63.4 2.4 %collective-permute-done.8.refs_2_.refs_9_ = bf16[2,2,432,128]{3,2,1,0:T(8,128)(2,1)S(1)} collective-permute-done((bf16[2,2,432,128]{3,2,1,0:T(8,128)(2,1)S(1)}, bf16[2,2,432,128]{3,2,1,0:T(8,128)(2,1)S(1)}, u32[]{:S(2)}, u32[]{:S(2)}) %collective-permute-start.8) | collective-permute-done | bytes 442400 | tf_op jit(solution)/shard_map/ppermute | solution.py:435
  65.8 0.6 collective-permute-done.9.refs_5_.refs_10_.refs_2_
  66.7 5.5 %collective-permute-done.10.refs_6_.refs_3_ = bf16[2,672,128]{2,1,0:T(8,128)(2,1)S(1)} collective-permute-done((bf16[2,672,128]{2,1,0:T(8,128)(2,1)S(1)}, bf16[2,672,128]{2,1,0:T(8,128)(2,1)S(1)}, u32[]{:S(2)}, u32[]{:S(2)}) %collective-permute-start.10) | collective-permute-done | bytes 344096 | tf_op jit(solution)/shard_map/ppermute | solution.py:435
  72.6 0.6 copy-done.3
  73.8 1.5 %collective-permute-start.13 = (bf16[2,432,128]{2,1,0:T(8,128)(2,1)S(1)}, bf16[2,432,128]{2,1,0:T(8,128)(2,1)S(1)}, u32[]{:S(2)}, u32[]{:S(2)}) collective-permute-start(bf16[2,432,128]{2,1,0:T(8,128)(2,1)S(1)} %get-tuple-element.70.refs_5_), channel_id=1, source_target_pairs={{0,1},{1,0},{2,3},{3,2},{4,5},{5,4},{6,7},{7,6},{8,9},{9,8},{10,11... | collective-permute-start | bytes 663560 | tf_op jit(solution)/shard_map/ppermute | solution.py:435
  75.3 0.5 collective-permute-start.15
  75.8 4.0 %counts.2.refs_5_ = bf16[4,512,128]{2,1,0:T(8,128)(2,1)S(1)} custom-call(s32[2,4,8192]{2,1,0:T(4,128)S(1)} %bitcast.45, bf16[2,2,256,128]{3,2,1,0:T(8,128)(2,1)S(1)} %copy-done.3, bf16[2,2,256,128]{3,2,1,0:T(8,128)(2,1)S(1)} %collective-permute-done.2.refs_1_.rest_1_, bf16[2,2,256,128]{3,2,1,0:T(8,128)(2,1)S(1)} %collective-permute-done.refs_6_.refs_2_.rest_2_, ...), custom_call_target="tpu_custom_call" | custom-call | tf_op jit(solution)/shard_map/counts/pallas_call | solution.py:632
  79.8 1.3 collective-permute-done.14.refs_4_.refs_6_
  81.3 1.1 collective-permute-done.15.refs_5_.refs_3_
  82.6 1.5 %collective-permute-start.17 = (bf16[2,432,128]{2,1,0:T(8,128)(2,1)S(1)}, bf16[2,432,128]{2,1,0:T(8,128)(2,1)S(1)}, u32[]{:S(2)}, u32[]{:S(2)}) collective-permute-start(bf16[2,432,128]{2,1,0:T(8,128)(2,1)S(1)} %sums.18.rest_6_), channel_id=1, source_target_pairs={{0,8},{4,12},{8,0},{12,4},{16,24},{20,28},{24,16},{28,20},{1,9},{5... | collective-permute-start | bytes 663560 | tf_op jit(solution)/shard_map/ppermute | solution.py:432
  84.0 4.0 %counts.3.refs_5_ = bf16[4,512,128]{2,1,0:T(8,128)(2,1)S(1)} custom-call(s32[2,4,8192]{2,1,0:T(4,128)S(1)} %bitcast.46, bf16[2,2,256,128]{3,2,1,0:T(8,128)(2,1)S(1)} %copy-done.3, bf16[2,2,256,128]{3,2,1,0:T(8,128)(2,1)S(1)} %collective-permute-done.2.refs_1_.rest_1_, bf16[2,2,256,128]{3,2,1,0:T(8,128)(2,1)S(1)} %collective-permute-done.refs_6_.refs_2_.rest_2_, ...), custom_call_target="tpu_custom_call" | custom-call | tf_op jit(solution)/shard_map/counts/pallas_call | solution.py:632
  88.1 3.3 %collective-permute-done.17.refs_4_.refs_6_ = bf16[2,432,128]{2,1,0:T(8,128)(2,1)S(1)} collective-permute-done((bf16[2,432,128]{2,1,0:T(8,128)(2,1)S(1)}, bf16[2,432,128]{2,1,0:T(8,128)(2,1)S(1)}, u32[]{:S(2)}, u32[]{:S(2)}) %collective-permute-start.17) | collective-permute-done | bytes 221216 | tf_op jit(solution)/shard_map/ppermute | solution.py:432
  91.5 2.0 %collective-permute-done.16.refs_5_ = bf16[1,672,128]{2,1,0:T(8,128)(2,1)S(1)} collective-permute-done((bf16[1,672,128]{2,1,0:T(8,128)(2,1)S(1)}, bf16[1,672,128]{2,1,0:T(8,128)(2,1)S(1)}, u32[]{:S(2)}, u32[]{:S(2)}) %collective-permute-start.16) | collective-permute-done | bytes 172064 | tf_op jit(solution)/shard_map/ppermute | solution.py:432
  93.8 1.5 %collective-permute-start.20 = (bf16[1,672,128]{2,1,0:T(8,128)(2,1)S(1)}, bf16[1,672,128]{2,1,0:T(8,128)(2,1)S(1)}, u32[]{:S(2)}, u32[]{:S(2)}) collective-permute-start(bf16[1,672,128]{2,1,0:T(8,128)(2,1)S(1)} %sums.20.refs_2_), channel_id=1, source_target_pairs={{0,16},{4,20},{8,24},{12,28},{16,0},{20,4},{24,8},{28,12},{1,17},{... | collective-permute-start | bytes 516104 | tf_op jit(solution)/shard_map/ppermute | solution.py:432
  95.4 0.7 collective-permute-start.18
  96.1 0.5 collective-permute-start.19
  96.6 1.5 %collective-permute-start.21 = (bf16[1,432,128]{2,1,0:T(8,128)(2,1)S(1)}, bf16[1,432,128]{2,1,0:T(8,128)(2,1)S(1)}, u32[]{:S(2)}, u32[]{:S(2)}) collective-permute-start(bf16[1,432,128]{2,1,0:T(8,128)(2,1)S(1)} %sums.19.refs_6_), channel_id=1, source_target_pairs={{0,16},{4,20},{8,24},{12,28},{16,0},{20,4},{24,8},{28,12},{1,17},{... | collective-permute-start | bytes 331784 | tf_op jit(solution)/shard_map/ppermute | solution.py:432
  98.1 7.7 %collective-permute-done.21.refs_5_ = bf16[1,432,128]{2,1,0:T(8,128)(2,1)S(1)} collective-permute-done((bf16[1,432,128]{2,1,0:T(8,128)(2,1)S(1)}, bf16[1,432,128]{2,1,0:T(8,128)(2,1)S(1)}, u32[]{:S(2)}, u32[]{:S(2)}) %collective-permute-start.21) | collective-permute-done | bytes 110624 | tf_op jit(solution)/shard_map/ppermute | solution.py:432
  106.2 0.6 collective-permute-start.22
  106.8 0.7 collective-permute-start.23
  107.5 2.5 %collective-permute-start.27 = (bf16[1,432,128]{2,1,0:T(8,128)(2,1)S(1)}, bf16[1,432,128]{2,1,0:T(8,128)(2,1)S(1)}, u32[]{:S(2)}, u32[]{:S(2)}) collective-permute-start(bf16[1,432,128]{2,1,0:T(8,128)(2,1)S(1)} %sums.22), channel_id=1, source_target_pairs={{0,16},{4,20},{8,24},{12,28},{16,0},{20,4},{24,8},{28,12},{1,17},{... | collective-permute-start | bytes 331784 | tf_op jit(solution)/shard_map/ppermute | solution.py:432
  110.0 1.5 %collective-permute-done.22.refs_2_ = bf16[512,128]{1,0:T(8,128)(2,1)S(1)} collective-permute-done((bf16[512,128]{1,0:T(8,128)(2,1)S(1)}, bf16[512,128]{1,0:T(8,128)(2,1)S(1)}, u32[]{:S(2)}, u32[]{:S(2)}) %collective-permute-start.22) | collective-permute-done | bytes 131104 | tf_op jit(solution)/shard_map/ppermute | solution.py:435
  111.8 0.9 rows.1
  112.6 5.0 %collective-permute-done.27 = bf16[1,432,128]{2,1,0:T(8,128)(2,1)S(1)} collective-permute-done((bf16[1,432,128]{2,1,0:T(8,128)(2,1)S(1)}, bf16[1,432,128]{2,1,0:T(8,128)(2,1)S(1)}, u32[]{:S(2)}, u32[]{:S(2)}) %collective-permute-start.27) | collective-permute-done | bytes 110624 | tf_op jit(solution)/shard_map/ppermute | solution.py:432
  117.7 0.9 collective-permute-start.28
  118.6 1.3 %collective-permute-done.24.refs_1_ = bf16[2,672,128]{2,1,0:T(8,128)(2,1)S(1)} collective-permute-done((bf16[2,672,128]{2,1,0:T(8,128)(2,1)S(1)}, bf16[2,672,128]{2,1,0:T(8,128)(2,1)S(1)}, u32[]{:S(2)}, u32[]{:S(2)}) %collective-permute-start.24) | collective-permute-done | bytes 344096 | tf_op jit(solution)/shard_map/ppermute | solution.py:432
  120.4 3.3 %collective-permute-done.28.refs_5_ = bf16[2,432,128]{2,1,0:T(8,128)(2,1)S(1)} collective-permute-done((bf16[2,432,128]{2,1,0:T(8,128)(2,1)S(1)}, bf16[2,432,128]{2,1,0:T(8,128)(2,1)S(1)}, u32[]{:S(2)}, u32[]{:S(2)}) %collective-permute-start.28) | collective-permute-done | bytes 221216 | tf_op jit(solution)/shard_map/ppermute | solution.py:432
  123.7 1.5 %collective-permute-done.30.refs_7_ = bf16[2,432,128]{2,1,0:T(8,128)(2,1)S(1)} collective-permute-done((bf16[2,432,128]{2,1,0:T(8,128)(2,1)S(1)}, bf16[2,432,128]{2,1,0:T(8,128)(2,1)S(1)}, u32[]{:S(2)}, u32[]{:S(2)}) %collective-permute-start.30) | collective-permute-done | bytes 221216 | tf_op jit(solution)/shard_map/ppermute | solution.py:429
  125.2 2.2 %unpack.1 = (f32[544,256]{1,0:T(8,128)}, f32[64,2176]{1,0:T(8,128)}, f32[544,1024]{1,0:T(8,128)}, f32[256,1024]{1,0:T(8,128)}, f32[544]{0:T(1024)}, /*index=5*/f32[256]{0:T(256)}, f32[256]{0:T(256)}, f32[256]{0:T(256)}) custom-call(bf16[2,672,128]{2,1,0:T(8,128)(2,1)S(1)} %pad_maximum_fusion.refs_4_.refs_0_, ...), custom_call_target="tpu_custom_call" | custom-call | tf_op jit(solution)/shard_map/unpack/pallas_call | solution.py:659
  (64 shorter events, 5.1 us)
Async XLA Ops:
  12.5 17.1 %collective-permute-start.3 = (bf16[2,4,2,672,128]{4,3,2,1,0:T(8,128)(2,1)}, bf16[2,4,2,672,128]{4,3,2,1,0:T(8,128)(2,1)S(1)}, u32[]{:S(2)}, u32[]{:S(2)}) collective-permute-start(bf16[2,4,2,672,128]{4,3,2,1,0:T(8,128)(2,1)} %get-tuple-element.56), channel_id=1, source_target_pairs={{0,4},{4,0},{8,12},{12,8},{16,20},{20,16},{24,28},{28,24},{1,5},{5... | collective-permute-start | bytes 8257544 | tf_op jit(solution)/shard_map/ppermute | solution.py:429
  13.0 8.2 %copy-start.1 = (bf16[2176,256]{1,0:T(8,128)(2,1)S(1)}, bf16[2176,256]{1,0:T(8,128)(2,1)}, u32[]{:S(2)}) copy-start(bf16[2176,256]{1,0:T(8,128)(2,1)} %refs_2_.5) | copy-start | bytes 3342340
  13.0 8.2 %copy-start.8 = (bf16[256,128]{1,0:T(8,128)(2,1)S(1)}, bf16[256,128]{1,0:T(8,128)(2,1)}, u32[]{:S(2)}) copy-start(bf16[256,128]{1,0:T(8,128)(2,1)} %refs_0_.5) | copy-start | bytes 196612
  13.0 8.2 %copy-start.10 = (f32[24,128]{1,0:T(8,128)S(1)}, f32[24,128]{1,0:T(8,128)}, u32[]{:S(2)}) copy-start(f32[24,128]{1,0:T(8,128)} %get-tuple-element.60.refs_7_) | copy-start | bytes 36868
  21.2 1.2 copy-start.2
  22.4 1.0 copy-start.4
  23.5 1.2 copy-start.5
  24.7 1.2 copy-start.6
  26.0 0.9 copy-start.9
  26.9 2.7 %copy-start = (bf16[2,4,2,672,128]{4,3,2,1,0:T(8,128)(2,1)S(1)}, bf16[2,4,2,672,128]{4,3,2,1,0:T(8,128)(2,1)}, u32[]{:S(2)}) copy-start(bf16[2,4,2,672,128]{4,3,2,1,0:T(8,128)(2,1)} %get-tuple-element.55) | copy-start | bytes 8257540
  29.5 22.9 %collective-permute-start.7 = (bf16[2,4,2,432,128]{4,3,2,1,0:T(8,128)(2,1)S(1)}, bf16[2,4,2,432,128]{4,3,2,1,0:T(8,128)(2,1)S(1)}, u32[]{:S(2)}, u32[]{:S(2)}) collective-permute-start(bf16[2,4,2,432,128]{4,3,2,1,0:T(8,128)(2,1)S(1)} %get-tuple-element.65), channel_id=1, source_target_pairs={{0,4},{4,0},{8,12},{12,8},{16,20},{20,16},{24,28},{28,24},{1,5},{5... | collective-permute-start | bytes 5308424 | tf_op jit(solution)/shard_map/ppermute | solution.py:429
  29.6 5.0 %copy-start.13 = (bf16[2,2,256,128]{3,2,1,0:T(8,128)(2,1)S(1)}, bf16[2,2,256,128]{3,2,1,0:T(8,128)(2,1)}, u32[]{:S(2)}) copy-start(bf16[2,2,256,128]{3,2,1,0:T(8,128)(2,1)} %get-tuple-element.52) | copy-start | bytes 786436
  29.6 19.3 %copy-start.12 = (bf16[2,2,256,128]{3,2,1,0:T(8,128)(2,1)S(1)}, bf16[2,2,256,128]{3,2,1,0:T(8,128)(2,1)}, u32[]{:S(2)}) copy-start(bf16[2,2,256,128]{3,2,1,0:T(8,128)(2,1)} %get-tuple-element.53) | copy-start | bytes 786436
  30.1 23.7 %collective-permute-start.5 = (bf16[2,2,672,128]{3,2,1,0:T(8,128)(2,1)S(1)}, bf16[2,2,672,128]{3,2,1,0:T(8,128)(2,1)S(1)}, u32[]{:S(2)}, u32[]{:S(2)}) collective-permute-start(bf16[2,2,672,128]{3,2,1,0:T(8,128)(2,1)S(1)} %get-tuple-element.63.refs_4_), channel_id=1, source_target_pairs={{0,1},{1,0},{2,3},{3,2},{4,5},{5,4},{6,7},{7,6},{8,9},{9,8},{10,11... | collective-permute-start | bytes 2064392 | tf_op jit(solution)/shard_map/ppermute | solution.py:435
  33.1 20.7 %collective-permute-start.4 = (bf16[2,2,672,128]{3,2,1,0:T(8,128)(2,1)S(1)}, bf16[2,2,672,128]{3,2,1,0:T(8,128)(2,1)S(1)}, u32[]{:S(2)}, u32[]{:S(2)}) collective-permute-start(bf16[2,2,672,128]{3,2,1,0:T(8,128)(2,1)S(1)} %get-tuple-element.62.refs_5_), channel_id=1, source_target_pairs={{0,2},{1,3},{2,0},{3,1},{4,6},{5,7},{6,4},{7,5},{8,10},{9,11},{10,... | collective-permute-start | bytes 2064392 | tf_op jit(solution)/shard_map/ppermute | solution.py:435
  34.7 14.2 %collective-permute-start = (bf16[2,2,256,128]{3,2,1,0:T(8,128)(2,1)S(1)}, bf16[2,2,256,128]{3,2,1,0:T(8,128)(2,1)S(1)}, u32[]{:S(2)}, u32[]{:S(2)}) collective-permute-start(bf16[2,2,256,128]{3,2,1,0:T(8,128)(2,1)S(1)} %copy-done.13), channel_id=1, source_target_pairs={{0,16},{4,20},{8,24},{12,28},{16,0},{20,4},{24,8},{28,12},{1,17},{... | collective-permute-start | bytes 786440 | tf_op jit(solution)/shard_map/ppermute | solution.py:432
  48.9 10.1 %collective-permute-start.1 = (bf16[2,2,256,128]{3,2,1,0:T(8,128)(2,1)S(1)}, bf16[2,2,256,128]{3,2,1,0:T(8,128)(2,1)S(1)}, u32[]{:S(2)}, u32[]{:S(2)}) collective-permute-start(bf16[2,2,256,128]{3,2,1,0:T(8,128)(2,1)S(1)} %copy-done.12), channel_id=1, source_target_pairs={{0,24},{4,28},{8,16},{12,20},{16,8},{20,12},{24,0},{28,4},{1,25},{... | collective-permute-start | bytes 786440 | tf_op jit(solution)/shard_map/ppermute | solution.py:432
  52.7 13.1 %collective-permute-start.8 = (bf16[2,2,432,128]{3,2,1,0:T(8,128)(2,1)S(1)}, bf16[2,2,432,128]{3,2,1,0:T(8,128)(2,1)S(1)}, u32[]{:S(2)}, u32[]{:S(2)}) collective-permute-start(bf16[2,2,432,128]{3,2,1,0:T(8,128)(2,1)S(1)} %get-tuple-element.66), channel_id=1, source_target_pairs={{0,1},{1,0},{2,3},{3,2},{4,5},{5,4},{6,7},{7,6},{8,9},{9,8},{10,11... | collective-permute-start | bytes 1327112 | tf_op jit(solution)/shard_map/ppermute | solution.py:435
  53.3 5.7 %copy-start.11 = (bf16[2,2,256,128]{3,2,1,0:T(8,128)(2,1)S(1)}, bf16[2,2,256,128]{3,2,1,0:T(8,128)(2,1)}, u32[]{:S(2)}) copy-start(bf16[2,2,256,128]{3,2,1,0:T(8,128)(2,1)} %get-tuple-element.54) | copy-start | bytes 786436
  53.3 13.1 %collective-permute-start.9 = (bf16[2,2,432,128]{3,2,1,0:T(8,128)(2,1)S(1)}, bf16[2,2,432,128]{3,2,1,0:T(8,128)(2,1)S(1)}, u32[]{:S(2)}, u32[]{:S(2)}) collective-permute-start(bf16[2,2,432,128]{3,2,1,0:T(8,128)(2,1)S(1)} %get-tuple-element.67), channel_id=1, source_target_pairs={{0,2},{1,3},{2,0},{3,1},{4,6},{5,7},{6,4},{7,5},{8,10},{9,11},{10,... | collective-permute-start | bytes 1327112 | tf_op jit(solution)/shard_map/ppermute | solution.py:435
  54.2 18.0 %collective-permute-start.10 = (bf16[2,672,128]{2,1,0:T(8,128)(2,1)S(1)}, bf16[2,672,128]{2,1,0:T(8,128)(2,1)S(1)}, u32[]{:S(2)}, u32[]{:S(2)}) collective-permute-start(bf16[2,672,128]{2,1,0:T(8,128)(2,1)S(1)} %get-tuple-element.68.refs_6_), channel_id=1, source_target_pairs={{0,2},{1,3},{2,0},{3,1},{4,6},{5,7},{6,4},{7,5},{8,10},{9,11},{10,... | collective-permute-start | bytes 1032200 | tf_op jit(solution)/shard_map/ppermute | solution.py:435
  55.8 16.4 %collective-permute-start.6 = (bf16[2,672,128]{2,1,0:T(8,128)(2,1)S(1)}, bf16[2,672,128]{2,1,0:T(8,128)(2,1)S(1)}, u32[]{:S(2)}, u32[]{:S(2)}) collective-permute-start(bf16[2,672,128]{2,1,0:T(8,128)(2,1)S(1)} %get-tuple-element.64.refs_7_), channel_id=1, source_target_pairs={{0,1},{1,0},{2,3},{3,2},{4,5},{5,4},{6,7},{7,6},{8,9},{9,8},{10,11... | collective-permute-start | bytes 1032200 | tf_op jit(solution)/shard_map/ppermute | solution.py:435
  59.0 13.6 %collective-permute-start.2 = (bf16[2,2,256,128]{3,2,1,0:T(8,128)(2,1)S(1)}, bf16[2,2,256,128]{3,2,1,0:T(8,128)(2,1)S(1)}, u32[]{:S(2)}, u32[]{:S(2)}) collective-permute-start(bf16[2,2,256,128]{3,2,1,0:T(8,128)(2,1)S(1)} %copy-done.11), channel_id=1, source_target_pairs={{0,8},{4,12},{8,0},{12,4},{16,24},{20,28},{24,16},{28,20},{1,9},{5... | collective-permute-start | bytes 786440 | tf_op jit(solution)/shard_map/ppermute | solution.py:432
  72.2 1.0 copy-start.3
  72.2 3.6 %copy-start.7 = (s32[2,8192,4]{1,2,0:T(4,128)S(1)}, s32[2,8192,4]{1,2,0:T(4,128)}, u32[]{:S(2)}) copy-start(s32[2,8192,4]{1,2,0:T(4,128)} %param.23) | copy-start | bytes 786436
  72.5 8.6 %collective-permute-start.14 = (bf16[2,672,128]{2,1,0:T(8,128)(2,1)S(1)}, bf16[2,672,128]{2,1,0:T(8,128)(2,1)S(1)}, u32[]{:S(2)}, u32[]{:S(2)}) collective-permute-start(bf16[2,672,128]{2,1,0:T(8,128)(2,1)S(1)} %sums.16.refs_4_), channel_id=1, source_target_pairs={{0,8},{4,12},{8,0},{12,4},{16,24},{20,28},{24,16},{28,20},{1,9},{5... | collective-permute-start | bytes 1032200 | tf_op jit(solution)/shard_map/ppermute | solution.py:432
  73.2 2.6 %collective-permute-start.11 = (bf16[2,2,256,128]{3,2,1,0:T(8,128)(2,1)S(1)}, bf16[2,2,256,128]{3,2,1,0:T(8,128)(2,1)S(1)}, u32[]{:S(2)}, u32[]{:S(2)}) collective-permute-start(bf16[2,2,256,128]{3,2,1,0:T(8,128)(2,1)S(1)} %get-tuple-element.71.rest_6_), channel_id=1, source_target_pairs={{0,4},{4,0},{8,12},{12,8},{16,20},{20,16},{24,28},{28,24},{1,5},{5... | collective-permute-start | bytes 786440 | tf_op jit(solution)/shard_map/ppermute | solution.py:429
  73.3 2.5 %collective-permute-start.12 = (bf16[2,2,256,128]{3,2,1,0:T(8,128)(2,1)S(1)}, bf16[2,2,256,128]{3,2,1,0:T(8,128)(2,1)S(1)}, u32[]{:S(2)}, u32[]{:S(2)}) collective-permute-start(bf16[2,2,256,128]{3,2,1,0:T(8,128)(2,1)S(1)} %get-tuple-element.72), channel_id=1, source_target_pairs={{0,4},{4,0},{8,12},{12,8},{16,20},{20,16},{24,28},{28,24},{1,5},{5... | collective-permute-start | bytes 786440 | tf_op jit(solution)/shard_map/ppermute | solution.py:429
  73.8 7.5 %collective-permute-start.13 = (bf16[2,432,128]{2,1,0:T(8,128)(2,1)S(1)}, bf16[2,432,128]{2,1,0:T(8,128)(2,1)S(1)}, u32[]{:S(2)}, u32[]{:S(2)}) collective-permute-start(bf16[2,432,128]{2,1,0:T(8,128)(2,1)S(1)} %get-tuple-element.70.refs_5_), channel_id=1, source_target_pairs={{0,1},{1,0},{2,3},{3,2},{4,5},{5,4},{6,7},{7,6},{8,9},{9,8},{10,11... | collective-permute-start | bytes 663560 | tf_op jit(solution)/shard_map/ppermute | solution.py:435
  75.3 7.1 %collective-permute-start.15 = (bf16[2,432,128]{2,1,0:T(8,128)(2,1)S(1)}, bf16[2,432,128]{2,1,0:T(8,128)(2,1)S(1)}, u32[]{:S(2)}, u32[]{:S(2)}) collective-permute-start(bf16[2,432,128]{2,1,0:T(8,128)(2,1)S(1)} %get-tuple-element.69.refs_4_), channel_id=1, source_target_pairs={{0,2},{1,3},{2,0},{3,1},{4,6},{5,7},{6,4},{7,5},{8,10},{9,11},{10,... | collective-permute-start | bytes 663560 | tf_op jit(solution)/shard_map/ppermute | solution.py:435
  82.6 8.8 %collective-permute-start.17 = (bf16[2,432,128]{2,1,0:T(8,128)(2,1)S(1)}, bf16[2,432,128]{2,1,0:T(8,128)(2,1)S(1)}, u32[]{:S(2)}, u32[]{:S(2)}) collective-permute-start(bf16[2,432,128]{2,1,0:T(8,128)(2,1)S(1)} %sums.18.rest_6_), channel_id=1, source_target_pairs={{0,8},{4,12},{8,0},{12,4},{16,24},{20,28},{24,16},{28,20},{1,9},{5... | collective-permute-start | bytes 663560 | tf_op jit(solution)/shard_map/ppermute | solution.py:432
  84.0 9.5 %collective-permute-start.16 = (bf16[1,672,128]{2,1,0:T(8,128)(2,1)S(1)}, bf16[1,672,128]{2,1,0:T(8,128)(2,1)S(1)}, u32[]{:S(2)}, u32[]{:S(2)}) collective-permute-start(bf16[1,672,128]{2,1,0:T(8,128)(2,1)S(1)} %sums.17.refs_4_), channel_id=1, source_target_pairs={{0,16},{4,20},{8,24},{12,28},{16,0},{20,4},{24,8},{28,12},{1,17},{... | collective-permute-start | bytes 516104 | tf_op jit(solution)/shard_map/ppermute | solution.py:432
  93.8 12.2 %collective-permute-start.20 = (bf16[1,672,128]{2,1,0:T(8,128)(2,1)S(1)}, bf16[1,672,128]{2,1,0:T(8,128)(2,1)S(1)}, u32[]{:S(2)}, u32[]{:S(2)}) collective-permute-start(bf16[1,672,128]{2,1,0:T(8,128)(2,1)S(1)} %sums.20.refs_2_), channel_id=1, source_target_pairs={{0,16},{4,20},{8,24},{12,28},{16,0},{20,4},{24,8},{28,12},{1,17},{... | collective-permute-start | bytes 516104 | tf_op jit(solution)/shard_map/ppermute | solution.py:432
  95.4 10.6 %collective-permute-start.18 = (bf16[2,512,128]{2,1,0:T(8,128)(2,1)S(1)}, bf16[2,512,128]{2,1,0:T(8,128)(2,1)S(1)}, u32[]{:S(2)}, u32[]{:S(2)}) collective-permute-start(bf16[2,512,128]{2,1,0:T(8,128)(2,1)S(1)} %get-tuple-element.73.refs_6_), channel_id=1, source_target_pairs={{0,1},{1,0},{2,3},{3,2},{4,5},{5,4},{6,7},{7,6},{8,9},{9,8},{10,11... | collective-permute-start | bytes 786440 | tf_op jit(solution)/shard_map/ppermute | solution.py:435
  96.1 9.9 %collective-permute-start.19 = (bf16[2,512,128]{2,1,0:T(8,128)(2,1)S(1)}, bf16[2,512,128]{2,1,0:T(8,128)(2,1)S(1)}, u32[]{:S(2)}, u32[]{:S(2)}) collective-permute-start(bf16[2,512,128]{2,1,0:T(8,128)(2,1)S(1)} %get-tuple-element.74.refs_7_), channel_id=1, source_target_pairs={{0,2},{1,3},{2,0},{3,1},{4,6},{5,7},{6,4},{7,5},{8,10},{9,11},{10,... | collective-permute-start | bytes 786440 | tf_op jit(solution)/shard_map/ppermute | solution.py:435
  96.6 9.2 %collective-permute-start.21 = (bf16[1,432,128]{2,1,0:T(8,128)(2,1)S(1)}, bf16[1,432,128]{2,1,0:T(8,128)(2,1)S(1)}, u32[]{:S(2)}, u32[]{:S(2)}) collective-permute-start(bf16[1,432,128]{2,1,0:T(8,128)(2,1)S(1)} %sums.19.refs_6_), channel_id=1, source_target_pairs={{0,16},{4,20},{8,24},{12,28},{16,0},{20,4},{24,8},{28,12},{1,17},{... | collective-permute-start | bytes 331784 | tf_op jit(solution)/shard_map/ppermute | solution.py:432
  106.2 5.2 %collective-permute-start.22 = (bf16[512,128]{1,0:T(8,128)(2,1)S(1)}, bf16[512,128]{1,0:T(8,128)(2,1)S(1)}, u32[]{:S(2)}, u32[]{:S(2)}) collective-permute-start(bf16[512,128]{1,0:T(8,128)(2,1)S(1)} %get-tuple-element.76.refs_6_), channel_id=1, source_target_pairs={{0,2},{1,3},{2,0},{3,1},{4,6},{5,7},{6,4},{7,5},{8,10},{9,11},{10,... | collective-permute-start | bytes 393224 | tf_op jit(solution)/shard_map/ppermute | solution.py:435
  106.8 5.0 %collective-permute-start.23 = (bf16[512,128]{1,0:T(8,128)(2,1)S(1)}, bf16[512,128]{1,0:T(8,128)(2,1)S(1)}, u32[]{:S(2)}, u32[]{:S(2)}) collective-permute-start(bf16[512,128]{1,0:T(8,128)(2,1)S(1)} %get-tuple-element.77.refs_7_), channel_id=1, source_target_pairs={{0,1},{1,0},{2,3},{3,2},{4,5},{5,4},{6,7},{7,6},{8,9},{9,8},{10,11... | collective-permute-start | bytes 393224 | tf_op jit(solution)/shard_map/ppermute | solution.py:435
  107.5 12.4 %collective-permute-start.24 = (bf16[2,672,128]{2,1,0:T(8,128)(2,1)S(1)}, bf16[2,672,128]{2,1,0:T(8,128)(2,1)S(1)}, u32[]{:S(2)}, u32[]{:S(2)}) collective-permute-start(bf16[2,672,128]{2,1,0:T(8,128)(2,1)S(1)} %pad_maximum_fusion.refs_4_.refs_0_), channel_id=1, source_target_pairs={{0,8},{4,12},{8,0},{12,4},{16,24},{20,28},{24,16},{28,20},{1,9},{5... | collective-permute-start | bytes 1032200 | tf_op jit(solution)/shard_map/ppermute | solution.py:432
  107.5 10.2 %collective-permute-start.27 = (bf16[1,432,128]{2,1,0:T(8,128)(2,1)S(1)}, bf16[1,432,128]{2,1,0:T(8,128)(2,1)S(1)}, u32[]{:S(2)}, u32[]{:S(2)}) collective-permute-start(bf16[1,432,128]{2,1,0:T(8,128)(2,1)S(1)} %sums.22), channel_id=1, source_target_pairs={{0,16},{4,20},{8,24},{12,28},{16,0},{20,4},{24,8},{28,12},{1,17},{... | collective-permute-start | bytes 331784 | tf_op jit(solution)/shard_map/ppermute | solution.py:432
  117.7 6.0 %collective-permute-start.28 = (bf16[2,432,128]{2,1,0:T(8,128)(2,1)S(1)}, bf16[2,432,128]{2,1,0:T(8,128)(2,1)S(1)}, u32[]{:S(2)}, u32[]{:S(2)}) collective-permute-start(bf16[2,432,128]{2,1,0:T(8,128)(2,1)S(1)} %pad_maximum_fusion.1.refs_4_), channel_id=1, source_target_pairs={{0,8},{4,12},{8,0},{12,4},{16,24},{20,28},{24,16},{28,20},{1,9},{5... | collective-permute-start | bytes 663560 | tf_op jit(solution)/shard_map/ppermute | solution.py:432
  118.6 5.1 %collective-permute-start.25 = (bf16[2,672,128]{2,1,0:T(8,128)(2,1)S(1)}, bf16[2,672,128]{2,1,0:T(8,128)(2,1)S(1)}, u32[]{:S(2)}, u32[]{:S(2)}) collective-permute-start(bf16[2,672,128]{2,1,0:T(8,128)(2,1)S(1)} %pad_maximum_fusion.refs_4_.refs_0_), channel_id=1, source_target_pairs={{0,4},{4,0},{8,12},{12,8},{16,20},{20,16},{24,28},{28,24},{1,5},{5... | collective-permute-start | bytes 1032200 | tf_op jit(solution)/shard_map/ppermute | solution.py:429
  119.9 5.3 %collective-permute-start.26 = (bf16[2,672,128]{2,1,0:T(8,128)(2,1)S(1)}, bf16[2,672,128]{2,1,0:T(8,128)(2,1)S(1)}, u32[]{:S(2)}, u32[]{:S(2)}) collective-permute-start(bf16[2,672,128]{2,1,0:T(8,128)(2,1)S(1)} %collective-permute-done.24.refs_1_), channel_id=1, source_target_pairs={{0,4},{4,0},{8,12},{12,8},{16,20},{20,16},{24,28},{28,24},{1,5},{5... | collective-permute-start | bytes 1032200 | tf_op jit(solution)/shard_map/ppermute | solution.py:429
  119.9 3.8 %collective-permute-start.29 = (bf16[2,432,128]{2,1,0:T(8,128)(2,1)S(1)}, bf16[2,432,128]{2,1,0:T(8,128)(2,1)S(1)}, u32[]{:S(2)}, u32[]{:S(2)}) collective-permute-start(bf16[2,432,128]{2,1,0:T(8,128)(2,1)S(1)} %pad_maximum_fusion.1.refs_4_), channel_id=1, source_target_pairs={{0,4},{4,0},{8,12},{12,8},{16,20},{20,16},{24,28},{28,24},{1,5},{5... | collective-permute-start | bytes 663560 | tf_op jit(solution)/shard_map/ppermute | solution.py:429
  123.7 1.5 %collective-permute-start.30 = (bf16[2,432,128]{2,1,0:T(8,128)(2,1)S(1)}, bf16[2,432,128]{2,1,0:T(8,128)(2,1)S(1)}, u32[]{:S(2)}, u32[]{:S(2)}) collective-permute-start(bf16[2,432,128]{2,1,0:T(8,128)(2,1)S(1)} %collective-permute-done.28.refs_5_), channel_id=1, source_target_pairs={{0,4},{4,0},{8,12},{12,8},{16,20},{20,16},{24,28},{28,24},{1,5},{5... | collective-permute-start | bytes 663560 | tf_op jit(solution)/shard_map/ppermute | solution.py:429

commit v7 on v6

--- a/solution.py
+++ b/solution.py
@@ -72,14 +72,18 @@
 
 
 class Loads:
-    def __init__(self, sources, targets, sems):
+    def __init__(self, sources, targets, sems, first):
         self.copies = [
             pltpu.make_async_copy(source, target, sems.at[at])
             for at, (source, target) in enumerate(zip(sources, targets))
         ]
-        self.targets = targets
+        self.targets, self.first = targets, first
         self.ready = set()
-        for copy in self.copies:
+        for copy in self.copies[:first]:
+            copy.start()
+
+    def more(self):
+        for copy in self.copies[self.first :]:
             copy.start()
 
     def __call__(self, at):
@@ -97,11 +101,13 @@
     sources, outs, targets = refs[:11], refs[11:16], refs[16:27]
     halves, thirds, sems = refs[27:]
     send, keep, crossed_t_out, first_out, small = outs
-    load = Loads(sources, targets, sems)
+    load = Loads(sources, targets, sems, 5)
     core, row_pos, table_pos = position()
     places = places_of(lax.div(table_pos, 2), 2 * send.shape[2])
     stacked = jnp.concatenate([load(0), load(1)], axis=1)
-    reduced = matmul(stacked, load(2)).astype(bf16)
+    cross_down = load(2)
+    load.more()
+    reduced = matmul(stacked, cross_down).astype(bf16)
     widened = matmul(reduced, load(3)) + as_row(load(4))
     wide = stacked.astype(f32)
     crossed = (wide * widened + wide).astype(bf16)
@@ -144,24 +150,26 @@
 
 
 def middle_kernel(n_z, *refs):
-    sources, delta_first = refs[:6], refs[6]
-    widened_out, reduced_out = refs[7:9]
-    pooled_outs = refs[9 : 9 + n_z]
-    rest = refs[9 + n_z :]
-    targets = rest[:6]
-    by_group, sems = rest[6:]
-    load = Loads(sources, targets, sems)
-    core, _, table_pos = position()
+    sources, send, keep = refs[:9], refs[9], refs[10]
+    pooled_outs = refs[11 : 11 + n_z]
+    rest = refs[11 + n_z :]
+    targets = rest[:9]
+    by_group, wide_delta, half_delta, sixths, small, sems = rest[9:]
+    load = Loads(sources, targets, sems, 6)
+    core, row_pos, table_pos = position()
     z_pos = lax.div(table_pos, 2)
+    places = places_of(z_pos, 2 * send.shape[2])
     stacked = jnp.concatenate([load(0), load(1)], axis=1)
-    cross_down, cross_up = load(2), load(3)
+    cross_down = load(2)
+    load.more()
     reduced = matmul(stacked, cross_down).astype(bf16)
+    cross_up = load(3)
     widened = matmul(reduced, cross_up) + as_row(load(4))
-    delta_crossed = matmul_rt(delta_first[...], load(5))
+    delta_first = load(5)
+    delta_crossed = matmul_rt(delta_first, load(6))
     delta_widened = (delta_crossed * stacked.astype(f32)).astype(bf16)
-    widened_out[...] = delta_widened
+    wide_delta[...] = delta_widened
     delta_reduced = matmul_rt(delta_widened, cross_up).astype(bf16)
-    reduced_out[...] = delta_reduced
     delta_stacked = delta_crossed * (widened + 1.0) + matmul_rt(delta_reduced, cross_down)
     width = targets[0].shape[1]
     per_group = by_group.shape[2]
@@ -174,36 +182,24 @@
         pooled_outs[which][0] = by_group[z_pos ^ which, core]
         pooled_outs[which][1] = by_group[z_pos ^ which, 1 - core]
 
-
-def back_kernel(*refs):
-    dense_feat, pooled, cross_down, crossed_t, delta_first, delta_widened, delta_reduced = refs[:7]
-    small_in = refs[7]
-    send, keep = refs[8:10]
-    half_delta, sixths, small = refs[10:]
-    core, row_pos, table_pos = position()
-    n_row = send.shape[1]
-    places = places_of(lax.div(table_pos, 2), 2 * send.shape[2])
-    rank = delta_reduced.shape[1]
-    feat = delta_widened.shape[1]
+    n_row, rank, feat = send.shape[1], delta_reduced.shape[1], delta_widened.shape[1]
     hid = delta_first.shape[1]
     part = hid // 2 - sixths.shape[2]
     half_delta[0] = delta_reduced[:, : rank // 2]
     half_delta[1] = delta_reduced[:, rank // 2 :]
     sixths[0] = delta_first[:, part : hid // 2]
     sixths[1] = delta_first[:, hid // 2 + part :]
-    put_rows(small, 24, jnp.sum(delta_widened[...].astype(f32), axis=0, keepdims=True))
-    small[0:24, :] = small_in[...]
+    put_rows(small, 24, jnp.sum(delta_widened.astype(f32), axis=0, keepdims=True))
+    small[0:24, :] = load(8)
     small[41:48, :] = jnp.zeros((7, LANES), f32)
     sums = jnp.concatenate([small[...]] * n_row, axis=0)
-    stacked = jnp.concatenate([dense_feat[...], pooled[...]], axis=1)
-    reduced_t = matmul(stacked, cross_down[...]).astype(bf16).T
-    stacked_t = stacked.T
+    crossed_t, reduced_t, stacked_t = load(7), reduced.T, stacked.T
     for ref, who in ((send, 1 - core), (keep, core)):
-        offset = put_blocks(ref, row_pos, places, 0, matmul(crossed_t[...], sixths[who]))
+        offset = put_blocks(ref, row_pos, places, 0, matmul(crossed_t, sixths[who]))
         offset = put_blocks(ref, row_pos, places, offset, matmul(stacked_t, half_delta[who]))
         start = pl.multiple_of(who * (feat - SPAN), LANES)
         offset = put_blocks(
-            ref, row_pos, places, offset, matmul(reduced_t, delta_widened[:, pl.ds(start, SPAN)])
+            ref, row_pos, places, offset, matmul(reduced_t, wide_delta[:, pl.ds(start, SPAN)])
         )
         offset = put_blocks(ref, row_pos, places, offset, sums)
         tail = 2 * ref.shape[2] * ref.shape[3] - offset
@@ -480,21 +476,34 @@
     )(*sources)
     got1 = swap_cores(send1)
 
-    sources = (dense_feat, pooled, cross_down, cross_up, cross_bias, w_hidden1)
-    outs = call(
+    sources = (
+        dense_feat,
+        pooled,
+        cross_down,
+        cross_up,
+        cross_bias,
+        delta_first,
+        w_hidden1,
+        crossed_t,
+        small,
+    )
+    send2, keep2, *pooled_out = call(
         functools.partial(middle_kernel, n_z),
-        [wide(batch, feat), wide(batch, rank)] + [wide(2, tab_grp, batch, width)] * n_z,
+        [packed(rows_back)] * 2 + [wide(2, tab_grp, batch, width)] * n_z,
         held_like(sources)
         + [
             pltpu.VMEM((n_z, 2, tab_grp, batch, width), bf16),
+            pltpu.VMEM((batch, feat), bf16),
+            pltpu.VMEM((2, batch, rank // 2), bf16),
+            pltpu.VMEM((2, batch, late), bf16),
+            pltpu.VMEM((48, LANES), f32),
             pltpu.SemaphoreType.DMA((len(sources),)),
         ],
-        [hbm] * len(sources) + [vmem],
+        [hbm] * len(sources),
         "middle",
         60,
-    )(*sources, delta_first)
-    delta_widened, delta_reduced = outs[:2]
-    pooled_out = outs[2:]
+    )(*sources)
+    got2 = swap_cores(send2)
 
     low_first = tuple(range(row_bits))
     high_first = low_first[::-1]
@@ -575,33 +584,8 @@
             self.pieces = [self.own, far, swap_cores(self.own), swap_cores(far)]
             return [self.own]
 
-    send2, keep2 = call(
-        back_kernel,
-        [packed(rows_back)] * 2,
-        [
-            pltpu.VMEM((2, batch, rank // 2), bf16),
-            pltpu.VMEM((2, batch, late), bf16),
-            pltpu.VMEM((48, LANES), f32),
-        ],
-        [vmem] * 8,
-        "back",
-        36,
-    )(
-        dense_feat,
-        pooled,
-        cross_down,
-        crossed_t,
-        delta_first,
-        delta_widened,
-        delta_reduced,
-        small,
-    )
-
-    got2 = swap_cores(send2)
-
     one, two = Dense(keep1, got1), Dense(keep2, got2)
-    last = one.row_step(0, [keep2])
-    two.row_step(0, last)
+    one.row_step(0, [keep2])
     values, chain = {0: pooled_out[0]}, [n_z // 2]
     chain += [which for which in range(n_z - 1, 0, -1) if which != n_z // 2]
     for at, which in enumerate(chain):
@@ -612,10 +596,13 @@
     last = [values[chain[0]]]
     for at in range(1, row_bits):
         last = one.row_step(at, last)
+    last = two.row_step(0, last)
+    last = one.z_step(0, last)
+    for stage in range(1, z_bits):
+        last = one.z_step(stage, last)
     last = [*last, values[chain[min(1, len(chain) - 1)]]]
     for at in range(1, row_bits):
         last = two.row_step(at, last)
-    last = one.z_step(0, last)
     values = [values[which] for which in range(n_z)]
     far_values = call(
         functools.partial(select_kernel, n_z),
@@ -642,17 +629,15 @@
         shares.append(Halving([sums], high_first if table % 2 else low_first))
         last = [sums]
         if table == 0:
-            for stage in range(1, z_bits):
-                last = one.z_step(stage, last)
             last = two.z_step(0, last)
+    last = one.z_own(last)
+    last = row_step(shares, 0, last)
     for stage in range(1, z_bits):
         last = two.z_step(stage, last)
-    last = one.z_own(last)
-    last = row_step(shares, 0, last)
+    for at in range(1, row_bits):
+        last = row_step(shares, at, last)
     last = two.z_own(last)
     last = one.z_back(last)
-    for at in range(1, row_bits):
-        last = row_step(shares, at, last)
     row_grads = sum_rows([share.items for share in shares], last)
     two.z_back([row_grads])
 

time: 128 us -> 125 us (0.977)
  local copies, waits for them, and re-layouts: 6.28 us -> 3.28 us
  waiting for transfers between devices: 50.2 us -> 47.2 us
  starting transfers between devices: 33.3 us -> 36.2 us
    unnamed x28 -> x18, local copies, waits for them, and re-layouts: 6.28 us -> 3.28 us
    ppermute x11, starting transfers between devices: 18.4 us -> 21 us  [swap_z(): lax.ppermute(value, 'table', [(at, at ^ 2 * which) for at in range(n_tabl...]
    ppermute x12, waiting for transfers between devices: 11.4 us -> 9.41 us  [swap_row(): lax.ppermute(value, 'row', [(at, at ^ 1 << bit) for at in range(n_row)])]
    pallas_call x2 -> x1, Pallas kernels: 10.7 us -> 10.5 us  [local(): call(functools.partial(middle_kernel, n_z), [packed(rows_back)] * 2 + [wi...]
  transfers between devices with their start and end apart: 31 -> 31, of which waited for: 16 -> 14; matrix products, arithmetic and copies ran while one was open for 0% -> 0% of each run, Pallas kernels for 17% -> 18%
where the time goes in v7:
time: 125 us
  waiting for transfers between devices  47.2 us (38%)
  Pallas kernels  37.1 us (30%)
  starting transfers between devices  36.2 us (29%)
  local copies, waits for them, and re-layouts  3.28 us (3%)
    ppermute x11, waiting for transfers between devices, swap_z(): lax.ppermute(value, 'table', [(at, at ^ 2 * which) for at in range(n_tabl...  36.3 us
    ppermute x11, starting transfers between devices, swap_z(): lax.ppermute(value, 'table', [(at, at ^ 2 * which) for at in range(n_tabl...  21 us
    ppermute x12, starting transfers between devices, swap_row(): lax.ppermute(value, 'row', [(at, at ^ 1 << bit) for at in range(n_row)])  13.4 us
    pallas_call x1, Pallas kernels, local(): call(front_kernel, [packed(rows_front)] * 2 + [wide(feat, batch), wide(ba...  12.5 us
    pallas_call x1, Pallas kernels, local(): call(functools.partial(middle_kernel, n_z), [packed(rows_back)] * 2 + [wi...  10.5 us
    ppermute x12, waiting for transfers between devices, swap_row(): lax.ppermute(value, 'row', [(at, at ^ 1 << bit) for at in range(n_row)])  9.41 us
    pallas_call x2, Pallas kernels, local(): pl.pallas_call(functools.partial(count_kernel, n_row, table, hot, n_z), o...  8.05 us
    unnamed x18, local copies, waits for them, and re-layouts  3.28 us
  transfers between devices with their start and end apart: 31, of which 14 were waited for; matrix products, arithmetic and copies ran while one was open for 0% of the time, Pallas kernels for 18%

profile of v7, /device:TPU:0, one launch (start us, length us, event | category | flops | bytes accessed | tf_op | source)
XLA Modules:
  0.0 124.7 jit_solution(17911897384721192092)
XLA Ops:
  0.6 12.5 %front.1 = (bf16[2,4,2,672,128]{4,3,2,1,0:T(8,128)(2,1)}, bf16[2,4,2,672,128]{4,3,2,1,0:T(8,128)(2,1)}, bf16[2176,256]{1,0:T(8,128)(2,1)}, bf16[256,1024]{1,0:T(8,128)(2,1)}, f32[24,128]{1,0:T(8,128)}) custom-call(bf16[256,128]{1,0:T(8,128)(2,1)} %refs_0_.3, bf16[256,2048]{1,0:T(8,128)(2,1)} %refs_1_.3, bf16[2176,256]{1,0:T(8,128)(2,1)} %refs_2_.3, ...), custom_call_target="tpu_custom_call" | custom-call | tf_op jit(solution)/shard_map/front/pallas_call | solution.py:463
  13.1 0.5 collective-permute-start.4
  13.6 10.5 %middle.1 = (bf16[2,4,2,432,128]{4,3,2,1,0:T(8,128)(2,1)}, bf16[2,4,2,432,128]{4,3,2,1,0:T(8,128)(2,1)}, bf16[2,2,256,128]{3,2,1,0:T(8,128)(2,1)}, bf16[2,2,256,...) custom-call(bf16[256,128]{1,0:T(8,128)(2,1)} %refs_0_.3, ...), custom_call_target="tpu_custom_call" | custom-call | tf_op jit(solution)/shard_map/middle/pallas_call | solution.py:490
  24.3 1.8 %copy-done = bf16[2,4,2,672,128]{4,3,2,1,0:T(8,128)(2,1)S(1)} copy-done((bf16[2,4,2,672,128]{4,3,2,1,0:T(8,128)(2,1)S(1)}, bf16[2,4,2,672,128]{4,3,2,1,0:T(8,128)(2,1)}, u32[]{:S(2)}) %copy-start) | copy-done | bytes 2752536
  26.1 1.5 %copy-done.2 = bf16[2,4,2,432,128]{4,3,2,1,0:T(8,128)(2,1)S(1)} copy-done((bf16[2,4,2,432,128]{4,3,2,1,0:T(8,128)(2,1)S(1)}, bf16[2,4,2,432,128]{4,3,2,1,0:T(8,128)(2,1)}, u32[]{:S(2)}) %copy-start.2) | copy-done | bytes 1769496
  27.6 0.5 sums.12
  28.1 3.0 %collective-permute-start.5 = (bf16[2,2,672,128]{3,2,1,0:T(8,128)(2,1)S(1)}, bf16[2,2,672,128]{3,2,1,0:T(8,128)(2,1)S(1)}, u32[]{:S(2)}, u32[]{:S(2)}) collective-permute-start(bf16[2,2,672,128]{3,2,1,0:T(8,128)(2,1)S(1)} %get-tuple-element.59), channel_id=1, source_target_pairs={{0,1},{1,0},{2,3},{3,2},{4,5},{5,4},{6,7},{7,6},{8,9},{9,8},{10,11... | collective-permute-start | bytes 2064392 | tf_op jit(solution)/shard_map/ppermute | solution.py:431
  31.1 1.5 %collective-permute-start.6 = (bf16[2,2,672,128]{3,2,1,0:T(8,128)(2,1)S(1)}, bf16[2,2,672,128]{3,2,1,0:T(8,128)(2,1)S(1)}, u32[]{:S(2)}, u32[]{:S(2)}) collective-permute-start(bf16[2,2,672,128]{3,2,1,0:T(8,128)(2,1)S(1)} %get-tuple-element.60), channel_id=1, source_target_pairs={{0,2},{1,3},{2,0},{3,1},{4,6},{5,7},{6,4},{7,5},{8,10},{9,11},{10,... | collective-permute-start | bytes 2064392 | tf_op jit(solution)/shard_map/ppermute | solution.py:431
  32.6 2.6 %collective-permute-start = (bf16[2,2,256,128]{3,2,1,0:T(8,128)(2,1)S(1)}, bf16[2,2,256,128]{3,2,1,0:T(8,128)(2,1)S(1)}, u32[]{:S(2)}, u32[]{:S(2)}) collective-permute-start(bf16[2,2,256,128]{3,2,1,0:T(8,128)(2,1)S(1)} %copy-done.8), channel_id=1, source_target_pairs={{0,16},{4,20},{8,24},{12,28},{16,0},{20,4},{24,8},{28,12},{1,17},{... | collective-permute-start | bytes 786440 | tf_op jit(solution)/shard_map/ppermute | solution.py:428
  35.2 11.6 %collective-permute-done.refs_6_.refs_2_.rest_2_ = bf16[2,2,256,128]{3,2,1,0:T(8,128)(2,1)S(1)} collective-permute-done((bf16[2,2,256,128]{3,2,1,0:T(8,128)(2,1)S(1)}, bf16[2,2,256,128]{3,2,1,0:T(8,128)(2,1)S(1)}, u32[]{:S(2)}, u32[]{:S(2)}) %collective-permute-start) | collective-permute-done | bytes 262176 | tf_op jit(solution)/shard_map/ppermute | solution.py:428
  46.8 1.4 %collective-permute-done.6.refs_5_.refs_8_.refs_2_ = bf16[2,2,672,128]{3,2,1,0:T(8,128)(2,1)S(1)} collective-permute-done((bf16[2,2,672,128]{3,2,1,0:T(8,128)(2,1)S(1)}, bf16[2,2,672,128]{3,2,1,0:T(8,128)(2,1)S(1)}, u32[]{:S(2)}, u32[]{:S(2)}) %collective-permute-start.6) | collective-permute-done | bytes 688160 | tf_op jit(solution)/shard_map/ppermute | solution.py:431
  48.1 0.4 sums.13
  48.6 1.6 %collective-permute-start.9 = (bf16[2,672,128]{2,1,0:T(8,128)(2,1)S(1)}, bf16[2,672,128]{2,1,0:T(8,128)(2,1)S(1)}, u32[]{:S(2)}, u32[]{:S(2)}) collective-permute-start(bf16[2,672,128]{2,1,0:T(8,128)(2,1)S(1)} %get-tuple-element.61.refs_4_), channel_id=1, source_target_pairs={{0,2},{1,3},{2,0},{3,1},{4,6},{5,7},{6,4},{7,5},{8,10},{9,11},{10,... | collective-permute-start | bytes 1032200 | tf_op jit(solution)/shard_map/ppermute | solution.py:431
  50.2 0.5 collective-permute-start.10
  50.7 3.6 %collective-permute-start.1 = (bf16[2,2,256,128]{3,2,1,0:T(8,128)(2,1)S(1)}, bf16[2,2,256,128]{3,2,1,0:T(8,128)(2,1)S(1)}, u32[]{:S(2)}, u32[]{:S(2)}) collective-permute-start(bf16[2,2,256,128]{3,2,1,0:T(8,128)(2,1)S(1)} %copy-done.7), channel_id=1, source_target_pairs={{0,24},{4,28},{8,16},{12,20},{16,8},{20,12},{24,0},{28,4},{1,25},{... | collective-permute-start | bytes 786440 | tf_op jit(solution)/shard_map/ppermute | solution.py:428
  54.6 1.5 %collective-permute-start.7 = (bf16[2,2,432,128]{3,2,1,0:T(8,128)(2,1)S(1)}, bf16[2,2,432,128]{3,2,1,0:T(8,128)(2,1)S(1)}, u32[]{:S(2)}, u32[]{:S(2)}) collective-permute-start(bf16[2,2,432,128]{3,2,1,0:T(8,128)(2,1)S(1)} %get-tuple-element.63.refs_4_), channel_id=1, source_target_pairs={{0,1},{1,0},{2,3},{3,2},{4,5},{5,4},{6,7},{7,6},{8,9},{9,8},{10,11... | collective-permute-start | bytes 1327112 | tf_op jit(solution)/shard_map/ppermute | solution.py:431
  56.2 0.5 collective-permute-start.8
  56.7 1.7 %collective-permute-done.9.refs_6_.refs_3_ = bf16[2,672,128]{2,1,0:T(8,128)(2,1)S(1)} collective-permute-done((bf16[2,672,128]{2,1,0:T(8,128)(2,1)S(1)}, bf16[2,672,128]{2,1,0:T(8,128)(2,1)S(1)}, u32[]{:S(2)}, u32[]{:S(2)}) %collective-permute-start.9) | collective-permute-done | bytes 344096 | tf_op jit(solution)/shard_map/ppermute | solution.py:431
  58.4 2.8 %collective-permute-done.10.refs_3_ = bf16[2,672,128]{2,1,0:T(8,128)(2,1)S(1)} collective-permute-done((bf16[2,672,128]{2,1,0:T(8,128)(2,1)S(1)}, bf16[2,672,128]{2,1,0:T(8,128)(2,1)S(1)}, u32[]{:S(2)}, u32[]{:S(2)}) %collective-permute-start.10) | collective-permute-done | bytes 344096 | tf_op jit(solution)/shard_map/ppermute | solution.py:431
  61.4 1.6 %collective-permute-start.11 = (bf16[2,672,128]{2,1,0:T(8,128)(2,1)S(1)}, bf16[2,672,128]{2,1,0:T(8,128)(2,1)S(1)}, u32[]{:S(2)}, u32[]{:S(2)}) collective-permute-start(bf16[2,672,128]{2,1,0:T(8,128)(2,1)S(1)} %sums.15.refs_5_), channel_id=1, source_target_pairs={{0,8},{4,12},{8,0},{12,4},{16,24},{20,28},{24,16},{28,20},{1,9},{5... | collective-permute-start | bytes 1032200 | tf_op jit(solution)/shard_map/ppermute | solution.py:428
  63.1 1.4 %collective-permute-start.2 = (bf16[2,2,256,128]{3,2,1,0:T(8,128)(2,1)S(1)}, bf16[2,2,256,128]{3,2,1,0:T(8,128)(2,1)S(1)}, u32[]{:S(2)}, u32[]{:S(2)}) collective-permute-start(bf16[2,2,256,128]{3,2,1,0:T(8,128)(2,1)S(1)} %copy-done.6), channel_id=1, source_target_pairs={{0,8},{4,12},{8,0},{12,4},{16,24},{20,28},{24,16},{28,20},{1,9},{5... | collective-permute-start | bytes 786440 | tf_op jit(solution)/shard_map/ppermute | solution.py:428
  64.5 6.5 %collective-permute-done.11.refs_4_.refs_6_ = bf16[2,672,128]{2,1,0:T(8,128)(2,1)S(1)} collective-permute-done((bf16[2,672,128]{2,1,0:T(8,128)(2,1)S(1)}, bf16[2,672,128]{2,1,0:T(8,128)(2,1)S(1)}, u32[]{:S(2)}, u32[]{:S(2)}) %collective-permute-start.11) | collective-permute-done | bytes 344096 | tf_op jit(solution)/shard_map/ppermute | solution.py:428
  71.5 2.3 %collective-permute-done.2.refs_1_.rest_1_ = bf16[2,2,256,128]{3,2,1,0:T(8,128)(2,1)S(1)} collective-permute-done((bf16[2,2,256,128]{3,2,1,0:T(8,128)(2,1)S(1)}, bf16[2,2,256,128]{3,2,1,0:T(8,128)(2,1)S(1)}, u32[]{:S(2)}, u32[]{:S(2)}) %collective-permute-start.2) | collective-permute-done | bytes 262176 | tf_op jit(solution)/shard_map/ppermute | solution.py:428
  73.9 0.5 collective-permute-start.13
  74.3 1.1 collective-permute-start.14
  75.5 0.3 collective-permute-start.15
  75.8 2.1 %collective-permute-start.16 = (bf16[1,672,128]{2,1,0:T(8,128)(2,1)S(1)}, bf16[1,672,128]{2,1,0:T(8,128)(2,1)S(1)}, u32[]{:S(2)}, u32[]{:S(2)}) collective-permute-start(bf16[1,672,128]{2,1,0:T(8,128)(2,1)S(1)} %sums.16.refs_6_), channel_id=1, source_target_pairs={{0,16},{4,20},{8,24},{12,28},{16,0},{20,4},{24,8},{28,12},{1,17},{... | collective-permute-start | bytes 516104 | tf_op jit(solution)/shard_map/ppermute | solution.py:428
  78.0 4.0 %counts.2.refs_4_ = bf16[4,512,128]{2,1,0:T(8,128)(2,1)S(1)} custom-call(s32[2,4,8192]{2,1,0:T(4,128)S(1)} %bitcast.45, bf16[2,2,256,128]{3,2,1,0:T(8,128)(2,1)S(1)} %copy-done.4, bf16[2,2,256,128]{3,2,1,0:T(8,128)(2,1)S(1)} %collective-permute-done.2.refs_1_.rest_1_, bf16[2,2,256,128]{3,2,1,0:T(8,128)(2,1)S(1)} %collective-permute-done.refs_6_.refs_2_.rest_2_, ...), custom_call_target="tpu_custom_call" | custom-call | tf_op jit(solution)/shard_map/counts/pallas_call | solution.py:619
  82.0 0.6 collective-permute-done.15.refs_5_.refs_3_
  82.8 1.6 %collective-permute-start.19 = (bf16[2,432,128]{2,1,0:T(8,128)(2,1)S(1)}, bf16[2,432,128]{2,1,0:T(8,128)(2,1)S(1)}, u32[]{:S(2)}, u32[]{:S(2)}) collective-permute-start(bf16[2,432,128]{2,1,0:T(8,128)(2,1)S(1)} %sums.18.rest_6_), channel_id=1, source_target_pairs={{0,8},{4,12},{8,0},{12,4},{16,24},{20,28},{24,16},{28,20},{1,9},{5... | collective-permute-start | bytes 663560 | tf_op jit(solution)/shard_map/ppermute | solution.py:428
  84.4 4.0 %counts.3.refs_6_ = bf16[4,512,128]{2,1,0:T(8,128)(2,1)S(1)} custom-call(s32[2,4,8192]{2,1,0:T(4,128)S(1)} %bitcast.46, bf16[2,2,256,128]{3,2,1,0:T(8,128)(2,1)S(1)} %copy-done.4, bf16[2,2,256,128]{3,2,1,0:T(8,128)(2,1)S(1)} %collective-permute-done.2.refs_1_.rest_1_, bf16[2,2,256,128]{3,2,1,0:T(8,128)(2,1)S(1)} %collective-permute-done.refs_6_.refs_2_.rest_2_, ...), custom_call_target="tpu_custom_call" | custom-call | tf_op jit(solution)/shard_map/counts/pallas_call | solution.py:619
  88.9 1.1 collective-permute-start.17
  90.0 0.5 collective-permute-start.18
  90.5 1.4 %collective-permute-start.22 = (bf16[1,672,128]{2,1,0:T(8,128)(2,1)S(1)}, bf16[1,672,128]{2,1,0:T(8,128)(2,1)S(1)}, u32[]{:S(2)}, u32[]{:S(2)}) collective-permute-start(bf16[1,672,128]{2,1,0:T(8,128)(2,1)S(1)} %sums.19.refs_2_), channel_id=1, source_target_pairs={{0,16},{4,20},{8,24},{12,28},{16,0},{20,4},{24,8},{28,12},{1,17},{... | collective-permute-start | bytes 516104 | tf_op jit(solution)/shard_map/ppermute | solution.py:428
  92.0 1.6 %collective-permute-start.23 = (bf16[1,432,128]{2,1,0:T(8,128)(2,1)S(1)}, bf16[1,432,128]{2,1,0:T(8,128)(2,1)S(1)}, u32[]{:S(2)}, u32[]{:S(2)}) collective-permute-start(bf16[1,432,128]{2,1,0:T(8,128)(2,1)S(1)} %sums.21.refs_4_), channel_id=1, source_target_pairs={{0,16},{4,20},{8,24},{12,28},{16,0},{20,4},{24,8},{28,12},{1,17},{... | collective-permute-start | bytes 331784 | tf_op jit(solution)/shard_map/ppermute | solution.py:428
  93.6 2.2 %collective-permute-done.17.refs_1_ = bf16[2,512,128]{2,1,0:T(8,128)(2,1)S(1)} collective-permute-done((bf16[2,512,128]{2,1,0:T(8,128)(2,1)S(1)}, bf16[2,512,128]{2,1,0:T(8,128)(2,1)S(1)}, u32[]{:S(2)}, u32[]{:S(2)}) %collective-permute-start.17) | collective-permute-done | bytes 262176 | tf_op jit(solution)/shard_map/ppermute | solution.py:431
  95.8 0.8 collective-permute-done.18.refs_3_.refs_4_
  96.7 0.6 collective-permute-start.20
  97.3 1.1 collective-permute-start.21
  98.4 5.8 %collective-permute-done.23.refs_5_ = bf16[1,432,128]{2,1,0:T(8,128)(2,1)S(1)} collective-permute-done((bf16[1,432,128]{2,1,0:T(8,128)(2,1)S(1)}, bf16[1,432,128]{2,1,0:T(8,128)(2,1)S(1)}, u32[]{:S(2)}, u32[]{:S(2)}) %collective-permute-start.23) | collective-permute-done | bytes 110624 | tf_op jit(solution)/shard_map/ppermute | solution.py:428
  104.5 2.4 %collective-permute-start.27 = (bf16[1,432,128]{2,1,0:T(8,128)(2,1)S(1)}, bf16[1,432,128]{2,1,0:T(8,128)(2,1)S(1)}, u32[]{:S(2)}, u32[]{:S(2)}) collective-permute-start(bf16[1,432,128]{2,1,0:T(8,128)(2,1)S(1)} %sums.23), channel_id=1, source_target_pairs={{0,16},{4,20},{8,24},{12,28},{16,0},{20,4},{24,8},{28,12},{1,17},{... | collective-permute-start | bytes 331784 | tf_op jit(solution)/shard_map/ppermute | solution.py:428
  106.8 0.9 rows.1
  107.7 6.3 %collective-permute-done.27 = bf16[1,432,128]{2,1,0:T(8,128)(2,1)S(1)} collective-permute-done((bf16[1,432,128]{2,1,0:T(8,128)(2,1)S(1)}, bf16[1,432,128]{2,1,0:T(8,128)(2,1)S(1)}, u32[]{:S(2)}, u32[]{:S(2)}) %collective-permute-start.27) | collective-permute-done | bytes 110624 | tf_op jit(solution)/shard_map/ppermute | solution.py:428
  114.1 2.6 %collective-permute-start.28 = (bf16[2,432,128]{2,1,0:T(8,128)(2,1)S(1)}, bf16[2,432,128]{2,1,0:T(8,128)(2,1)S(1)}, u32[]{:S(2)}, u32[]{:S(2)}) collective-permute-start(bf16[2,432,128]{2,1,0:T(8,128)(2,1)S(1)} %pad_maximum_fusion.1.refs_4_), channel_id=1, source_target_pairs={{0,8},{4,12},{8,0},{12,4},{16,24},{20,28},{24,16},{28,20},{1,9},{5... | collective-permute-start | bytes 663560 | tf_op jit(solution)/shard_map/ppermute | solution.py:428
  116.7 0.4 collective-permute-start.26
  117.2 3.7 %collective-permute-done.28.refs_5_ = bf16[2,432,128]{2,1,0:T(8,128)(2,1)S(1)} collective-permute-done((bf16[2,432,128]{2,1,0:T(8,128)(2,1)S(1)}, bf16[2,432,128]{2,1,0:T(8,128)(2,1)S(1)}, u32[]{:S(2)}, u32[]{:S(2)}) %collective-permute-start.28) | collective-permute-done | bytes 221216 | tf_op jit(solution)/shard_map/ppermute | solution.py:428
  121.0 1.5 %collective-permute-done.30.refs_7_ = bf16[2,432,128]{2,1,0:T(8,128)(2,1)S(1)} collective-permute-done((bf16[2,432,128]{2,1,0:T(8,128)(2,1)S(1)}, bf16[2,432,128]{2,1,0:T(8,128)(2,1)S(1)}, u32[]{:S(2)}, u32[]{:S(2)}) %collective-permute-start.30) | collective-permute-done | bytes 221216 | tf_op jit(solution)/shard_map/ppermute | solution.py:425
  122.4 2.2 %unpack.1 = (f32[544,256]{1,0:T(8,128)}, f32[64,2176]{1,0:T(8,128)}, f32[544,1024]{1,0:T(8,128)}, f32[256,1024]{1,0:T(8,128)}, f32[544]{0:T(1024)}, /*index=5*/f32[256]{0:T(256)}, f32[256]{0:T(256)}, f32[256]{0:T(256)}) custom-call(bf16[2,672,128]{2,1,0:T(8,128)(2,1)S(1)} %pad_maximum_fusion.refs_6_.refs_0_, ...), custom_call_target="tpu_custom_call" | custom-call | tf_op jit(solution)/shard_map/unpack/pallas_call | solution.py:644
  (53 shorter events, 2.6 us)
Async XLA Ops:
  13.1 11.2 %collective-permute-start.4 = (bf16[2,4,2,672,128]{4,3,2,1,0:T(8,128)(2,1)}, bf16[2,4,2,672,128]{4,3,2,1,0:T(8,128)(2,1)S(1)}, u32[]{:S(2)}, u32[]{:S(2)}) collective-permute-start(bf16[2,4,2,672,128]{4,3,2,1,0:T(8,128)(2,1)} %get-tuple-element.58), channel_id=1, source_target_pairs={{0,4},{4,0},{8,12},{12,8},{16,20},{20,16},{24,28},{28,24},{1,5},{5... | collective-permute-start | bytes 8257544 | tf_op jit(solution)/shard_map/ppermute | solution.py:425
  24.2 30.1 %collective-permute-start.3 = (bf16[2,4,2,432,128]{4,3,2,1,0:T(8,128)(2,1)}, bf16[2,4,2,432,128]{4,3,2,1,0:T(8,128)(2,1)S(1)}, u32[]{:S(2)}, u32[]{:S(2)}) collective-permute-start(bf16[2,4,2,432,128]{4,3,2,1,0:T(8,128)(2,1)} %get-tuple-element.56), channel_id=1, source_target_pairs={{0,4},{4,0},{8,12},{12,8},{16,20},{20,16},{24,28},{28,24},{1,5},{5... | collective-permute-start | bytes 5308424 | tf_op jit(solution)/shard_map/ppermute | solution.py:425
  24.3 1.8 %copy-start = (bf16[2,4,2,672,128]{4,3,2,1,0:T(8,128)(2,1)S(1)}, bf16[2,4,2,672,128]{4,3,2,1,0:T(8,128)(2,1)}, u32[]{:S(2)}) copy-start(bf16[2,4,2,672,128]{4,3,2,1,0:T(8,128)(2,1)} %get-tuple-element.57) | copy-start | bytes 8257540
  26.1 1.5 %copy-start.2 = (bf16[2,4,2,432,128]{4,3,2,1,0:T(8,128)(2,1)S(1)}, bf16[2,4,2,432,128]{4,3,2,1,0:T(8,128)(2,1)}, u32[]{:S(2)}) copy-start(bf16[2,4,2,432,128]{4,3,2,1,0:T(8,128)(2,1)} %get-tuple-element.55.refs_4_) | copy-start | bytes 5308420
  27.6 5.0 %copy-start.8 = (bf16[2,2,256,128]{3,2,1,0:T(8,128)(2,1)S(1)}, bf16[2,2,256,128]{3,2,1,0:T(8,128)(2,1)}, u32[]{:S(2)}) copy-start(bf16[2,2,256,128]{3,2,1,0:T(8,128)(2,1)} %get-tuple-element.52) | copy-start | bytes 786436
  28.1 18.7 %collective-permute-start.5 = (bf16[2,2,672,128]{3,2,1,0:T(8,128)(2,1)S(1)}, bf16[2,2,672,128]{3,2,1,0:T(8,128)(2,1)S(1)}, u32[]{:S(2)}, u32[]{:S(2)}) collective-permute-start(bf16[2,2,672,128]{3,2,1,0:T(8,128)(2,1)S(1)} %get-tuple-element.59), channel_id=1, source_target_pairs={{0,1},{1,0},{2,3},{3,2},{4,5},{5,4},{6,7},{7,6},{8,9},{9,8},{10,11... | collective-permute-start | bytes 2064392 | tf_op jit(solution)/shard_map/ppermute | solution.py:431
  31.1 17.1 %collective-permute-start.6 = (bf16[2,2,672,128]{3,2,1,0:T(8,128)(2,1)S(1)}, bf16[2,2,672,128]{3,2,1,0:T(8,128)(2,1)S(1)}, u32[]{:S(2)}, u32[]{:S(2)}) collective-permute-start(bf16[2,2,672,128]{3,2,1,0:T(8,128)(2,1)S(1)} %get-tuple-element.60), channel_id=1, source_target_pairs={{0,2},{1,3},{2,0},{3,1},{4,6},{5,7},{6,4},{7,5},{8,10},{9,11},{10,... | collective-permute-start | bytes 2064392 | tf_op jit(solution)/shard_map/ppermute | solution.py:431
  32.6 18.1 %copy-start.7 = (bf16[2,2,256,128]{3,2,1,0:T(8,128)(2,1)S(1)}, bf16[2,2,256,128]{3,2,1,0:T(8,128)(2,1)}, u32[]{:S(2)}) copy-start(bf16[2,2,256,128]{3,2,1,0:T(8,128)(2,1)} %get-tuple-element.53) | copy-start | bytes 786436
  32.6 21.7 %copy-start.3 = (bf16[2,4,2,432,128]{4,3,2,1,0:T(8,128)(2,1)S(1)}, bf16[2,4,2,432,128]{4,3,2,1,0:T(8,128)(2,1)}, u32[]{:S(2)}) copy-start(bf16[2,4,2,432,128]{4,3,2,1,0:T(8,128)(2,1)} %get-tuple-element.55.refs_4_) | copy-start | bytes 5308420
  32.6 14.2 %collective-permute-start = (bf16[2,2,256,128]{3,2,1,0:T(8,128)(2,1)S(1)}, bf16[2,2,256,128]{3,2,1,0:T(8,128)(2,1)S(1)}, u32[]{:S(2)}, u32[]{:S(2)}) collective-permute-start(bf16[2,2,256,128]{3,2,1,0:T(8,128)(2,1)S(1)} %copy-done.8), channel_id=1, source_target_pairs={{0,16},{4,20},{8,24},{12,28},{16,0},{20,4},{24,8},{28,12},{1,17},{... | collective-permute-start | bytes 786440 | tf_op jit(solution)/shard_map/ppermute | solution.py:428
  48.6 9.8 %collective-permute-start.9 = (bf16[2,672,128]{2,1,0:T(8,128)(2,1)S(1)}, bf16[2,672,128]{2,1,0:T(8,128)(2,1)S(1)}, u32[]{:S(2)}, u32[]{:S(2)}) collective-permute-start(bf16[2,672,128]{2,1,0:T(8,128)(2,1)S(1)} %get-tuple-element.61.refs_4_), channel_id=1, source_target_pairs={{0,2},{1,3},{2,0},{3,1},{4,6},{5,7},{6,4},{7,5},{8,10},{9,11},{10,... | collective-permute-start | bytes 1032200 | tf_op jit(solution)/shard_map/ppermute | solution.py:431
  50.2 11.0 %collective-permute-start.10 = (bf16[2,672,128]{2,1,0:T(8,128)(2,1)S(1)}, bf16[2,672,128]{2,1,0:T(8,128)(2,1)S(1)}, u32[]{:S(2)}, u32[]{:S(2)}) collective-permute-start(bf16[2,672,128]{2,1,0:T(8,128)(2,1)S(1)} %get-tuple-element.62.refs_5_), channel_id=1, source_target_pairs={{0,1},{1,0},{2,3},{3,2},{4,5},{5,4},{6,7},{7,6},{8,9},{9,8},{10,11... | collective-permute-start | bytes 1032200 | tf_op jit(solution)/shard_map/ppermute | solution.py:431
  50.7 12.4 %collective-permute-start.1 = (bf16[2,2,256,128]{3,2,1,0:T(8,128)(2,1)S(1)}, bf16[2,2,256,128]{3,2,1,0:T(8,128)(2,1)S(1)}, u32[]{:S(2)}, u32[]{:S(2)}) collective-permute-start(bf16[2,2,256,128]{3,2,1,0:T(8,128)(2,1)S(1)} %copy-done.7), channel_id=1, source_target_pairs={{0,24},{4,28},{8,16},{12,20},{16,8},{20,12},{24,0},{28,4},{1,25},{... | collective-permute-start | bytes 786440 | tf_op jit(solution)/shard_map/ppermute | solution.py:428
  54.3 6.8 %copy-start.1 = (bf16[2,4,2,672,128]{4,3,2,1,0:T(8,128)(2,1)S(1)}, bf16[2,4,2,672,128]{4,3,2,1,0:T(8,128)(2,1)}, u32[]{:S(2)}) copy-start(bf16[2,4,2,672,128]{4,3,2,1,0:T(8,128)(2,1)} %get-tuple-element.57) | copy-start | bytes 8257540
  54.6 16.5 %collective-permute-start.7 = (bf16[2,2,432,128]{3,2,1,0:T(8,128)(2,1)S(1)}, bf16[2,2,432,128]{3,2,1,0:T(8,128)(2,1)S(1)}, u32[]{:S(2)}, u32[]{:S(2)}) collective-permute-start(bf16[2,2,432,128]{3,2,1,0:T(8,128)(2,1)S(1)} %get-tuple-element.63.refs_4_), channel_id=1, source_target_pairs={{0,1},{1,0},{2,3},{3,2},{4,5},{5,4},{6,7},{7,6},{8,9},{9,8},{10,11... | collective-permute-start | bytes 1327112 | tf_op jit(solution)/shard_map/ppermute | solution.py:431
  56.2 6.9 %copy-start.6 = (bf16[2,2,256,128]{3,2,1,0:T(8,128)(2,1)S(1)}, bf16[2,2,256,128]{3,2,1,0:T(8,128)(2,1)}, u32[]{:S(2)}) copy-start(bf16[2,2,256,128]{3,2,1,0:T(8,128)(2,1)} %get-tuple-element.54) | copy-start | bytes 786436
  56.2 15.0 %collective-permute-start.8 = (bf16[2,2,432,128]{3,2,1,0:T(8,128)(2,1)S(1)}, bf16[2,2,432,128]{3,2,1,0:T(8,128)(2,1)S(1)}, u32[]{:S(2)}, u32[]{:S(2)}) collective-permute-start(bf16[2,2,432,128]{3,2,1,0:T(8,128)(2,1)S(1)} %get-tuple-element.64.refs_5_), channel_id=1, source_target_pairs={{0,2},{1,3},{2,0},{3,1},{4,6},{5,7},{6,4},{7,5},{8,10},{9,11},{10,... | collective-permute-start | bytes 1327112 | tf_op jit(solution)/shard_map/ppermute | solution.py:431
  61.4 9.5 %collective-permute-start.11 = (bf16[2,672,128]{2,1,0:T(8,128)(2,1)S(1)}, bf16[2,672,128]{2,1,0:T(8,128)(2,1)S(1)}, u32[]{:S(2)}, u32[]{:S(2)}) collective-permute-start(bf16[2,672,128]{2,1,0:T(8,128)(2,1)S(1)} %sums.15.refs_5_), channel_id=1, source_target_pairs={{0,8},{4,12},{8,0},{12,4},{16,24},{20,28},{24,16},{28,20},{1,9},{5... | collective-permute-start | bytes 1032200 | tf_op jit(solution)/shard_map/ppermute | solution.py:428
  63.1 10.7 %collective-permute-start.2 = (bf16[2,2,256,128]{3,2,1,0:T(8,128)(2,1)S(1)}, bf16[2,2,256,128]{3,2,1,0:T(8,128)(2,1)S(1)}, u32[]{:S(2)}, u32[]{:S(2)}) collective-permute-start(bf16[2,2,256,128]{3,2,1,0:T(8,128)(2,1)S(1)} %copy-done.6), channel_id=1, source_target_pairs={{0,8},{4,12},{8,0},{12,4},{16,24},{20,28},{24,16},{28,20},{1,9},{5... | collective-permute-start | bytes 786440 | tf_op jit(solution)/shard_map/ppermute | solution.py:428
  71.1 2.6 %copy-start.4 = (bf16[2,2,256,128]{3,2,1,0:T(8,128)(2,1)S(1)}, bf16[2,2,256,128]{3,2,1,0:T(8,128)(2,1)}, u32[]{:S(2)}) copy-start(bf16[2,2,256,128]{3,2,1,0:T(8,128)(2,1)} %get-tuple-element.49.refs_0_.rest_0_) | copy-start | bytes 786436
  71.1 6.8 %copy-start.5 = (s32[2,8192,4]{1,2,0:T(4,128)S(1)}, s32[2,8192,4]{1,2,0:T(4,128)}, u32[]{:S(2)}) copy-start(s32[2,8192,4]{1,2,0:T(4,128)} %param.23) | copy-start | bytes 786436
  73.8 4.2 %collective-permute-start.12 = (bf16[2,2,256,128]{3,2,1,0:T(8,128)(2,1)S(1)}, bf16[2,2,256,128]{3,2,1,0:T(8,128)(2,1)S(1)}, u32[]{:S(2)}, u32[]{:S(2)}) collective-permute-start(bf16[2,2,256,128]{3,2,1,0:T(8,128)(2,1)S(1)} %get-tuple-element.66.rest_6_), channel_id=1, source_target_pairs={{0,4},{4,0},{8,12},{12,8},{16,20},{20,16},{24,28},{28,24},{1,5},{5... | collective-permute-start | bytes 786440 | tf_op jit(solution)/shard_map/ppermute | solution.py:425
  73.9 4.1 %collective-permute-start.13 = (bf16[2,2,256,128]{3,2,1,0:T(8,128)(2,1)S(1)}, bf16[2,2,256,128]{3,2,1,0:T(8,128)(2,1)S(1)}, u32[]{:S(2)}, u32[]{:S(2)}) collective-permute-start(bf16[2,2,256,128]{3,2,1,0:T(8,128)(2,1)S(1)} %get-tuple-element.67), channel_id=1, source_target_pairs={{0,4},{4,0},{8,12},{12,8},{16,20},{20,16},{24,28},{28,24},{1,5},{5... | collective-permute-start | bytes 786440 | tf_op jit(solution)/shard_map/ppermute | solution.py:425
  74.3 7.7 %collective-permute-start.14 = (bf16[2,432,128]{2,1,0:T(8,128)(2,1)S(1)}, bf16[2,432,128]{2,1,0:T(8,128)(2,1)S(1)}, u32[]{:S(2)}, u32[]{:S(2)}) collective-permute-start(bf16[2,432,128]{2,1,0:T(8,128)(2,1)S(1)} %get-tuple-element.68), channel_id=1, source_target_pairs={{0,1},{1,0},{2,3},{3,2},{4,5},{5,4},{6,7},{7,6},{8,9},{9,8},{10,11... | collective-permute-start | bytes 663560 | tf_op jit(solution)/shard_map/ppermute | solution.py:431
  75.5 7.1 %collective-permute-start.15 = (bf16[2,432,128]{2,1,0:T(8,128)(2,1)S(1)}, bf16[2,432,128]{2,1,0:T(8,128)(2,1)S(1)}, u32[]{:S(2)}, u32[]{:S(2)}) collective-permute-start(bf16[2,432,128]{2,1,0:T(8,128)(2,1)S(1)} %get-tuple-element.65.refs_4_), channel_id=1, source_target_pairs={{0,2},{1,3},{2,0},{3,1},{4,6},{5,7},{6,4},{7,5},{8,10},{9,11},{10,... | collective-permute-start | bytes 663560 | tf_op jit(solution)/shard_map/ppermute | solution.py:431
  75.8 12.6 %collective-permute-start.16 = (bf16[1,672,128]{2,1,0:T(8,128)(2,1)S(1)}, bf16[1,672,128]{2,1,0:T(8,128)(2,1)S(1)}, u32[]{:S(2)}, u32[]{:S(2)}) collective-permute-start(bf16[1,672,128]{2,1,0:T(8,128)(2,1)S(1)} %sums.16.refs_6_), channel_id=1, source_target_pairs={{0,16},{4,20},{8,24},{12,28},{16,0},{20,4},{24,8},{28,12},{1,17},{... | collective-permute-start | bytes 516104 | tf_op jit(solution)/shard_map/ppermute | solution.py:428
  82.8 9.1 %collective-permute-start.19 = (bf16[2,432,128]{2,1,0:T(8,128)(2,1)S(1)}, bf16[2,432,128]{2,1,0:T(8,128)(2,1)S(1)}, u32[]{:S(2)}, u32[]{:S(2)}) collective-permute-start(bf16[2,432,128]{2,1,0:T(8,128)(2,1)S(1)} %sums.18.rest_6_), channel_id=1, source_target_pairs={{0,8},{4,12},{8,0},{12,4},{16,24},{20,28},{24,16},{28,20},{1,9},{5... | collective-permute-start | bytes 663560 | tf_op jit(solution)/shard_map/ppermute | solution.py:428
  88.9 6.9 %collective-permute-start.17 = (bf16[2,512,128]{2,1,0:T(8,128)(2,1)S(1)}, bf16[2,512,128]{2,1,0:T(8,128)(2,1)S(1)}, u32[]{:S(2)}, u32[]{:S(2)}) collective-permute-start(bf16[2,512,128]{2,1,0:T(8,128)(2,1)S(1)} %get-tuple-element.69.refs_5_), channel_id=1, source_target_pairs={{0,1},{1,0},{2,3},{3,2},{4,5},{5,4},{6,7},{7,6},{8,9},{9,8},{10,11... | collective-permute-start | bytes 786440 | tf_op jit(solution)/shard_map/ppermute | solution.py:431
  90.0 6.6 %collective-permute-start.18 = (bf16[2,512,128]{2,1,0:T(8,128)(2,1)S(1)}, bf16[2,512,128]{2,1,0:T(8,128)(2,1)S(1)}, u32[]{:S(2)}, u32[]{:S(2)}) collective-permute-start(bf16[2,512,128]{2,1,0:T(8,128)(2,1)S(1)} %get-tuple-element.70.refs_6_), channel_id=1, source_target_pairs={{0,2},{1,3},{2,0},{3,1},{4,6},{5,7},{6,4},{7,5},{8,10},{9,11},{10,... | collective-permute-start | bytes 786440 | tf_op jit(solution)/shard_map/ppermute | solution.py:431
  90.5 13.8 %collective-permute-start.22 = (bf16[1,672,128]{2,1,0:T(8,128)(2,1)S(1)}, bf16[1,672,128]{2,1,0:T(8,128)(2,1)S(1)}, u32[]{:S(2)}, u32[]{:S(2)}) collective-permute-start(bf16[1,672,128]{2,1,0:T(8,128)(2,1)S(1)} %sums.19.refs_2_), channel_id=1, source_target_pairs={{0,16},{4,20},{8,24},{12,28},{16,0},{20,4},{24,8},{28,12},{1,17},{... | collective-permute-start | bytes 516104 | tf_op jit(solution)/shard_map/ppermute | solution.py:428
  92.0 12.1 %collective-permute-start.23 = (bf16[1,432,128]{2,1,0:T(8,128)(2,1)S(1)}, bf16[1,432,128]{2,1,0:T(8,128)(2,1)S(1)}, u32[]{:S(2)}, u32[]{:S(2)}) collective-permute-start(bf16[1,432,128]{2,1,0:T(8,128)(2,1)S(1)} %sums.21.refs_4_), channel_id=1, source_target_pairs={{0,16},{4,20},{8,24},{12,28},{16,0},{20,4},{24,8},{28,12},{1,17},{... | collective-permute-start | bytes 331784 | tf_op jit(solution)/shard_map/ppermute | solution.py:428
  96.7 10.1 %collective-permute-start.20 = (bf16[512,128]{1,0:T(8,128)(2,1)S(1)}, bf16[512,128]{1,0:T(8,128)(2,1)S(1)}, u32[]{:S(2)}, u32[]{:S(2)}) collective-permute-start(bf16[512,128]{1,0:T(8,128)(2,1)S(1)} %get-tuple-element.71.refs_6_), channel_id=1, source_target_pairs={{0,2},{1,3},{2,0},{3,1},{4,6},{5,7},{6,4},{7,5},{8,10},{9,11},{10,... | collective-permute-start | bytes 393224 | tf_op jit(solution)/shard_map/ppermute | solution.py:431
  97.3 9.5 %collective-permute-start.21 = (bf16[512,128]{1,0:T(8,128)(2,1)S(1)}, bf16[512,128]{1,0:T(8,128)(2,1)S(1)}, u32[]{:S(2)}, u32[]{:S(2)}) collective-permute-start(bf16[512,128]{1,0:T(8,128)(2,1)S(1)} %get-tuple-element.72.refs_7_), channel_id=1, source_target_pairs={{0,1},{1,0},{2,3},{3,2},{4,5},{5,4},{6,7},{7,6},{8,9},{9,8},{10,11... | collective-permute-start | bytes 393224 | tf_op jit(solution)/shard_map/ppermute | solution.py:431
  104.4 12.3 %collective-permute-start.24 = (bf16[2,672,128]{2,1,0:T(8,128)(2,1)S(1)}, bf16[2,672,128]{2,1,0:T(8,128)(2,1)S(1)}, u32[]{:S(2)}, u32[]{:S(2)}) collective-permute-start(bf16[2,672,128]{2,1,0:T(8,128)(2,1)S(1)} %pad_maximum_fusion.refs_6_.refs_0_), channel_id=1, source_target_pairs={{0,8},{4,12},{8,0},{12,4},{16,24},{20,28},{24,16},{28,20},{1,9},{5... | collective-permute-start | bytes 1032200 | tf_op jit(solution)/shard_map/ppermute | solution.py:428
  104.5 9.6 %collective-permute-start.27 = (bf16[1,432,128]{2,1,0:T(8,128)(2,1)S(1)}, bf16[1,432,128]{2,1,0:T(8,128)(2,1)S(1)}, u32[]{:S(2)}, u32[]{:S(2)}) collective-permute-start(bf16[1,432,128]{2,1,0:T(8,128)(2,1)S(1)} %sums.23), channel_id=1, source_target_pairs={{0,16},{4,20},{8,24},{12,28},{16,0},{20,4},{24,8},{28,12},{1,17},{... | collective-permute-start | bytes 331784 | tf_op jit(solution)/shard_map/ppermute | solution.py:428
  114.1 6.9 %collective-permute-start.28 = (bf16[2,432,128]{2,1,0:T(8,128)(2,1)S(1)}, bf16[2,432,128]{2,1,0:T(8,128)(2,1)S(1)}, u32[]{:S(2)}, u32[]{:S(2)}) collective-permute-start(bf16[2,432,128]{2,1,0:T(8,128)(2,1)S(1)} %pad_maximum_fusion.1.refs_4_), channel_id=1, source_target_pairs={{0,8},{4,12},{8,0},{12,4},{16,24},{20,28},{24,16},{28,20},{1,9},{5... | collective-permute-start | bytes 663560 | tf_op jit(solution)/shard_map/ppermute | solution.py:428
  116.6 4.3 %collective-permute-start.25 = (bf16[2,672,128]{2,1,0:T(8,128)(2,1)S(1)}, bf16[2,672,128]{2,1,0:T(8,128)(2,1)S(1)}, u32[]{:S(2)}, u32[]{:S(2)}) collective-permute-start(bf16[2,672,128]{2,1,0:T(8,128)(2,1)S(1)} %pad_maximum_fusion.refs_6_.refs_0_), channel_id=1, source_target_pairs={{0,4},{4,0},{8,12},{12,8},{16,20},{20,16},{24,28},{28,24},{1,5},{5... | collective-permute-start | bytes 1032200 | tf_op jit(solution)/shard_map/ppermute | solution.py:425
  116.7 5.7 %collective-permute-start.26 = (bf16[2,672,128]{2,1,0:T(8,128)(2,1)S(1)}, bf16[2,672,128]{2,1,0:T(8,128)(2,1)S(1)}, u32[]{:S(2)}, u32[]{:S(2)}) collective-permute-start(bf16[2,672,128]{2,1,0:T(8,128)(2,1)S(1)} %collective-permute-done.24.refs_1_), channel_id=1, source_target_pairs={{0,4},{4,0},{8,12},{12,8},{16,20},{20,16},{24,28},{28,24},{1,5},{5... | collective-permute-start | bytes 1032200 | tf_op jit(solution)/shard_map/ppermute | solution.py:425
  117.1 3.8 %collective-permute-start.29 = (bf16[2,432,128]{2,1,0:T(8,128)(2,1)S(1)}, bf16[2,432,128]{2,1,0:T(8,128)(2,1)S(1)}, u32[]{:S(2)}, u32[]{:S(2)}) collective-permute-start(bf16[2,432,128]{2,1,0:T(8,128)(2,1)S(1)} %pad_maximum_fusion.1.refs_4_), channel_id=1, source_target_pairs={{0,4},{4,0},{8,12},{12,8},{16,20},{20,16},{24,28},{28,24},{1,5},{5... | collective-permute-start | bytes 663560 | tf_op jit(solution)/shard_map/ppermute | solution.py:425
  121.0 1.5 %collective-permute-start.30 = (bf16[2,432,128]{2,1,0:T(8,128)(2,1)S(1)}, bf16[2,432,128]{2,1,0:T(8,128)(2,1)S(1)}, u32[]{:S(2)}, u32[]{:S(2)}) collective-permute-start(bf16[2,432,128]{2,1,0:T(8,128)(2,1)S(1)} %collective-permute-done.28.refs_5_), channel_id=1, source_target_pairs={{0,4},{4,0},{8,12},{12,8},{16,20},{20,16},{24,28},{28,24},{1,5},{5... | collective-permute-start | bytes 663560 | tf_op jit(solution)/shard_map/ppermute | solution.py:425

commit v8 on v7

--- a/solution.py
+++ b/solution.py
@@ -72,18 +72,14 @@
 
 
 class Loads:
-    def __init__(self, sources, targets, sems, first):
+    def __init__(self, sources, targets, sems):
         self.copies = [
             pltpu.make_async_copy(source, target, sems.at[at])
             for at, (source, target) in enumerate(zip(sources, targets))
         ]
-        self.targets, self.first = targets, first
+        self.targets = targets
         self.ready = set()
-        for copy in self.copies[:first]:
-            copy.start()
-
-    def more(self):
-        for copy in self.copies[self.first :]:
+        for copy in self.copies:
             copy.start()
 
     def __call__(self, at):
@@ -101,12 +97,11 @@
     sources, outs, targets = refs[:11], refs[11:16], refs[16:27]
     halves, thirds, sems = refs[27:]
     send, keep, crossed_t_out, first_out, small = outs
-    load = Loads(sources, targets, sems, 5)
+    load = Loads(sources, targets, sems)
     core, row_pos, table_pos = position()
     places = places_of(lax.div(table_pos, 2), 2 * send.shape[2])
     stacked = jnp.concatenate([load(0), load(1)], axis=1)
     cross_down = load(2)
-    load.more()
     reduced = matmul(stacked, cross_down).astype(bf16)
     widened = matmul(reduced, load(3)) + as_row(load(4))
     wide = stacked.astype(f32)
@@ -155,13 +150,12 @@
     rest = refs[11 + n_z :]
     targets = rest[:9]
     by_group, wide_delta, half_delta, sixths, small, sems = rest[9:]
-    load = Loads(sources, targets, sems, 6)
+    load = Loads(sources, targets, sems)
     core, row_pos, table_pos = position()
     z_pos = lax.div(table_pos, 2)
     places = places_of(z_pos, 2 * send.shape[2])
     stacked = jnp.concatenate([load(0), load(1)], axis=1)
     cross_down = load(2)
-    load.more()
     reduced = matmul(stacked, cross_down).astype(bf16)
     cross_up = load(3)
     widened = matmul(reduced, cross_up) + as_row(load(4))
@@ -557,7 +551,8 @@
             self.high = Halving([keep, got], high_first, [1])
 
         def row_step(self, at, deps):
-            deps = [*deps, self.low.items[-1][0], self.high.items[-1][0]]
+            if at > 0:
+                deps = [*deps, self.low.items[-1][0], self.high.items[-1][0]]
             return row_step((self.low, self.high), at, deps)
 
         def z_step(self, stage, deps):
@@ -584,25 +579,20 @@
             self.pieces = [self.own, far, swap_cores(self.own), swap_cores(far)]
             return [self.own]
 
+    (got1,) = after([got1], [pooled_out[0]])
     one, two = Dense(keep1, got1), Dense(keep2, got2)
-    one.row_step(0, [keep2])
-    values, chain = {0: pooled_out[0]}, [n_z // 2]
-    chain += [which for which in range(n_z - 1, 0, -1) if which != n_z // 2]
-    for at, which in enumerate(chain):
-        moved = pooled_out[which]
-        if at > 0:
-            (moved,) = after([moved], [values[chain[at - 1]]])
+    one.row_step(0, [])
+    values, half = {0: pooled_out[0]}, n_z // 2
+    for which in [half, *range(1, half)]:
+        values[which] = swap_z(pooled_out[which], which)
+    for which in range(half + 1, n_z):
+        (moved,) = after([pooled_out[which]], [values[half], values[which - half]])
         values[which] = swap_z(moved, which)
-    last = [values[chain[0]]]
+    last = [values[which] for which in range(1, half + 1)]
     for at in range(1, row_bits):
         last = one.row_step(at, last)
     last = two.row_step(0, last)
     last = one.z_step(0, last)
-    for stage in range(1, z_bits):
-        last = one.z_step(stage, last)
-    last = [*last, values[chain[min(1, len(chain) - 1)]]]
-    for at in range(1, row_bits):
-        last = two.row_step(at, last)
     values = [values[which] for which in range(n_z)]
     far_values = call(
         functools.partial(select_kernel, n_z),
@@ -629,9 +619,13 @@
         shares.append(Halving([sums], high_first if table % 2 else low_first))
         last = [sums]
         if table == 0:
+            for at in range(1, row_bits):
+                last = two.row_step(at, last)
+            for stage in range(1, z_bits):
+                last = one.z_step(stage, last)
             last = two.z_step(0, last)
+    last = row_step(shares, 0, last)
     last = one.z_own(last)
-    last = row_step(shares, 0, last)
     for stage in range(1, z_bits):
         last = two.z_step(stage, last)
     for at in range(1, row_bits):

time: 125 us -> 126 us (level)
  waiting for transfers between devices: 47.2 us -> 37 us
  Pallas kernels: 37.1 us -> 46.7 us
  starting transfers between devices: 36.2 us -> 41.5 us
  local copies, waits for them, and re-layouts: 3.28 us -> 0.03 us
    pallas_call x12, Pallas kernels: 2.88 us -> 13.5 us  [take_sums(): call(functools.partial(sum_kernel, plan, len(arrays)), shapes, [], [whole...]
    ppermute x12, waiting for transfers between devices: 9.41 us -> 3.52 us  [swap_row(): lax.ppermute(value, 'row', [(at, at ^ 1 << bit) for at in range(n_row)])]
    ppermute x11, waiting for transfers between devices: 36.3 us -> 32 us  [swap_z(): lax.ppermute(value, 'table', [(at, at ^ 2 * which) for at in range(n_tabl...]
    unnamed x18 -> x14, local copies, waits for them, and re-layouts: 3.28 us -> 0.03 us
    ppermute x11, starting transfers between devices: 21 us -> 24 us  [swap_z(): lax.ppermute(value, 'table', [(at, at ^ 2 * which) for at in range(n_tabl...]
    ppermute x12, starting transfers between devices: 13.4 us -> 15.8 us  [swap_row(): lax.ppermute(value, 'row', [(at, at ^ 1 << bit) for at in range(n_row)])]
  transfers between devices with their start and end apart: 31 -> 31, of which waited for: 14 -> 9; matrix products, arithmetic and copies ran while one was open for 0% -> 0% of each run, Pallas kernels for 18% -> 26%
where the time goes in v8:
time: 126 us
  Pallas kernels  46.7 us (37%)
  starting transfers between devices  41.5 us (33%)
  waiting for transfers between devices  37 us (29%)
    ppermute x11, waiting for transfers between devices, swap_z(): lax.ppermute(value, 'table', [(at, at ^ 2 * which) for at in range(n_tabl...  32 us
    ppermute x11, starting transfers between devices, swap_z(): lax.ppermute(value, 'table', [(at, at ^ 2 * which) for at in range(n_tabl...  24 us
    ppermute x12, starting transfers between devices, swap_row(): lax.ppermute(value, 'row', [(at, at ^ 1 << bit) for at in range(n_row)])  15.8 us
    pallas_call x12, Pallas kernels, take_sums(): call(functools.partial(sum_kernel, plan, len(arrays)), shapes, [], [whole...  13.5 us
    pallas_call x1, Pallas kernels, local(): call(front_kernel, [packed(rows_front)] * 2 + [wide(feat, batch), wide(ba...  11.9 us
    pallas_call x1, Pallas kernels, local(): call(functools.partial(middle_kernel, n_z), [packed(rows_back)] * 2 + [wi...  10.1 us
    pallas_call x2, Pallas kernels, local(): pl.pallas_call(functools.partial(count_kernel, n_row, table, hot, n_z), o...  8.04 us
    ppermute x12, waiting for transfers between devices, swap_row(): lax.ppermute(value, 'row', [(at, at ^ 1 << bit) for at in range(n_row)])  3.52 us
  transfers between devices with their start and end apart: 31, of which 9 were waited for; matrix products, arithmetic and copies ran while one was open for 0% of the time, Pallas kernels for 26%

profile of v8, /device:TPU:0, one launch (start us, length us, event | category | flops | bytes accessed | tf_op | source)
XLA Modules:
  0.0 126.2 jit_solution(3213509020716852034)
XLA Ops:
  0.6 11.9 %front.1 = (bf16[2,4,2,672,128]{4,3,2,1,0:T(8,128)(2,1)}, bf16[2,4,2,672,128]{4,3,2,1,0:T(8,128)(2,1)}, bf16[2176,256]{1,0:T(8,128)(2,1)}, bf16[256,1024]{1,0:T(8,128)(2,1)}, f32[24,128]{1,0:T(8,128)}) custom-call(bf16[256,128]{1,0:T(8,128)(2,1)} %refs_0_.3, bf16[256,2048]{1,0:T(8,128)(2,1)} %refs_1_.3, bf16[2176,256]{1,0:T(8,128)(2,1)} %refs_2_.3, ...), custom_call_target="tpu_custom_call" | custom-call | tf_op jit(solution)/shard_map/front/pallas_call | solution.py:457
  12.5 0.5 collective-permute-start.3
  13.0 10.1 %middle.1 = (bf16[2,4,2,432,128]{4,3,2,1,0:T(8,128)(2,1)}, bf16[2,4,2,432,128]{4,3,2,1,0:T(8,128)(2,1)}, bf16[2,2,256,128]{3,2,1,0:T(8,128)(2,1)}, bf16[2,2,256,...) custom-call(bf16[256,128]{1,0:T(8,128)(2,1)} %refs_0_.3, ...), custom_call_target="tpu_custom_call" | custom-call | tf_op jit(solution)/shard_map/middle/pallas_call | solution.py:484
  23.4 3.1 %sums.12 = (bf16[2,2,672,128]{3,2,1,0:T(8,128)(2,1)S(1)}, bf16[2,2,672,128]{3,2,1,0:T(8,128)(2,1)S(1)}) custom-call(bf16[2,2,2,2,672,128]{5,4,3,2,1,0:T(8,128)(2,1)S(1)} %bitcast.7, bf16[2,2,2,2,672,128]{5,4,3,2,1,0:T(8,128)(2,1)} %bitcast.2.refs_1_.refs_3_.refs_4_, bf16[2,2,2,2,672,128]{5,4,3,2,1,0:T(8,128)(2,1)S(1)} %bitcast.8, ...), custom_call_target="tpu_custom_call" | custom-call | tf_op jit(solution)/shard_map/sums/pallas_call | solution.py:383
  26.5 3.0 %collective-permute-start.5 = (bf16[2,2,672,128]{3,2,1,0:T(8,128)(2,1)S(1)}, bf16[2,2,672,128]{3,2,1,0:T(8,128)(2,1)S(1)}, u32[]{:S(2)}, u32[]{:S(2)}) collective-permute-start(bf16[2,2,672,128]{3,2,1,0:T(8,128)(2,1)S(1)} %get-tuple-element.58), channel_id=1, source_target_pairs={{0,1},{1,0},{2,3},{3,2},{4,5},{5,4},{6,7},{7,6},{8,9},{9,8},{10,11... | collective-permute-start | bytes 2064392 | tf_op jit(solution)/shard_map/ppermute | solution.py:425
  29.5 1.5 %collective-permute-start.4 = (bf16[2,2,672,128]{3,2,1,0:T(8,128)(2,1)S(1)}, bf16[2,2,672,128]{3,2,1,0:T(8,128)(2,1)S(1)}, u32[]{:S(2)}, u32[]{:S(2)}) collective-permute-start(bf16[2,2,672,128]{3,2,1,0:T(8,128)(2,1)S(1)} %get-tuple-element.57), channel_id=1, source_target_pairs={{0,2},{1,3},{2,0},{3,1},{4,6},{5,7},{6,4},{7,5},{8,10},{9,11},{10,... | collective-permute-start | bytes 2064392 | tf_op jit(solution)/shard_map/ppermute | solution.py:425
  31.0 1.6 %collective-permute-start = (bf16[2,2,256,128]{3,2,1,0:T(8,128)(2,1)S(1)}, bf16[2,2,256,128]{3,2,1,0:T(8,128)(2,1)S(1)}, u32[]{:S(2)}, u32[]{:S(2)}) collective-permute-start(bf16[2,2,256,128]{3,2,1,0:T(8,128)(2,1)S(1)} %copy-done.6), channel_id=1, source_target_pairs={{0,8},{4,12},{8,0},{12,4},{16,24},{20,28},{24,16},{28,20},{1,9},{5... | collective-permute-start | bytes 786440 | tf_op jit(solution)/shard_map/ppermute | solution.py:422
  32.6 2.6 %collective-permute-start.1 = (bf16[2,2,256,128]{3,2,1,0:T(8,128)(2,1)S(1)}, bf16[2,2,256,128]{3,2,1,0:T(8,128)(2,1)S(1)}, u32[]{:S(2)}, u32[]{:S(2)}) collective-permute-start(bf16[2,2,256,128]{3,2,1,0:T(8,128)(2,1)S(1)} %copy-done.5), channel_id=1, source_target_pairs={{0,16},{4,20},{8,24},{12,28},{16,0},{20,4},{24,8},{28,12},{1,17},{... | collective-permute-start | bytes 786440 | tf_op jit(solution)/shard_map/ppermute | solution.py:422
  35.2 9.0 %collective-permute-done.refs_6_.refs_1_.rest_1_ = bf16[2,2,256,128]{3,2,1,0:T(8,128)(2,1)S(1)} collective-permute-done((bf16[2,2,256,128]{3,2,1,0:T(8,128)(2,1)S(1)}, bf16[2,2,256,128]{3,2,1,0:T(8,128)(2,1)S(1)}, u32[]{:S(2)}, u32[]{:S(2)}) %collective-permute-start) | collective-permute-done | bytes 262176 | tf_op jit(solution)/shard_map/ppermute | solution.py:422
  44.2 2.4 %collective-permute-done.1.refs_7_.refs_2_.rest_2_ = bf16[2,2,256,128]{3,2,1,0:T(8,128)(2,1)S(1)} collective-permute-done((bf16[2,2,256,128]{3,2,1,0:T(8,128)(2,1)S(1)}, bf16[2,2,256,128]{3,2,1,0:T(8,128)(2,1)S(1)}, u32[]{:S(2)}, u32[]{:S(2)}) %collective-permute-start.1) | collective-permute-done | bytes 262176 | tf_op jit(solution)/shard_map/ppermute | solution.py:422
  46.6 3.0 %sums.13 = (bf16[2,672,128]{2,1,0:T(8,128)(2,1)S(1)}, bf16[2,672,128]{2,1,0:T(8,128)(2,1)S(1)}) custom-call(bf16[2,2,2,2,672,128]{5,4,3,2,1,0:T(8,128)(2,1)S(1)} %bitcast.9, bf16[2,2,2,2,672,128]{5,4,3,2,1,0:T(8,128)(2,1)} %bitcast.2.refs_1_.refs_3_.refs_4_, bf16[2,2,672,128]{3,2,1,0:T(8,128)(2,1)S(1)} %collective-permute-done.5.refs_2_.refs_8_, ...), custom_call_target="tpu_custom_call" | custom-call | tf_op jit(solution)/shard_map/sums/pallas_call | solution.py:383
  49.6 0.6 collective-permute-start.6
  50.2 1.5 %collective-permute-start.8 = (bf16[2,672,128]{2,1,0:T(8,128)(2,1)S(1)}, bf16[2,672,128]{2,1,0:T(8,128)(2,1)S(1)}, u32[]{:S(2)}, u32[]{:S(2)}) collective-permute-start(bf16[2,672,128]{2,1,0:T(8,128)(2,1)S(1)} %get-tuple-element.62.refs_4_), channel_id=1, source_target_pairs={{0,2},{1,3},{2,0},{3,1},{4,6},{5,7},{6,4},{7,5},{8,10},{9,11},{10,... | collective-permute-start | bytes 1032200 | tf_op jit(solution)/shard_map/ppermute | solution.py:425
  51.8 3.6 %collective-permute-start.2 = (bf16[2,2,256,128]{3,2,1,0:T(8,128)(2,1)S(1)}, bf16[2,2,256,128]{3,2,1,0:T(8,128)(2,1)S(1)}, u32[]{:S(2)}, u32[]{:S(2)}) collective-permute-start(bf16[2,2,256,128]{3,2,1,0:T(8,128)(2,1)S(1)} %copy-done.4), channel_id=1, source_target_pairs={{0,24},{4,28},{8,16},{12,20},{16,8},{20,12},{24,0},{28,4},{1,25},{... | collective-permute-start | bytes 786440 | tf_op jit(solution)/shard_map/ppermute | solution.py:422
  55.4 0.3 sums.14
  55.7 0.6 collective-permute-start.11
  56.3 1.5 %collective-permute-start.12 = (bf16[2,2,432,128]{3,2,1,0:T(8,128)(2,1)S(1)}, bf16[2,2,432,128]{3,2,1,0:T(8,128)(2,1)S(1)}, u32[]{:S(2)}, u32[]{:S(2)}) collective-permute-start(bf16[2,2,432,128]{3,2,1,0:T(8,128)(2,1)S(1)} %get-tuple-element.63.refs_4_), channel_id=1, source_target_pairs={{0,1},{1,0},{2,3},{3,2},{4,5},{5,4},{6,7},{7,6},{8,9},{9,8},{10,11... | collective-permute-start | bytes 1327112 | tf_op jit(solution)/shard_map/ppermute | solution.py:425
  57.7 2.6 %collective-permute-done.6.refs_3_ = bf16[2,672,128]{2,1,0:T(8,128)(2,1)S(1)} collective-permute-done((bf16[2,672,128]{2,1,0:T(8,128)(2,1)S(1)}, bf16[2,672,128]{2,1,0:T(8,128)(2,1)S(1)}, u32[]{:S(2)}, u32[]{:S(2)}) %collective-permute-start.6) | collective-permute-done | bytes 344096 | tf_op jit(solution)/shard_map/ppermute | solution.py:425
  60.4 0.9 collective-permute-done.8.refs_6_.refs_3_
  61.2 2.0 %sums.15.refs_4_ = bf16[2,672,128]{2,1,0:T(8,128)(2,1)S(1)} custom-call(bf16[2,2,2,2,672,128]{5,4,3,2,1,0:T(8,128)(2,1)S(1)} %bitcast.11, bf16[2,2,2,2,672,128]{5,4,3,2,1,0:T(8,128)(2,1)} %bitcast.2.refs_1_.refs_3_.refs_4_, bf16[2,2,672,128]{3,2,1,0:T(8,128)(2,1)S(1)} %collective-permute-done.4.refs_5_.refs_9_.refs_2_, ...), custom_call_target="tpu_custom_call" | custom-call | tf_op jit(solution)/shard_map/sums/pallas_call | solution.py:383
  63.4 0.5 collective-permute-start.9
  63.9 2.3 %collective-permute-start.14 = (bf16[2,672,128]{2,1,0:T(8,128)(2,1)S(1)}, bf16[2,672,128]{2,1,0:T(8,128)(2,1)S(1)}, u32[]{:S(2)}, u32[]{:S(2)}) collective-permute-start(bf16[2,672,128]{2,1,0:T(8,128)(2,1)S(1)} %sums.15.refs_4_), channel_id=1, source_target_pairs={{0,8},{4,12},{8,0},{12,4},{16,24},{20,28},{24,16},{28,20},{1,9},{5... | collective-permute-start | bytes 1032200 | tf_op jit(solution)/shard_map/ppermute | solution.py:422
  66.2 4.0 %counts.2.refs_6_ = bf16[4,512,128]{2,1,0:T(8,128)(2,1)S(1)} custom-call(s32[2,4,8192]{2,1,0:T(4,128)S(1)} %bitcast.34, bf16[2,2,256,128]{3,2,1,0:T(8,128)(2,1)S(1)} %copy-done.2, bf16[2,2,256,128]{3,2,1,0:T(8,128)(2,1)S(1)} %collective-permute-done.refs_6_.refs_1_.rest_1_, bf16[2,2,256,128]{3,2,1,0:T(8,128)(2,1)S(1)} %collective-permute-done.1.refs_7_.refs_2_.rest_2_, ...), custom_call_target="tpu_custom_call" | custom-call | tf_op jit(solution)/shard_map/counts/pallas_call | solution.py:609
  70.2 0.3 sums.16
  70.5 1.5 %collective-permute-start.13 = (bf16[2,432,128]{2,1,0:T(8,128)(2,1)S(1)}, bf16[2,432,128]{2,1,0:T(8,128)(2,1)S(1)}, u32[]{:S(2)}, u32[]{:S(2)}) collective-permute-start(bf16[2,432,128]{2,1,0:T(8,128)(2,1)S(1)} %get-tuple-element.67.refs_6_), channel_id=1, source_target_pairs={{0,1},{1,0},{2,3},{3,2},{4,5},{5,4},{6,7},{7,6},{8,9},{9,8},{10,11... | collective-permute-start | bytes 663560 | tf_op jit(solution)/shard_map/ppermute | solution.py:425
  72.0 0.9 collective-permute-start.15
  72.9 1.5 %collective-permute-done.14.refs_4_.refs_7_ = bf16[2,672,128]{2,1,0:T(8,128)(2,1)S(1)} collective-permute-done((bf16[2,672,128]{2,1,0:T(8,128)(2,1)S(1)}, bf16[2,672,128]{2,1,0:T(8,128)(2,1)S(1)}, u32[]{:S(2)}, u32[]{:S(2)}) %collective-permute-start.14) | collective-permute-done | bytes 344096 | tf_op jit(solution)/shard_map/ppermute | solution.py:422
  74.5 2.0 %sums.17.refs_4_ = bf16[1,672,128]{2,1,0:T(8,128)(2,1)S(1)} custom-call(bf16[2,2,2,2,672,128]{5,4,3,2,1,0:T(8,128)(2,1)S(1)} %bitcast.12, bf16[2,2,2,2,672,128]{5,4,3,2,1,0:T(8,128)(2,1)} %bitcast.2.refs_1_.refs_3_.refs_4_, bf16[2,2,672,128]{3,2,1,0:T(8,128)(2,1)S(1)} %collective-permute-done.5.refs_2_.refs_8_, ...), custom_call_target="tpu_custom_call" | custom-call | tf_op jit(solution)/shard_map/sums/pallas_call | solution.py:383
  76.5 2.8 %collective-permute-start.19 = (bf16[1,672,128]{2,1,0:T(8,128)(2,1)S(1)}, bf16[1,672,128]{2,1,0:T(8,128)(2,1)S(1)}, u32[]{:S(2)}, u32[]{:S(2)}) collective-permute-start(bf16[1,672,128]{2,1,0:T(8,128)(2,1)S(1)} %sums.17.refs_4_), channel_id=1, source_target_pairs={{0,16},{4,20},{8,24},{12,28},{16,0},{20,4},{24,8},{28,12},{1,17},{... | collective-permute-start | bytes 516104 | tf_op jit(solution)/shard_map/ppermute | solution.py:422
  79.4 1.4 %collective-permute-start.18 = (bf16[2,432,128]{2,1,0:T(8,128)(2,1)S(1)}, bf16[2,432,128]{2,1,0:T(8,128)(2,1)S(1)}, u32[]{:S(2)}, u32[]{:S(2)}) collective-permute-start(bf16[2,432,128]{2,1,0:T(8,128)(2,1)S(1)} %sums.18.rest_6_), channel_id=1, source_target_pairs={{0,8},{4,12},{8,0},{12,4},{16,24},{20,28},{24,16},{28,20},{1,9},{5... | collective-permute-start | bytes 663560 | tf_op jit(solution)/shard_map/ppermute | solution.py:422
  80.8 4.0 %counts.3.refs_2_ = bf16[4,512,128]{2,1,0:T(8,128)(2,1)S(1)} custom-call(s32[2,4,8192]{2,1,0:T(4,128)S(1)} %bitcast.35, bf16[2,2,256,128]{3,2,1,0:T(8,128)(2,1)S(1)} %copy-done.2, bf16[2,2,256,128]{3,2,1,0:T(8,128)(2,1)S(1)} %collective-permute-done.refs_6_.refs_1_.rest_1_, bf16[2,2,256,128]{3,2,1,0:T(8,128)(2,1)S(1)} %collective-permute-done.1.refs_7_.refs_2_.rest_2_, ...), custom_call_target="tpu_custom_call" | custom-call | tf_op jit(solution)/shard_map/counts/pallas_call | solution.py:609
  84.8 0.2 sums.19
  85.0 1.2 collective-permute-start.16
  86.2 1.5 %collective-permute-start.17 = (bf16[2,512,128]{2,1,0:T(8,128)(2,1)S(1)}, bf16[2,512,128]{2,1,0:T(8,128)(2,1)S(1)}, u32[]{:S(2)}, u32[]{:S(2)}) collective-permute-start(bf16[2,512,128]{2,1,0:T(8,128)(2,1)S(1)} %get-tuple-element.70.refs_7_), channel_id=1, source_target_pairs={{0,2},{1,3},{2,0},{3,1},{4,6},{5,7},{6,4},{7,5},{8,10},{9,11},{10,... | collective-permute-start | bytes 786440 | tf_op jit(solution)/shard_map/ppermute | solution.py:425
  87.7 2.0 %sums.20.refs_5_ = bf16[1,672,128]{2,1,0:T(8,128)(2,1)S(1)} custom-call(bf16[2,2,2,2,672,128]{5,4,3,2,1,0:T(8,128)(2,1)S(1)} %bitcast.13, bf16[2,2,2,2,672,128]{5,4,3,2,1,0:T(8,128)(2,1)} %bitcast.2.refs_1_.refs_3_.refs_4_, bf16[2,2,672,128]{3,2,1,0:T(8,128)(2,1)S(1)} %collective-permute-done.5.refs_2_.refs_8_, ...), custom_call_target="tpu_custom_call" | custom-call | tf_op jit(solution)/shard_map/sums/pallas_call | solution.py:383
  89.7 1.5 %collective-permute-start.22 = (bf16[1,672,128]{2,1,0:T(8,128)(2,1)S(1)}, bf16[1,672,128]{2,1,0:T(8,128)(2,1)S(1)}, u32[]{:S(2)}, u32[]{:S(2)}) collective-permute-start(bf16[1,672,128]{2,1,0:T(8,128)(2,1)S(1)} %sums.20.refs_5_), channel_id=1, source_target_pairs={{0,16},{4,20},{8,24},{12,28},{16,0},{20,4},{24,8},{28,12},{1,17},{... | collective-permute-start | bytes 516104 | tf_op jit(solution)/shard_map/ppermute | solution.py:422
  91.3 1.6 %collective-permute-start.23 = (bf16[1,432,128]{2,1,0:T(8,128)(2,1)S(1)}, bf16[1,432,128]{2,1,0:T(8,128)(2,1)S(1)}, u32[]{:S(2)}, u32[]{:S(2)}) collective-permute-start(bf16[1,432,128]{2,1,0:T(8,128)(2,1)S(1)} %sums.21.refs_4_), channel_id=1, source_target_pairs={{0,16},{4,20},{8,24},{12,28},{16,0},{20,4},{24,8},{28,12},{1,17},{... | collective-permute-start | bytes 331784 | tf_op jit(solution)/shard_map/ppermute | solution.py:422
  93.0 1.5 %collective-permute-start.20 = (bf16[512,128]{1,0:T(8,128)(2,1)S(1)}, bf16[512,128]{1,0:T(8,128)(2,1)S(1)}, u32[]{:S(2)}, u32[]{:S(2)}) collective-permute-start(bf16[512,128]{1,0:T(8,128)(2,1)S(1)} %get-tuple-element.71.refs_6_), channel_id=1, source_target_pairs={{0,2},{1,3},{2,0},{3,1},{4,6},{5,7},{6,4},{7,5},{8,10},{9,11},{10,... | collective-permute-start | bytes 393224 | tf_op jit(solution)/shard_map/ppermute | solution.py:425
  94.5 0.5 collective-permute-start.21
  95.1 8.6 %collective-permute-done.23.refs_5_ = bf16[1,432,128]{2,1,0:T(8,128)(2,1)S(1)} collective-permute-done((bf16[1,432,128]{2,1,0:T(8,128)(2,1)S(1)}, bf16[1,432,128]{2,1,0:T(8,128)(2,1)S(1)}, u32[]{:S(2)}, u32[]{:S(2)}) %collective-permute-start.23) | collective-permute-done | bytes 110624 | tf_op jit(solution)/shard_map/ppermute | solution.py:422
  104.0 2.7 %collective-permute-start.27 = (bf16[1,432,128]{2,1,0:T(8,128)(2,1)S(1)}, bf16[1,432,128]{2,1,0:T(8,128)(2,1)S(1)}, u32[]{:S(2)}, u32[]{:S(2)}) collective-permute-start(bf16[1,432,128]{2,1,0:T(8,128)(2,1)S(1)} %sums.23), channel_id=1, source_target_pairs={{0,16},{4,20},{8,24},{12,28},{16,0},{20,4},{24,8},{28,12},{1,17},{... | collective-permute-start | bytes 331784 | tf_op jit(solution)/shard_map/ppermute | solution.py:422
  106.7 0.9 rows.1
  107.6 5.9 %collective-permute-done.27 = bf16[1,432,128]{2,1,0:T(8,128)(2,1)S(1)} collective-permute-done((bf16[1,432,128]{2,1,0:T(8,128)(2,1)S(1)}, bf16[1,432,128]{2,1,0:T(8,128)(2,1)S(1)}, u32[]{:S(2)}, u32[]{:S(2)}) %collective-permute-start.27) | collective-permute-done | bytes 110624 | tf_op jit(solution)/shard_map/ppermute | solution.py:422
  113.5 3.9 %collective-permute-start.28 = (bf16[2,432,128]{2,1,0:T(8,128)(2,1)S(1)}, bf16[2,432,128]{2,1,0:T(8,128)(2,1)S(1)}, u32[]{:S(2)}, u32[]{:S(2)}) collective-permute-start(bf16[2,432,128]{2,1,0:T(8,128)(2,1)S(1)} %pad_maximum_fusion.1.refs_4_), channel_id=1, source_target_pairs={{0,8},{4,12},{8,0},{12,4},{16,24},{20,28},{24,16},{28,20},{1,9},{5... | collective-permute-start | bytes 663560 | tf_op jit(solution)/shard_map/ppermute | solution.py:422
  117.4 0.5 collective-permute-start.26
  118.0 4.6 %collective-permute-done.28.refs_5_ = bf16[2,432,128]{2,1,0:T(8,128)(2,1)S(1)} collective-permute-done((bf16[2,432,128]{2,1,0:T(8,128)(2,1)S(1)}, bf16[2,432,128]{2,1,0:T(8,128)(2,1)S(1)}, u32[]{:S(2)}, u32[]{:S(2)}) %collective-permute-start.28) | collective-permute-done | bytes 221216 | tf_op jit(solution)/shard_map/ppermute | solution.py:422
  122.5 1.5 %collective-permute-done.30.refs_7_ = bf16[2,432,128]{2,1,0:T(8,128)(2,1)S(1)} collective-permute-done((bf16[2,432,128]{2,1,0:T(8,128)(2,1)S(1)}, bf16[2,432,128]{2,1,0:T(8,128)(2,1)S(1)}, u32[]{:S(2)}, u32[]{:S(2)}) %collective-permute-start.30) | collective-permute-done | bytes 221216 | tf_op jit(solution)/shard_map/ppermute | solution.py:419
  124.0 2.2 %unpack.1 = (f32[544,256]{1,0:T(8,128)}, f32[64,2176]{1,0:T(8,128)}, f32[544,1024]{1,0:T(8,128)}, f32[256,1024]{1,0:T(8,128)}, f32[544]{0:T(1024)}, /*index=5*/f32[256]{0:T(256)}, f32[256]{0:T(256)}, f32[256]{0:T(256)}) custom-call(bf16[2,672,128]{2,1,0:T(8,128)(2,1)S(1)} %pad_maximum_fusion.refs_6_.refs_0_, ...), custom_call_target="tpu_custom_call" | custom-call | tf_op jit(solution)/shard_map/unpack/pallas_call | solution.py:638
  (49 shorter events, 1.0 us)
Async XLA Ops:
  12.5 10.8 %collective-permute-start.3 = (bf16[2,4,2,672,128]{4,3,2,1,0:T(8,128)(2,1)}, bf16[2,4,2,672,128]{4,3,2,1,0:T(8,128)(2,1)}, u32[]{:S(2)}, u32[]{:S(2)}) collective-permute-start(bf16[2,4,2,672,128]{4,3,2,1,0:T(8,128)(2,1)} %get-tuple-element.55), channel_id=1, source_target_pairs={{0,4},{4,0},{8,12},{12,8},{16,20},{20,16},{24,28},{28,24},{1,5},{5... | collective-permute-start | bytes 8257544 | tf_op jit(solution)/shard_map/ppermute | solution.py:419
  13.0 10.3 %copy-start = (bf16[2,4,2,672,128]{4,3,2,1,0:T(8,128)(2,1)S(1)}, bf16[2,4,2,672,128]{4,3,2,1,0:T(8,128)(2,1)}, u32[]{:S(2)}) copy-start(bf16[2,4,2,672,128]{4,3,2,1,0:T(8,128)(2,1)} %get-tuple-element.54) | copy-start | bytes 8257540
  23.2 32.2 %collective-permute-start.7 = (bf16[2,4,2,432,128]{4,3,2,1,0:T(8,128)(2,1)}, bf16[2,4,2,432,128]{4,3,2,1,0:T(8,128)(2,1)S(1)}, u32[]{:S(2)}, u32[]{:S(2)}) collective-permute-start(bf16[2,4,2,432,128]{4,3,2,1,0:T(8,128)(2,1)} %get-tuple-element.61), channel_id=1, source_target_pairs={{0,4},{4,0},{8,12},{12,8},{16,20},{20,16},{24,28},{28,24},{1,5},{5... | collective-permute-start | bytes 5308424 | tf_op jit(solution)/shard_map/ppermute | solution.py:419
  23.3 7.7 %copy-start.6 = (bf16[2,2,256,128]{3,2,1,0:T(8,128)(2,1)S(1)}, bf16[2,2,256,128]{3,2,1,0:T(8,128)(2,1)}, u32[]{:S(2)}) copy-start(bf16[2,2,256,128]{3,2,1,0:T(8,128)(2,1)} %get-tuple-element.50) | copy-start | bytes 786436
  23.3 9.3 %copy-start.5 = (bf16[2,2,256,128]{3,2,1,0:T(8,128)(2,1)S(1)}, bf16[2,2,256,128]{3,2,1,0:T(8,128)(2,1)}, u32[]{:S(2)}) copy-start(bf16[2,2,256,128]{3,2,1,0:T(8,128)(2,1)} %get-tuple-element.51) | copy-start | bytes 786436
  26.5 20.1 %collective-permute-start.5 = (bf16[2,2,672,128]{3,2,1,0:T(8,128)(2,1)S(1)}, bf16[2,2,672,128]{3,2,1,0:T(8,128)(2,1)S(1)}, u32[]{:S(2)}, u32[]{:S(2)}) collective-permute-start(bf16[2,2,672,128]{3,2,1,0:T(8,128)(2,1)S(1)} %get-tuple-element.58), channel_id=1, source_target_pairs={{0,1},{1,0},{2,3},{3,2},{4,5},{5,4},{6,7},{7,6},{8,9},{9,8},{10,11... | collective-permute-start | bytes 2064392 | tf_op jit(solution)/shard_map/ppermute | solution.py:425
  29.5 17.1 %collective-permute-start.4 = (bf16[2,2,672,128]{3,2,1,0:T(8,128)(2,1)S(1)}, bf16[2,2,672,128]{3,2,1,0:T(8,128)(2,1)S(1)}, u32[]{:S(2)}, u32[]{:S(2)}) collective-permute-start(bf16[2,2,672,128]{3,2,1,0:T(8,128)(2,1)S(1)} %get-tuple-element.57), channel_id=1, source_target_pairs={{0,2},{1,3},{2,0},{3,1},{4,6},{5,7},{6,4},{7,5},{8,10},{9,11},{10,... | collective-permute-start | bytes 2064392 | tf_op jit(solution)/shard_map/ppermute | solution.py:425
  31.0 13.2 %collective-permute-start = (bf16[2,2,256,128]{3,2,1,0:T(8,128)(2,1)S(1)}, bf16[2,2,256,128]{3,2,1,0:T(8,128)(2,1)S(1)}, u32[]{:S(2)}, u32[]{:S(2)}) collective-permute-start(bf16[2,2,256,128]{3,2,1,0:T(8,128)(2,1)S(1)} %copy-done.6), channel_id=1, source_target_pairs={{0,8},{4,12},{8,0},{12,4},{16,24},{20,28},{24,16},{28,20},{1,9},{5... | collective-permute-start | bytes 786440 | tf_op jit(solution)/shard_map/ppermute | solution.py:422
  32.6 19.1 %copy-start.4 = (bf16[2,2,256,128]{3,2,1,0:T(8,128)(2,1)S(1)}, bf16[2,2,256,128]{3,2,1,0:T(8,128)(2,1)}, u32[]{:S(2)}) copy-start(bf16[2,2,256,128]{3,2,1,0:T(8,128)(2,1)} %get-tuple-element.53) | copy-start | bytes 786436
  32.6 22.8 %copy-start.1 = (bf16[2,4,2,432,128]{4,3,2,1,0:T(8,128)(2,1)S(1)}, bf16[2,4,2,432,128]{4,3,2,1,0:T(8,128)(2,1)}, u32[]{:S(2)}) copy-start(bf16[2,4,2,432,128]{4,3,2,1,0:T(8,128)(2,1)} %get-tuple-element.60) | copy-start | bytes 5308420
  32.6 14.0 %collective-permute-start.1 = (bf16[2,2,256,128]{3,2,1,0:T(8,128)(2,1)S(1)}, bf16[2,2,256,128]{3,2,1,0:T(8,128)(2,1)S(1)}, u32[]{:S(2)}, u32[]{:S(2)}) collective-permute-start(bf16[2,2,256,128]{3,2,1,0:T(8,128)(2,1)S(1)} %copy-done.5), channel_id=1, source_target_pairs={{0,16},{4,20},{8,24},{12,28},{16,0},{20,4},{24,8},{28,12},{1,17},{... | collective-permute-start | bytes 786440 | tf_op jit(solution)/shard_map/ppermute | solution.py:422
  49.6 10.7 %collective-permute-start.6 = (bf16[2,672,128]{2,1,0:T(8,128)(2,1)S(1)}, bf16[2,672,128]{2,1,0:T(8,128)(2,1)S(1)}, u32[]{:S(2)}, u32[]{:S(2)}) collective-permute-start(bf16[2,672,128]{2,1,0:T(8,128)(2,1)S(1)} %get-tuple-element.59.refs_5_), channel_id=1, source_target_pairs={{0,1},{1,0},{2,3},{3,2},{4,5},{5,4},{6,7},{7,6},{8,9},{9,8},{10,11... | collective-permute-start | bytes 1032200 | tf_op jit(solution)/shard_map/ppermute | solution.py:425
  50.2 11.0 %collective-permute-start.8 = (bf16[2,672,128]{2,1,0:T(8,128)(2,1)S(1)}, bf16[2,672,128]{2,1,0:T(8,128)(2,1)S(1)}, u32[]{:S(2)}, u32[]{:S(2)}) collective-permute-start(bf16[2,672,128]{2,1,0:T(8,128)(2,1)S(1)} %get-tuple-element.62.refs_4_), channel_id=1, source_target_pairs={{0,2},{1,3},{2,0},{3,1},{4,6},{5,7},{6,4},{7,5},{8,10},{9,11},{10,... | collective-permute-start | bytes 1032200 | tf_op jit(solution)/shard_map/ppermute | solution.py:425
  51.8 11.5 %collective-permute-start.2 = (bf16[2,2,256,128]{3,2,1,0:T(8,128)(2,1)S(1)}, bf16[2,2,256,128]{3,2,1,0:T(8,128)(2,1)S(1)}, u32[]{:S(2)}, u32[]{:S(2)}) collective-permute-start(bf16[2,2,256,128]{3,2,1,0:T(8,128)(2,1)S(1)} %copy-done.4), channel_id=1, source_target_pairs={{0,24},{4,28},{8,16},{12,20},{16,8},{20,12},{24,0},{28,4},{1,25},{... | collective-permute-start | bytes 786440 | tf_op jit(solution)/shard_map/ppermute | solution.py:422
  55.7 14.5 %collective-permute-start.11 = (bf16[2,2,432,128]{3,2,1,0:T(8,128)(2,1)S(1)}, bf16[2,2,432,128]{3,2,1,0:T(8,128)(2,1)S(1)}, u32[]{:S(2)}, u32[]{:S(2)}) collective-permute-start(bf16[2,2,432,128]{3,2,1,0:T(8,128)(2,1)S(1)} %get-tuple-element.64.refs_5_), channel_id=1, source_target_pairs={{0,2},{1,3},{2,0},{3,1},{4,6},{5,7},{6,4},{7,5},{8,10},{9,11},{10,... | collective-permute-start | bytes 1327112 | tf_op jit(solution)/shard_map/ppermute | solution.py:425
  56.2 7.0 %copy-start.2 = (bf16[2,2,256,128]{3,2,1,0:T(8,128)(2,1)S(1)}, bf16[2,2,256,128]{3,2,1,0:T(8,128)(2,1)}, u32[]{:S(2)}) copy-start(bf16[2,2,256,128]{3,2,1,0:T(8,128)(2,1)} %get-tuple-element.49.refs_0_.rest_0_) | copy-start | bytes 786436
  56.3 9.9 %copy-start.3 = (s32[2,8192,4]{1,2,0:T(4,128)S(1)}, s32[2,8192,4]{1,2,0:T(4,128)}, u32[]{:S(2)}) copy-start(s32[2,8192,4]{1,2,0:T(4,128)} %param.23) | copy-start | bytes 786436
  56.3 14.0 %collective-permute-start.12 = (bf16[2,2,432,128]{3,2,1,0:T(8,128)(2,1)S(1)}, bf16[2,2,432,128]{3,2,1,0:T(8,128)(2,1)S(1)}, u32[]{:S(2)}, u32[]{:S(2)}) collective-permute-start(bf16[2,2,432,128]{3,2,1,0:T(8,128)(2,1)S(1)} %get-tuple-element.63.refs_4_), channel_id=1, source_target_pairs={{0,1},{1,0},{2,3},{3,2},{4,5},{5,4},{6,7},{7,6},{8,9},{9,8},{10,11... | collective-permute-start | bytes 1327112 | tf_op jit(solution)/shard_map/ppermute | solution.py:425
  63.3 2.8 %collective-permute-start.10 = (bf16[2,2,256,128]{3,2,1,0:T(8,128)(2,1)S(1)}, bf16[2,2,256,128]{3,2,1,0:T(8,128)(2,1)S(1)}, u32[]{:S(2)}, u32[]{:S(2)}) collective-permute-start(bf16[2,2,256,128]{3,2,1,0:T(8,128)(2,1)S(1)} %get-tuple-element.66), channel_id=1, source_target_pairs={{0,4},{4,0},{8,12},{12,8},{16,20},{20,16},{24,28},{28,24},{1,5},{5... | collective-permute-start | bytes 786440 | tf_op jit(solution)/shard_map/ppermute | solution.py:419
  63.4 2.8 %collective-permute-start.9 = (bf16[2,2,256,128]{3,2,1,0:T(8,128)(2,1)S(1)}, bf16[2,2,256,128]{3,2,1,0:T(8,128)(2,1)S(1)}, u32[]{:S(2)}, u32[]{:S(2)}) collective-permute-start(bf16[2,2,256,128]{3,2,1,0:T(8,128)(2,1)S(1)} %get-tuple-element.65.rest_6_), channel_id=1, source_target_pairs={{0,4},{4,0},{8,12},{12,8},{16,20},{20,16},{24,28},{28,24},{1,5},{5... | collective-permute-start | bytes 786440 | tf_op jit(solution)/shard_map/ppermute | solution.py:419
  63.9 10.6 %collective-permute-start.14 = (bf16[2,672,128]{2,1,0:T(8,128)(2,1)S(1)}, bf16[2,672,128]{2,1,0:T(8,128)(2,1)S(1)}, u32[]{:S(2)}, u32[]{:S(2)}) collective-permute-start(bf16[2,672,128]{2,1,0:T(8,128)(2,1)S(1)} %sums.15.refs_4_), channel_id=1, source_target_pairs={{0,8},{4,12},{8,0},{12,4},{16,24},{20,28},{24,16},{28,20},{1,9},{5... | collective-permute-start | bytes 1032200 | tf_op jit(solution)/shard_map/ppermute | solution.py:422
  70.5 8.7 %collective-permute-start.13 = (bf16[2,432,128]{2,1,0:T(8,128)(2,1)S(1)}, bf16[2,432,128]{2,1,0:T(8,128)(2,1)S(1)}, u32[]{:S(2)}, u32[]{:S(2)}) collective-permute-start(bf16[2,432,128]{2,1,0:T(8,128)(2,1)S(1)} %get-tuple-element.67.refs_6_), channel_id=1, source_target_pairs={{0,1},{1,0},{2,3},{3,2},{4,5},{5,4},{6,7},{7,6},{8,9},{9,8},{10,11... | collective-permute-start | bytes 663560 | tf_op jit(solution)/shard_map/ppermute | solution.py:425
  72.0 7.3 %collective-permute-start.15 = (bf16[2,432,128]{2,1,0:T(8,128)(2,1)S(1)}, bf16[2,432,128]{2,1,0:T(8,128)(2,1)S(1)}, u32[]{:S(2)}, u32[]{:S(2)}) collective-permute-start(bf16[2,432,128]{2,1,0:T(8,128)(2,1)S(1)} %get-tuple-element.68.refs_5_), channel_id=1, source_target_pairs={{0,2},{1,3},{2,0},{3,1},{4,6},{5,7},{6,4},{7,5},{8,10},{9,11},{10,... | collective-permute-start | bytes 663560 | tf_op jit(solution)/shard_map/ppermute | solution.py:425
  76.5 11.2 %collective-permute-start.19 = (bf16[1,672,128]{2,1,0:T(8,128)(2,1)S(1)}, bf16[1,672,128]{2,1,0:T(8,128)(2,1)S(1)}, u32[]{:S(2)}, u32[]{:S(2)}) collective-permute-start(bf16[1,672,128]{2,1,0:T(8,128)(2,1)S(1)} %sums.17.refs_4_), channel_id=1, source_target_pairs={{0,16},{4,20},{8,24},{12,28},{16,0},{20,4},{24,8},{28,12},{1,17},{... | collective-permute-start | bytes 516104 | tf_op jit(solution)/shard_map/ppermute | solution.py:422
  79.4 11.8 %collective-permute-start.18 = (bf16[2,432,128]{2,1,0:T(8,128)(2,1)S(1)}, bf16[2,432,128]{2,1,0:T(8,128)(2,1)S(1)}, u32[]{:S(2)}, u32[]{:S(2)}) collective-permute-start(bf16[2,432,128]{2,1,0:T(8,128)(2,1)S(1)} %sums.18.rest_6_), channel_id=1, source_target_pairs={{0,8},{4,12},{8,0},{12,4},{16,24},{20,28},{24,16},{28,20},{1,9},{5... | collective-permute-start | bytes 663560 | tf_op jit(solution)/shard_map/ppermute | solution.py:422
  85.0 7.9 %collective-permute-start.16 = (bf16[2,512,128]{2,1,0:T(8,128)(2,1)S(1)}, bf16[2,512,128]{2,1,0:T(8,128)(2,1)S(1)}, u32[]{:S(2)}, u32[]{:S(2)}) collective-permute-start(bf16[2,512,128]{2,1,0:T(8,128)(2,1)S(1)} %get-tuple-element.69.refs_6_), channel_id=1, source_target_pairs={{0,1},{1,0},{2,3},{3,2},{4,5},{5,4},{6,7},{7,6},{8,9},{9,8},{10,11... | collective-permute-start | bytes 786440 | tf_op jit(solution)/shard_map/ppermute | solution.py:425
  86.2 6.7 %collective-permute-start.17 = (bf16[2,512,128]{2,1,0:T(8,128)(2,1)S(1)}, bf16[2,512,128]{2,1,0:T(8,128)(2,1)S(1)}, u32[]{:S(2)}, u32[]{:S(2)}) collective-permute-start(bf16[2,512,128]{2,1,0:T(8,128)(2,1)S(1)} %get-tuple-element.70.refs_7_), channel_id=1, source_target_pairs={{0,2},{1,3},{2,0},{3,1},{4,6},{5,7},{6,4},{7,5},{8,10},{9,11},{10,... | collective-permute-start | bytes 786440 | tf_op jit(solution)/shard_map/ppermute | solution.py:425
  89.7 14.2 %collective-permute-start.22 = (bf16[1,672,128]{2,1,0:T(8,128)(2,1)S(1)}, bf16[1,672,128]{2,1,0:T(8,128)(2,1)S(1)}, u32[]{:S(2)}, u32[]{:S(2)}) collective-permute-start(bf16[1,672,128]{2,1,0:T(8,128)(2,1)S(1)} %sums.20.refs_5_), channel_id=1, source_target_pairs={{0,16},{4,20},{8,24},{12,28},{16,0},{20,4},{24,8},{28,12},{1,17},{... | collective-permute-start | bytes 516104 | tf_op jit(solution)/shard_map/ppermute | solution.py:422
  91.3 12.4 %collective-permute-start.23 = (bf16[1,432,128]{2,1,0:T(8,128)(2,1)S(1)}, bf16[1,432,128]{2,1,0:T(8,128)(2,1)S(1)}, u32[]{:S(2)}, u32[]{:S(2)}) collective-permute-start(bf16[1,432,128]{2,1,0:T(8,128)(2,1)S(1)} %sums.21.refs_4_), channel_id=1, source_target_pairs={{0,16},{4,20},{8,24},{12,28},{16,0},{20,4},{24,8},{28,12},{1,17},{... | collective-permute-start | bytes 331784 | tf_op jit(solution)/shard_map/ppermute | solution.py:422
  93.0 13.7 %collective-permute-start.20 = (bf16[512,128]{1,0:T(8,128)(2,1)S(1)}, bf16[512,128]{1,0:T(8,128)(2,1)S(1)}, u32[]{:S(2)}, u32[]{:S(2)}) collective-permute-start(bf16[512,128]{1,0:T(8,128)(2,1)S(1)} %get-tuple-element.71.refs_6_), channel_id=1, source_target_pairs={{0,2},{1,3},{2,0},{3,1},{4,6},{5,7},{6,4},{7,5},{8,10},{9,11},{10,... | collective-permute-start | bytes 393224 | tf_op jit(solution)/shard_map/ppermute | solution.py:425
  94.5 12.2 %collective-permute-start.21 = (bf16[512,128]{1,0:T(8,128)(2,1)S(1)}, bf16[512,128]{1,0:T(8,128)(2,1)S(1)}, u32[]{:S(2)}, u32[]{:S(2)}) collective-permute-start(bf16[512,128]{1,0:T(8,128)(2,1)S(1)} %get-tuple-element.72.refs_7_), channel_id=1, source_target_pairs={{0,1},{1,0},{2,3},{3,2},{4,5},{5,4},{6,7},{7,6},{8,9},{9,8},{10,11... | collective-permute-start | bytes 393224 | tf_op jit(solution)/shard_map/ppermute | solution.py:425
  103.9 13.5 %collective-permute-start.24 = (bf16[2,672,128]{2,1,0:T(8,128)(2,1)S(1)}, bf16[2,672,128]{2,1,0:T(8,128)(2,1)S(1)}, u32[]{:S(2)}, u32[]{:S(2)}) collective-permute-start(bf16[2,672,128]{2,1,0:T(8,128)(2,1)S(1)} %pad_maximum_fusion.refs_6_.refs_0_), channel_id=1, source_target_pairs={{0,8},{4,12},{8,0},{12,4},{16,24},{20,28},{24,16},{28,20},{1,9},{5... | collective-permute-start | bytes 1032200 | tf_op jit(solution)/shard_map/ppermute | solution.py:422
  104.0 9.5 %collective-permute-start.27 = (bf16[1,432,128]{2,1,0:T(8,128)(2,1)S(1)}, bf16[1,432,128]{2,1,0:T(8,128)(2,1)S(1)}, u32[]{:S(2)}, u32[]{:S(2)}) collective-permute-start(bf16[1,432,128]{2,1,0:T(8,128)(2,1)S(1)} %sums.23), channel_id=1, source_target_pairs={{0,16},{4,20},{8,24},{12,28},{16,0},{20,4},{24,8},{28,12},{1,17},{... | collective-permute-start | bytes 331784 | tf_op jit(solution)/shard_map/ppermute | solution.py:422
  113.5 9.0 %collective-permute-start.28 = (bf16[2,432,128]{2,1,0:T(8,128)(2,1)S(1)}, bf16[2,432,128]{2,1,0:T(8,128)(2,1)S(1)}, u32[]{:S(2)}, u32[]{:S(2)}) collective-permute-start(bf16[2,432,128]{2,1,0:T(8,128)(2,1)S(1)} %pad_maximum_fusion.1.refs_4_), channel_id=1, source_target_pairs={{0,8},{4,12},{8,0},{12,4},{16,24},{20,28},{24,16},{28,20},{1,9},{5... | collective-permute-start | bytes 663560 | tf_op jit(solution)/shard_map/ppermute | solution.py:422
  117.4 5.1 %collective-permute-start.25 = (bf16[2,672,128]{2,1,0:T(8,128)(2,1)S(1)}, bf16[2,672,128]{2,1,0:T(8,128)(2,1)S(1)}, u32[]{:S(2)}, u32[]{:S(2)}) collective-permute-start(bf16[2,672,128]{2,1,0:T(8,128)(2,1)S(1)} %pad_maximum_fusion.refs_6_.refs_0_), channel_id=1, source_target_pairs={{0,4},{4,0},{8,12},{12,8},{16,20},{20,16},{24,28},{28,24},{1,5},{5... | collective-permute-start | bytes 1032200 | tf_op jit(solution)/shard_map/ppermute | solution.py:419
  117.4 6.6 %collective-permute-start.26 = (bf16[2,672,128]{2,1,0:T(8,128)(2,1)S(1)}, bf16[2,672,128]{2,1,0:T(8,128)(2,1)S(1)}, u32[]{:S(2)}, u32[]{:S(2)}) collective-permute-start(bf16[2,672,128]{2,1,0:T(8,128)(2,1)S(1)} %collective-permute-done.24.refs_1_), channel_id=1, source_target_pairs={{0,4},{4,0},{8,12},{12,8},{16,20},{20,16},{24,28},{28,24},{1,5},{5... | collective-permute-start | bytes 1032200 | tf_op jit(solution)/shard_map/ppermute | solution.py:419
  117.9 4.6 %collective-permute-start.29 = (bf16[2,432,128]{2,1,0:T(8,128)(2,1)S(1)}, bf16[2,432,128]{2,1,0:T(8,128)(2,1)S(1)}, u32[]{:S(2)}, u32[]{:S(2)}) collective-permute-start(bf16[2,432,128]{2,1,0:T(8,128)(2,1)S(1)} %pad_maximum_fusion.1.refs_4_), channel_id=1, source_target_pairs={{0,4},{4,0},{8,12},{12,8},{16,20},{20,16},{24,28},{28,24},{1,5},{5... | collective-permute-start | bytes 663560 | tf_op jit(solution)/shard_map/ppermute | solution.py:419
  122.5 1.5 %collective-permute-start.30 = (bf16[2,432,128]{2,1,0:T(8,128)(2,1)S(1)}, bf16[2,432,128]{2,1,0:T(8,128)(2,1)S(1)}, u32[]{:S(2)}, u32[]{:S(2)}) collective-permute-start(bf16[2,432,128]{2,1,0:T(8,128)(2,1)S(1)} %collective-permute-done.28.refs_5_), channel_id=1, source_target_pairs={{0,4},{4,0},{8,12},{12,8},{16,20},{20,16},{24,28},{28,24},{1,5},{5... | collective-permute-start | bytes 663560 | tf_op jit(solution)/shard_map/ppermute | solution.py:419

commit v9 on v8

--- a/solution.py
+++ b/solution.py
@@ -368,6 +368,53 @@
         lax.fori_loop(0, rows // chunk, one_chunk, 0)
 
 
+def fetch_sum_kernel(plan, n_in, *refs):
+    outs = refs[n_in : n_in + len(plan)]
+    held, sems = refs[n_in + len(plan) : -1], refs[-1]
+    copies, by_out = [], []
+    for terms in plan:
+        parts = []
+        for which, picks in terms:
+            at = len(copies)
+            place = tuple(
+                pl.ds(pick.start, pick.stop - pick.start) if isinstance(pick, slice) else pick
+                for pick in picks
+            )
+            copies.append(pltpu.make_async_copy(refs[which].at[place], held[at], sems.at[at]))
+            parts.append((at, tuple(slice(0, size) for size in held[at].shape)))
+        by_out.append(parts)
+    for copy in copies:
+        copy.start()
+    for out, parts in zip(outs, by_out):
+        for at, _ in parts:
+            copies[at].wait()
+        sum_kernel([parts], 0, *held, out)
+
+
+def fetch_sums(groups, deps):
+    arrays, plan, shapes, scratch = [], [], [], []
+    for items in groups:
+        kept = tuple(pick.stop - pick.start for pick in items[0][1] if isinstance(pick, slice))
+        shapes.append(jax.ShapeDtypeStruct(kept, bf16))
+        terms = []
+        for array, picks in items:
+            found = [at for at, known in enumerate(arrays) if known is array]
+            if not found:
+                arrays.append(array)
+            terms.append((found[0] if found else len(arrays) - 1, tuple(picks)))
+            scratch.append(pltpu.VMEM(kept, array.dtype))
+        plan.append(terms)
+    n_in = len(arrays) + len(deps)
+    return call(
+        functools.partial(fetch_sum_kernel, plan, n_in),
+        shapes,
+        scratch + [pltpu.SemaphoreType.DMA((len(scratch),))],
+        [whole(pltpu.HBM)] * len(arrays) + [whole(pl.ANY)] * len(deps),
+        "first_sums",
+        24,
+    )(*arrays, *deps)
+
+
 def take_sums(groups, deps, dtype=bf16):
     arrays, plan, shapes = [], [], []
     for items in groups:
@@ -550,9 +597,22 @@
             self.low = Halving([keep, got], low_first, [0])
             self.high = Halving([keep, got], high_first, [1])
 
+        def first_step(self, deps):
+            halves = (self.low, self.high)
+            sent = fetch_sums([half.part(0) for half in halves], deps)
+            self.near = [half.items for half in halves]
+            for half, value in zip(halves, sent):
+                half.items = []
+                half.add(swap_row(value, half.order[0]))
+            return list(sent)
+
+        def settle(self, deps):
+            for half, value in zip((self.low, self.high), fetch_sums(self.near, deps)):
+                half.add(value)
+                half.items.reverse()
+
         def row_step(self, at, deps):
-            if at > 0:
-                deps = [*deps, self.low.items[-1][0], self.high.items[-1][0]]
+            deps = [*deps, self.low.items[-1][0], self.high.items[-1][0]]
             return row_step((self.low, self.high), at, deps)
 
         def z_step(self, stage, deps):
@@ -581,18 +641,20 @@
 
     (got1,) = after([got1], [pooled_out[0]])
     one, two = Dense(keep1, got1), Dense(keep2, got2)
-    one.row_step(0, [])
+    one.first_step([])
     values, half = {0: pooled_out[0]}, n_z // 2
     for which in [half, *range(1, half)]:
         values[which] = swap_z(pooled_out[which], which)
     for which in range(half + 1, n_z):
         (moved,) = after([pooled_out[which]], [values[half], values[which - half]])
         values[which] = swap_z(moved, which)
+    one.settle([values[1]])
     last = [values[which] for which in range(1, half + 1)]
     for at in range(1, row_bits):
         last = one.row_step(at, last)
-    last = two.row_step(0, last)
+    last = two.first_step(last)
     last = one.z_step(0, last)
+    two.settle(last)
     values = [values[which] for which in range(n_z)]
     far_values = call(
         functools.partial(select_kernel, n_z),

time: 126 us -> 119 us (0.944)
  Pallas kernels: 46.7 us -> 41 us
  waiting for transfers between devices: 37 us -> 34.7 us
    pallas_call x12 -> x10, Pallas kernels: 13.5 us -> 1.75 us  [take_sums(): call(functools.partial(sum_kernel, plan, len(arrays)), shapes, [], [whole...]
    pallas_call x0 -> x4, Pallas kernels: none -> 6 us  [fetch_sums(): call(functools.partial(fetch_sum_kernel, plan, n_in), shapes, scratch + [...]
    ppermute x11, waiting for transfers between devices: 32 us -> 26.3 us  [swap_z(): lax.ppermute(value, 'table', [(at, at ^ 2 * which) for at in range(n_tabl...]
    ppermute x12, waiting for transfers between devices: 3.52 us -> 6.89 us  [swap_row(): lax.ppermute(value, 'row', [(at, at ^ 1 << bit) for at in range(n_row)])]
  transfers between devices with their start and end apart: 31 -> 31, of which waited for: 9 -> 13; matrix products, arithmetic and copies ran while one was open for 0% -> 0% of each run, Pallas kernels for 26% -> 23%
where the time goes in v9:
time: 119 us; the launch traced here: 118 us
  starting transfers between devices  41.7 us (35%)
  Pallas kernels  41 us (34%)
  waiting for transfers between devices  34.7 us (29%)
    ppermute x11, waiting for transfers between devices, swap_z(): lax.ppermute(value, 'table', [(at, at ^ 2 * which) for at in range(n_tabl...  26.3 us
    ppermute x11, starting transfers between devices, swap_z(): lax.ppermute(value, 'table', [(at, at ^ 2 * which) for at in range(n_tabl...  24.2 us
    ppermute x12, starting transfers between devices, swap_row(): lax.ppermute(value, 'row', [(at, at ^ 1 << bit) for at in range(n_row)])  15.8 us
    pallas_call x1, Pallas kernels, local(): call(front_kernel, [packed(rows_front)] * 2 + [wide(feat, batch), wide(ba...  11.9 us
    pallas_call x1, Pallas kernels, local(): call(functools.partial(middle_kernel, n_z), [packed(rows_back)] * 2 + [wi...  10.1 us
    pallas_call x2, Pallas kernels, local(): pl.pallas_call(functools.partial(count_kernel, n_row, table, hot, n_z), o...  8.04 us
    ppermute x12, waiting for transfers between devices, swap_row(): lax.ppermute(value, 'row', [(at, at ^ 1 << bit) for at in range(n_row)])  6.89 us
    pallas_call x4, Pallas kernels, fetch_sums(): call(functools.partial(fetch_sum_kernel, plan, n_in), shapes, scratch + [...  6 us
  transfers between devices with their start and end apart: 31, of which 13 were waited for; matrix products, arithmetic and copies ran while one was open for 0% of the time, Pallas kernels for 23%

profile of v9, /device:TPU:0, one launch (start us, length us, event | category | flops | bytes accessed | tf_op | source)
XLA Modules:
  0.0 118.4 jit_solution(13620349805848582304)
XLA Ops:
  0.6 11.9 %front.1 = (bf16[2,4,2,672,128]{4,3,2,1,0:T(8,128)(2,1)}, bf16[2,4,2,672,128]{4,3,2,1,0:T(8,128)(2,1)}, bf16[2176,256]{1,0:T(8,128)(2,1)}, bf16[256,1024]{1,0:T(8,128)(2,1)}, f32[24,128]{1,0:T(8,128)}) custom-call(bf16[256,128]{1,0:T(8,128)(2,1)} %refs_0_.3, bf16[256,2048]{1,0:T(8,128)(2,1)} %refs_1_.3, bf16[2176,256]{1,0:T(8,128)(2,1)} %refs_2_.3, ...), custom_call_target="tpu_custom_call" | custom-call | tf_op jit(solution)/shard_map/front/pallas_call | solution.py:504
  12.5 0.5 collective-permute-start.3
  13.1 10.1 %middle.1 = (bf16[2,4,2,432,128]{4,3,2,1,0:T(8,128)(2,1)}, bf16[2,4,2,432,128]{4,3,2,1,0:T(8,128)(2,1)}, bf16[2,2,256,128]{3,2,1,0:T(8,128)(2,1)}, bf16[2,2,256,...) custom-call(bf16[256,128]{1,0:T(8,128)(2,1)} %refs_0_.3, ...), custom_call_target="tpu_custom_call" | custom-call | tf_op jit(solution)/shard_map/middle/pallas_call | solution.py:531
  23.4 2.0 %first_sums.5 = (bf16[2,2,672,128]{3,2,1,0:T(8,128)(2,1)S(1)}, bf16[2,2,672,128]{3,2,1,0:T(8,128)(2,1)S(1)}) custom-call(bf16[2,2,2,2,672,128]{5,4,3,2,1,0:T(8,128)(2,1)S(1)} %bitcast.7, bf16[2,2,2,2,672,128]{5,4,3,2,1,0:T(8,128)(2,1)} %bitcast.2.refs_1_.refs_3_, bf16[2,2,2,2,672,128]{5,4,3,2,1,0:T(8,128)(2,1)S(1)} %bitcast.8, ...), custom_call_target="tpu_custom_call" | custom-call | tf_op jit(solution)/shard_map/first_sums/pallas_call | solution.py:408
  25.4 3.0 %collective-permute-start.4 = (bf16[2,2,672,128]{3,2,1,0:T(8,128)(2,1)S(1)}, bf16[2,2,672,128]{3,2,1,0:T(8,128)(2,1)S(1)}, u32[]{:S(2)}, u32[]{:S(2)}) collective-permute-start(bf16[2,2,672,128]{3,2,1,0:T(8,128)(2,1)S(1)} %get-tuple-element.62), channel_id=1, source_target_pairs={{0,2},{1,3},{2,0},{3,1},{4,6},{5,7},{6,4},{7,5},{8,10},{9,11},{10,... | collective-permute-start | bytes 2064392 | tf_op jit(solution)/shard_map/ppermute | solution.py:472
  28.4 1.5 %collective-permute-start.5 = (bf16[2,2,672,128]{3,2,1,0:T(8,128)(2,1)S(1)}, bf16[2,2,672,128]{3,2,1,0:T(8,128)(2,1)S(1)}, u32[]{:S(2)}, u32[]{:S(2)}) collective-permute-start(bf16[2,2,672,128]{3,2,1,0:T(8,128)(2,1)S(1)} %get-tuple-element.64), channel_id=1, source_target_pairs={{0,1},{1,0},{2,3},{3,2},{4,5},{5,4},{6,7},{7,6},{8,9},{9,8},{10,11... | collective-permute-start | bytes 2064392 | tf_op jit(solution)/shard_map/ppermute | solution.py:472
  29.9 1.6 %collective-permute-start = (bf16[2,2,256,128]{3,2,1,0:T(8,128)(2,1)S(1)}, bf16[2,2,256,128]{3,2,1,0:T(8,128)(2,1)S(1)}, u32[]{:S(2)}, u32[]{:S(2)}) collective-permute-start(bf16[2,2,256,128]{3,2,1,0:T(8,128)(2,1)S(1)} %copy-done.6), channel_id=1, source_target_pairs={{0,8},{4,12},{8,0},{12,4},{16,24},{20,28},{24,16},{28,20},{1,9},{5... | collective-permute-start | bytes 786440 | tf_op jit(solution)/shard_map/ppermute | solution.py:469
  31.5 2.6 %collective-permute-start.1 = (bf16[2,2,256,128]{3,2,1,0:T(8,128)(2,1)S(1)}, bf16[2,2,256,128]{3,2,1,0:T(8,128)(2,1)S(1)}, u32[]{:S(2)}, u32[]{:S(2)}) collective-permute-start(bf16[2,2,256,128]{3,2,1,0:T(8,128)(2,1)S(1)} %copy-done.5), channel_id=1, source_target_pairs={{0,16},{4,20},{8,24},{12,28},{16,0},{20,4},{24,8},{28,12},{1,17},{... | collective-permute-start | bytes 786440 | tf_op jit(solution)/shard_map/ppermute | solution.py:469
  34.1 9.0 %collective-permute-done.refs_4_.refs_1_.rest_1_ = bf16[2,2,256,128]{3,2,1,0:T(8,128)(2,1)S(1)} collective-permute-done((bf16[2,2,256,128]{3,2,1,0:T(8,128)(2,1)S(1)}, bf16[2,2,256,128]{3,2,1,0:T(8,128)(2,1)S(1)}, u32[]{:S(2)}, u32[]{:S(2)}) %collective-permute-start) | collective-permute-done | bytes 262176 | tf_op jit(solution)/shard_map/ppermute | solution.py:469
  43.1 1.8 %first_sums.4 = (bf16[2,2,672,128]{3,2,1,0:T(8,128)(2,1)S(1)}, bf16[2,2,672,128]{3,2,1,0:T(8,128)(2,1)S(1)}) custom-call(bf16[2,2,2,2,672,128]{5,4,3,2,1,0:T(8,128)(2,1)S(1)} %bitcast.9, bf16[2,2,2,2,672,128]{5,4,3,2,1,0:T(8,128)(2,1)} %bitcast.2.refs_1_.refs_3_, bf16[2,2,2,2,672,128]{5,4,3,2,1,0:T(8,128)(2,1)S(1)} %bitcast.10, ...), custom_call_target="tpu_custom_call" | custom-call | tf_op jit(solution)/shard_map/first_sums/pallas_call | solution.py:408
  44.9 0.6 collective-permute-done.1.refs_5_.refs_2_.rest_2_
  45.5 0.3 sums.10
  45.8 1.6 %collective-permute-start.6 = (bf16[2,672,128]{2,1,0:T(8,128)(2,1)S(1)}, bf16[2,672,128]{2,1,0:T(8,128)(2,1)S(1)}, u32[]{:S(2)}, u32[]{:S(2)}) collective-permute-start(bf16[2,672,128]{2,1,0:T(8,128)(2,1)S(1)} %get-tuple-element.65.refs_5_), channel_id=1, source_target_pairs={{0,1},{1,0},{2,3},{3,2},{4,5},{5,4},{6,7},{7,6},{8,9},{9,8},{10,11... | collective-permute-start | bytes 1032200 | tf_op jit(solution)/shard_map/ppermute | solution.py:472
  47.4 0.5 collective-permute-start.8
  47.9 3.6 %collective-permute-start.2 = (bf16[2,2,256,128]{3,2,1,0:T(8,128)(2,1)S(1)}, bf16[2,2,256,128]{3,2,1,0:T(8,128)(2,1)S(1)}, u32[]{:S(2)}, u32[]{:S(2)}) collective-permute-start(bf16[2,2,256,128]{3,2,1,0:T(8,128)(2,1)S(1)} %copy-done.4), channel_id=1, source_target_pairs={{0,24},{4,28},{8,16},{12,20},{16,8},{20,12},{24,0},{28,4},{1,25},{... | collective-permute-start | bytes 786440 | tf_op jit(solution)/shard_map/ppermute | solution.py:469
  51.5 1.1 first_sums.6
  52.6 0.6 collective-permute-start.12
  53.2 1.5 %collective-permute-start.11 = (bf16[2,2,432,128]{3,2,1,0:T(8,128)(2,1)S(1)}, bf16[2,2,432,128]{3,2,1,0:T(8,128)(2,1)S(1)}, u32[]{:S(2)}, u32[]{:S(2)}) collective-permute-start(bf16[2,2,432,128]{3,2,1,0:T(8,128)(2,1)S(1)} %get-tuple-element.70.refs_4_), channel_id=1, source_target_pairs={{0,2},{1,3},{2,0},{3,1},{4,6},{5,7},{6,4},{7,5},{8,10},{9,11},{10,... | collective-permute-start | bytes 1327112 | tf_op jit(solution)/shard_map/ppermute | solution.py:472
  54.7 1.2 %collective-permute-done.6.refs_2_ = bf16[2,672,128]{2,1,0:T(8,128)(2,1)S(1)} collective-permute-done((bf16[2,672,128]{2,1,0:T(8,128)(2,1)S(1)}, bf16[2,672,128]{2,1,0:T(8,128)(2,1)S(1)}, u32[]{:S(2)}, u32[]{:S(2)}) %collective-permute-start.6) | collective-permute-done | bytes 344096 | tf_op jit(solution)/shard_map/ppermute | solution.py:472
  56.0 2.2 %collective-permute-done.8.refs_5_.refs_2_ = bf16[2,672,128]{2,1,0:T(8,128)(2,1)S(1)} collective-permute-done((bf16[2,672,128]{2,1,0:T(8,128)(2,1)S(1)}, bf16[2,672,128]{2,1,0:T(8,128)(2,1)S(1)}, u32[]{:S(2)}, u32[]{:S(2)}) %collective-permute-start.8) | collective-permute-done | bytes 344096 | tf_op jit(solution)/shard_map/ppermute | solution.py:472
  58.5 0.5 collective-permute-start.9
  59.0 3.3 %collective-permute-start.14 = (bf16[2,672,128]{2,1,0:T(8,128)(2,1)S(1)}, bf16[2,672,128]{2,1,0:T(8,128)(2,1)S(1)}, u32[]{:S(2)}, u32[]{:S(2)}) collective-permute-start(bf16[2,672,128]{2,1,0:T(8,128)(2,1)S(1)} %sums.11.refs_4_), channel_id=1, source_target_pairs={{0,8},{4,12},{8,0},{12,4},{16,24},{20,28},{24,16},{28,20},{1,9},{5... | collective-permute-start | bytes 1032200 | tf_op jit(solution)/shard_map/ppermute | solution.py:469
  62.3 1.1 first_sums.7
  63.5 4.0 %counts.2.refs_4_ = bf16[4,512,128]{2,1,0:T(8,128)(2,1)S(1)} custom-call(s32[2,4,8192]{2,1,0:T(4,128)S(1)} %bitcast.25, bf16[2,2,256,128]{3,2,1,0:T(8,128)(2,1)S(1)} %copy-done.2, bf16[2,2,256,128]{3,2,1,0:T(8,128)(2,1)S(1)} %collective-permute-done.refs_4_.refs_1_.rest_1_, bf16[2,2,256,128]{3,2,1,0:T(8,128)(2,1)S(1)} %collective-permute-done.1.refs_5_.refs_2_.rest_2_, ...), custom_call_target="tpu_custom_call" | custom-call | tf_op jit(solution)/shard_map/counts/pallas_call | solution.py:671
  67.7 0.6 collective-permute-start.13
  68.3 1.4 %collective-permute-start.15 = (bf16[2,432,128]{2,1,0:T(8,128)(2,1)S(1)}, bf16[2,432,128]{2,1,0:T(8,128)(2,1)S(1)}, u32[]{:S(2)}, u32[]{:S(2)}) collective-permute-start(bf16[2,432,128]{2,1,0:T(8,128)(2,1)S(1)} %get-tuple-element.76.refs_4_), channel_id=1, source_target_pairs={{0,2},{1,3},{2,0},{3,1},{4,6},{5,7},{6,4},{7,5},{8,10},{9,11},{10,... | collective-permute-start | bytes 663560 | tf_op jit(solution)/shard_map/ppermute | solution.py:472
  69.8 0.9 collective-permute-done.14.refs_3_.refs_6_
  70.8 2.8 %collective-permute-start.19 = (bf16[1,672,128]{2,1,0:T(8,128)(2,1)S(1)}, bf16[1,672,128]{2,1,0:T(8,128)(2,1)S(1)}, u32[]{:S(2)}, u32[]{:S(2)}) collective-permute-start(bf16[1,672,128]{2,1,0:T(8,128)(2,1)S(1)} %sums.13.refs_3_), channel_id=1, source_target_pairs={{0,16},{4,20},{8,24},{12,28},{16,0},{20,4},{24,8},{28,12},{1,17},{... | collective-permute-start | bytes 516104 | tf_op jit(solution)/shard_map/ppermute | solution.py:469
  73.6 1.3 %collective-permute-done.13.refs_2_ = bf16[2,432,128]{2,1,0:T(8,128)(2,1)S(1)} collective-permute-done((bf16[2,432,128]{2,1,0:T(8,128)(2,1)S(1)}, bf16[2,432,128]{2,1,0:T(8,128)(2,1)S(1)}, u32[]{:S(2)}, u32[]{:S(2)}) %collective-permute-start.13) | collective-permute-done | bytes 221216 | tf_op jit(solution)/shard_map/ppermute | solution.py:472
  75.3 0.6 collective-permute-start.18
  76.0 4.0 %counts.3.refs_2_ = bf16[4,512,128]{2,1,0:T(8,128)(2,1)S(1)} custom-call(s32[2,4,8192]{2,1,0:T(4,128)S(1)} %bitcast.26, bf16[2,2,256,128]{3,2,1,0:T(8,128)(2,1)S(1)} %copy-done.2, bf16[2,2,256,128]{3,2,1,0:T(8,128)(2,1)S(1)} %collective-permute-done.refs_4_.refs_1_.rest_1_, bf16[2,2,256,128]{3,2,1,0:T(8,128)(2,1)S(1)} %collective-permute-done.1.refs_5_.refs_2_.rest_2_, ...), custom_call_target="tpu_custom_call" | custom-call | tf_op jit(solution)/shard_map/counts/pallas_call | solution.py:671
  80.2 1.6 %collective-permute-start.16 = (bf16[2,512,128]{2,1,0:T(8,128)(2,1)S(1)}, bf16[2,512,128]{2,1,0:T(8,128)(2,1)S(1)}, u32[]{:S(2)}, u32[]{:S(2)}) collective-permute-start(bf16[2,512,128]{2,1,0:T(8,128)(2,1)S(1)} %get-tuple-element.77.refs_5_), channel_id=1, source_target_pairs={{0,1},{1,0},{2,3},{3,2},{4,5},{5,4},{6,7},{7,6},{8,9},{9,8},{10,11... | collective-permute-start | bytes 786440 | tf_op jit(solution)/shard_map/ppermute | solution.py:472
  81.8 1.4 %collective-permute-start.17 = (bf16[2,512,128]{2,1,0:T(8,128)(2,1)S(1)}, bf16[2,512,128]{2,1,0:T(8,128)(2,1)S(1)}, u32[]{:S(2)}, u32[]{:S(2)}) collective-permute-start(bf16[2,512,128]{2,1,0:T(8,128)(2,1)S(1)} %get-tuple-element.78.refs_6_), channel_id=1, source_target_pairs={{0,2},{1,3},{2,0},{3,1},{4,6},{5,7},{6,4},{7,5},{8,10},{9,11},{10,... | collective-permute-start | bytes 786440 | tf_op jit(solution)/shard_map/ppermute | solution.py:472
  83.4 2.5 %collective-permute-start.22 = (bf16[1,672,128]{2,1,0:T(8,128)(2,1)S(1)}, bf16[1,672,128]{2,1,0:T(8,128)(2,1)S(1)}, u32[]{:S(2)}, u32[]{:S(2)}) collective-permute-start(bf16[1,672,128]{2,1,0:T(8,128)(2,1)S(1)} %sums.16.refs_4_), channel_id=1, source_target_pairs={{0,16},{4,20},{8,24},{12,28},{16,0},{20,4},{24,8},{28,12},{1,17},{... | collective-permute-start | bytes 516104 | tf_op jit(solution)/shard_map/ppermute | solution.py:469
  86.0 0.5 collective-permute-start.23
  86.5 0.7 collective-permute-done.16.refs_1_
  87.2 1.1 collective-permute-done.17.refs_3_.refs_4_
  88.5 1.5 %collective-permute-start.20 = (bf16[512,128]{1,0:T(8,128)(2,1)S(1)}, bf16[512,128]{1,0:T(8,128)(2,1)S(1)}, u32[]{:S(2)}, u32[]{:S(2)}) collective-permute-start(bf16[512,128]{1,0:T(8,128)(2,1)S(1)} %get-tuple-element.79.refs_5_), channel_id=1, source_target_pairs={{0,2},{1,3},{2,0},{3,1},{4,6},{5,7},{6,4},{7,5},{8,10},{9,11},{10,... | collective-permute-start | bytes 393224 | tf_op jit(solution)/shard_map/ppermute | solution.py:472
  90.0 0.6 collective-permute-start.21
  90.6 6.6 %collective-permute-done.23.refs_4_ = bf16[1,432,128]{2,1,0:T(8,128)(2,1)S(1)} collective-permute-done((bf16[1,432,128]{2,1,0:T(8,128)(2,1)S(1)}, bf16[1,432,128]{2,1,0:T(8,128)(2,1)S(1)}, u32[]{:S(2)}, u32[]{:S(2)}) %collective-permute-start.23) | collective-permute-done | bytes 110624 | tf_op jit(solution)/shard_map/ppermute | solution.py:469
  97.4 3.0 %collective-permute-start.27 = (bf16[1,432,128]{2,1,0:T(8,128)(2,1)S(1)}, bf16[1,432,128]{2,1,0:T(8,128)(2,1)S(1)}, u32[]{:S(2)}, u32[]{:S(2)}) collective-permute-start(bf16[1,432,128]{2,1,0:T(8,128)(2,1)S(1)} %sums.19), channel_id=1, source_target_pairs={{0,16},{4,20},{8,24},{12,28},{16,0},{20,4},{24,8},{28,12},{1,17},{... | collective-permute-start | bytes 331784 | tf_op jit(solution)/shard_map/ppermute | solution.py:469
  100.5 0.9 rows.1
  101.4 5.6 %collective-permute-done.27 = bf16[1,432,128]{2,1,0:T(8,128)(2,1)S(1)} collective-permute-done((bf16[1,432,128]{2,1,0:T(8,128)(2,1)S(1)}, bf16[1,432,128]{2,1,0:T(8,128)(2,1)S(1)}, u32[]{:S(2)}, u32[]{:S(2)}) %collective-permute-start.27) | collective-permute-done | bytes 110624 | tf_op jit(solution)/shard_map/ppermute | solution.py:469
  107.0 3.5 %collective-permute-start.28 = (bf16[2,432,128]{2,1,0:T(8,128)(2,1)S(1)}, bf16[2,432,128]{2,1,0:T(8,128)(2,1)S(1)}, u32[]{:S(2)}, u32[]{:S(2)}) collective-permute-start(bf16[2,432,128]{2,1,0:T(8,128)(2,1)S(1)} %pad_maximum_fusion.1.refs_4_), channel_id=1, source_target_pairs={{0,8},{4,12},{8,0},{12,4},{16,24},{20,28},{24,16},{28,20},{1,9},{5... | collective-permute-start | bytes 663560 | tf_op jit(solution)/shard_map/ppermute | solution.py:469
  110.6 0.5 collective-permute-start.26
  111.1 3.6 %collective-permute-done.28.refs_5_ = bf16[2,432,128]{2,1,0:T(8,128)(2,1)S(1)} collective-permute-done((bf16[2,432,128]{2,1,0:T(8,128)(2,1)S(1)}, bf16[2,432,128]{2,1,0:T(8,128)(2,1)S(1)}, u32[]{:S(2)}, u32[]{:S(2)}) %collective-permute-start.28) | collective-permute-done | bytes 221216 | tf_op jit(solution)/shard_map/ppermute | solution.py:469
  114.7 1.5 %collective-permute-done.30.refs_7_ = bf16[2,432,128]{2,1,0:T(8,128)(2,1)S(1)} collective-permute-done((bf16[2,432,128]{2,1,0:T(8,128)(2,1)S(1)}, bf16[2,432,128]{2,1,0:T(8,128)(2,1)S(1)}, u32[]{:S(2)}, u32[]{:S(2)}) %collective-permute-start.30) | collective-permute-done | bytes 221216 | tf_op jit(solution)/shard_map/ppermute | solution.py:466
  116.2 2.2 %unpack.1 = (f32[544,256]{1,0:T(8,128)}, f32[64,2176]{1,0:T(8,128)}, f32[544,1024]{1,0:T(8,128)}, f32[256,1024]{1,0:T(8,128)}, f32[544]{0:T(1024)}, /*index=5*/f32[256]{0:T(256)}, f32[256]{0:T(256)}, f32[256]{0:T(256)}) custom-call(bf16[2,672,128]{2,1,0:T(8,128)(2,1)S(1)} %pad_maximum_fusion.refs_6_.refs_0_, ...), custom_call_target="tpu_custom_call" | custom-call | tf_op jit(solution)/shard_map/unpack/pallas_call | solution.py:700
  (51 shorter events, 2.2 us)
Async XLA Ops:
  12.5 10.8 %collective-permute-start.3 = (bf16[2,4,2,672,128]{4,3,2,1,0:T(8,128)(2,1)}, bf16[2,4,2,672,128]{4,3,2,1,0:T(8,128)(2,1)}, u32[]{:S(2)}, u32[]{:S(2)}) collective-permute-start(bf16[2,4,2,672,128]{4,3,2,1,0:T(8,128)(2,1)} %get-tuple-element.59), channel_id=1, source_target_pairs={{0,4},{4,0},{8,12},{12,8},{16,20},{20,16},{24,28},{28,24},{1,5},{5... | collective-permute-start | bytes 8257544 | tf_op jit(solution)/shard_map/ppermute | solution.py:466
  13.1 10.3 %copy-start = (bf16[2,4,2,672,128]{4,3,2,1,0:T(8,128)(2,1)S(1)}, bf16[2,4,2,672,128]{4,3,2,1,0:T(8,128)(2,1)}, u32[]{:S(2)}) copy-start(bf16[2,4,2,672,128]{4,3,2,1,0:T(8,128)(2,1)} %get-tuple-element.58) | copy-start | bytes 8257540
  23.2 28.3 %collective-permute-start.7 = (bf16[2,4,2,432,128]{4,3,2,1,0:T(8,128)(2,1)}, bf16[2,4,2,432,128]{4,3,2,1,0:T(8,128)(2,1)S(1)}, u32[]{:S(2)}, u32[]{:S(2)}) collective-permute-start(bf16[2,4,2,432,128]{4,3,2,1,0:T(8,128)(2,1)} %get-tuple-element.67), channel_id=1, source_target_pairs={{0,4},{4,0},{8,12},{12,8},{16,20},{20,16},{24,28},{28,24},{1,5},{5... | collective-permute-start | bytes 5308424 | tf_op jit(solution)/shard_map/ppermute | solution.py:466
  23.4 6.5 %copy-start.6 = (bf16[2,2,256,128]{3,2,1,0:T(8,128)(2,1)S(1)}, bf16[2,2,256,128]{3,2,1,0:T(8,128)(2,1)}, u32[]{:S(2)}) copy-start(bf16[2,2,256,128]{3,2,1,0:T(8,128)(2,1)} %get-tuple-element.54) | copy-start | bytes 786436
  23.4 8.1 %copy-start.5 = (bf16[2,2,256,128]{3,2,1,0:T(8,128)(2,1)S(1)}, bf16[2,2,256,128]{3,2,1,0:T(8,128)(2,1)}, u32[]{:S(2)}) copy-start(bf16[2,2,256,128]{3,2,1,0:T(8,128)(2,1)} %get-tuple-element.55) | copy-start | bytes 786436
  25.4 20.1 %collective-permute-start.4 = (bf16[2,2,672,128]{3,2,1,0:T(8,128)(2,1)S(1)}, bf16[2,2,672,128]{3,2,1,0:T(8,128)(2,1)S(1)}, u32[]{:S(2)}, u32[]{:S(2)}) collective-permute-start(bf16[2,2,672,128]{3,2,1,0:T(8,128)(2,1)S(1)} %get-tuple-element.62), channel_id=1, source_target_pairs={{0,2},{1,3},{2,0},{3,1},{4,6},{5,7},{6,4},{7,5},{8,10},{9,11},{10,... | collective-permute-start | bytes 2064392 | tf_op jit(solution)/shard_map/ppermute | solution.py:472
  28.4 17.1 %collective-permute-start.5 = (bf16[2,2,672,128]{3,2,1,0:T(8,128)(2,1)S(1)}, bf16[2,2,672,128]{3,2,1,0:T(8,128)(2,1)S(1)}, u32[]{:S(2)}, u32[]{:S(2)}) collective-permute-start(bf16[2,2,672,128]{3,2,1,0:T(8,128)(2,1)S(1)} %get-tuple-element.64), channel_id=1, source_target_pairs={{0,1},{1,0},{2,3},{3,2},{4,5},{5,4},{6,7},{7,6},{8,9},{9,8},{10,11... | collective-permute-start | bytes 2064392 | tf_op jit(solution)/shard_map/ppermute | solution.py:472
  29.9 13.2 %collective-permute-start = (bf16[2,2,256,128]{3,2,1,0:T(8,128)(2,1)S(1)}, bf16[2,2,256,128]{3,2,1,0:T(8,128)(2,1)S(1)}, u32[]{:S(2)}, u32[]{:S(2)}) collective-permute-start(bf16[2,2,256,128]{3,2,1,0:T(8,128)(2,1)S(1)} %copy-done.6), channel_id=1, source_target_pairs={{0,8},{4,12},{8,0},{12,4},{16,24},{20,28},{24,16},{28,20},{1,9},{5... | collective-permute-start | bytes 786440 | tf_op jit(solution)/shard_map/ppermute | solution.py:469
  31.5 14.0 %collective-permute-start.1 = (bf16[2,2,256,128]{3,2,1,0:T(8,128)(2,1)S(1)}, bf16[2,2,256,128]{3,2,1,0:T(8,128)(2,1)S(1)}, u32[]{:S(2)}, u32[]{:S(2)}) collective-permute-start(bf16[2,2,256,128]{3,2,1,0:T(8,128)(2,1)S(1)} %copy-done.5), channel_id=1, source_target_pairs={{0,16},{4,20},{8,24},{12,28},{16,0},{20,4},{24,8},{28,12},{1,17},{... | collective-permute-start | bytes 786440 | tf_op jit(solution)/shard_map/ppermute | solution.py:469
  45.5 2.4 %copy-start.4 = (bf16[2,2,256,128]{3,2,1,0:T(8,128)(2,1)S(1)}, bf16[2,2,256,128]{3,2,1,0:T(8,128)(2,1)}, u32[]{:S(2)}) copy-start(bf16[2,2,256,128]{3,2,1,0:T(8,128)(2,1)} %get-tuple-element.57) | copy-start | bytes 786436
  45.5 6.0 %copy-start.1 = (bf16[2,4,2,432,128]{4,3,2,1,0:T(8,128)(2,1)S(1)}, bf16[2,4,2,432,128]{4,3,2,1,0:T(8,128)(2,1)}, u32[]{:S(2)}) copy-start(bf16[2,4,2,432,128]{4,3,2,1,0:T(8,128)(2,1)} %get-tuple-element.66) | copy-start | bytes 5308420
  45.8 10.2 %collective-permute-start.6 = (bf16[2,672,128]{2,1,0:T(8,128)(2,1)S(1)}, bf16[2,672,128]{2,1,0:T(8,128)(2,1)S(1)}, u32[]{:S(2)}, u32[]{:S(2)}) collective-permute-start(bf16[2,672,128]{2,1,0:T(8,128)(2,1)S(1)} %get-tuple-element.65.refs_5_), channel_id=1, source_target_pairs={{0,1},{1,0},{2,3},{3,2},{4,5},{5,4},{6,7},{7,6},{8,9},{9,8},{10,11... | collective-permute-start | bytes 1032200 | tf_op jit(solution)/shard_map/ppermute | solution.py:472
  47.4 10.8 %collective-permute-start.8 = (bf16[2,672,128]{2,1,0:T(8,128)(2,1)S(1)}, bf16[2,672,128]{2,1,0:T(8,128)(2,1)S(1)}, u32[]{:S(2)}, u32[]{:S(2)}) collective-permute-start(bf16[2,672,128]{2,1,0:T(8,128)(2,1)S(1)} %get-tuple-element.68.refs_4_), channel_id=1, source_target_pairs={{0,2},{1,3},{2,0},{3,1},{4,6},{5,7},{6,4},{7,5},{8,10},{9,11},{10,... | collective-permute-start | bytes 1032200 | tf_op jit(solution)/shard_map/ppermute | solution.py:472
  47.9 10.5 %collective-permute-start.2 = (bf16[2,2,256,128]{3,2,1,0:T(8,128)(2,1)S(1)}, bf16[2,2,256,128]{3,2,1,0:T(8,128)(2,1)S(1)}, u32[]{:S(2)}, u32[]{:S(2)}) collective-permute-start(bf16[2,2,256,128]{3,2,1,0:T(8,128)(2,1)S(1)} %copy-done.4), channel_id=1, source_target_pairs={{0,24},{4,28},{8,16},{12,20},{16,8},{20,12},{24,0},{28,4},{1,25},{... | collective-permute-start | bytes 786440 | tf_op jit(solution)/shard_map/ppermute | solution.py:469
  52.6 5.8 %copy-start.2 = (bf16[2,2,256,128]{3,2,1,0:T(8,128)(2,1)S(1)}, bf16[2,2,256,128]{3,2,1,0:T(8,128)(2,1)}, u32[]{:S(2)}) copy-start(bf16[2,2,256,128]{3,2,1,0:T(8,128)(2,1)} %get-tuple-element.53.refs_0_.rest_0_) | copy-start | bytes 786436
  52.6 14.9 %collective-permute-start.12 = (bf16[2,2,432,128]{3,2,1,0:T(8,128)(2,1)S(1)}, bf16[2,2,432,128]{3,2,1,0:T(8,128)(2,1)S(1)}, u32[]{:S(2)}, u32[]{:S(2)}) collective-permute-start(bf16[2,2,432,128]{3,2,1,0:T(8,128)(2,1)S(1)} %get-tuple-element.69.refs_3_), channel_id=1, source_target_pairs={{0,1},{1,0},{2,3},{3,2},{4,5},{5,4},{6,7},{7,6},{8,9},{9,8},{10,11... | collective-permute-start | bytes 1327112 | tf_op jit(solution)/shard_map/ppermute | solution.py:472
  53.2 14.3 %collective-permute-start.11 = (bf16[2,2,432,128]{3,2,1,0:T(8,128)(2,1)S(1)}, bf16[2,2,432,128]{3,2,1,0:T(8,128)(2,1)S(1)}, u32[]{:S(2)}, u32[]{:S(2)}) collective-permute-start(bf16[2,2,432,128]{3,2,1,0:T(8,128)(2,1)S(1)} %get-tuple-element.70.refs_4_), channel_id=1, source_target_pairs={{0,2},{1,3},{2,0},{3,1},{4,6},{5,7},{6,4},{7,5},{8,10},{9,11},{10,... | collective-permute-start | bytes 1327112 | tf_op jit(solution)/shard_map/ppermute | solution.py:472
  58.4 5.0 %collective-permute-start.10 = (bf16[2,2,256,128]{3,2,1,0:T(8,128)(2,1)S(1)}, bf16[2,2,256,128]{3,2,1,0:T(8,128)(2,1)S(1)}, u32[]{:S(2)}, u32[]{:S(2)}) collective-permute-start(bf16[2,2,256,128]{3,2,1,0:T(8,128)(2,1)S(1)} %get-tuple-element.72), channel_id=1, source_target_pairs={{0,4},{4,0},{8,12},{12,8},{16,20},{20,16},{24,28},{28,24},{1,5},{5... | collective-permute-start | bytes 786440 | tf_op jit(solution)/shard_map/ppermute | solution.py:466
  58.5 5.0 %copy-start.3 = (s32[2,8192,4]{1,2,0:T(4,128)S(1)}, s32[2,8192,4]{1,2,0:T(4,128)}, u32[]{:S(2)}) copy-start(s32[2,8192,4]{1,2,0:T(4,128)} %param.23) | copy-start | bytes 786436
  58.5 4.9 %collective-permute-start.9 = (bf16[2,2,256,128]{3,2,1,0:T(8,128)(2,1)S(1)}, bf16[2,2,256,128]{3,2,1,0:T(8,128)(2,1)S(1)}, u32[]{:S(2)}, u32[]{:S(2)}) collective-permute-start(bf16[2,2,256,128]{3,2,1,0:T(8,128)(2,1)S(1)} %get-tuple-element.71.rest_6_), channel_id=1, source_target_pairs={{0,4},{4,0},{8,12},{12,8},{16,20},{20,16},{24,28},{28,24},{1,5},{5... | collective-permute-start | bytes 786440 | tf_op jit(solution)/shard_map/ppermute | solution.py:466
  59.0 11.6 %collective-permute-start.14 = (bf16[2,672,128]{2,1,0:T(8,128)(2,1)S(1)}, bf16[2,672,128]{2,1,0:T(8,128)(2,1)S(1)}, u32[]{:S(2)}, u32[]{:S(2)}) collective-permute-start(bf16[2,672,128]{2,1,0:T(8,128)(2,1)S(1)} %sums.11.refs_4_), channel_id=1, source_target_pairs={{0,8},{4,12},{8,0},{12,4},{16,24},{20,28},{24,16},{28,20},{1,9},{5... | collective-permute-start | bytes 1032200 | tf_op jit(solution)/shard_map/ppermute | solution.py:469
  67.7 7.2 %collective-permute-start.13 = (bf16[2,432,128]{2,1,0:T(8,128)(2,1)S(1)}, bf16[2,432,128]{2,1,0:T(8,128)(2,1)S(1)}, u32[]{:S(2)}, u32[]{:S(2)}) collective-permute-start(bf16[2,432,128]{2,1,0:T(8,128)(2,1)S(1)} %get-tuple-element.75.refs_5_), channel_id=1, source_target_pairs={{0,1},{1,0},{2,3},{3,2},{4,5},{5,4},{6,7},{7,6},{8,9},{9,8},{10,11... | collective-permute-start | bytes 663560 | tf_op jit(solution)/shard_map/ppermute | solution.py:472
  68.3 6.9 %collective-permute-start.15 = (bf16[2,432,128]{2,1,0:T(8,128)(2,1)S(1)}, bf16[2,432,128]{2,1,0:T(8,128)(2,1)S(1)}, u32[]{:S(2)}, u32[]{:S(2)}) collective-permute-start(bf16[2,432,128]{2,1,0:T(8,128)(2,1)S(1)} %get-tuple-element.76.refs_4_), channel_id=1, source_target_pairs={{0,2},{1,3},{2,0},{3,1},{4,6},{5,7},{6,4},{7,5},{8,10},{9,11},{10,... | collective-permute-start | bytes 663560 | tf_op jit(solution)/shard_map/ppermute | solution.py:472
  70.8 12.4 %collective-permute-start.19 = (bf16[1,672,128]{2,1,0:T(8,128)(2,1)S(1)}, bf16[1,672,128]{2,1,0:T(8,128)(2,1)S(1)}, u32[]{:S(2)}, u32[]{:S(2)}) collective-permute-start(bf16[1,672,128]{2,1,0:T(8,128)(2,1)S(1)} %sums.13.refs_3_), channel_id=1, source_target_pairs={{0,16},{4,20},{8,24},{12,28},{16,0},{20,4},{24,8},{28,12},{1,17},{... | collective-permute-start | bytes 516104 | tf_op jit(solution)/shard_map/ppermute | solution.py:469
  75.3 10.6 %collective-permute-start.18 = (bf16[2,432,128]{2,1,0:T(8,128)(2,1)S(1)}, bf16[2,432,128]{2,1,0:T(8,128)(2,1)S(1)}, u32[]{:S(2)}, u32[]{:S(2)}) collective-permute-start(bf16[2,432,128]{2,1,0:T(8,128)(2,1)S(1)} %sums.14.rest_6_), channel_id=1, source_target_pairs={{0,8},{4,12},{8,0},{12,4},{16,24},{20,28},{24,16},{28,20},{1,9},{5... | collective-permute-start | bytes 663560 | tf_op jit(solution)/shard_map/ppermute | solution.py:469
  80.2 7.1 %collective-permute-start.16 = (bf16[2,512,128]{2,1,0:T(8,128)(2,1)S(1)}, bf16[2,512,128]{2,1,0:T(8,128)(2,1)S(1)}, u32[]{:S(2)}, u32[]{:S(2)}) collective-permute-start(bf16[2,512,128]{2,1,0:T(8,128)(2,1)S(1)} %get-tuple-element.77.refs_5_), channel_id=1, source_target_pairs={{0,1},{1,0},{2,3},{3,2},{4,5},{5,4},{6,7},{7,6},{8,9},{9,8},{10,11... | collective-permute-start | bytes 786440 | tf_op jit(solution)/shard_map/ppermute | solution.py:472
  81.8 6.6 %collective-permute-start.17 = (bf16[2,512,128]{2,1,0:T(8,128)(2,1)S(1)}, bf16[2,512,128]{2,1,0:T(8,128)(2,1)S(1)}, u32[]{:S(2)}, u32[]{:S(2)}) collective-permute-start(bf16[2,512,128]{2,1,0:T(8,128)(2,1)S(1)} %get-tuple-element.78.refs_6_), channel_id=1, source_target_pairs={{0,2},{1,3},{2,0},{3,1},{4,6},{5,7},{6,4},{7,5},{8,10},{9,11},{10,... | collective-permute-start | bytes 786440 | tf_op jit(solution)/shard_map/ppermute | solution.py:472
  83.4 13.9 %collective-permute-start.22 = (bf16[1,672,128]{2,1,0:T(8,128)(2,1)S(1)}, bf16[1,672,128]{2,1,0:T(8,128)(2,1)S(1)}, u32[]{:S(2)}, u32[]{:S(2)}) collective-permute-start(bf16[1,672,128]{2,1,0:T(8,128)(2,1)S(1)} %sums.16.refs_4_), channel_id=1, source_target_pairs={{0,16},{4,20},{8,24},{12,28},{16,0},{20,4},{24,8},{28,12},{1,17},{... | collective-permute-start | bytes 516104 | tf_op jit(solution)/shard_map/ppermute | solution.py:469
  86.0 11.2 %collective-permute-start.23 = (bf16[1,432,128]{2,1,0:T(8,128)(2,1)S(1)}, bf16[1,432,128]{2,1,0:T(8,128)(2,1)S(1)}, u32[]{:S(2)}, u32[]{:S(2)}) collective-permute-start(bf16[1,432,128]{2,1,0:T(8,128)(2,1)S(1)} %sums.17.refs_4_), channel_id=1, source_target_pairs={{0,16},{4,20},{8,24},{12,28},{16,0},{20,4},{24,8},{28,12},{1,17},{... | collective-permute-start | bytes 331784 | tf_op jit(solution)/shard_map/ppermute | solution.py:469
  88.5 11.9 %collective-permute-start.20 = (bf16[512,128]{1,0:T(8,128)(2,1)S(1)}, bf16[512,128]{1,0:T(8,128)(2,1)S(1)}, u32[]{:S(2)}, u32[]{:S(2)}) collective-permute-start(bf16[512,128]{1,0:T(8,128)(2,1)S(1)} %get-tuple-element.79.refs_5_), channel_id=1, source_target_pairs={{0,2},{1,3},{2,0},{3,1},{4,6},{5,7},{6,4},{7,5},{8,10},{9,11},{10,... | collective-permute-start | bytes 393224 | tf_op jit(solution)/shard_map/ppermute | solution.py:472
  90.0 10.5 %collective-permute-start.21 = (bf16[512,128]{1,0:T(8,128)(2,1)S(1)}, bf16[512,128]{1,0:T(8,128)(2,1)S(1)}, u32[]{:S(2)}, u32[]{:S(2)}) collective-permute-start(bf16[512,128]{1,0:T(8,128)(2,1)S(1)} %get-tuple-element.80.refs_6_), channel_id=1, source_target_pairs={{0,1},{1,0},{2,3},{3,2},{4,5},{5,4},{6,7},{7,6},{8,9},{9,8},{10,11... | collective-permute-start | bytes 393224 | tf_op jit(solution)/shard_map/ppermute | solution.py:472
  97.4 13.2 %collective-permute-start.24 = (bf16[2,672,128]{2,1,0:T(8,128)(2,1)S(1)}, bf16[2,672,128]{2,1,0:T(8,128)(2,1)S(1)}, u32[]{:S(2)}, u32[]{:S(2)}) collective-permute-start(bf16[2,672,128]{2,1,0:T(8,128)(2,1)S(1)} %pad_maximum_fusion.refs_6_.refs_0_), channel_id=1, source_target_pairs={{0,8},{4,12},{8,0},{12,4},{16,24},{20,28},{24,16},{28,20},{1,9},{5... | collective-permute-start | bytes 1032200 | tf_op jit(solution)/shard_map/ppermute | solution.py:469
  97.4 9.6 %collective-permute-start.27 = (bf16[1,432,128]{2,1,0:T(8,128)(2,1)S(1)}, bf16[1,432,128]{2,1,0:T(8,128)(2,1)S(1)}, u32[]{:S(2)}, u32[]{:S(2)}) collective-permute-start(bf16[1,432,128]{2,1,0:T(8,128)(2,1)S(1)} %sums.19), channel_id=1, source_target_pairs={{0,16},{4,20},{8,24},{12,28},{16,0},{20,4},{24,8},{28,12},{1,17},{... | collective-permute-start | bytes 331784 | tf_op jit(solution)/shard_map/ppermute | solution.py:469
  107.0 7.6 %collective-permute-start.28 = (bf16[2,432,128]{2,1,0:T(8,128)(2,1)S(1)}, bf16[2,432,128]{2,1,0:T(8,128)(2,1)S(1)}, u32[]{:S(2)}, u32[]{:S(2)}) collective-permute-start(bf16[2,432,128]{2,1,0:T(8,128)(2,1)S(1)} %pad_maximum_fusion.1.refs_4_), channel_id=1, source_target_pairs={{0,8},{4,12},{8,0},{12,4},{16,24},{20,28},{24,16},{28,20},{1,9},{5... | collective-permute-start | bytes 663560 | tf_op jit(solution)/shard_map/ppermute | solution.py:469
  110.6 4.1 %collective-permute-start.25 = (bf16[2,672,128]{2,1,0:T(8,128)(2,1)S(1)}, bf16[2,672,128]{2,1,0:T(8,128)(2,1)S(1)}, u32[]{:S(2)}, u32[]{:S(2)}) collective-permute-start(bf16[2,672,128]{2,1,0:T(8,128)(2,1)S(1)} %pad_maximum_fusion.refs_6_.refs_0_), channel_id=1, source_target_pairs={{0,4},{4,0},{8,12},{12,8},{16,20},{20,16},{24,28},{28,24},{1,5},{5... | collective-permute-start | bytes 1032200 | tf_op jit(solution)/shard_map/ppermute | solution.py:466
  110.6 5.6 %collective-permute-start.26 = (bf16[2,672,128]{2,1,0:T(8,128)(2,1)S(1)}, bf16[2,672,128]{2,1,0:T(8,128)(2,1)S(1)}, u32[]{:S(2)}, u32[]{:S(2)}) collective-permute-start(bf16[2,672,128]{2,1,0:T(8,128)(2,1)S(1)} %collective-permute-done.24.refs_1_), channel_id=1, source_target_pairs={{0,4},{4,0},{8,12},{12,8},{16,20},{20,16},{24,28},{28,24},{1,5},{5... | collective-permute-start | bytes 1032200 | tf_op jit(solution)/shard_map/ppermute | solution.py:466
  111.1 3.6 %collective-permute-start.29 = (bf16[2,432,128]{2,1,0:T(8,128)(2,1)S(1)}, bf16[2,432,128]{2,1,0:T(8,128)(2,1)S(1)}, u32[]{:S(2)}, u32[]{:S(2)}) collective-permute-start(bf16[2,432,128]{2,1,0:T(8,128)(2,1)S(1)} %pad_maximum_fusion.1.refs_4_), channel_id=1, source_target_pairs={{0,4},{4,0},{8,12},{12,8},{16,20},{20,16},{24,28},{28,24},{1,5},{5... | collective-permute-start | bytes 663560 | tf_op jit(solution)/shard_map/ppermute | solution.py:466
  114.7 1.5 %collective-permute-start.30 = (bf16[2,432,128]{2,1,0:T(8,128)(2,1)S(1)}, bf16[2,432,128]{2,1,0:T(8,128)(2,1)S(1)}, u32[]{:S(2)}, u32[]{:S(2)}) collective-permute-start(bf16[2,432,128]{2,1,0:T(8,128)(2,1)S(1)} %collective-permute-done.28.refs_5_), channel_id=1, source_target_pairs={{0,4},{4,0},{8,12},{12,8},{16,20},{20,16},{24,28},{28,24},{1,5},{5... | collective-permute-start | bytes 663560 | tf_op jit(solution)/shard_map/ppermute | solution.py:466

commit v10 on v9

--- a/solution.py
+++ b/solution.py
@@ -645,17 +645,26 @@
     values, half = {0: pooled_out[0]}, n_z // 2
     for which in [half, *range(1, half)]:
         values[which] = swap_z(pooled_out[which], which)
-    for which in range(half + 1, n_z):
-        (moved,) = after([pooled_out[which]], [values[half], values[which - half]])
-        values[which] = swap_z(moved, which)
     one.settle([values[1]])
     last = [values[which] for which in range(1, half + 1)]
     for at in range(1, row_bits):
         last = one.row_step(at, last)
     last = two.first_step(last)
+    for which in range(half + 1, n_z):
+        (moved,) = after([pooled_out[which]], [*last, values[which - half]])
+        values[which] = swap_z(moved, which)
     last = one.z_step(0, last)
     two.settle(last)
     values = [values[which] for which in range(n_z)]
+    last = [*last, *values[half + 1 :]]
+    for at in range(1, row_bits):
+        last = two.row_step(at, last)
+    for stage in range(1, z_bits):
+        last = one.z_step(stage, last)
+    last = two.z_step(0, last)
+    last = one.z_own(last)
+    for stage in range(1, z_bits):
+        last = two.z_step(stage, last)
     far_values = call(
         functools.partial(select_kernel, n_z),
         [wide(n_z // 2, tab_grp, batch, width)] * 2,
@@ -681,21 +690,13 @@
         shares.append(Halving([sums], high_first if table % 2 else low_first))
         last = [sums]
         if table == 0:
-            for at in range(1, row_bits):
-                last = two.row_step(at, last)
-            for stage in range(1, z_bits):
-                last = one.z_step(stage, last)
-            last = two.z_step(0, last)
+            last = two.z_own(last)
     last = row_step(shares, 0, last)
-    last = one.z_own(last)
-    for stage in range(1, z_bits):
-        last = two.z_step(stage, last)
+    last = two.z_back(last)
+    last = one.z_back(last)
     for at in range(1, row_bits):
         last = row_step(shares, at, last)
-    last = two.z_own(last)
-    last = one.z_back(last)
     row_grads = sum_rows([share.items for share in shares], last)
-    two.z_back([row_grads])
 
     g_down, g_up, g_first, g_second, g_cbias, g_bias1, g_bias2, g_logit = call(
         unpack_kernel,

time: 119 us -> 129 us (1.084)
  waiting for transfers between devices: 34.7 us -> 49.4 us
  starting transfers between devices: 41.7 us -> 37.1 us
    ppermute x12, waiting for transfers between devices: 6.89 us -> 21.1 us  [swap_row(): lax.ppermute(value, 'row', [(at, at ^ 1 << bit) for at in range(n_row)])]
    ppermute x11, starting transfers between devices: 24.2 us -> 21.3 us  [swap_z(): lax.ppermute(value, 'table', [(at, at ^ 2 * which) for at in range(n_tabl...]
    ppermute x11, waiting for transfers between devices: 26.3 us -> 28.3 us  [swap_z(): lax.ppermute(value, 'table', [(at, at ^ 2 * which) for at in range(n_tabl...]
    ppermute x8, waiting for transfers between devices: 1.48 us -> 0.02 us  [swap_cores(): return lax.ppermute(value, 'table', [(at, at ^ 1) for at in range(n_table)])]
    ppermute x12, starting transfers between devices: 15.8 us -> 14.3 us  [swap_row(): lax.ppermute(value, 'row', [(at, at ^ 1 << bit) for at in range(n_row)])]
  transfers between devices with their start and end apart: 31 -> 31, of which waited for: 13 -> 16; matrix products, arithmetic and copies ran while one was open for 0% -> 0% of each run, Pallas kernels for 23% -> 21%
where the time goes in v10:
time: 129 us; the launch traced here: 128 us
  waiting for transfers between devices  49.4 us (38%)
  Pallas kernels  41 us (32%)
  starting transfers between devices  37.1 us (29%)
    ppermute x11, waiting for transfers between devices, swap_z(): lax.ppermute(value, 'table', [(at, at ^ 2 * which) for at in range(n_tabl...  28.3 us
    ppermute x11, starting transfers between devices, swap_z(): lax.ppermute(value, 'table', [(at, at ^ 2 * which) for at in range(n_tabl...  21.3 us
    ppermute x12, waiting for transfers between devices, swap_row(): lax.ppermute(value, 'row', [(at, at ^ 1 << bit) for at in range(n_row)])  21.1 us
    ppermute x12, starting transfers between devices, swap_row(): lax.ppermute(value, 'row', [(at, at ^ 1 << bit) for at in range(n_row)])  14.3 us
    pallas_call x1, Pallas kernels, local(): call(front_kernel, [packed(rows_front)] * 2 + [wide(feat, batch), wide(ba...  11.9 us
    pallas_call x1, Pallas kernels, local(): call(functools.partial(middle_kernel, n_z), [packed(rows_back)] * 2 + [wi...  10.1 us
    pallas_call x2, Pallas kernels, local(): pl.pallas_call(functools.partial(count_kernel, n_row, table, hot, n_z), o...  8.05 us
    pallas_call x4, Pallas kernels, fetch_sums(): call(functools.partial(fetch_sum_kernel, plan, n_in), shapes, scratch + [...  6 us
  transfers between devices with their start and end apart: 31, of which 16 were waited for; matrix products, arithmetic and copies ran while one was open for 0% of the time, Pallas kernels for 21%

profile of v10, /device:TPU:0, one launch (start us, length us, event | category | flops | bytes accessed | tf_op | source)
XLA Modules:
  0.0 128.5 jit_solution(15430411116850026109)
XLA Ops:
  0.6 11.9 %front.1 = (bf16[2,4,2,672,128]{4,3,2,1,0:T(8,128)(2,1)}, bf16[2,4,2,672,128]{4,3,2,1,0:T(8,128)(2,1)}, bf16[2176,256]{1,0:T(8,128)(2,1)}, bf16[256,1024]{1,0:T(8,128)(2,1)}, f32[24,128]{1,0:T(8,128)}) custom-call(bf16[256,128]{1,0:T(8,128)(2,1)} %refs_0_.3, bf16[256,2048]{1,0:T(8,128)(2,1)} %refs_1_.3, bf16[2176,256]{1,0:T(8,128)(2,1)} %refs_2_.3, ...), custom_call_target="tpu_custom_call" | custom-call | tf_op jit(solution)/shard_map/front/pallas_call | solution.py:504
  12.5 0.5 collective-permute-start.3
  13.1 10.1 %middle.1 = (bf16[2,4,2,432,128]{4,3,2,1,0:T(8,128)(2,1)}, bf16[2,4,2,432,128]{4,3,2,1,0:T(8,128)(2,1)}, bf16[2,2,256,128]{3,2,1,0:T(8,128)(2,1)}, bf16[2,2,256,...) custom-call(bf16[256,128]{1,0:T(8,128)(2,1)} %refs_0_.3, ...), custom_call_target="tpu_custom_call" | custom-call | tf_op jit(solution)/shard_map/middle/pallas_call | solution.py:531
  23.4 2.0 %first_sums.5 = (bf16[2,2,672,128]{3,2,1,0:T(8,128)(2,1)S(1)}, bf16[2,2,672,128]{3,2,1,0:T(8,128)(2,1)S(1)}) custom-call(bf16[2,2,2,2,672,128]{5,4,3,2,1,0:T(8,128)(2,1)S(1)} %bitcast.7, bf16[2,2,2,2,672,128]{5,4,3,2,1,0:T(8,128)(2,1)} %bitcast.4.refs_1_.refs_3_, bf16[2,2,2,2,672,128]{5,4,3,2,1,0:T(8,128)(2,1)S(1)} %bitcast.8, ...), custom_call_target="tpu_custom_call" | custom-call | tf_op jit(solution)/shard_map/first_sums/pallas_call | solution.py:408
  25.4 3.0 %collective-permute-start.4 = (bf16[2,2,672,128]{3,2,1,0:T(8,128)(2,1)S(1)}, bf16[2,2,672,128]{3,2,1,0:T(8,128)(2,1)S(1)}, u32[]{:S(2)}, u32[]{:S(2)}) collective-permute-start(bf16[2,2,672,128]{3,2,1,0:T(8,128)(2,1)S(1)} %get-tuple-element.63), channel_id=1, source_target_pairs={{0,1},{1,0},{2,3},{3,2},{4,5},{5,4},{6,7},{7,6},{8,9},{9,8},{10,11... | collective-permute-start | bytes 2064392 | tf_op jit(solution)/shard_map/ppermute | solution.py:472
  28.4 1.5 %collective-permute-start.5 = (bf16[2,2,672,128]{3,2,1,0:T(8,128)(2,1)S(1)}, bf16[2,2,672,128]{3,2,1,0:T(8,128)(2,1)S(1)}, u32[]{:S(2)}, u32[]{:S(2)}) collective-permute-start(bf16[2,2,672,128]{3,2,1,0:T(8,128)(2,1)S(1)} %get-tuple-element.65), channel_id=1, source_target_pairs={{0,2},{1,3},{2,0},{3,1},{4,6},{5,7},{6,4},{7,5},{8,10},{9,11},{10,... | collective-permute-start | bytes 2064392 | tf_op jit(solution)/shard_map/ppermute | solution.py:472
  29.9 1.6 %collective-permute-start = (bf16[2,2,256,128]{3,2,1,0:T(8,128)(2,1)S(1)}, bf16[2,2,256,128]{3,2,1,0:T(8,128)(2,1)S(1)}, u32[]{:S(2)}, u32[]{:S(2)}) collective-permute-start(bf16[2,2,256,128]{3,2,1,0:T(8,128)(2,1)S(1)} %copy-done.6), channel_id=1, source_target_pairs={{0,8},{4,12},{8,0},{12,4},{16,24},{20,28},{24,16},{28,20},{1,9},{5... | collective-permute-start | bytes 786440 | tf_op jit(solution)/shard_map/ppermute | solution.py:469
  31.5 2.6 %collective-permute-start.1 = (bf16[2,2,256,128]{3,2,1,0:T(8,128)(2,1)S(1)}, bf16[2,2,256,128]{3,2,1,0:T(8,128)(2,1)S(1)}, u32[]{:S(2)}, u32[]{:S(2)}) collective-permute-start(bf16[2,2,256,128]{3,2,1,0:T(8,128)(2,1)S(1)} %copy-done.5), channel_id=1, source_target_pairs={{0,16},{4,20},{8,24},{12,28},{16,0},{20,4},{24,8},{28,12},{1,17},{... | collective-permute-start | bytes 786440 | tf_op jit(solution)/shard_map/ppermute | solution.py:469
  34.1 9.0 %collective-permute-done.refs_4_.refs_1_.rest_1_ = bf16[2,2,256,128]{3,2,1,0:T(8,128)(2,1)S(1)} collective-permute-done((bf16[2,2,256,128]{3,2,1,0:T(8,128)(2,1)S(1)}, bf16[2,2,256,128]{3,2,1,0:T(8,128)(2,1)S(1)}, u32[]{:S(2)}, u32[]{:S(2)}) %collective-permute-start) | collective-permute-done | bytes 262176 | tf_op jit(solution)/shard_map/ppermute | solution.py:469
  43.1 1.8 %first_sums.4 = (bf16[2,2,672,128]{3,2,1,0:T(8,128)(2,1)S(1)}, bf16[2,2,672,128]{3,2,1,0:T(8,128)(2,1)S(1)}) custom-call(bf16[2,2,2,2,672,128]{5,4,3,2,1,0:T(8,128)(2,1)S(1)} %bitcast.9, bf16[2,2,2,2,672,128]{5,4,3,2,1,0:T(8,128)(2,1)} %bitcast.4.refs_1_.refs_3_, bf16[2,2,2,2,672,128]{5,4,3,2,1,0:T(8,128)(2,1)S(1)} %bitcast.10, ...), custom_call_target="tpu_custom_call" | custom-call | tf_op jit(solution)/shard_map/first_sums/pallas_call | solution.py:408
  44.9 0.6 collective-permute-done.1.refs_5_.refs_2_.rest_2_
  45.8 1.6 %collective-permute-start.8 = (bf16[2,672,128]{2,1,0:T(8,128)(2,1)S(1)}, bf16[2,672,128]{2,1,0:T(8,128)(2,1)S(1)}, u32[]{:S(2)}, u32[]{:S(2)}) collective-permute-start(bf16[2,672,128]{2,1,0:T(8,128)(2,1)S(1)} %get-tuple-element.66.refs_4_), channel_id=1, source_target_pairs={{0,2},{1,3},{2,0},{3,1},{4,6},{5,7},{6,4},{7,5},{8,10},{9,11},{10,... | collective-permute-start | bytes 1032200 | tf_op jit(solution)/shard_map/ppermute | solution.py:472
  47.4 0.5 collective-permute-start.7
  47.9 1.1 first_sums.6
  49.0 1.6 %collective-permute-start.9 = (bf16[2,2,432,128]{3,2,1,0:T(8,128)(2,1)S(1)}, bf16[2,2,432,128]{3,2,1,0:T(8,128)(2,1)S(1)}, u32[]{:S(2)}, u32[]{:S(2)}) collective-permute-start(bf16[2,2,432,128]{3,2,1,0:T(8,128)(2,1)S(1)} %get-tuple-element.68.refs_3_), channel_id=1, source_target_pairs={{0,1},{1,0},{2,3},{3,2},{4,5},{5,4},{6,7},{7,6},{8,9},{9,8},{10,11... | collective-permute-start | bytes 1327112 | tf_op jit(solution)/shard_map/ppermute | solution.py:472
  50.6 0.5 collective-permute-start.10
  51.1 3.6 %collective-permute-start.6 = (bf16[2,2,256,128]{3,2,1,0:T(8,128)(2,1)S(1)}, bf16[2,2,256,128]{3,2,1,0:T(8,128)(2,1)S(1)}, u32[]{:S(2)}, u32[]{:S(2)}) collective-permute-start(bf16[2,2,256,128]{3,2,1,0:T(8,128)(2,1)S(1)} %copy-done.4), channel_id=1, source_target_pairs={{0,24},{4,28},{8,16},{12,20},{16,8},{20,12},{24,0},{28,4},{1,25},{... | collective-permute-start | bytes 786440 | tf_op jit(solution)/shard_map/ppermute | solution.py:469
  54.7 2.2 %collective-permute-done.8.refs_5_.refs_2_ = bf16[2,672,128]{2,1,0:T(8,128)(2,1)S(1)} collective-permute-done((bf16[2,672,128]{2,1,0:T(8,128)(2,1)S(1)}, bf16[2,672,128]{2,1,0:T(8,128)(2,1)S(1)}, u32[]{:S(2)}, u32[]{:S(2)}) %collective-permute-start.8) | collective-permute-done | bytes 344096 | tf_op jit(solution)/shard_map/ppermute | solution.py:472
  56.9 1.5 %collective-permute-done.7.refs_2_ = bf16[2,672,128]{2,1,0:T(8,128)(2,1)S(1)} collective-permute-done((bf16[2,672,128]{2,1,0:T(8,128)(2,1)S(1)}, bf16[2,672,128]{2,1,0:T(8,128)(2,1)S(1)}, u32[]{:S(2)}, u32[]{:S(2)}) %collective-permute-start.7) | collective-permute-done | bytes 344096 | tf_op jit(solution)/shard_map/ppermute | solution.py:472
  58.6 1.6 %collective-permute-start.13 = (bf16[2,672,128]{2,1,0:T(8,128)(2,1)S(1)}, bf16[2,672,128]{2,1,0:T(8,128)(2,1)S(1)}, u32[]{:S(2)}, u32[]{:S(2)}) collective-permute-start(bf16[2,672,128]{2,1,0:T(8,128)(2,1)S(1)} %sums.11.refs_4_), channel_id=1, source_target_pairs={{0,8},{4,12},{8,0},{12,4},{16,24},{20,28},{24,16},{28,20},{1,9},{5... | collective-permute-start | bytes 1032200 | tf_op jit(solution)/shard_map/ppermute | solution.py:469
  60.2 1.1 first_sums.7
  61.4 4.0 %collective-permute-done.9.refs_1_.refs_6_ = bf16[2,2,432,128]{3,2,1,0:T(8,128)(2,1)S(1)} collective-permute-done((bf16[2,2,432,128]{3,2,1,0:T(8,128)(2,1)S(1)}, bf16[2,2,432,128]{3,2,1,0:T(8,128)(2,1)S(1)}, u32[]{:S(2)}, u32[]{:S(2)}) %collective-permute-start.9) | collective-permute-done | bytes 442400 | tf_op jit(solution)/shard_map/ppermute | solution.py:472
  65.6 0.6 collective-permute-start.11
  66.2 0.7 collective-permute-start.12
  67.1 4.6 %collective-permute-done.11.refs_4_.refs_2_ = bf16[2,432,128]{2,1,0:T(8,128)(2,1)S(1)} collective-permute-done((bf16[2,432,128]{2,1,0:T(8,128)(2,1)S(1)}, bf16[2,432,128]{2,1,0:T(8,128)(2,1)S(1)}, u32[]{:S(2)}, u32[]{:S(2)}) %collective-permute-start.11) | collective-permute-done | bytes 221216 | tf_op jit(solution)/shard_map/ppermute | solution.py:472
  71.6 0.5 collective-permute-done.12.refs_2_
  72.3 1.6 %collective-permute-start.14 = (bf16[2,432,128]{2,1,0:T(8,128)(2,1)S(1)}, bf16[2,432,128]{2,1,0:T(8,128)(2,1)S(1)}, u32[]{:S(2)}, u32[]{:S(2)}) collective-permute-start(bf16[2,432,128]{2,1,0:T(8,128)(2,1)S(1)} %sums.14.refs_5_), channel_id=1, source_target_pairs={{0,8},{4,12},{8,0},{12,4},{16,24},{20,28},{24,16},{28,20},{1,9},{5... | collective-permute-start | bytes 663560 | tf_op jit(solution)/shard_map/ppermute | solution.py:469
  73.9 2.6 %collective-permute-start.15 = (bf16[1,672,128]{2,1,0:T(8,128)(2,1)S(1)}, bf16[1,672,128]{2,1,0:T(8,128)(2,1)S(1)}, u32[]{:S(2)}, u32[]{:S(2)}) collective-permute-start(bf16[1,672,128]{2,1,0:T(8,128)(2,1)S(1)} %sums.13.refs_3_), channel_id=1, source_target_pairs={{0,16},{4,20},{8,24},{12,28},{16,0},{20,4},{24,8},{28,12},{1,17},{... | collective-permute-start | bytes 516104 | tf_op jit(solution)/shard_map/ppermute | solution.py:469
  76.5 3.7 %collective-permute-done.15.refs_4_ = bf16[1,672,128]{2,1,0:T(8,128)(2,1)S(1)} collective-permute-done((bf16[1,672,128]{2,1,0:T(8,128)(2,1)S(1)}, bf16[1,672,128]{2,1,0:T(8,128)(2,1)S(1)}, u32[]{:S(2)}, u32[]{:S(2)}) %collective-permute-start.15) | collective-permute-done | bytes 172064 | tf_op jit(solution)/shard_map/ppermute | solution.py:469
  80.7 0.5 collective-permute-start.16
  81.2 2.7 %collective-permute-start.18 = (bf16[1,432,128]{2,1,0:T(8,128)(2,1)S(1)}, bf16[1,432,128]{2,1,0:T(8,128)(2,1)S(1)}, u32[]{:S(2)}, u32[]{:S(2)}) collective-permute-start(bf16[1,432,128]{2,1,0:T(8,128)(2,1)S(1)} %sums.16.refs_4_), channel_id=1, source_target_pairs={{0,16},{4,20},{8,24},{12,28},{16,0},{20,4},{24,8},{28,12},{1,17},{... | collective-permute-start | bytes 331784 | tf_op jit(solution)/shard_map/ppermute | solution.py:469
  83.9 4.0 %counts.2.refs_5_ = bf16[4,512,128]{2,1,0:T(8,128)(2,1)S(1)} custom-call(s32[2,4,8192]{2,1,0:T(4,128)S(1)} %bitcast.25, bf16[2,2,256,128]{3,2,1,0:T(8,128)(2,1)S(1)} %copy-done.2, bf16[2,2,256,128]{3,2,1,0:T(8,128)(2,1)S(1)} %collective-permute-done.refs_4_.refs_1_.rest_1_, bf16[2,2,256,128]{3,2,1,0:T(8,128)(2,1)S(1)} %collective-permute-done.1.refs_5_.refs_2_.rest_2_, ...), custom_call_target="tpu_custom_call" | custom-call | tf_op jit(solution)/shard_map/counts/pallas_call | solution.py:680
  87.9 1.6 %collective-permute-done.18.refs_4_ = bf16[1,432,128]{2,1,0:T(8,128)(2,1)S(1)} collective-permute-done((bf16[1,432,128]{2,1,0:T(8,128)(2,1)S(1)}, bf16[1,432,128]{2,1,0:T(8,128)(2,1)S(1)}, u32[]{:S(2)}, u32[]{:S(2)}) %collective-permute-start.18) | collective-permute-done | bytes 110624 | tf_op jit(solution)/shard_map/ppermute | solution.py:469
  89.7 0.4 collective-permute-start.22
  90.1 2.6 %collective-permute-start.21 = (bf16[1,672,128]{2,1,0:T(8,128)(2,1)S(1)}, bf16[1,672,128]{2,1,0:T(8,128)(2,1)S(1)}, u32[]{:S(2)}, u32[]{:S(2)}) collective-permute-start(bf16[1,672,128]{2,1,0:T(8,128)(2,1)S(1)} %sums.15.refs_4_), channel_id=1, source_target_pairs={{0,16},{4,20},{8,24},{12,28},{16,0},{20,4},{24,8},{28,12},{1,17},{... | collective-permute-start | bytes 516104 | tf_op jit(solution)/shard_map/ppermute | solution.py:469
  92.7 4.0 %counts.3.refs_2_ = bf16[4,512,128]{2,1,0:T(8,128)(2,1)S(1)} custom-call(s32[2,4,8192]{2,1,0:T(4,128)S(1)} %bitcast.26, bf16[2,2,256,128]{3,2,1,0:T(8,128)(2,1)S(1)} %copy-done.2, bf16[2,2,256,128]{3,2,1,0:T(8,128)(2,1)S(1)} %collective-permute-done.refs_4_.refs_1_.rest_1_, bf16[2,2,256,128]{3,2,1,0:T(8,128)(2,1)S(1)} %collective-permute-done.1.refs_5_.refs_2_.rest_2_, ...), custom_call_target="tpu_custom_call" | custom-call | tf_op jit(solution)/shard_map/counts/pallas_call | solution.py:680
  96.9 5.1 %collective-permute-done.22 = bf16[1,432,128]{2,1,0:T(8,128)(2,1)S(1)} collective-permute-done((bf16[1,432,128]{2,1,0:T(8,128)(2,1)S(1)}, bf16[1,432,128]{2,1,0:T(8,128)(2,1)S(1)}, u32[]{:S(2)}, u32[]{:S(2)}) %collective-permute-start.22) | collective-permute-done | bytes 110624 | tf_op jit(solution)/shard_map/ppermute | solution.py:469
  102.0 1.8 %collective-permute-done.21 = bf16[1,672,128]{2,1,0:T(8,128)(2,1)S(1)} collective-permute-done((bf16[1,672,128]{2,1,0:T(8,128)(2,1)S(1)}, bf16[1,672,128]{2,1,0:T(8,128)(2,1)S(1)}, u32[]{:S(2)}, u32[]{:S(2)}) %collective-permute-start.21) | collective-permute-done | bytes 172064 | tf_op jit(solution)/shard_map/ppermute | solution.py:469
  103.9 0.7 collective-permute-start.19
  104.6 1.5 %collective-permute-start.20 = (bf16[2,512,128]{2,1,0:T(8,128)(2,1)S(1)}, bf16[2,512,128]{2,1,0:T(8,128)(2,1)S(1)}, u32[]{:S(2)}, u32[]{:S(2)}) collective-permute-start(bf16[2,512,128]{2,1,0:T(8,128)(2,1)S(1)} %get-tuple-element.78), channel_id=1, source_target_pairs={{0,2},{1,3},{2,0},{3,1},{4,6},{5,7},{6,4},{7,5},{8,10},{9,11},{10,... | collective-permute-start | bytes 786440 | tf_op jit(solution)/shard_map/ppermute | solution.py:472
  106.1 1.9 %collective-permute-start.28 = (bf16[2,432,128]{2,1,0:T(8,128)(2,1)S(1)}, bf16[2,432,128]{2,1,0:T(8,128)(2,1)S(1)}, u32[]{:S(2)}, u32[]{:S(2)}) collective-permute-start(bf16[2,432,128]{2,1,0:T(8,128)(2,1)S(1)} %pad_maximum_fusion.1.refs_4_), channel_id=1, source_target_pairs={{0,8},{4,12},{8,0},{12,4},{16,24},{20,28},{24,16},{28,20},{1,9},{5... | collective-permute-start | bytes 663560 | tf_op jit(solution)/shard_map/ppermute | solution.py:469
  108.1 6.0 %collective-permute-done.25.refs_1_ = bf16[2,672,128]{2,1,0:T(8,128)(2,1)S(1)} collective-permute-done((bf16[2,672,128]{2,1,0:T(8,128)(2,1)S(1)}, bf16[2,672,128]{2,1,0:T(8,128)(2,1)S(1)}, u32[]{:S(2)}, u32[]{:S(2)}) %collective-permute-start.25) | collective-permute-done | bytes 344096 | tf_op jit(solution)/shard_map/ppermute | solution.py:469
  114.2 1.6 %collective-permute-start.23 = (bf16[512,128]{1,0:T(8,128)(2,1)S(1)}, bf16[512,128]{1,0:T(8,128)(2,1)S(1)}, u32[]{:S(2)}, u32[]{:S(2)}) collective-permute-start(bf16[512,128]{1,0:T(8,128)(2,1)S(1)} %get-tuple-element.81.refs_6_), channel_id=1, source_target_pairs={{0,2},{1,3},{2,0},{3,1},{4,6},{5,7},{6,4},{7,5},{8,10},{9,11},{10,... | collective-permute-start | bytes 393224 | tf_op jit(solution)/shard_map/ppermute | solution.py:472
  116.5 3.8 %collective-permute-done.23.refs_2_ = bf16[512,128]{1,0:T(8,128)(2,1)S(1)} collective-permute-done((bf16[512,128]{1,0:T(8,128)(2,1)S(1)}, bf16[512,128]{1,0:T(8,128)(2,1)S(1)}, u32[]{:S(2)}, u32[]{:S(2)}) %collective-permute-start.23) | collective-permute-done | bytes 131104 | tf_op jit(solution)/shard_map/ppermute | solution.py:472
  120.2 0.6 collective-permute-start.24
  120.8 4.5 %collective-permute-done.24.refs_5_ = bf16[512,128]{1,0:T(8,128)(2,1)S(1)} collective-permute-done((bf16[512,128]{1,0:T(8,128)(2,1)S(1)}, bf16[512,128]{1,0:T(8,128)(2,1)S(1)}, u32[]{:S(2)}, u32[]{:S(2)}) %collective-permute-start.24) | collective-permute-done | bytes 131104 | tf_op jit(solution)/shard_map/ppermute | solution.py:472
  125.3 0.9 rows.1
  126.2 2.3 %unpack.1 = (f32[544,256]{1,0:T(8,128)}, f32[64,2176]{1,0:T(8,128)}, f32[544,1024]{1,0:T(8,128)}, f32[256,1024]{1,0:T(8,128)}, f32[544]{0:T(1024)}, /*index=5*/f32[256]{0:T(256)}, f32[256]{0:T(256)}, f32[256]{0:T(256)}) custom-call(bf16[2,672,128]{2,1,0:T(8,128)(2,1)S(1)} %pad_maximum_fusion.refs_4_.refs_0_, ...), custom_call_target="tpu_custom_call" | custom-call | tf_op jit(solution)/shard_map/unpack/pallas_call | solution.py:701
  (51 shorter events, 2.9 us)
Async XLA Ops:
  12.5 10.8 %collective-permute-start.3 = (bf16[2,4,2,672,128]{4,3,2,1,0:T(8,128)(2,1)}, bf16[2,4,2,672,128]{4,3,2,1,0:T(8,128)(2,1)}, u32[]{:S(2)}, u32[]{:S(2)}) collective-permute-start(bf16[2,4,2,672,128]{4,3,2,1,0:T(8,128)(2,1)} %get-tuple-element.60), channel_id=1, source_target_pairs={{0,4},{4,0},{8,12},{12,8},{16,20},{20,16},{24,28},{28,24},{1,5},{5... | collective-permute-start | bytes 8257544 | tf_op jit(solution)/shard_map/ppermute | solution.py:466
  13.1 10.3 %copy-start = (bf16[2,4,2,672,128]{4,3,2,1,0:T(8,128)(2,1)S(1)}, bf16[2,4,2,672,128]{4,3,2,1,0:T(8,128)(2,1)}, u32[]{:S(2)}) copy-start(bf16[2,4,2,672,128]{4,3,2,1,0:T(8,128)(2,1)} %get-tuple-element.59) | copy-start | bytes 8257540
  23.2 24.7 %collective-permute-start.2 = (bf16[2,4,2,432,128]{4,3,2,1,0:T(8,128)(2,1)}, bf16[2,4,2,432,128]{4,3,2,1,0:T(8,128)(2,1)S(1)}, u32[]{:S(2)}, u32[]{:S(2)}) collective-permute-start(bf16[2,4,2,432,128]{4,3,2,1,0:T(8,128)(2,1)} %get-tuple-element.58), channel_id=1, source_target_pairs={{0,4},{4,0},{8,12},{12,8},{16,20},{20,16},{24,28},{28,24},{1,5},{5... | collective-permute-start | bytes 5308424 | tf_op jit(solution)/shard_map/ppermute | solution.py:466
  23.4 6.5 %copy-start.6 = (bf16[2,2,256,128]{3,2,1,0:T(8,128)(2,1)S(1)}, bf16[2,2,256,128]{3,2,1,0:T(8,128)(2,1)}, u32[]{:S(2)}) copy-start(bf16[2,2,256,128]{3,2,1,0:T(8,128)(2,1)} %get-tuple-element.54) | copy-start | bytes 786436
  23.4 8.1 %copy-start.5 = (bf16[2,2,256,128]{3,2,1,0:T(8,128)(2,1)S(1)}, bf16[2,2,256,128]{3,2,1,0:T(8,128)(2,1)}, u32[]{:S(2)}) copy-start(bf16[2,2,256,128]{3,2,1,0:T(8,128)(2,1)} %get-tuple-element.55) | copy-start | bytes 786436
  25.4 20.1 %collective-permute-start.4 = (bf16[2,2,672,128]{3,2,1,0:T(8,128)(2,1)S(1)}, bf16[2,2,672,128]{3,2,1,0:T(8,128)(2,1)S(1)}, u32[]{:S(2)}, u32[]{:S(2)}) collective-permute-start(bf16[2,2,672,128]{3,2,1,0:T(8,128)(2,1)S(1)} %get-tuple-element.63), channel_id=1, source_target_pairs={{0,1},{1,0},{2,3},{3,2},{4,5},{5,4},{6,7},{7,6},{8,9},{9,8},{10,11... | collective-permute-start | bytes 2064392 | tf_op jit(solution)/shard_map/ppermute | solution.py:472
  28.4 17.1 %collective-permute-start.5 = (bf16[2,2,672,128]{3,2,1,0:T(8,128)(2,1)S(1)}, bf16[2,2,672,128]{3,2,1,0:T(8,128)(2,1)S(1)}, u32[]{:S(2)}, u32[]{:S(2)}) collective-permute-start(bf16[2,2,672,128]{3,2,1,0:T(8,128)(2,1)S(1)} %get-tuple-element.65), channel_id=1, source_target_pairs={{0,2},{1,3},{2,0},{3,1},{4,6},{5,7},{6,4},{7,5},{8,10},{9,11},{10,... | collective-permute-start | bytes 2064392 | tf_op jit(solution)/shard_map/ppermute | solution.py:472
  29.9 13.2 %collective-permute-start = (bf16[2,2,256,128]{3,2,1,0:T(8,128)(2,1)S(1)}, bf16[2,2,256,128]{3,2,1,0:T(8,128)(2,1)S(1)}, u32[]{:S(2)}, u32[]{:S(2)}) collective-permute-start(bf16[2,2,256,128]{3,2,1,0:T(8,128)(2,1)S(1)} %copy-done.6), channel_id=1, source_target_pairs={{0,8},{4,12},{8,0},{12,4},{16,24},{20,28},{24,16},{28,20},{1,9},{5... | collective-permute-start | bytes 786440 | tf_op jit(solution)/shard_map/ppermute | solution.py:469
  31.5 14.0 %collective-permute-start.1 = (bf16[2,2,256,128]{3,2,1,0:T(8,128)(2,1)S(1)}, bf16[2,2,256,128]{3,2,1,0:T(8,128)(2,1)S(1)}, u32[]{:S(2)}, u32[]{:S(2)}) collective-permute-start(bf16[2,2,256,128]{3,2,1,0:T(8,128)(2,1)S(1)} %copy-done.5), channel_id=1, source_target_pairs={{0,16},{4,20},{8,24},{12,28},{16,0},{20,4},{24,8},{28,12},{1,17},{... | collective-permute-start | bytes 786440 | tf_op jit(solution)/shard_map/ppermute | solution.py:469
  45.5 2.4 %copy-start.1 = (bf16[2,4,2,432,128]{4,3,2,1,0:T(8,128)(2,1)S(1)}, bf16[2,4,2,432,128]{4,3,2,1,0:T(8,128)(2,1)}, u32[]{:S(2)}) copy-start(bf16[2,4,2,432,128]{4,3,2,1,0:T(8,128)(2,1)} %get-tuple-element.57) | copy-start | bytes 5308420
  45.8 11.1 %collective-permute-start.8 = (bf16[2,672,128]{2,1,0:T(8,128)(2,1)S(1)}, bf16[2,672,128]{2,1,0:T(8,128)(2,1)S(1)}, u32[]{:S(2)}, u32[]{:S(2)}) collective-permute-start(bf16[2,672,128]{2,1,0:T(8,128)(2,1)S(1)} %get-tuple-element.66.refs_4_), channel_id=1, source_target_pairs={{0,2},{1,3},{2,0},{3,1},{4,6},{5,7},{6,4},{7,5},{8,10},{9,11},{10,... | collective-permute-start | bytes 1032200 | tf_op jit(solution)/shard_map/ppermute | solution.py:472
  47.4 11.0 %collective-permute-start.7 = (bf16[2,672,128]{2,1,0:T(8,128)(2,1)S(1)}, bf16[2,672,128]{2,1,0:T(8,128)(2,1)S(1)}, u32[]{:S(2)}, u32[]{:S(2)}) collective-permute-start(bf16[2,672,128]{2,1,0:T(8,128)(2,1)S(1)} %get-tuple-element.67.refs_5_), channel_id=1, source_target_pairs={{0,1},{1,0},{2,3},{3,2},{4,5},{5,4},{6,7},{7,6},{8,9},{9,8},{10,11... | collective-permute-start | bytes 1032200 | tf_op jit(solution)/shard_map/ppermute | solution.py:472
  47.9 3.2 %copy-start.4 = (bf16[2,2,256,128]{3,2,1,0:T(8,128)(2,1)S(1)}, bf16[2,2,256,128]{3,2,1,0:T(8,128)(2,1)}, u32[]{:S(2)}) copy-start(bf16[2,2,256,128]{3,2,1,0:T(8,128)(2,1)} %get-tuple-element.70) | copy-start | bytes 786436
  49.0 16.4 %collective-permute-start.9 = (bf16[2,2,432,128]{3,2,1,0:T(8,128)(2,1)S(1)}, bf16[2,2,432,128]{3,2,1,0:T(8,128)(2,1)S(1)}, u32[]{:S(2)}, u32[]{:S(2)}) collective-permute-start(bf16[2,2,432,128]{3,2,1,0:T(8,128)(2,1)S(1)} %get-tuple-element.68.refs_3_), channel_id=1, source_target_pairs={{0,1},{1,0},{2,3},{3,2},{4,5},{5,4},{6,7},{7,6},{8,9},{9,8},{10,11... | collective-permute-start | bytes 1327112 | tf_op jit(solution)/shard_map/ppermute | solution.py:472
  50.6 14.8 %collective-permute-start.10 = (bf16[2,2,432,128]{3,2,1,0:T(8,128)(2,1)S(1)}, bf16[2,2,432,128]{3,2,1,0:T(8,128)(2,1)S(1)}, u32[]{:S(2)}, u32[]{:S(2)}) collective-permute-start(bf16[2,2,432,128]{3,2,1,0:T(8,128)(2,1)S(1)} %get-tuple-element.69.refs_4_), channel_id=1, source_target_pairs={{0,2},{1,3},{2,0},{3,1},{4,6},{5,7},{6,4},{7,5},{8,10},{9,11},{10,... | collective-permute-start | bytes 1327112 | tf_op jit(solution)/shard_map/ppermute | solution.py:472
  51.1 10.3 %collective-permute-start.6 = (bf16[2,2,256,128]{3,2,1,0:T(8,128)(2,1)S(1)}, bf16[2,2,256,128]{3,2,1,0:T(8,128)(2,1)S(1)}, u32[]{:S(2)}, u32[]{:S(2)}) collective-permute-start(bf16[2,2,256,128]{3,2,1,0:T(8,128)(2,1)S(1)} %copy-done.4), channel_id=1, source_target_pairs={{0,24},{4,28},{8,16},{12,20},{16,8},{20,12},{24,0},{28,4},{1,25},{... | collective-permute-start | bytes 786440 | tf_op jit(solution)/shard_map/ppermute | solution.py:469
  58.6 8.3 %collective-permute-start.13 = (bf16[2,672,128]{2,1,0:T(8,128)(2,1)S(1)}, bf16[2,672,128]{2,1,0:T(8,128)(2,1)S(1)}, u32[]{:S(2)}, u32[]{:S(2)}) collective-permute-start(bf16[2,672,128]{2,1,0:T(8,128)(2,1)S(1)} %sums.11.refs_4_), channel_id=1, source_target_pairs={{0,8},{4,12},{8,0},{12,4},{16,24},{20,28},{24,16},{28,20},{1,9},{5... | collective-permute-start | bytes 1032200 | tf_op jit(solution)/shard_map/ppermute | solution.py:469
  65.6 6.0 %collective-permute-start.11 = (bf16[2,432,128]{2,1,0:T(8,128)(2,1)S(1)}, bf16[2,432,128]{2,1,0:T(8,128)(2,1)S(1)}, u32[]{:S(2)}, u32[]{:S(2)}) collective-permute-start(bf16[2,432,128]{2,1,0:T(8,128)(2,1)S(1)} %get-tuple-element.73.refs_4_), channel_id=1, source_target_pairs={{0,2},{1,3},{2,0},{3,1},{4,6},{5,7},{6,4},{7,5},{8,10},{9,11},{10,... | collective-permute-start | bytes 663560 | tf_op jit(solution)/shard_map/ppermute | solution.py:472
  66.2 5.9 %collective-permute-start.12 = (bf16[2,432,128]{2,1,0:T(8,128)(2,1)S(1)}, bf16[2,432,128]{2,1,0:T(8,128)(2,1)S(1)}, u32[]{:S(2)}, u32[]{:S(2)}) collective-permute-start(bf16[2,432,128]{2,1,0:T(8,128)(2,1)S(1)} %get-tuple-element.74.refs_5_), channel_id=1, source_target_pairs={{0,1},{1,0},{2,3},{3,2},{4,5},{5,4},{6,7},{7,6},{8,9},{9,8},{10,11... | collective-permute-start | bytes 663560 | tf_op jit(solution)/shard_map/ppermute | solution.py:472
  72.3 8.3 %copy-start.2 = (bf16[2,2,256,128]{3,2,1,0:T(8,128)(2,1)S(1)}, bf16[2,2,256,128]{3,2,1,0:T(8,128)(2,1)}, u32[]{:S(2)}) copy-start(bf16[2,2,256,128]{3,2,1,0:T(8,128)(2,1)} %get-tuple-element.53.refs_0_.rest_0_) | copy-start | bytes 786436
  72.3 8.2 %collective-permute-start.14 = (bf16[2,432,128]{2,1,0:T(8,128)(2,1)S(1)}, bf16[2,432,128]{2,1,0:T(8,128)(2,1)S(1)}, u32[]{:S(2)}, u32[]{:S(2)}) collective-permute-start(bf16[2,432,128]{2,1,0:T(8,128)(2,1)S(1)} %sums.14.refs_5_), channel_id=1, source_target_pairs={{0,8},{4,12},{8,0},{12,4},{16,24},{20,28},{24,16},{28,20},{1,9},{5... | collective-permute-start | bytes 663560 | tf_op jit(solution)/shard_map/ppermute | solution.py:469
  73.9 6.3 %collective-permute-start.15 = (bf16[1,672,128]{2,1,0:T(8,128)(2,1)S(1)}, bf16[1,672,128]{2,1,0:T(8,128)(2,1)S(1)}, u32[]{:S(2)}, u32[]{:S(2)}) collective-permute-start(bf16[1,672,128]{2,1,0:T(8,128)(2,1)S(1)} %sums.13.refs_3_), channel_id=1, source_target_pairs={{0,16},{4,20},{8,24},{12,28},{16,0},{20,4},{24,8},{28,12},{1,17},{... | collective-permute-start | bytes 516104 | tf_op jit(solution)/shard_map/ppermute | solution.py:469
  80.4 3.5 %copy-start.3 = (s32[2,8192,4]{1,2,0:T(4,128)S(1)}, s32[2,8192,4]{1,2,0:T(4,128)}, u32[]{:S(2)}) copy-start(s32[2,8192,4]{1,2,0:T(4,128)} %param.23) | copy-start | bytes 786436
  80.6 3.3 %collective-permute-start.17 = (bf16[2,2,256,128]{3,2,1,0:T(8,128)(2,1)S(1)}, bf16[2,2,256,128]{3,2,1,0:T(8,128)(2,1)S(1)}, u32[]{:S(2)}, u32[]{:S(2)}) collective-permute-start(bf16[2,2,256,128]{3,2,1,0:T(8,128)(2,1)S(1)} %get-tuple-element.76), channel_id=1, source_target_pairs={{0,4},{4,0},{8,12},{12,8},{16,20},{20,16},{24,28},{28,24},{1,5},{5... | collective-permute-start | bytes 786440 | tf_op jit(solution)/shard_map/ppermute | solution.py:466
  80.7 3.2 %collective-permute-start.16 = (bf16[2,2,256,128]{3,2,1,0:T(8,128)(2,1)S(1)}, bf16[2,2,256,128]{3,2,1,0:T(8,128)(2,1)S(1)}, u32[]{:S(2)}, u32[]{:S(2)}) collective-permute-start(bf16[2,2,256,128]{3,2,1,0:T(8,128)(2,1)S(1)} %get-tuple-element.75.rest_6_), channel_id=1, source_target_pairs={{0,4},{4,0},{8,12},{12,8},{16,20},{20,16},{24,28},{28,24},{1,5},{5... | collective-permute-start | bytes 786440 | tf_op jit(solution)/shard_map/ppermute | solution.py:466
  81.2 8.4 %collective-permute-start.18 = (bf16[1,432,128]{2,1,0:T(8,128)(2,1)S(1)}, bf16[1,432,128]{2,1,0:T(8,128)(2,1)S(1)}, u32[]{:S(2)}, u32[]{:S(2)}) collective-permute-start(bf16[1,432,128]{2,1,0:T(8,128)(2,1)S(1)} %sums.16.refs_4_), channel_id=1, source_target_pairs={{0,16},{4,20},{8,24},{12,28},{16,0},{20,4},{24,8},{28,12},{1,17},{... | collective-permute-start | bytes 331784 | tf_op jit(solution)/shard_map/ppermute | solution.py:469
  89.7 12.3 %collective-permute-start.22 = (bf16[1,432,128]{2,1,0:T(8,128)(2,1)S(1)}, bf16[1,432,128]{2,1,0:T(8,128)(2,1)S(1)}, u32[]{:S(2)}, u32[]{:S(2)}) collective-permute-start(bf16[1,432,128]{2,1,0:T(8,128)(2,1)S(1)} %sums.17.rest_6_), channel_id=1, source_target_pairs={{0,16},{4,20},{8,24},{12,28},{16,0},{20,4},{24,8},{28,12},{1,17},{... | collective-permute-start | bytes 331784 | tf_op jit(solution)/shard_map/ppermute | solution.py:469
  90.1 13.7 %collective-permute-start.21 = (bf16[1,672,128]{2,1,0:T(8,128)(2,1)S(1)}, bf16[1,672,128]{2,1,0:T(8,128)(2,1)S(1)}, u32[]{:S(2)}, u32[]{:S(2)}) collective-permute-start(bf16[1,672,128]{2,1,0:T(8,128)(2,1)S(1)} %sums.15.refs_4_), channel_id=1, source_target_pairs={{0,16},{4,20},{8,24},{12,28},{16,0},{20,4},{24,8},{28,12},{1,17},{... | collective-permute-start | bytes 516104 | tf_op jit(solution)/shard_map/ppermute | solution.py:469
  103.8 10.2 %collective-permute-start.25 = (bf16[2,672,128]{2,1,0:T(8,128)(2,1)S(1)}, bf16[2,672,128]{2,1,0:T(8,128)(2,1)S(1)}, u32[]{:S(2)}, u32[]{:S(2)}) collective-permute-start(bf16[2,672,128]{2,1,0:T(8,128)(2,1)S(1)} %pad_maximum_fusion.refs_4_.refs_0_), channel_id=1, source_target_pairs={{0,8},{4,12},{8,0},{12,4},{16,24},{20,28},{24,16},{28,20},{1,9},{5... | collective-permute-start | bytes 1032200 | tf_op jit(solution)/shard_map/ppermute | solution.py:469
  103.9 10.2 %collective-permute-start.19 = (bf16[2,512,128]{2,1,0:T(8,128)(2,1)S(1)}, bf16[2,512,128]{2,1,0:T(8,128)(2,1)S(1)}, u32[]{:S(2)}, u32[]{:S(2)}) collective-permute-start(bf16[2,512,128]{2,1,0:T(8,128)(2,1)S(1)} %get-tuple-element.77), channel_id=1, source_target_pairs={{0,1},{1,0},{2,3},{3,2},{4,5},{5,4},{6,7},{7,6},{8,9},{9,8},{10,11... | collective-permute-start | bytes 786440 | tf_op jit(solution)/shard_map/ppermute | solution.py:472
  104.6 9.5 %collective-permute-start.20 = (bf16[2,512,128]{2,1,0:T(8,128)(2,1)S(1)}, bf16[2,512,128]{2,1,0:T(8,128)(2,1)S(1)}, u32[]{:S(2)}, u32[]{:S(2)}) collective-permute-start(bf16[2,512,128]{2,1,0:T(8,128)(2,1)S(1)} %get-tuple-element.78), channel_id=1, source_target_pairs={{0,2},{1,3},{2,0},{3,1},{4,6},{5,7},{6,4},{7,5},{8,10},{9,11},{10,... | collective-permute-start | bytes 786440 | tf_op jit(solution)/shard_map/ppermute | solution.py:472
  106.1 10.3 %collective-permute-start.28 = (bf16[2,432,128]{2,1,0:T(8,128)(2,1)S(1)}, bf16[2,432,128]{2,1,0:T(8,128)(2,1)S(1)}, u32[]{:S(2)}, u32[]{:S(2)}) collective-permute-start(bf16[2,432,128]{2,1,0:T(8,128)(2,1)S(1)} %pad_maximum_fusion.1.refs_4_), channel_id=1, source_target_pairs={{0,8},{4,12},{8,0},{12,4},{16,24},{20,28},{24,16},{28,20},{1,9},{5... | collective-permute-start | bytes 663560 | tf_op jit(solution)/shard_map/ppermute | solution.py:469
  108.1 18.2 %collective-permute-start.26 = (bf16[2,672,128]{2,1,0:T(8,128)(2,1)S(1)}, bf16[2,672,128]{2,1,0:T(8,128)(2,1)S(1)}, u32[]{:S(2)}, u32[]{:S(2)}) collective-permute-start(bf16[2,672,128]{2,1,0:T(8,128)(2,1)S(1)} %pad_maximum_fusion.refs_4_.refs_0_), channel_id=1, source_target_pairs={{0,4},{4,0},{8,12},{12,8},{16,20},{20,16},{24,28},{28,24},{1,5},{5... | collective-permute-start | bytes 1032200 | tf_op jit(solution)/shard_map/ppermute | solution.py:466
  114.1 12.1 %collective-permute-start.27 = (bf16[2,672,128]{2,1,0:T(8,128)(2,1)S(1)}, bf16[2,672,128]{2,1,0:T(8,128)(2,1)S(1)}, u32[]{:S(2)}, u32[]{:S(2)}) collective-permute-start(bf16[2,672,128]{2,1,0:T(8,128)(2,1)S(1)} %collective-permute-done.25.refs_1_), channel_id=1, source_target_pairs={{0,4},{4,0},{8,12},{12,8},{16,20},{20,16},{24,28},{28,24},{1,5},{5... | collective-permute-start | bytes 1032200 | tf_op jit(solution)/shard_map/ppermute | solution.py:466
  114.2 6.0 %collective-permute-start.23 = (bf16[512,128]{1,0:T(8,128)(2,1)S(1)}, bf16[512,128]{1,0:T(8,128)(2,1)S(1)}, u32[]{:S(2)}, u32[]{:S(2)}) collective-permute-start(bf16[512,128]{1,0:T(8,128)(2,1)S(1)} %get-tuple-element.81.refs_6_), channel_id=1, source_target_pairs={{0,2},{1,3},{2,0},{3,1},{4,6},{5,7},{6,4},{7,5},{8,10},{9,11},{10,... | collective-permute-start | bytes 393224 | tf_op jit(solution)/shard_map/ppermute | solution.py:472
  115.8 10.4 %collective-permute-start.29 = (bf16[2,432,128]{2,1,0:T(8,128)(2,1)S(1)}, bf16[2,432,128]{2,1,0:T(8,128)(2,1)S(1)}, u32[]{:S(2)}, u32[]{:S(2)}) collective-permute-start(bf16[2,432,128]{2,1,0:T(8,128)(2,1)S(1)} %pad_maximum_fusion.1.refs_4_), channel_id=1, source_target_pairs={{0,4},{4,0},{8,12},{12,8},{16,20},{20,16},{24,28},{28,24},{1,5},{5... | collective-permute-start | bytes 663560 | tf_op jit(solution)/shard_map/ppermute | solution.py:466
  116.4 9.8 %collective-permute-start.30 = (bf16[2,432,128]{2,1,0:T(8,128)(2,1)S(1)}, bf16[2,432,128]{2,1,0:T(8,128)(2,1)S(1)}, u32[]{:S(2)}, u32[]{:S(2)}) collective-permute-start(bf16[2,432,128]{2,1,0:T(8,128)(2,1)S(1)} %collective-permute-done.28.refs_5_), channel_id=1, source_target_pairs={{0,4},{4,0},{8,12},{12,8},{16,20},{20,16},{24,28},{28,24},{1,5},{5... | collective-permute-start | bytes 663560 | tf_op jit(solution)/shard_map/ppermute | solution.py:466
  120.2 5.1 %collective-permute-start.24 = (bf16[512,128]{1,0:T(8,128)(2,1)S(1)}, bf16[512,128]{1,0:T(8,128)(2,1)S(1)}, u32[]{:S(2)}, u32[]{:S(2)}) collective-permute-start(bf16[512,128]{1,0:T(8,128)(2,1)S(1)} %get-tuple-element.82.refs_7_), channel_id=1, source_target_pairs={{0,1},{1,0},{2,3},{3,2},{4,5},{5,4},{6,7},{7,6},{8,9},{9,8},{10,11... | collective-permute-start | bytes 393224 | tf_op jit(solution)/shard_map/ppermute | solution.py:472

commit v11 on v9

--- a/solution.py
+++ b/solution.py
@@ -681,10 +681,10 @@
         shares.append(Halving([sums], high_first if table % 2 else low_first))
         last = [sums]
         if table == 0:
+            for stage in range(1, z_bits):
+                last = one.z_step(stage, last)
             for at in range(1, row_bits):
                 last = two.row_step(at, last)
-            for stage in range(1, z_bits):
-                last = one.z_step(stage, last)
             last = two.z_step(0, last)
     last = row_step(shares, 0, last)
     last = one.z_own(last)

time: 119 us -> 120 us (level)
  waiting for transfers between devices: 34.7 us -> 36.5 us
    ppermute x12, waiting for transfers between devices: 6.89 us -> 8.59 us  [swap_row(): lax.ppermute(value, 'row', [(at, at ^ 1 << bit) for at in range(n_row)])]
  transfers between devices with their start and end apart: 31 -> 31, of which waited for: 13 -> 13; matrix products, arithmetic and copies ran while one was open for 0% -> 0% of each run, Pallas kernels for 23% -> 22%
where the time goes in v11:
time: 120 us
  starting transfers between devices  41.4 us (34%)
  Pallas kernels  41 us (34%)
  waiting for transfers between devices  36.5 us (30%)
    ppermute x11, waiting for transfers between devices, swap_z(): lax.ppermute(value, 'table', [(at, at ^ 2 * which) for at in range(n_tabl...  26.2 us
    ppermute x11, starting transfers between devices, swap_z(): lax.ppermute(value, 'table', [(at, at ^ 2 * which) for at in range(n_tabl...  24.8 us
    ppermute x12, starting transfers between devices, swap_row(): lax.ppermute(value, 'row', [(at, at ^ 1 << bit) for at in range(n_row)])  14.9 us
    pallas_call x1, Pallas kernels, local(): call(front_kernel, [packed(rows_front)] * 2 + [wide(feat, batch), wide(ba...  11.9 us
    pallas_call x1, Pallas kernels, local(): call(functools.partial(middle_kernel, n_z), [packed(rows_back)] * 2 + [wi...  10.1 us
    ppermute x12, waiting for transfers between devices, swap_row(): lax.ppermute(value, 'row', [(at, at ^ 1 << bit) for at in range(n_row)])  8.59 us
    pallas_call x2, Pallas kernels, local(): pl.pallas_call(functools.partial(count_kernel, n_row, table, hot, n_z), o...  8.03 us
    pallas_call x4, Pallas kernels, fetch_sums(): call(functools.partial(fetch_sum_kernel, plan, n_in), shapes, scratch + [...  6 us
  transfers between devices with their start and end apart: 31, of which 13 were waited for; matrix products, arithmetic and copies ran while one was open for 0% of the time, Pallas kernels for 22%

profile of v11, /device:TPU:0, one launch (start us, length us, event | category | flops | bytes accessed | tf_op | source)
XLA Modules:
  0.0 119.9 jit_solution(14123888442561873545)
XLA Ops:
  0.6 11.9 %front.1 = (bf16[2,4,2,672,128]{4,3,2,1,0:T(8,128)(2,1)}, bf16[2,4,2,672,128]{4,3,2,1,0:T(8,128)(2,1)}, bf16[2176,256]{1,0:T(8,128)(2,1)}, bf16[256,1024]{1,0:T(8,128)(2,1)}, f32[24,128]{1,0:T(8,128)}) custom-call(bf16[256,128]{1,0:T(8,128)(2,1)} %refs_0_.3, bf16[256,2048]{1,0:T(8,128)(2,1)} %refs_1_.3, bf16[2176,256]{1,0:T(8,128)(2,1)} %refs_2_.3, ...), custom_call_target="tpu_custom_call" | custom-call | tf_op jit(solution)/shard_map/front/pallas_call | solution.py:504
  12.5 0.5 collective-permute-start.3
  13.1 10.1 %middle.1 = (bf16[2,4,2,432,128]{4,3,2,1,0:T(8,128)(2,1)}, bf16[2,4,2,432,128]{4,3,2,1,0:T(8,128)(2,1)}, bf16[2,2,256,128]{3,2,1,0:T(8,128)(2,1)}, bf16[2,2,256,...) custom-call(bf16[256,128]{1,0:T(8,128)(2,1)} %refs_0_.3, ...), custom_call_target="tpu_custom_call" | custom-call | tf_op jit(solution)/shard_map/middle/pallas_call | solution.py:531
  23.4 2.0 %first_sums.5 = (bf16[2,2,672,128]{3,2,1,0:T(8,128)(2,1)S(1)}, bf16[2,2,672,128]{3,2,1,0:T(8,128)(2,1)S(1)}) custom-call(bf16[2,2,2,2,672,128]{5,4,3,2,1,0:T(8,128)(2,1)S(1)} %bitcast.7, bf16[2,2,2,2,672,128]{5,4,3,2,1,0:T(8,128)(2,1)} %bitcast.2.refs_1_.refs_3_, bf16[2,2,2,2,672,128]{5,4,3,2,1,0:T(8,128)(2,1)S(1)} %bitcast.8, ...), custom_call_target="tpu_custom_call" | custom-call | tf_op jit(solution)/shard_map/first_sums/pallas_call | solution.py:408
  25.4 3.0 %collective-permute-start.4 = (bf16[2,2,672,128]{3,2,1,0:T(8,128)(2,1)S(1)}, bf16[2,2,672,128]{3,2,1,0:T(8,128)(2,1)S(1)}, u32[]{:S(2)}, u32[]{:S(2)}) collective-permute-start(bf16[2,2,672,128]{3,2,1,0:T(8,128)(2,1)S(1)} %get-tuple-element.62), channel_id=1, source_target_pairs={{0,2},{1,3},{2,0},{3,1},{4,6},{5,7},{6,4},{7,5},{8,10},{9,11},{10,... | collective-permute-start | bytes 2064392 | tf_op jit(solution)/shard_map/ppermute | solution.py:472
  28.4 1.5 %collective-permute-start.5 = (bf16[2,2,672,128]{3,2,1,0:T(8,128)(2,1)S(1)}, bf16[2,2,672,128]{3,2,1,0:T(8,128)(2,1)S(1)}, u32[]{:S(2)}, u32[]{:S(2)}) collective-permute-start(bf16[2,2,672,128]{3,2,1,0:T(8,128)(2,1)S(1)} %get-tuple-element.64), channel_id=1, source_target_pairs={{0,1},{1,0},{2,3},{3,2},{4,5},{5,4},{6,7},{7,6},{8,9},{9,8},{10,11... | collective-permute-start | bytes 2064392 | tf_op jit(solution)/shard_map/ppermute | solution.py:472
  29.9 1.6 %collective-permute-start = (bf16[2,2,256,128]{3,2,1,0:T(8,128)(2,1)S(1)}, bf16[2,2,256,128]{3,2,1,0:T(8,128)(2,1)S(1)}, u32[]{:S(2)}, u32[]{:S(2)}) collective-permute-start(bf16[2,2,256,128]{3,2,1,0:T(8,128)(2,1)S(1)} %copy-done.6), channel_id=1, source_target_pairs={{0,8},{4,12},{8,0},{12,4},{16,24},{20,28},{24,16},{28,20},{1,9},{5... | collective-permute-start | bytes 786440 | tf_op jit(solution)/shard_map/ppermute | solution.py:469
  31.5 2.6 %collective-permute-start.1 = (bf16[2,2,256,128]{3,2,1,0:T(8,128)(2,1)S(1)}, bf16[2,2,256,128]{3,2,1,0:T(8,128)(2,1)S(1)}, u32[]{:S(2)}, u32[]{:S(2)}) collective-permute-start(bf16[2,2,256,128]{3,2,1,0:T(8,128)(2,1)S(1)} %copy-done.5), channel_id=1, source_target_pairs={{0,16},{4,20},{8,24},{12,28},{16,0},{20,4},{24,8},{28,12},{1,17},{... | collective-permute-start | bytes 786440 | tf_op jit(solution)/shard_map/ppermute | solution.py:469
  34.1 9.0 %collective-permute-done.refs_4_.refs_1_.rest_1_ = bf16[2,2,256,128]{3,2,1,0:T(8,128)(2,1)S(1)} collective-permute-done((bf16[2,2,256,128]{3,2,1,0:T(8,128)(2,1)S(1)}, bf16[2,2,256,128]{3,2,1,0:T(8,128)(2,1)S(1)}, u32[]{:S(2)}, u32[]{:S(2)}) %collective-permute-start) | collective-permute-done | bytes 262176 | tf_op jit(solution)/shard_map/ppermute | solution.py:469
  43.1 1.8 %first_sums.4 = (bf16[2,2,672,128]{3,2,1,0:T(8,128)(2,1)S(1)}, bf16[2,2,672,128]{3,2,1,0:T(8,128)(2,1)S(1)}) custom-call(bf16[2,2,2,2,672,128]{5,4,3,2,1,0:T(8,128)(2,1)S(1)} %bitcast.9, bf16[2,2,2,2,672,128]{5,4,3,2,1,0:T(8,128)(2,1)} %bitcast.2.refs_1_.refs_3_, bf16[2,2,2,2,672,128]{5,4,3,2,1,0:T(8,128)(2,1)S(1)} %bitcast.10, ...), custom_call_target="tpu_custom_call" | custom-call | tf_op jit(solution)/shard_map/first_sums/pallas_call | solution.py:408
  44.9 0.6 collective-permute-done.1.refs_5_.refs_2_.rest_2_
  45.5 0.3 sums.10
  45.8 1.6 %collective-permute-start.6 = (bf16[2,672,128]{2,1,0:T(8,128)(2,1)S(1)}, bf16[2,672,128]{2,1,0:T(8,128)(2,1)S(1)}, u32[]{:S(2)}, u32[]{:S(2)}) collective-permute-start(bf16[2,672,128]{2,1,0:T(8,128)(2,1)S(1)} %get-tuple-element.65.refs_5_), channel_id=1, source_target_pairs={{0,1},{1,0},{2,3},{3,2},{4,5},{5,4},{6,7},{7,6},{8,9},{9,8},{10,11... | collective-permute-start | bytes 1032200 | tf_op jit(solution)/shard_map/ppermute | solution.py:472
  47.4 0.5 collective-permute-start.8
  47.9 3.6 %collective-permute-start.2 = (bf16[2,2,256,128]{3,2,1,0:T(8,128)(2,1)S(1)}, bf16[2,2,256,128]{3,2,1,0:T(8,128)(2,1)S(1)}, u32[]{:S(2)}, u32[]{:S(2)}) collective-permute-start(bf16[2,2,256,128]{3,2,1,0:T(8,128)(2,1)S(1)} %copy-done.4), channel_id=1, source_target_pairs={{0,24},{4,28},{8,16},{12,20},{16,8},{20,12},{24,0},{28,4},{1,25},{... | collective-permute-start | bytes 786440 | tf_op jit(solution)/shard_map/ppermute | solution.py:469
  51.5 1.1 first_sums.6
  52.6 0.6 collective-permute-start.12
  53.2 1.5 %collective-permute-start.11 = (bf16[2,2,432,128]{3,2,1,0:T(8,128)(2,1)S(1)}, bf16[2,2,432,128]{3,2,1,0:T(8,128)(2,1)S(1)}, u32[]{:S(2)}, u32[]{:S(2)}) collective-permute-start(bf16[2,2,432,128]{3,2,1,0:T(8,128)(2,1)S(1)} %get-tuple-element.70.refs_4_), channel_id=1, source_target_pairs={{0,2},{1,3},{2,0},{3,1},{4,6},{5,7},{6,4},{7,5},{8,10},{9,11},{10,... | collective-permute-start | bytes 1327112 | tf_op jit(solution)/shard_map/ppermute | solution.py:472
  54.7 1.2 %collective-permute-done.6.refs_2_ = bf16[2,672,128]{2,1,0:T(8,128)(2,1)S(1)} collective-permute-done((bf16[2,672,128]{2,1,0:T(8,128)(2,1)S(1)}, bf16[2,672,128]{2,1,0:T(8,128)(2,1)S(1)}, u32[]{:S(2)}, u32[]{:S(2)}) %collective-permute-start.6) | collective-permute-done | bytes 344096 | tf_op jit(solution)/shard_map/ppermute | solution.py:472
  56.0 2.2 %collective-permute-done.8.refs_5_.refs_2_ = bf16[2,672,128]{2,1,0:T(8,128)(2,1)S(1)} collective-permute-done((bf16[2,672,128]{2,1,0:T(8,128)(2,1)S(1)}, bf16[2,672,128]{2,1,0:T(8,128)(2,1)S(1)}, u32[]{:S(2)}, u32[]{:S(2)}) %collective-permute-start.8) | collective-permute-done | bytes 344096 | tf_op jit(solution)/shard_map/ppermute | solution.py:472
  58.4 1.9 %collective-permute-start.13 = (bf16[2,672,128]{2,1,0:T(8,128)(2,1)S(1)}, bf16[2,672,128]{2,1,0:T(8,128)(2,1)S(1)}, u32[]{:S(2)}, u32[]{:S(2)}) collective-permute-start(bf16[2,672,128]{2,1,0:T(8,128)(2,1)S(1)} %sums.11.refs_4_), channel_id=1, source_target_pairs={{0,8},{4,12},{8,0},{12,4},{16,24},{20,28},{24,16},{28,20},{1,9},{5... | collective-permute-start | bytes 1032200 | tf_op jit(solution)/shard_map/ppermute | solution.py:469
  60.4 0.5 collective-permute-start.9
  60.9 1.1 first_sums.7
  62.0 0.3 collective-permute-done.9.rest_4_
  62.3 4.0 %counts.2.refs_4_ = bf16[4,512,128]{2,1,0:T(8,128)(2,1)S(1)} custom-call(s32[2,4,8192]{2,1,0:T(4,128)S(1)} %bitcast.25, bf16[2,2,256,128]{3,2,1,0:T(8,128)(2,1)S(1)} %copy-done.2, bf16[2,2,256,128]{3,2,1,0:T(8,128)(2,1)S(1)} %collective-permute-done.refs_4_.refs_1_.rest_1_, bf16[2,2,256,128]{3,2,1,0:T(8,128)(2,1)S(1)} %collective-permute-done.1.refs_5_.refs_2_.rest_2_, ...), custom_call_target="tpu_custom_call" | custom-call | tf_op jit(solution)/shard_map/counts/pallas_call | solution.py:671
  66.7 0.6 collective-permute-start.14
  67.3 0.5 collective-permute-start.15
  67.8 3.4 %collective-permute-start.19 = (bf16[1,672,128]{2,1,0:T(8,128)(2,1)S(1)}, bf16[1,672,128]{2,1,0:T(8,128)(2,1)S(1)}, u32[]{:S(2)}, u32[]{:S(2)}) collective-permute-start(bf16[1,672,128]{2,1,0:T(8,128)(2,1)S(1)} %sums.12.refs_4_), channel_id=1, source_target_pairs={{0,16},{4,20},{8,24},{12,28},{16,0},{20,4},{24,8},{28,12},{1,17},{... | collective-permute-start | bytes 516104 | tf_op jit(solution)/shard_map/ppermute | solution.py:469
  71.2 3.0 %collective-permute-done.14.refs_2_ = bf16[2,432,128]{2,1,0:T(8,128)(2,1)S(1)} collective-permute-done((bf16[2,432,128]{2,1,0:T(8,128)(2,1)S(1)}, bf16[2,432,128]{2,1,0:T(8,128)(2,1)S(1)}, u32[]{:S(2)}, u32[]{:S(2)}) %collective-permute-start.14) | collective-permute-done | bytes 221216 | tf_op jit(solution)/shard_map/ppermute | solution.py:472
  74.6 1.5 %collective-permute-start.18 = (bf16[2,432,128]{2,1,0:T(8,128)(2,1)S(1)}, bf16[2,432,128]{2,1,0:T(8,128)(2,1)S(1)}, u32[]{:S(2)}, u32[]{:S(2)}) collective-permute-start(bf16[2,432,128]{2,1,0:T(8,128)(2,1)S(1)} %sums.14.rest_6_), channel_id=1, source_target_pairs={{0,8},{4,12},{8,0},{12,4},{16,24},{20,28},{24,16},{28,20},{1,9},{5... | collective-permute-start | bytes 663560 | tf_op jit(solution)/shard_map/ppermute | solution.py:469
  76.2 4.0 %counts.3.refs_2_ = bf16[4,512,128]{2,1,0:T(8,128)(2,1)S(1)} custom-call(s32[2,4,8192]{2,1,0:T(4,128)S(1)} %bitcast.26, bf16[2,2,256,128]{3,2,1,0:T(8,128)(2,1)S(1)} %copy-done.2, bf16[2,2,256,128]{3,2,1,0:T(8,128)(2,1)S(1)} %collective-permute-done.refs_4_.refs_1_.rest_1_, bf16[2,2,256,128]{3,2,1,0:T(8,128)(2,1)S(1)} %collective-permute-done.1.refs_5_.refs_2_.rest_2_, ...), custom_call_target="tpu_custom_call" | custom-call | tf_op jit(solution)/shard_map/counts/pallas_call | solution.py:671
  80.4 1.6 %collective-permute-start.16 = (bf16[2,512,128]{2,1,0:T(8,128)(2,1)S(1)}, bf16[2,512,128]{2,1,0:T(8,128)(2,1)S(1)}, u32[]{:S(2)}, u32[]{:S(2)}) collective-permute-start(bf16[2,512,128]{2,1,0:T(8,128)(2,1)S(1)} %get-tuple-element.77.refs_5_), channel_id=1, source_target_pairs={{0,1},{1,0},{2,3},{3,2},{4,5},{5,4},{6,7},{7,6},{8,9},{9,8},{10,11... | collective-permute-start | bytes 786440 | tf_op jit(solution)/shard_map/ppermute | solution.py:472
  81.9 1.4 %collective-permute-start.17 = (bf16[2,512,128]{2,1,0:T(8,128)(2,1)S(1)}, bf16[2,512,128]{2,1,0:T(8,128)(2,1)S(1)}, u32[]{:S(2)}, u32[]{:S(2)}) collective-permute-start(bf16[2,512,128]{2,1,0:T(8,128)(2,1)S(1)} %get-tuple-element.78.refs_6_), channel_id=1, source_target_pairs={{0,2},{1,3},{2,0},{3,1},{4,6},{5,7},{6,4},{7,5},{8,10},{9,11},{10,... | collective-permute-start | bytes 786440 | tf_op jit(solution)/shard_map/ppermute | solution.py:472
  83.6 1.1 collective-permute-start.22
  84.8 2.0 %collective-permute-start.23 = (bf16[1,432,128]{2,1,0:T(8,128)(2,1)S(1)}, bf16[1,432,128]{2,1,0:T(8,128)(2,1)S(1)}, u32[]{:S(2)}, u32[]{:S(2)}) collective-permute-start(bf16[1,432,128]{2,1,0:T(8,128)(2,1)S(1)} %sums.17.refs_4_), channel_id=1, source_target_pairs={{0,16},{4,20},{8,24},{12,28},{16,0},{20,4},{24,8},{28,12},{1,17},{... | collective-permute-start | bytes 331784 | tf_op jit(solution)/shard_map/ppermute | solution.py:469
  86.7 0.7 collective-permute-done.16.refs_1_
  87.4 1.1 collective-permute-done.17.refs_3_.refs_4_
  88.7 1.5 %collective-permute-start.20 = (bf16[512,128]{1,0:T(8,128)(2,1)S(1)}, bf16[512,128]{1,0:T(8,128)(2,1)S(1)}, u32[]{:S(2)}, u32[]{:S(2)}) collective-permute-start(bf16[512,128]{1,0:T(8,128)(2,1)S(1)} %get-tuple-element.79.refs_5_), channel_id=1, source_target_pairs={{0,2},{1,3},{2,0},{3,1},{4,6},{5,7},{6,4},{7,5},{8,10},{9,11},{10,... | collective-permute-start | bytes 393224 | tf_op jit(solution)/shard_map/ppermute | solution.py:472
  90.2 0.6 collective-permute-start.21
  90.8 6.4 %collective-permute-done.23.refs_4_ = bf16[1,432,128]{2,1,0:T(8,128)(2,1)S(1)} collective-permute-done((bf16[1,432,128]{2,1,0:T(8,128)(2,1)S(1)}, bf16[1,432,128]{2,1,0:T(8,128)(2,1)S(1)}, u32[]{:S(2)}, u32[]{:S(2)}) %collective-permute-start.23) | collective-permute-done | bytes 110624 | tf_op jit(solution)/shard_map/ppermute | solution.py:469
  97.5 2.9 %collective-permute-start.27 = (bf16[1,432,128]{2,1,0:T(8,128)(2,1)S(1)}, bf16[1,432,128]{2,1,0:T(8,128)(2,1)S(1)}, u32[]{:S(2)}, u32[]{:S(2)}) collective-permute-start(bf16[1,432,128]{2,1,0:T(8,128)(2,1)S(1)} %sums.19), channel_id=1, source_target_pairs={{0,16},{4,20},{8,24},{12,28},{16,0},{20,4},{24,8},{28,12},{1,17},{... | collective-permute-start | bytes 331784 | tf_op jit(solution)/shard_map/ppermute | solution.py:469
  100.4 0.9 rows.1
  101.3 5.6 %collective-permute-done.27 = bf16[1,432,128]{2,1,0:T(8,128)(2,1)S(1)} collective-permute-done((bf16[1,432,128]{2,1,0:T(8,128)(2,1)S(1)}, bf16[1,432,128]{2,1,0:T(8,128)(2,1)S(1)}, u32[]{:S(2)}, u32[]{:S(2)}) %collective-permute-start.27) | collective-permute-done | bytes 110624 | tf_op jit(solution)/shard_map/ppermute | solution.py:469
  106.9 4.2 %collective-permute-start.28 = (bf16[2,432,128]{2,1,0:T(8,128)(2,1)S(1)}, bf16[2,432,128]{2,1,0:T(8,128)(2,1)S(1)}, u32[]{:S(2)}, u32[]{:S(2)}) collective-permute-start(bf16[2,432,128]{2,1,0:T(8,128)(2,1)S(1)} %pad_maximum_fusion.1.refs_4_), channel_id=1, source_target_pairs={{0,8},{4,12},{8,0},{12,4},{16,24},{20,28},{24,16},{28,20},{1,9},{5... | collective-permute-start | bytes 663560 | tf_op jit(solution)/shard_map/ppermute | solution.py:469
  111.1 0.5 collective-permute-start.26
  111.6 4.6 %collective-permute-done.28.refs_5_ = bf16[2,432,128]{2,1,0:T(8,128)(2,1)S(1)} collective-permute-done((bf16[2,432,128]{2,1,0:T(8,128)(2,1)S(1)}, bf16[2,432,128]{2,1,0:T(8,128)(2,1)S(1)}, u32[]{:S(2)}, u32[]{:S(2)}) %collective-permute-start.28) | collective-permute-done | bytes 221216 | tf_op jit(solution)/shard_map/ppermute | solution.py:469
  116.2 1.5 %collective-permute-done.30.refs_7_ = bf16[2,432,128]{2,1,0:T(8,128)(2,1)S(1)} collective-permute-done((bf16[2,432,128]{2,1,0:T(8,128)(2,1)S(1)}, bf16[2,432,128]{2,1,0:T(8,128)(2,1)S(1)}, u32[]{:S(2)}, u32[]{:S(2)}) %collective-permute-start.30) | collective-permute-done | bytes 221216 | tf_op jit(solution)/shard_map/ppermute | solution.py:466
  117.7 2.2 %unpack.1 = (f32[544,256]{1,0:T(8,128)}, f32[64,2176]{1,0:T(8,128)}, f32[544,1024]{1,0:T(8,128)}, f32[256,1024]{1,0:T(8,128)}, f32[544]{0:T(1024)}, /*index=5*/f32[256]{0:T(256)}, f32[256]{0:T(256)}, f32[256]{0:T(256)}) custom-call(bf16[2,672,128]{2,1,0:T(8,128)(2,1)S(1)} %pad_maximum_fusion.refs_6_.refs_0_, ...), custom_call_target="tpu_custom_call" | custom-call | tf_op jit(solution)/shard_map/unpack/pallas_call | solution.py:700
  (51 shorter events, 2.2 us)
Async XLA Ops:
  12.5 10.8 %collective-permute-start.3 = (bf16[2,4,2,672,128]{4,3,2,1,0:T(8,128)(2,1)}, bf16[2,4,2,672,128]{4,3,2,1,0:T(8,128)(2,1)}, u32[]{:S(2)}, u32[]{:S(2)}) collective-permute-start(bf16[2,4,2,672,128]{4,3,2,1,0:T(8,128)(2,1)} %get-tuple-element.59), channel_id=1, source_target_pairs={{0,4},{4,0},{8,12},{12,8},{16,20},{20,16},{24,28},{28,24},{1,5},{5... | collective-permute-start | bytes 8257544 | tf_op jit(solution)/shard_map/ppermute | solution.py:466
  13.1 10.3 %copy-start = (bf16[2,4,2,672,128]{4,3,2,1,0:T(8,128)(2,1)S(1)}, bf16[2,4,2,672,128]{4,3,2,1,0:T(8,128)(2,1)}, u32[]{:S(2)}) copy-start(bf16[2,4,2,672,128]{4,3,2,1,0:T(8,128)(2,1)} %get-tuple-element.58) | copy-start | bytes 8257540
  23.2 28.3 %collective-permute-start.7 = (bf16[2,4,2,432,128]{4,3,2,1,0:T(8,128)(2,1)}, bf16[2,4,2,432,128]{4,3,2,1,0:T(8,128)(2,1)S(1)}, u32[]{:S(2)}, u32[]{:S(2)}) collective-permute-start(bf16[2,4,2,432,128]{4,3,2,1,0:T(8,128)(2,1)} %get-tuple-element.67), channel_id=1, source_target_pairs={{0,4},{4,0},{8,12},{12,8},{16,20},{20,16},{24,28},{28,24},{1,5},{5... | collective-permute-start | bytes 5308424 | tf_op jit(solution)/shard_map/ppermute | solution.py:466
  23.4 6.5 %copy-start.6 = (bf16[2,2,256,128]{3,2,1,0:T(8,128)(2,1)S(1)}, bf16[2,2,256,128]{3,2,1,0:T(8,128)(2,1)}, u32[]{:S(2)}) copy-start(bf16[2,2,256,128]{3,2,1,0:T(8,128)(2,1)} %get-tuple-element.54) | copy-start | bytes 786436
  23.4 8.1 %copy-start.5 = (bf16[2,2,256,128]{3,2,1,0:T(8,128)(2,1)S(1)}, bf16[2,2,256,128]{3,2,1,0:T(8,128)(2,1)}, u32[]{:S(2)}) copy-start(bf16[2,2,256,128]{3,2,1,0:T(8,128)(2,1)} %get-tuple-element.55) | copy-start | bytes 786436
  25.4 20.1 %collective-permute-start.4 = (bf16[2,2,672,128]{3,2,1,0:T(8,128)(2,1)S(1)}, bf16[2,2,672,128]{3,2,1,0:T(8,128)(2,1)S(1)}, u32[]{:S(2)}, u32[]{:S(2)}) collective-permute-start(bf16[2,2,672,128]{3,2,1,0:T(8,128)(2,1)S(1)} %get-tuple-element.62), channel_id=1, source_target_pairs={{0,2},{1,3},{2,0},{3,1},{4,6},{5,7},{6,4},{7,5},{8,10},{9,11},{10,... | collective-permute-start | bytes 2064392 | tf_op jit(solution)/shard_map/ppermute | solution.py:472
  28.4 17.1 %collective-permute-start.5 = (bf16[2,2,672,128]{3,2,1,0:T(8,128)(2,1)S(1)}, bf16[2,2,672,128]{3,2,1,0:T(8,128)(2,1)S(1)}, u32[]{:S(2)}, u32[]{:S(2)}) collective-permute-start(bf16[2,2,672,128]{3,2,1,0:T(8,128)(2,1)S(1)} %get-tuple-element.64), channel_id=1, source_target_pairs={{0,1},{1,0},{2,3},{3,2},{4,5},{5,4},{6,7},{7,6},{8,9},{9,8},{10,11... | collective-permute-start | bytes 2064392 | tf_op jit(solution)/shard_map/ppermute | solution.py:472
  29.9 13.2 %collective-permute-start = (bf16[2,2,256,128]{3,2,1,0:T(8,128)(2,1)S(1)}, bf16[2,2,256,128]{3,2,1,0:T(8,128)(2,1)S(1)}, u32[]{:S(2)}, u32[]{:S(2)}) collective-permute-start(bf16[2,2,256,128]{3,2,1,0:T(8,128)(2,1)S(1)} %copy-done.6), channel_id=1, source_target_pairs={{0,8},{4,12},{8,0},{12,4},{16,24},{20,28},{24,16},{28,20},{1,9},{5... | collective-permute-start | bytes 786440 | tf_op jit(solution)/shard_map/ppermute | solution.py:469
  31.5 14.0 %collective-permute-start.1 = (bf16[2,2,256,128]{3,2,1,0:T(8,128)(2,1)S(1)}, bf16[2,2,256,128]{3,2,1,0:T(8,128)(2,1)S(1)}, u32[]{:S(2)}, u32[]{:S(2)}) collective-permute-start(bf16[2,2,256,128]{3,2,1,0:T(8,128)(2,1)S(1)} %copy-done.5), channel_id=1, source_target_pairs={{0,16},{4,20},{8,24},{12,28},{16,0},{20,4},{24,8},{28,12},{1,17},{... | collective-permute-start | bytes 786440 | tf_op jit(solution)/shard_map/ppermute | solution.py:469
  45.5 2.4 %copy-start.4 = (bf16[2,2,256,128]{3,2,1,0:T(8,128)(2,1)S(1)}, bf16[2,2,256,128]{3,2,1,0:T(8,128)(2,1)}, u32[]{:S(2)}) copy-start(bf16[2,2,256,128]{3,2,1,0:T(8,128)(2,1)} %get-tuple-element.57) | copy-start | bytes 786436
  45.5 6.0 %copy-start.1 = (bf16[2,4,2,432,128]{4,3,2,1,0:T(8,128)(2,1)S(1)}, bf16[2,4,2,432,128]{4,3,2,1,0:T(8,128)(2,1)}, u32[]{:S(2)}) copy-start(bf16[2,4,2,432,128]{4,3,2,1,0:T(8,128)(2,1)} %get-tuple-element.66) | copy-start | bytes 5308420
  45.8 10.2 %collective-permute-start.6 = (bf16[2,672,128]{2,1,0:T(8,128)(2,1)S(1)}, bf16[2,672,128]{2,1,0:T(8,128)(2,1)S(1)}, u32[]{:S(2)}, u32[]{:S(2)}) collective-permute-start(bf16[2,672,128]{2,1,0:T(8,128)(2,1)S(1)} %get-tuple-element.65.refs_5_), channel_id=1, source_target_pairs={{0,1},{1,0},{2,3},{3,2},{4,5},{5,4},{6,7},{7,6},{8,9},{9,8},{10,11... | collective-permute-start | bytes 1032200 | tf_op jit(solution)/shard_map/ppermute | solution.py:472
  47.4 10.8 %collective-permute-start.8 = (bf16[2,672,128]{2,1,0:T(8,128)(2,1)S(1)}, bf16[2,672,128]{2,1,0:T(8,128)(2,1)S(1)}, u32[]{:S(2)}, u32[]{:S(2)}) collective-permute-start(bf16[2,672,128]{2,1,0:T(8,128)(2,1)S(1)} %get-tuple-element.68.refs_4_), channel_id=1, source_target_pairs={{0,2},{1,3},{2,0},{3,1},{4,6},{5,7},{6,4},{7,5},{8,10},{9,11},{10,... | collective-permute-start | bytes 1032200 | tf_op jit(solution)/shard_map/ppermute | solution.py:472
  47.9 12.3 %collective-permute-start.2 = (bf16[2,2,256,128]{3,2,1,0:T(8,128)(2,1)S(1)}, bf16[2,2,256,128]{3,2,1,0:T(8,128)(2,1)S(1)}, u32[]{:S(2)}, u32[]{:S(2)}) collective-permute-start(bf16[2,2,256,128]{3,2,1,0:T(8,128)(2,1)S(1)} %copy-done.4), channel_id=1, source_target_pairs={{0,24},{4,28},{8,16},{12,20},{16,8},{20,12},{24,0},{28,4},{1,25},{... | collective-permute-start | bytes 786440 | tf_op jit(solution)/shard_map/ppermute | solution.py:469
  52.6 7.6 %copy-start.2 = (bf16[2,2,256,128]{3,2,1,0:T(8,128)(2,1)S(1)}, bf16[2,2,256,128]{3,2,1,0:T(8,128)(2,1)}, u32[]{:S(2)}) copy-start(bf16[2,2,256,128]{3,2,1,0:T(8,128)(2,1)} %get-tuple-element.53.refs_0_.rest_0_) | copy-start | bytes 786436
  52.6 13.9 %collective-permute-start.12 = (bf16[2,2,432,128]{3,2,1,0:T(8,128)(2,1)S(1)}, bf16[2,2,432,128]{3,2,1,0:T(8,128)(2,1)S(1)}, u32[]{:S(2)}, u32[]{:S(2)}) collective-permute-start(bf16[2,2,432,128]{3,2,1,0:T(8,128)(2,1)S(1)} %get-tuple-element.69.refs_3_), channel_id=1, source_target_pairs={{0,1},{1,0},{2,3},{3,2},{4,5},{5,4},{6,7},{7,6},{8,9},{9,8},{10,11... | collective-permute-start | bytes 1327112 | tf_op jit(solution)/shard_map/ppermute | solution.py:472
  53.2 13.3 %collective-permute-start.11 = (bf16[2,2,432,128]{3,2,1,0:T(8,128)(2,1)S(1)}, bf16[2,2,432,128]{3,2,1,0:T(8,128)(2,1)S(1)}, u32[]{:S(2)}, u32[]{:S(2)}) collective-permute-start(bf16[2,2,432,128]{3,2,1,0:T(8,128)(2,1)S(1)} %get-tuple-element.70.refs_4_), channel_id=1, source_target_pairs={{0,2},{1,3},{2,0},{3,1},{4,6},{5,7},{6,4},{7,5},{8,10},{9,11},{10,... | collective-permute-start | bytes 1327112 | tf_op jit(solution)/shard_map/ppermute | solution.py:472
  58.4 7.9 %collective-permute-start.13 = (bf16[2,672,128]{2,1,0:T(8,128)(2,1)S(1)}, bf16[2,672,128]{2,1,0:T(8,128)(2,1)S(1)}, u32[]{:S(2)}, u32[]{:S(2)}) collective-permute-start(bf16[2,672,128]{2,1,0:T(8,128)(2,1)S(1)} %sums.11.refs_4_), channel_id=1, source_target_pairs={{0,8},{4,12},{8,0},{12,4},{16,24},{20,28},{24,16},{28,20},{1,9},{5... | collective-permute-start | bytes 1032200 | tf_op jit(solution)/shard_map/ppermute | solution.py:469
  60.3 1.7 %collective-permute-start.10 = (bf16[2,2,256,128]{3,2,1,0:T(8,128)(2,1)S(1)}, bf16[2,2,256,128]{3,2,1,0:T(8,128)(2,1)S(1)}, u32[]{:S(2)}, u32[]{:S(2)}) collective-permute-start(bf16[2,2,256,128]{3,2,1,0:T(8,128)(2,1)S(1)} %get-tuple-element.72), channel_id=1, source_target_pairs={{0,4},{4,0},{8,12},{12,8},{16,20},{20,16},{24,28},{28,24},{1,5},{5... | collective-permute-start | bytes 786440 | tf_op jit(solution)/shard_map/ppermute | solution.py:466
  60.4 1.9 %copy-start.3 = (s32[2,8192,4]{1,2,0:T(4,128)S(1)}, s32[2,8192,4]{1,2,0:T(4,128)}, u32[]{:S(2)}) copy-start(s32[2,8192,4]{1,2,0:T(4,128)} %param.23) | copy-start | bytes 786436
  60.4 1.9 %collective-permute-start.9 = (bf16[2,2,256,128]{3,2,1,0:T(8,128)(2,1)S(1)}, bf16[2,2,256,128]{3,2,1,0:T(8,128)(2,1)S(1)}, u32[]{:S(2)}, u32[]{:S(2)}) collective-permute-start(bf16[2,2,256,128]{3,2,1,0:T(8,128)(2,1)S(1)} %get-tuple-element.71.rest_6_), channel_id=1, source_target_pairs={{0,4},{4,0},{8,12},{12,8},{16,20},{20,16},{24,28},{28,24},{1,5},{5... | collective-permute-start | bytes 786440 | tf_op jit(solution)/shard_map/ppermute | solution.py:466
  66.7 7.5 %collective-permute-start.14 = (bf16[2,432,128]{2,1,0:T(8,128)(2,1)S(1)}, bf16[2,432,128]{2,1,0:T(8,128)(2,1)S(1)}, u32[]{:S(2)}, u32[]{:S(2)}) collective-permute-start(bf16[2,432,128]{2,1,0:T(8,128)(2,1)S(1)} %get-tuple-element.75.refs_4_), channel_id=1, source_target_pairs={{0,1},{1,0},{2,3},{3,2},{4,5},{5,4},{6,7},{7,6},{8,9},{9,8},{10,11... | collective-permute-start | bytes 663560 | tf_op jit(solution)/shard_map/ppermute | solution.py:472
  67.3 7.2 %collective-permute-start.15 = (bf16[2,432,128]{2,1,0:T(8,128)(2,1)S(1)}, bf16[2,432,128]{2,1,0:T(8,128)(2,1)S(1)}, u32[]{:S(2)}, u32[]{:S(2)}) collective-permute-start(bf16[2,432,128]{2,1,0:T(8,128)(2,1)S(1)} %get-tuple-element.76.refs_3_), channel_id=1, source_target_pairs={{0,2},{1,3},{2,0},{3,1},{4,6},{5,7},{6,4},{7,5},{8,10},{9,11},{10,... | collective-permute-start | bytes 663560 | tf_op jit(solution)/shard_map/ppermute | solution.py:472
  67.8 15.6 %collective-permute-start.19 = (bf16[1,672,128]{2,1,0:T(8,128)(2,1)S(1)}, bf16[1,672,128]{2,1,0:T(8,128)(2,1)S(1)}, u32[]{:S(2)}, u32[]{:S(2)}) collective-permute-start(bf16[1,672,128]{2,1,0:T(8,128)(2,1)S(1)} %sums.12.refs_4_), channel_id=1, source_target_pairs={{0,16},{4,20},{8,24},{12,28},{16,0},{20,4},{24,8},{28,12},{1,17},{... | collective-permute-start | bytes 516104 | tf_op jit(solution)/shard_map/ppermute | solution.py:469
  74.6 10.0 %collective-permute-start.18 = (bf16[2,432,128]{2,1,0:T(8,128)(2,1)S(1)}, bf16[2,432,128]{2,1,0:T(8,128)(2,1)S(1)}, u32[]{:S(2)}, u32[]{:S(2)}) collective-permute-start(bf16[2,432,128]{2,1,0:T(8,128)(2,1)S(1)} %sums.14.rest_6_), channel_id=1, source_target_pairs={{0,8},{4,12},{8,0},{12,4},{16,24},{20,28},{24,16},{28,20},{1,9},{5... | collective-permute-start | bytes 663560 | tf_op jit(solution)/shard_map/ppermute | solution.py:469
  80.4 7.1 %collective-permute-start.16 = (bf16[2,512,128]{2,1,0:T(8,128)(2,1)S(1)}, bf16[2,512,128]{2,1,0:T(8,128)(2,1)S(1)}, u32[]{:S(2)}, u32[]{:S(2)}) collective-permute-start(bf16[2,512,128]{2,1,0:T(8,128)(2,1)S(1)} %get-tuple-element.77.refs_5_), channel_id=1, source_target_pairs={{0,1},{1,0},{2,3},{3,2},{4,5},{5,4},{6,7},{7,6},{8,9},{9,8},{10,11... | collective-permute-start | bytes 786440 | tf_op jit(solution)/shard_map/ppermute | solution.py:472
  81.9 6.6 %collective-permute-start.17 = (bf16[2,512,128]{2,1,0:T(8,128)(2,1)S(1)}, bf16[2,512,128]{2,1,0:T(8,128)(2,1)S(1)}, u32[]{:S(2)}, u32[]{:S(2)}) collective-permute-start(bf16[2,512,128]{2,1,0:T(8,128)(2,1)S(1)} %get-tuple-element.78.refs_6_), channel_id=1, source_target_pairs={{0,2},{1,3},{2,0},{3,1},{4,6},{5,7},{6,4},{7,5},{8,10},{9,11},{10,... | collective-permute-start | bytes 786440 | tf_op jit(solution)/shard_map/ppermute | solution.py:472
  83.6 13.8 %collective-permute-start.22 = (bf16[1,672,128]{2,1,0:T(8,128)(2,1)S(1)}, bf16[1,672,128]{2,1,0:T(8,128)(2,1)S(1)}, u32[]{:S(2)}, u32[]{:S(2)}) collective-permute-start(bf16[1,672,128]{2,1,0:T(8,128)(2,1)S(1)} %sums.16.refs_4_), channel_id=1, source_target_pairs={{0,16},{4,20},{8,24},{12,28},{16,0},{20,4},{24,8},{28,12},{1,17},{... | collective-permute-start | bytes 516104 | tf_op jit(solution)/shard_map/ppermute | solution.py:469
  84.8 12.4 %collective-permute-start.23 = (bf16[1,432,128]{2,1,0:T(8,128)(2,1)S(1)}, bf16[1,432,128]{2,1,0:T(8,128)(2,1)S(1)}, u32[]{:S(2)}, u32[]{:S(2)}) collective-permute-start(bf16[1,432,128]{2,1,0:T(8,128)(2,1)S(1)} %sums.17.refs_4_), channel_id=1, source_target_pairs={{0,16},{4,20},{8,24},{12,28},{16,0},{20,4},{24,8},{28,12},{1,17},{... | collective-permute-start | bytes 331784 | tf_op jit(solution)/shard_map/ppermute | solution.py:469
  88.7 11.7 %collective-permute-start.20 = (bf16[512,128]{1,0:T(8,128)(2,1)S(1)}, bf16[512,128]{1,0:T(8,128)(2,1)S(1)}, u32[]{:S(2)}, u32[]{:S(2)}) collective-permute-start(bf16[512,128]{1,0:T(8,128)(2,1)S(1)} %get-tuple-element.79.refs_5_), channel_id=1, source_target_pairs={{0,2},{1,3},{2,0},{3,1},{4,6},{5,7},{6,4},{7,5},{8,10},{9,11},{10,... | collective-permute-start | bytes 393224 | tf_op jit(solution)/shard_map/ppermute | solution.py:472
  90.2 10.2 %collective-permute-start.21 = (bf16[512,128]{1,0:T(8,128)(2,1)S(1)}, bf16[512,128]{1,0:T(8,128)(2,1)S(1)}, u32[]{:S(2)}, u32[]{:S(2)}) collective-permute-start(bf16[512,128]{1,0:T(8,128)(2,1)S(1)} %get-tuple-element.80.refs_6_), channel_id=1, source_target_pairs={{0,1},{1,0},{2,3},{3,2},{4,5},{5,4},{6,7},{7,6},{8,9},{9,8},{10,11... | collective-permute-start | bytes 393224 | tf_op jit(solution)/shard_map/ppermute | solution.py:472
  97.4 13.7 %collective-permute-start.24 = (bf16[2,672,128]{2,1,0:T(8,128)(2,1)S(1)}, bf16[2,672,128]{2,1,0:T(8,128)(2,1)S(1)}, u32[]{:S(2)}, u32[]{:S(2)}) collective-permute-start(bf16[2,672,128]{2,1,0:T(8,128)(2,1)S(1)} %pad_maximum_fusion.refs_6_.refs_0_), channel_id=1, source_target_pairs={{0,8},{4,12},{8,0},{12,4},{16,24},{20,28},{24,16},{28,20},{1,9},{5... | collective-permute-start | bytes 1032200 | tf_op jit(solution)/shard_map/ppermute | solution.py:469
  97.5 9.4 %collective-permute-start.27 = (bf16[1,432,128]{2,1,0:T(8,128)(2,1)S(1)}, bf16[1,432,128]{2,1,0:T(8,128)(2,1)S(1)}, u32[]{:S(2)}, u32[]{:S(2)}) collective-permute-start(bf16[1,432,128]{2,1,0:T(8,128)(2,1)S(1)} %sums.19), channel_id=1, source_target_pairs={{0,16},{4,20},{8,24},{12,28},{16,0},{20,4},{24,8},{28,12},{1,17},{... | collective-permute-start | bytes 331784 | tf_op jit(solution)/shard_map/ppermute | solution.py:469
  106.9 9.3 %collective-permute-start.28 = (bf16[2,432,128]{2,1,0:T(8,128)(2,1)S(1)}, bf16[2,432,128]{2,1,0:T(8,128)(2,1)S(1)}, u32[]{:S(2)}, u32[]{:S(2)}) collective-permute-start(bf16[2,432,128]{2,1,0:T(8,128)(2,1)S(1)} %pad_maximum_fusion.1.refs_4_), channel_id=1, source_target_pairs={{0,8},{4,12},{8,0},{12,4},{16,24},{20,28},{24,16},{28,20},{1,9},{5... | collective-permute-start | bytes 663560 | tf_op jit(solution)/shard_map/ppermute | solution.py:469
  111.1 5.1 %collective-permute-start.25 = (bf16[2,672,128]{2,1,0:T(8,128)(2,1)S(1)}, bf16[2,672,128]{2,1,0:T(8,128)(2,1)S(1)}, u32[]{:S(2)}, u32[]{:S(2)}) collective-permute-start(bf16[2,672,128]{2,1,0:T(8,128)(2,1)S(1)} %pad_maximum_fusion.refs_6_.refs_0_), channel_id=1, source_target_pairs={{0,4},{4,0},{8,12},{12,8},{16,20},{20,16},{24,28},{28,24},{1,5},{5... | collective-permute-start | bytes 1032200 | tf_op jit(solution)/shard_map/ppermute | solution.py:466
  111.1 6.6 %collective-permute-start.26 = (bf16[2,672,128]{2,1,0:T(8,128)(2,1)S(1)}, bf16[2,672,128]{2,1,0:T(8,128)(2,1)S(1)}, u32[]{:S(2)}, u32[]{:S(2)}) collective-permute-start(bf16[2,672,128]{2,1,0:T(8,128)(2,1)S(1)} %collective-permute-done.24.refs_1_), channel_id=1, source_target_pairs={{0,4},{4,0},{8,12},{12,8},{16,20},{20,16},{24,28},{28,24},{1,5},{5... | collective-permute-start | bytes 1032200 | tf_op jit(solution)/shard_map/ppermute | solution.py:466
  111.6 4.6 %collective-permute-start.29 = (bf16[2,432,128]{2,1,0:T(8,128)(2,1)S(1)}, bf16[2,432,128]{2,1,0:T(8,128)(2,1)S(1)}, u32[]{:S(2)}, u32[]{:S(2)}) collective-permute-start(bf16[2,432,128]{2,1,0:T(8,128)(2,1)S(1)} %pad_maximum_fusion.1.refs_4_), channel_id=1, source_target_pairs={{0,4},{4,0},{8,12},{12,8},{16,20},{20,16},{24,28},{28,24},{1,5},{5... | collective-permute-start | bytes 663560 | tf_op jit(solution)/shard_map/ppermute | solution.py:466
  116.2 1.5 %collective-permute-start.30 = (bf16[2,432,128]{2,1,0:T(8,128)(2,1)S(1)}, bf16[2,432,128]{2,1,0:T(8,128)(2,1)S(1)}, u32[]{:S(2)}, u32[]{:S(2)}) collective-permute-start(bf16[2,432,128]{2,1,0:T(8,128)(2,1)S(1)} %collective-permute-done.28.refs_5_), channel_id=1, source_target_pairs={{0,4},{4,0},{8,12},{12,8},{16,20},{20,16},{24,28},{28,24},{1,5},{5... | collective-permute-start | bytes 663560 | tf_op jit(solution)/shard_map/ppermute | solution.py:466

commit v12 on v9

--- a/solution.py
+++ b/solution.py
@@ -236,9 +236,21 @@
 
 def unpack_kernel(*refs):
     parts = refs[0:8]
-    g_down, g_up, g_first, g_second = refs[8:12]
+    outs = refs[8:12]
     small_outs = refs[12:16]
     held, small = refs[16:18], refs[18]
+    g_down, g_up, g_first, g_second = made = refs[19:23]
+    sems = refs[23]
+    copies = []
+
+    def send(which, columns):
+        span = (slice(None), pl.ds(columns.start * LANES, len(columns) * LANES))
+        copy = pltpu.make_async_copy(
+            made[which].at[span], outs[which].at[span], sems.at[len(copies)]
+        )
+        copy.start()
+        copies.append(copy)
+
     core, row_pos, table_pos = position()
     z_pos = lax.div(table_pos, 2)
     for stream in range(2):
@@ -263,17 +275,28 @@
             offset += step
         return offset
 
+    blocks = g_first.shape[1] // LANES // 2
+    early = blocks - blocks // 4
     for half in range(2):
-        blocks = g_second.shape[1] // LANES // 2
-        offset = take(front, g_second, half, 0, range(half * blocks, (half + 1) * blocks))
-        blocks = g_first.shape[1] // LANES // 2
-        early = blocks - blocks // 4
-        take(front, g_first, half, offset, range(half * blocks, half * blocks + early))
-        offset = take(back, g_first, half, 0, range(half * blocks + early, (half + 1) * blocks))
-        blocks = g_down.shape[1] // LANES // 2
-        offset = take(back, g_down, half, offset, range(half * blocks, (half + 1) * blocks))
-        blocks = g_up.shape[1] // LANES
-        offset = take(back, g_up, half, offset, range(half * (blocks - 9), half * (blocks - 9) + 9))
+        count = g_second.shape[1] // LANES // 2
+        columns = range(half * count, (half + 1) * count)
+        offset = take(front, g_second, half, 0, columns)
+        send(3, columns)
+        columns = range(half * blocks, half * blocks + early)
+        take(front, g_first, half, offset, columns)
+        send(2, columns)
+    for half in range(2):
+        columns = range(half * blocks + early, (half + 1) * blocks)
+        offset = take(back, g_first, half, 0, columns)
+        send(2, columns)
+        count = g_down.shape[1] // LANES // 2
+        columns = range(half * count, (half + 1) * count)
+        offset = take(back, g_down, half, offset, columns)
+        send(0, columns)
+        count = g_up.shape[1] // LANES
+        columns = range(half * (count - 9), half * (count - 9) + 9)
+        offset = take(back, g_up, half, offset, columns)
+    send(1, range(g_up.shape[1] // LANES))
     small[0:48, :] = back[0, offset : offset + 48, :].astype(f32)
     small[48:, :] = jnp.zeros((small.shape[0] - 48, LANES), f32)
     for out, first in zip(small_outs, (24, 0, 8, 16)):
@@ -288,6 +311,8 @@
             both = jnp.where(lanes < lane, later, this)
             turned = pltpu.roll(both, lax.rem(LANES - lane, LANES), 1)
             out[start : start + length] = turned.reshape(LANES)[:length]
+    for copy in copies:
+        copy.wait()
 
 
 def whole(memory=pltpu.VMEM):
@@ -697,21 +722,20 @@
     row_grads = sum_rows([share.items for share in shares], last)
     two.z_back([row_grads])
 
-    g_down, g_up, g_first, g_second, g_cbias, g_bias1, g_bias2, g_logit = call(
+    shapes = [(feat // n_row, rank), (rank // n_row, feat), (feat // n_row, hid), (hid // n_row, hid)]
+    shapes += [(feat // n_row,)] + [(hid // n_row,)] * 3
+    g_down, g_up, g_first, g_second, g_cbias, g_bias1, g_bias2, g_logit = pl.pallas_call(
         unpack_kernel,
-        [
-            jax.ShapeDtypeStruct((feat // n_row, rank), f32),
-            jax.ShapeDtypeStruct((rank // n_row, feat), f32),
-            jax.ShapeDtypeStruct((feat // n_row, hid), f32),
-            jax.ShapeDtypeStruct((hid // n_row, hid), f32),
-            jax.ShapeDtypeStruct((feat // n_row,), f32),
-        ]
-        + [jax.ShapeDtypeStruct((hid // n_row,), f32)] * 3,
-        [pltpu.VMEM((2, rows, LANES), bf16) for rows in (rows_front, rows_back)]
-        + [pltpu.VMEM((56, LANES), f32)],
-        [vmem] * 8,
-        "unpack",
-        24,
+        out_shape=[jax.ShapeDtypeStruct(shape, f32) for shape in shapes],
+        in_specs=[vmem] * 8,
+        out_specs=[hbm] * 4 + [vmem] * 4,
+        scratch_shapes=[pltpu.VMEM((2, rows, LANES), bf16) for rows in (rows_front, rows_back)]
+        + [pltpu.VMEM((56, LANES), f32)]
+        + [pltpu.VMEM(shape, f32) for shape in shapes[:4]]
+        + [pltpu.SemaphoreType.DMA((9,))],
+        compiler_params=pltpu.CompilerParams(vmem_limit_bytes=24 * MIB),
+        cost_estimate=no_cost(),
+        name="unpack",
     )(*one.pieces, *two.pieces)
     return (row_grads, g_down, g_up, g_cbias, g_first, g_bias1, g_second, g_bias2, g_logit)
 

time: 119 us -> 119 us (level)
  no operation moved by 1% of the time
where the time goes in v12:
time: 119 us
  Pallas kernels  41.7 us (35%)
  starting transfers between devices  41.7 us (35%)
  waiting for transfers between devices  34.7 us (29%)
    ppermute x11, waiting for transfers between devices, swap_z(): lax.ppermute(value, 'table', [(at, at ^ 2 * which) for at in range(n_tabl...  26.3 us
    ppermute x11, starting transfers between devices, swap_z(): lax.ppermute(value, 'table', [(at, at ^ 2 * which) for at in range(n_tabl...  24.2 us
    ppermute x12, starting transfers between devices, swap_row(): lax.ppermute(value, 'row', [(at, at ^ 1 << bit) for at in range(n_row)])  15.8 us
    pallas_call x1, Pallas kernels, local(): call(front_kernel, [packed(rows_front)] * 2 + [wide(feat, batch), wide(ba...  11.9 us
    pallas_call x1, Pallas kernels, local(): call(functools.partial(middle_kernel, n_z), [packed(rows_back)] * 2 + [wi...  10.1 us
    pallas_call x2, Pallas kernels, local(): pl.pallas_call(functools.partial(count_kernel, n_row, table, hot, n_z), o...  8.04 us
    ppermute x12, waiting for transfers between devices, swap_row(): lax.ppermute(value, 'row', [(at, at ^ 1 << bit) for at in range(n_row)])  6.89 us
    pallas_call x4, Pallas kernels, fetch_sums(): call(functools.partial(fetch_sum_kernel, plan, n_in), shapes, scratch + [...  6 us
  transfers between devices with their start and end apart: 31, of which 13 were waited for; matrix products, arithmetic and copies ran while one was open for 0% of the time, Pallas kernels for 23%

profile of v12, /device:TPU:0, one launch (start us, length us, event | category | flops | bytes accessed | tf_op | source)
XLA Modules:
  0.0 119.3 jit_solution(748876620963323743)
XLA Ops:
  0.6 11.9 %front.1 = (bf16[2,4,2,672,128]{4,3,2,1,0:T(8,128)(2,1)}, bf16[2,4,2,672,128]{4,3,2,1,0:T(8,128)(2,1)}, bf16[2176,256]{1,0:T(8,128)(2,1)}, bf16[256,1024]{1,0:T(8,128)(2,1)}, f32[24,128]{1,0:T(8,128)}) custom-call(bf16[256,128]{1,0:T(8,128)(2,1)} %refs_0_.3, bf16[256,2048]{1,0:T(8,128)(2,1)} %refs_1_.3, bf16[2176,256]{1,0:T(8,128)(2,1)} %refs_2_.3, ...), custom_call_target="tpu_custom_call" | custom-call | tf_op jit(solution)/shard_map/front/pallas_call | solution.py:529
  12.5 0.5 collective-permute-start.3
  13.1 10.1 %middle.1 = (bf16[2,4,2,432,128]{4,3,2,1,0:T(8,128)(2,1)}, bf16[2,4,2,432,128]{4,3,2,1,0:T(8,128)(2,1)}, bf16[2,2,256,128]{3,2,1,0:T(8,128)(2,1)}, bf16[2,2,256,...) custom-call(bf16[256,128]{1,0:T(8,128)(2,1)} %refs_0_.3, ...), custom_call_target="tpu_custom_call" | custom-call | tf_op jit(solution)/shard_map/middle/pallas_call | solution.py:556
  23.4 2.0 %first_sums.5 = (bf16[2,2,672,128]{3,2,1,0:T(8,128)(2,1)S(1)}, bf16[2,2,672,128]{3,2,1,0:T(8,128)(2,1)S(1)}) custom-call(bf16[2,2,2,2,672,128]{5,4,3,2,1,0:T(8,128)(2,1)S(1)} %bitcast.7, bf16[2,2,2,2,672,128]{5,4,3,2,1,0:T(8,128)(2,1)} %bitcast.2.refs_1_.refs_3_, bf16[2,2,2,2,672,128]{5,4,3,2,1,0:T(8,128)(2,1)S(1)} %bitcast.8, ...), custom_call_target="tpu_custom_call" | custom-call | tf_op jit(solution)/shard_map/first_sums/pallas_call | solution.py:433
  25.4 3.0 %collective-permute-start.4 = (bf16[2,2,672,128]{3,2,1,0:T(8,128)(2,1)S(1)}, bf16[2,2,672,128]{3,2,1,0:T(8,128)(2,1)S(1)}, u32[]{:S(2)}, u32[]{:S(2)}) collective-permute-start(bf16[2,2,672,128]{3,2,1,0:T(8,128)(2,1)S(1)} %get-tuple-element.62), channel_id=1, source_target_pairs={{0,2},{1,3},{2,0},{3,1},{4,6},{5,7},{6,4},{7,5},{8,10},{9,11},{10,... | collective-permute-start | bytes 2064392 | tf_op jit(solution)/shard_map/ppermute | solution.py:497
  28.4 1.5 %collective-permute-start.5 = (bf16[2,2,672,128]{3,2,1,0:T(8,128)(2,1)S(1)}, bf16[2,2,672,128]{3,2,1,0:T(8,128)(2,1)S(1)}, u32[]{:S(2)}, u32[]{:S(2)}) collective-permute-start(bf16[2,2,672,128]{3,2,1,0:T(8,128)(2,1)S(1)} %get-tuple-element.64), channel_id=1, source_target_pairs={{0,1},{1,0},{2,3},{3,2},{4,5},{5,4},{6,7},{7,6},{8,9},{9,8},{10,11... | collective-permute-start | bytes 2064392 | tf_op jit(solution)/shard_map/ppermute | solution.py:497
  29.9 1.6 %collective-permute-start = (bf16[2,2,256,128]{3,2,1,0:T(8,128)(2,1)S(1)}, bf16[2,2,256,128]{3,2,1,0:T(8,128)(2,1)S(1)}, u32[]{:S(2)}, u32[]{:S(2)}) collective-permute-start(bf16[2,2,256,128]{3,2,1,0:T(8,128)(2,1)S(1)} %copy-done.6), channel_id=1, source_target_pairs={{0,8},{4,12},{8,0},{12,4},{16,24},{20,28},{24,16},{28,20},{1,9},{5... | collective-permute-start | bytes 786440 | tf_op jit(solution)/shard_map/ppermute | solution.py:494
  31.5 2.6 %collective-permute-start.1 = (bf16[2,2,256,128]{3,2,1,0:T(8,128)(2,1)S(1)}, bf16[2,2,256,128]{3,2,1,0:T(8,128)(2,1)S(1)}, u32[]{:S(2)}, u32[]{:S(2)}) collective-permute-start(bf16[2,2,256,128]{3,2,1,0:T(8,128)(2,1)S(1)} %copy-done.5), channel_id=1, source_target_pairs={{0,16},{4,20},{8,24},{12,28},{16,0},{20,4},{24,8},{28,12},{1,17},{... | collective-permute-start | bytes 786440 | tf_op jit(solution)/shard_map/ppermute | solution.py:494
  34.1 9.0 %collective-permute-done.refs_4_.refs_1_.rest_1_ = bf16[2,2,256,128]{3,2,1,0:T(8,128)(2,1)S(1)} collective-permute-done((bf16[2,2,256,128]{3,2,1,0:T(8,128)(2,1)S(1)}, bf16[2,2,256,128]{3,2,1,0:T(8,128)(2,1)S(1)}, u32[]{:S(2)}, u32[]{:S(2)}) %collective-permute-start) | collective-permute-done | bytes 262176 | tf_op jit(solution)/shard_map/ppermute | solution.py:494
  43.1 1.8 %first_sums.4 = (bf16[2,2,672,128]{3,2,1,0:T(8,128)(2,1)S(1)}, bf16[2,2,672,128]{3,2,1,0:T(8,128)(2,1)S(1)}) custom-call(bf16[2,2,2,2,672,128]{5,4,3,2,1,0:T(8,128)(2,1)S(1)} %bitcast.9, bf16[2,2,2,2,672,128]{5,4,3,2,1,0:T(8,128)(2,1)} %bitcast.2.refs_1_.refs_3_, bf16[2,2,2,2,672,128]{5,4,3,2,1,0:T(8,128)(2,1)S(1)} %bitcast.10, ...), custom_call_target="tpu_custom_call" | custom-call | tf_op jit(solution)/shard_map/first_sums/pallas_call | solution.py:433
  44.9 0.6 collective-permute-done.1.refs_5_.refs_2_.rest_2_
  45.5 0.3 sums.10
  45.8 1.6 %collective-permute-start.6 = (bf16[2,672,128]{2,1,0:T(8,128)(2,1)S(1)}, bf16[2,672,128]{2,1,0:T(8,128)(2,1)S(1)}, u32[]{:S(2)}, u32[]{:S(2)}) collective-permute-start(bf16[2,672,128]{2,1,0:T(8,128)(2,1)S(1)} %get-tuple-element.65.refs_5_), channel_id=1, source_target_pairs={{0,1},{1,0},{2,3},{3,2},{4,5},{5,4},{6,7},{7,6},{8,9},{9,8},{10,11... | collective-permute-start | bytes 1032200 | tf_op jit(solution)/shard_map/ppermute | solution.py:497
  47.4 0.5 collective-permute-start.8
  47.9 3.6 %collective-permute-start.2 = (bf16[2,2,256,128]{3,2,1,0:T(8,128)(2,1)S(1)}, bf16[2,2,256,128]{3,2,1,0:T(8,128)(2,1)S(1)}, u32[]{:S(2)}, u32[]{:S(2)}) collective-permute-start(bf16[2,2,256,128]{3,2,1,0:T(8,128)(2,1)S(1)} %copy-done.4), channel_id=1, source_target_pairs={{0,24},{4,28},{8,16},{12,20},{16,8},{20,12},{24,0},{28,4},{1,25},{... | collective-permute-start | bytes 786440 | tf_op jit(solution)/shard_map/ppermute | solution.py:494
  51.5 1.1 first_sums.6
  52.6 0.6 collective-permute-start.12
  53.2 1.5 %collective-permute-start.11 = (bf16[2,2,432,128]{3,2,1,0:T(8,128)(2,1)S(1)}, bf16[2,2,432,128]{3,2,1,0:T(8,128)(2,1)S(1)}, u32[]{:S(2)}, u32[]{:S(2)}) collective-permute-start(bf16[2,2,432,128]{3,2,1,0:T(8,128)(2,1)S(1)} %get-tuple-element.70.refs_4_), channel_id=1, source_target_pairs={{0,2},{1,3},{2,0},{3,1},{4,6},{5,7},{6,4},{7,5},{8,10},{9,11},{10,... | collective-permute-start | bytes 1327112 | tf_op jit(solution)/shard_map/ppermute | solution.py:497
  54.7 1.2 %collective-permute-done.6.refs_2_ = bf16[2,672,128]{2,1,0:T(8,128)(2,1)S(1)} collective-permute-done((bf16[2,672,128]{2,1,0:T(8,128)(2,1)S(1)}, bf16[2,672,128]{2,1,0:T(8,128)(2,1)S(1)}, u32[]{:S(2)}, u32[]{:S(2)}) %collective-permute-start.6) | collective-permute-done | bytes 344096 | tf_op jit(solution)/shard_map/ppermute | solution.py:497
  56.0 2.2 %collective-permute-done.8.refs_5_.refs_2_ = bf16[2,672,128]{2,1,0:T(8,128)(2,1)S(1)} collective-permute-done((bf16[2,672,128]{2,1,0:T(8,128)(2,1)S(1)}, bf16[2,672,128]{2,1,0:T(8,128)(2,1)S(1)}, u32[]{:S(2)}, u32[]{:S(2)}) %collective-permute-start.8) | collective-permute-done | bytes 344096 | tf_op jit(solution)/shard_map/ppermute | solution.py:497
  58.5 0.5 collective-permute-start.9
  59.0 3.3 %collective-permute-start.14 = (bf16[2,672,128]{2,1,0:T(8,128)(2,1)S(1)}, bf16[2,672,128]{2,1,0:T(8,128)(2,1)S(1)}, u32[]{:S(2)}, u32[]{:S(2)}) collective-permute-start(bf16[2,672,128]{2,1,0:T(8,128)(2,1)S(1)} %sums.11.refs_4_), channel_id=1, source_target_pairs={{0,8},{4,12},{8,0},{12,4},{16,24},{20,28},{24,16},{28,20},{1,9},{5... | collective-permute-start | bytes 1032200 | tf_op jit(solution)/shard_map/ppermute | solution.py:494
  62.3 1.1 first_sums.7
  63.5 4.0 %counts.2.refs_4_ = bf16[4,512,128]{2,1,0:T(8,128)(2,1)S(1)} custom-call(s32[2,4,8192]{2,1,0:T(4,128)S(1)} %bitcast.25, bf16[2,2,256,128]{3,2,1,0:T(8,128)(2,1)S(1)} %copy-done.2, bf16[2,2,256,128]{3,2,1,0:T(8,128)(2,1)S(1)} %collective-permute-done.refs_4_.refs_1_.rest_1_, bf16[2,2,256,128]{3,2,1,0:T(8,128)(2,1)S(1)} %collective-permute-done.1.refs_5_.refs_2_.rest_2_, ...), custom_call_target="tpu_custom_call" | custom-call | tf_op jit(solution)/shard_map/counts/pallas_call | solution.py:696
  67.7 0.6 collective-permute-start.13
  68.3 1.4 %collective-permute-start.15 = (bf16[2,432,128]{2,1,0:T(8,128)(2,1)S(1)}, bf16[2,432,128]{2,1,0:T(8,128)(2,1)S(1)}, u32[]{:S(2)}, u32[]{:S(2)}) collective-permute-start(bf16[2,432,128]{2,1,0:T(8,128)(2,1)S(1)} %get-tuple-element.76.refs_4_), channel_id=1, source_target_pairs={{0,2},{1,3},{2,0},{3,1},{4,6},{5,7},{6,4},{7,5},{8,10},{9,11},{10,... | collective-permute-start | bytes 663560 | tf_op jit(solution)/shard_map/ppermute | solution.py:497
  69.8 0.9 collective-permute-done.14.refs_3_.refs_6_
  70.8 2.8 %collective-permute-start.19 = (bf16[1,672,128]{2,1,0:T(8,128)(2,1)S(1)}, bf16[1,672,128]{2,1,0:T(8,128)(2,1)S(1)}, u32[]{:S(2)}, u32[]{:S(2)}) collective-permute-start(bf16[1,672,128]{2,1,0:T(8,128)(2,1)S(1)} %sums.13.refs_3_), channel_id=1, source_target_pairs={{0,16},{4,20},{8,24},{12,28},{16,0},{20,4},{24,8},{28,12},{1,17},{... | collective-permute-start | bytes 516104 | tf_op jit(solution)/shard_map/ppermute | solution.py:494
  73.6 1.3 %collective-permute-done.13.refs_2_ = bf16[2,432,128]{2,1,0:T(8,128)(2,1)S(1)} collective-permute-done((bf16[2,432,128]{2,1,0:T(8,128)(2,1)S(1)}, bf16[2,432,128]{2,1,0:T(8,128)(2,1)S(1)}, u32[]{:S(2)}, u32[]{:S(2)}) %collective-permute-start.13) | collective-permute-done | bytes 221216 | tf_op jit(solution)/shard_map/ppermute | solution.py:497
  75.3 0.6 collective-permute-start.18
  76.0 4.0 %counts.3.refs_2_ = bf16[4,512,128]{2,1,0:T(8,128)(2,1)S(1)} custom-call(s32[2,4,8192]{2,1,0:T(4,128)S(1)} %bitcast.26, bf16[2,2,256,128]{3,2,1,0:T(8,128)(2,1)S(1)} %copy-done.2, bf16[2,2,256,128]{3,2,1,0:T(8,128)(2,1)S(1)} %collective-permute-done.refs_4_.refs_1_.rest_1_, bf16[2,2,256,128]{3,2,1,0:T(8,128)(2,1)S(1)} %collective-permute-done.1.refs_5_.refs_2_.rest_2_, ...), custom_call_target="tpu_custom_call" | custom-call | tf_op jit(solution)/shard_map/counts/pallas_call | solution.py:696
  80.2 1.6 %collective-permute-start.16 = (bf16[2,512,128]{2,1,0:T(8,128)(2,1)S(1)}, bf16[2,512,128]{2,1,0:T(8,128)(2,1)S(1)}, u32[]{:S(2)}, u32[]{:S(2)}) collective-permute-start(bf16[2,512,128]{2,1,0:T(8,128)(2,1)S(1)} %get-tuple-element.77.refs_5_), channel_id=1, source_target_pairs={{0,1},{1,0},{2,3},{3,2},{4,5},{5,4},{6,7},{7,6},{8,9},{9,8},{10,11... | collective-permute-start | bytes 786440 | tf_op jit(solution)/shard_map/ppermute | solution.py:497
  81.8 1.4 %collective-permute-start.17 = (bf16[2,512,128]{2,1,0:T(8,128)(2,1)S(1)}, bf16[2,512,128]{2,1,0:T(8,128)(2,1)S(1)}, u32[]{:S(2)}, u32[]{:S(2)}) collective-permute-start(bf16[2,512,128]{2,1,0:T(8,128)(2,1)S(1)} %get-tuple-element.78.refs_6_), channel_id=1, source_target_pairs={{0,2},{1,3},{2,0},{3,1},{4,6},{5,7},{6,4},{7,5},{8,10},{9,11},{10,... | collective-permute-start | bytes 786440 | tf_op jit(solution)/shard_map/ppermute | solution.py:497
  83.4 2.5 %collective-permute-start.22 = (bf16[1,672,128]{2,1,0:T(8,128)(2,1)S(1)}, bf16[1,672,128]{2,1,0:T(8,128)(2,1)S(1)}, u32[]{:S(2)}, u32[]{:S(2)}) collective-permute-start(bf16[1,672,128]{2,1,0:T(8,128)(2,1)S(1)} %sums.16.refs_4_), channel_id=1, source_target_pairs={{0,16},{4,20},{8,24},{12,28},{16,0},{20,4},{24,8},{28,12},{1,17},{... | collective-permute-start | bytes 516104 | tf_op jit(solution)/shard_map/ppermute | solution.py:494
  86.0 0.5 collective-permute-start.23
  86.5 0.7 collective-permute-done.16.refs_1_
  87.2 1.1 collective-permute-done.17.refs_3_.refs_4_
  88.5 1.5 %collective-permute-start.20 = (bf16[512,128]{1,0:T(8,128)(2,1)S(1)}, bf16[512,128]{1,0:T(8,128)(2,1)S(1)}, u32[]{:S(2)}, u32[]{:S(2)}) collective-permute-start(bf16[512,128]{1,0:T(8,128)(2,1)S(1)} %get-tuple-element.79.refs_5_), channel_id=1, source_target_pairs={{0,2},{1,3},{2,0},{3,1},{4,6},{5,7},{6,4},{7,5},{8,10},{9,11},{10,... | collective-permute-start | bytes 393224 | tf_op jit(solution)/shard_map/ppermute | solution.py:497
  90.0 0.6 collective-permute-start.21
  90.6 6.6 %collective-permute-done.23.refs_4_ = bf16[1,432,128]{2,1,0:T(8,128)(2,1)S(1)} collective-permute-done((bf16[1,432,128]{2,1,0:T(8,128)(2,1)S(1)}, bf16[1,432,128]{2,1,0:T(8,128)(2,1)S(1)}, u32[]{:S(2)}, u32[]{:S(2)}) %collective-permute-start.23) | collective-permute-done | bytes 110624 | tf_op jit(solution)/shard_map/ppermute | solution.py:494
  97.4 3.0 %collective-permute-start.27 = (bf16[1,432,128]{2,1,0:T(8,128)(2,1)S(1)}, bf16[1,432,128]{2,1,0:T(8,128)(2,1)S(1)}, u32[]{:S(2)}, u32[]{:S(2)}) collective-permute-start(bf16[1,432,128]{2,1,0:T(8,128)(2,1)S(1)} %sums.19), channel_id=1, source_target_pairs={{0,16},{4,20},{8,24},{12,28},{16,0},{20,4},{24,8},{28,12},{1,17},{... | collective-permute-start | bytes 331784 | tf_op jit(solution)/shard_map/ppermute | solution.py:494
  100.5 0.9 rows.1
  101.4 5.6 %collective-permute-done.27 = bf16[1,432,128]{2,1,0:T(8,128)(2,1)S(1)} collective-permute-done((bf16[1,432,128]{2,1,0:T(8,128)(2,1)S(1)}, bf16[1,432,128]{2,1,0:T(8,128)(2,1)S(1)}, u32[]{:S(2)}, u32[]{:S(2)}) %collective-permute-start.27) | collective-permute-done | bytes 110624 | tf_op jit(solution)/shard_map/ppermute | solution.py:494
  107.0 3.5 %collective-permute-start.28 = (bf16[2,432,128]{2,1,0:T(8,128)(2,1)S(1)}, bf16[2,432,128]{2,1,0:T(8,128)(2,1)S(1)}, u32[]{:S(2)}, u32[]{:S(2)}) collective-permute-start(bf16[2,432,128]{2,1,0:T(8,128)(2,1)S(1)} %pad_maximum_fusion.1.refs_4_), channel_id=1, source_target_pairs={{0,8},{4,12},{8,0},{12,4},{16,24},{20,28},{24,16},{28,20},{1,9},{5... | collective-permute-start | bytes 663560 | tf_op jit(solution)/shard_map/ppermute | solution.py:494
  110.6 0.5 collective-permute-start.26
  111.1 3.6 %collective-permute-done.28.refs_5_ = bf16[2,432,128]{2,1,0:T(8,128)(2,1)S(1)} collective-permute-done((bf16[2,432,128]{2,1,0:T(8,128)(2,1)S(1)}, bf16[2,432,128]{2,1,0:T(8,128)(2,1)S(1)}, u32[]{:S(2)}, u32[]{:S(2)}) %collective-permute-start.28) | collective-permute-done | bytes 221216 | tf_op jit(solution)/shard_map/ppermute | solution.py:494
  114.7 1.5 %collective-permute-done.30.refs_7_ = bf16[2,432,128]{2,1,0:T(8,128)(2,1)S(1)} collective-permute-done((bf16[2,432,128]{2,1,0:T(8,128)(2,1)S(1)}, bf16[2,432,128]{2,1,0:T(8,128)(2,1)S(1)}, u32[]{:S(2)}, u32[]{:S(2)}) %collective-permute-start.30) | collective-permute-done | bytes 221216 | tf_op jit(solution)/shard_map/ppermute | solution.py:491
  116.2 3.0 %unpack.1 = (f32[544,256]{1,0:T(8,128)}, f32[64,2176]{1,0:T(8,128)}, f32[544,1024]{1,0:T(8,128)}, f32[256,1024]{1,0:T(8,128)}, f32[544]{0:T(1024)}, /*index=5*/f32[256]{0:T(256)}, f32[256]{0:T(256)}, f32[256]{0:T(256)}) custom-call(bf16[2,672,128]{2,1,0:T(8,128)(2,1)S(1)} %pad_maximum_fusion.refs_6_.refs_0_, ...), custom_call_target="tpu_custom_call" | custom-call | tf_op jit(solution)/shard_map/unpack/pallas_call | solution.py:727
  (51 shorter events, 2.2 us)
Async XLA Ops:
  12.5 10.8 %collective-permute-start.3 = (bf16[2,4,2,672,128]{4,3,2,1,0:T(8,128)(2,1)}, bf16[2,4,2,672,128]{4,3,2,1,0:T(8,128)(2,1)}, u32[]{:S(2)}, u32[]{:S(2)}) collective-permute-start(bf16[2,4,2,672,128]{4,3,2,1,0:T(8,128)(2,1)} %get-tuple-element.59), channel_id=1, source_target_pairs={{0,4},{4,0},{8,12},{12,8},{16,20},{20,16},{24,28},{28,24},{1,5},{5... | collective-permute-start | bytes 8257544 | tf_op jit(solution)/shard_map/ppermute | solution.py:491
  13.1 10.3 %copy-start = (bf16[2,4,2,672,128]{4,3,2,1,0:T(8,128)(2,1)S(1)}, bf16[2,4,2,672,128]{4,3,2,1,0:T(8,128)(2,1)}, u32[]{:S(2)}) copy-start(bf16[2,4,2,672,128]{4,3,2,1,0:T(8,128)(2,1)} %get-tuple-element.58) | copy-start | bytes 8257540
  23.2 28.3 %collective-permute-start.7 = (bf16[2,4,2,432,128]{4,3,2,1,0:T(8,128)(2,1)}, bf16[2,4,2,432,128]{4,3,2,1,0:T(8,128)(2,1)S(1)}, u32[]{:S(2)}, u32[]{:S(2)}) collective-permute-start(bf16[2,4,2,432,128]{4,3,2,1,0:T(8,128)(2,1)} %get-tuple-element.67), channel_id=1, source_target_pairs={{0,4},{4,0},{8,12},{12,8},{16,20},{20,16},{24,28},{28,24},{1,5},{5... | collective-permute-start | bytes 5308424 | tf_op jit(solution)/shard_map/ppermute | solution.py:491
  23.4 6.5 %copy-start.6 = (bf16[2,2,256,128]{3,2,1,0:T(8,128)(2,1)S(1)}, bf16[2,2,256,128]{3,2,1,0:T(8,128)(2,1)}, u32[]{:S(2)}) copy-start(bf16[2,2,256,128]{3,2,1,0:T(8,128)(2,1)} %get-tuple-element.54) | copy-start | bytes 786436
  23.4 8.1 %copy-start.5 = (bf16[2,2,256,128]{3,2,1,0:T(8,128)(2,1)S(1)}, bf16[2,2,256,128]{3,2,1,0:T(8,128)(2,1)}, u32[]{:S(2)}) copy-start(bf16[2,2,256,128]{3,2,1,0:T(8,128)(2,1)} %get-tuple-element.55) | copy-start | bytes 786436
  25.4 20.1 %collective-permute-start.4 = (bf16[2,2,672,128]{3,2,1,0:T(8,128)(2,1)S(1)}, bf16[2,2,672,128]{3,2,1,0:T(8,128)(2,1)S(1)}, u32[]{:S(2)}, u32[]{:S(2)}) collective-permute-start(bf16[2,2,672,128]{3,2,1,0:T(8,128)(2,1)S(1)} %get-tuple-element.62), channel_id=1, source_target_pairs={{0,2},{1,3},{2,0},{3,1},{4,6},{5,7},{6,4},{7,5},{8,10},{9,11},{10,... | collective-permute-start | bytes 2064392 | tf_op jit(solution)/shard_map/ppermute | solution.py:497
  28.4 17.1 %collective-permute-start.5 = (bf16[2,2,672,128]{3,2,1,0:T(8,128)(2,1)S(1)}, bf16[2,2,672,128]{3,2,1,0:T(8,128)(2,1)S(1)}, u32[]{:S(2)}, u32[]{:S(2)}) collective-permute-start(bf16[2,2,672,128]{3,2,1,0:T(8,128)(2,1)S(1)} %get-tuple-element.64), channel_id=1, source_target_pairs={{0,1},{1,0},{2,3},{3,2},{4,5},{5,4},{6,7},{7,6},{8,9},{9,8},{10,11... | collective-permute-start | bytes 2064392 | tf_op jit(solution)/shard_map/ppermute | solution.py:497
  29.9 13.2 %collective-permute-start = (bf16[2,2,256,128]{3,2,1,0:T(8,128)(2,1)S(1)}, bf16[2,2,256,128]{3,2,1,0:T(8,128)(2,1)S(1)}, u32[]{:S(2)}, u32[]{:S(2)}) collective-permute-start(bf16[2,2,256,128]{3,2,1,0:T(8,128)(2,1)S(1)} %copy-done.6), channel_id=1, source_target_pairs={{0,8},{4,12},{8,0},{12,4},{16,24},{20,28},{24,16},{28,20},{1,9},{5... | collective-permute-start | bytes 786440 | tf_op jit(solution)/shard_map/ppermute | solution.py:494
  31.5 14.0 %collective-permute-start.1 = (bf16[2,2,256,128]{3,2,1,0:T(8,128)(2,1)S(1)}, bf16[2,2,256,128]{3,2,1,0:T(8,128)(2,1)S(1)}, u32[]{:S(2)}, u32[]{:S(2)}) collective-permute-start(bf16[2,2,256,128]{3,2,1,0:T(8,128)(2,1)S(1)} %copy-done.5), channel_id=1, source_target_pairs={{0,16},{4,20},{8,24},{12,28},{16,0},{20,4},{24,8},{28,12},{1,17},{... | collective-permute-start | bytes 786440 | tf_op jit(solution)/shard_map/ppermute | solution.py:494
  45.5 2.4 %copy-start.4 = (bf16[2,2,256,128]{3,2,1,0:T(8,128)(2,1)S(1)}, bf16[2,2,256,128]{3,2,1,0:T(8,128)(2,1)}, u32[]{:S(2)}) copy-start(bf16[2,2,256,128]{3,2,1,0:T(8,128)(2,1)} %get-tuple-element.57) | copy-start | bytes 786436
  45.5 6.0 %copy-start.1 = (bf16[2,4,2,432,128]{4,3,2,1,0:T(8,128)(2,1)S(1)}, bf16[2,4,2,432,128]{4,3,2,1,0:T(8,128)(2,1)}, u32[]{:S(2)}) copy-start(bf16[2,4,2,432,128]{4,3,2,1,0:T(8,128)(2,1)} %get-tuple-element.66) | copy-start | bytes 5308420
  45.8 10.2 %collective-permute-start.6 = (bf16[2,672,128]{2,1,0:T(8,128)(2,1)S(1)}, bf16[2,672,128]{2,1,0:T(8,128)(2,1)S(1)}, u32[]{:S(2)}, u32[]{:S(2)}) collective-permute-start(bf16[2,672,128]{2,1,0:T(8,128)(2,1)S(1)} %get-tuple-element.65.refs_5_), channel_id=1, source_target_pairs={{0,1},{1,0},{2,3},{3,2},{4,5},{5,4},{6,7},{7,6},{8,9},{9,8},{10,11... | collective-permute-start | bytes 1032200 | tf_op jit(solution)/shard_map/ppermute | solution.py:497
  47.4 10.8 %collective-permute-start.8 = (bf16[2,672,128]{2,1,0:T(8,128)(2,1)S(1)}, bf16[2,672,128]{2,1,0:T(8,128)(2,1)S(1)}, u32[]{:S(2)}, u32[]{:S(2)}) collective-permute-start(bf16[2,672,128]{2,1,0:T(8,128)(2,1)S(1)} %get-tuple-element.68.refs_4_), channel_id=1, source_target_pairs={{0,2},{1,3},{2,0},{3,1},{4,6},{5,7},{6,4},{7,5},{8,10},{9,11},{10,... | collective-permute-start | bytes 1032200 | tf_op jit(solution)/shard_map/ppermute | solution.py:497
  47.9 10.5 %collective-permute-start.2 = (bf16[2,2,256,128]{3,2,1,0:T(8,128)(2,1)S(1)}, bf16[2,2,256,128]{3,2,1,0:T(8,128)(2,1)S(1)}, u32[]{:S(2)}, u32[]{:S(2)}) collective-permute-start(bf16[2,2,256,128]{3,2,1,0:T(8,128)(2,1)S(1)} %copy-done.4), channel_id=1, source_target_pairs={{0,24},{4,28},{8,16},{12,20},{16,8},{20,12},{24,0},{28,4},{1,25},{... | collective-permute-start | bytes 786440 | tf_op jit(solution)/shard_map/ppermute | solution.py:494
  52.6 5.8 %copy-start.2 = (bf16[2,2,256,128]{3,2,1,0:T(8,128)(2,1)S(1)}, bf16[2,2,256,128]{3,2,1,0:T(8,128)(2,1)}, u32[]{:S(2)}) copy-start(bf16[2,2,256,128]{3,2,1,0:T(8,128)(2,1)} %get-tuple-element.53.refs_0_.rest_0_) | copy-start | bytes 786436
  52.6 14.9 %collective-permute-start.12 = (bf16[2,2,432,128]{3,2,1,0:T(8,128)(2,1)S(1)}, bf16[2,2,432,128]{3,2,1,0:T(8,128)(2,1)S(1)}, u32[]{:S(2)}, u32[]{:S(2)}) collective-permute-start(bf16[2,2,432,128]{3,2,1,0:T(8,128)(2,1)S(1)} %get-tuple-element.69.refs_3_), channel_id=1, source_target_pairs={{0,1},{1,0},{2,3},{3,2},{4,5},{5,4},{6,7},{7,6},{8,9},{9,8},{10,11... | collective-permute-start | bytes 1327112 | tf_op jit(solution)/shard_map/ppermute | solution.py:497
  53.2 14.3 %collective-permute-start.11 = (bf16[2,2,432,128]{3,2,1,0:T(8,128)(2,1)S(1)}, bf16[2,2,432,128]{3,2,1,0:T(8,128)(2,1)S(1)}, u32[]{:S(2)}, u32[]{:S(2)}) collective-permute-start(bf16[2,2,432,128]{3,2,1,0:T(8,128)(2,1)S(1)} %get-tuple-element.70.refs_4_), channel_id=1, source_target_pairs={{0,2},{1,3},{2,0},{3,1},{4,6},{5,7},{6,4},{7,5},{8,10},{9,11},{10,... | collective-permute-start | bytes 1327112 | tf_op jit(solution)/shard_map/ppermute | solution.py:497
  58.4 5.0 %collective-permute-start.10 = (bf16[2,2,256,128]{3,2,1,0:T(8,128)(2,1)S(1)}, bf16[2,2,256,128]{3,2,1,0:T(8,128)(2,1)S(1)}, u32[]{:S(2)}, u32[]{:S(2)}) collective-permute-start(bf16[2,2,256,128]{3,2,1,0:T(8,128)(2,1)S(1)} %get-tuple-element.72), channel_id=1, source_target_pairs={{0,4},{4,0},{8,12},{12,8},{16,20},{20,16},{24,28},{28,24},{1,5},{5... | collective-permute-start | bytes 786440 | tf_op jit(solution)/shard_map/ppermute | solution.py:491
  58.5 5.0 %copy-start.3 = (s32[2,8192,4]{1,2,0:T(4,128)S(1)}, s32[2,8192,4]{1,2,0:T(4,128)}, u32[]{:S(2)}) copy-start(s32[2,8192,4]{1,2,0:T(4,128)} %param.23) | copy-start | bytes 786436
  58.5 4.9 %collective-permute-start.9 = (bf16[2,2,256,128]{3,2,1,0:T(8,128)(2,1)S(1)}, bf16[2,2,256,128]{3,2,1,0:T(8,128)(2,1)S(1)}, u32[]{:S(2)}, u32[]{:S(2)}) collective-permute-start(bf16[2,2,256,128]{3,2,1,0:T(8,128)(2,1)S(1)} %get-tuple-element.71.rest_6_), channel_id=1, source_target_pairs={{0,4},{4,0},{8,12},{12,8},{16,20},{20,16},{24,28},{28,24},{1,5},{5... | collective-permute-start | bytes 786440 | tf_op jit(solution)/shard_map/ppermute | solution.py:491
  59.0 11.6 %collective-permute-start.14 = (bf16[2,672,128]{2,1,0:T(8,128)(2,1)S(1)}, bf16[2,672,128]{2,1,0:T(8,128)(2,1)S(1)}, u32[]{:S(2)}, u32[]{:S(2)}) collective-permute-start(bf16[2,672,128]{2,1,0:T(8,128)(2,1)S(1)} %sums.11.refs_4_), channel_id=1, source_target_pairs={{0,8},{4,12},{8,0},{12,4},{16,24},{20,28},{24,16},{28,20},{1,9},{5... | collective-permute-start | bytes 1032200 | tf_op jit(solution)/shard_map/ppermute | solution.py:494
  67.7 7.2 %collective-permute-start.13 = (bf16[2,432,128]{2,1,0:T(8,128)(2,1)S(1)}, bf16[2,432,128]{2,1,0:T(8,128)(2,1)S(1)}, u32[]{:S(2)}, u32[]{:S(2)}) collective-permute-start(bf16[2,432,128]{2,1,0:T(8,128)(2,1)S(1)} %get-tuple-element.75.refs_5_), channel_id=1, source_target_pairs={{0,1},{1,0},{2,3},{3,2},{4,5},{5,4},{6,7},{7,6},{8,9},{9,8},{10,11... | collective-permute-start | bytes 663560 | tf_op jit(solution)/shard_map/ppermute | solution.py:497
  68.3 6.9 %collective-permute-start.15 = (bf16[2,432,128]{2,1,0:T(8,128)(2,1)S(1)}, bf16[2,432,128]{2,1,0:T(8,128)(2,1)S(1)}, u32[]{:S(2)}, u32[]{:S(2)}) collective-permute-start(bf16[2,432,128]{2,1,0:T(8,128)(2,1)S(1)} %get-tuple-element.76.refs_4_), channel_id=1, source_target_pairs={{0,2},{1,3},{2,0},{3,1},{4,6},{5,7},{6,4},{7,5},{8,10},{9,11},{10,... | collective-permute-start | bytes 663560 | tf_op jit(solution)/shard_map/ppermute | solution.py:497
  70.8 12.4 %collective-permute-start.19 = (bf16[1,672,128]{2,1,0:T(8,128)(2,1)S(1)}, bf16[1,672,128]{2,1,0:T(8,128)(2,1)S(1)}, u32[]{:S(2)}, u32[]{:S(2)}) collective-permute-start(bf16[1,672,128]{2,1,0:T(8,128)(2,1)S(1)} %sums.13.refs_3_), channel_id=1, source_target_pairs={{0,16},{4,20},{8,24},{12,28},{16,0},{20,4},{24,8},{28,12},{1,17},{... | collective-permute-start | bytes 516104 | tf_op jit(solution)/shard_map/ppermute | solution.py:494
  75.3 10.6 %collective-permute-start.18 = (bf16[2,432,128]{2,1,0:T(8,128)(2,1)S(1)}, bf16[2,432,128]{2,1,0:T(8,128)(2,1)S(1)}, u32[]{:S(2)}, u32[]{:S(2)}) collective-permute-start(bf16[2,432,128]{2,1,0:T(8,128)(2,1)S(1)} %sums.14.rest_6_), channel_id=1, source_target_pairs={{0,8},{4,12},{8,0},{12,4},{16,24},{20,28},{24,16},{28,20},{1,9},{5... | collective-permute-start | bytes 663560 | tf_op jit(solution)/shard_map/ppermute | solution.py:494
  80.2 7.1 %collective-permute-start.16 = (bf16[2,512,128]{2,1,0:T(8,128)(2,1)S(1)}, bf16[2,512,128]{2,1,0:T(8,128)(2,1)S(1)}, u32[]{:S(2)}, u32[]{:S(2)}) collective-permute-start(bf16[2,512,128]{2,1,0:T(8,128)(2,1)S(1)} %get-tuple-element.77.refs_5_), channel_id=1, source_target_pairs={{0,1},{1,0},{2,3},{3,2},{4,5},{5,4},{6,7},{7,6},{8,9},{9,8},{10,11... | collective-permute-start | bytes 786440 | tf_op jit(solution)/shard_map/ppermute | solution.py:497
  81.8 6.6 %collective-permute-start.17 = (bf16[2,512,128]{2,1,0:T(8,128)(2,1)S(1)}, bf16[2,512,128]{2,1,0:T(8,128)(2,1)S(1)}, u32[]{:S(2)}, u32[]{:S(2)}) collective-permute-start(bf16[2,512,128]{2,1,0:T(8,128)(2,1)S(1)} %get-tuple-element.78.refs_6_), channel_id=1, source_target_pairs={{0,2},{1,3},{2,0},{3,1},{4,6},{5,7},{6,4},{7,5},{8,10},{9,11},{10,... | collective-permute-start | bytes 786440 | tf_op jit(solution)/shard_map/ppermute | solution.py:497
  83.4 13.9 %collective-permute-start.22 = (bf16[1,672,128]{2,1,0:T(8,128)(2,1)S(1)}, bf16[1,672,128]{2,1,0:T(8,128)(2,1)S(1)}, u32[]{:S(2)}, u32[]{:S(2)}) collective-permute-start(bf16[1,672,128]{2,1,0:T(8,128)(2,1)S(1)} %sums.16.refs_4_), channel_id=1, source_target_pairs={{0,16},{4,20},{8,24},{12,28},{16,0},{20,4},{24,8},{28,12},{1,17},{... | collective-permute-start | bytes 516104 | tf_op jit(solution)/shard_map/ppermute | solution.py:494
  86.0 11.2 %collective-permute-start.23 = (bf16[1,432,128]{2,1,0:T(8,128)(2,1)S(1)}, bf16[1,432,128]{2,1,0:T(8,128)(2,1)S(1)}, u32[]{:S(2)}, u32[]{:S(2)}) collective-permute-start(bf16[1,432,128]{2,1,0:T(8,128)(2,1)S(1)} %sums.17.refs_4_), channel_id=1, source_target_pairs={{0,16},{4,20},{8,24},{12,28},{16,0},{20,4},{24,8},{28,12},{1,17},{... | collective-permute-start | bytes 331784 | tf_op jit(solution)/shard_map/ppermute | solution.py:494
  88.5 11.9 %collective-permute-start.20 = (bf16[512,128]{1,0:T(8,128)(2,1)S(1)}, bf16[512,128]{1,0:T(8,128)(2,1)S(1)}, u32[]{:S(2)}, u32[]{:S(2)}) collective-permute-start(bf16[512,128]{1,0:T(8,128)(2,1)S(1)} %get-tuple-element.79.refs_5_), channel_id=1, source_target_pairs={{0,2},{1,3},{2,0},{3,1},{4,6},{5,7},{6,4},{7,5},{8,10},{9,11},{10,... | collective-permute-start | bytes 393224 | tf_op jit(solution)/shard_map/ppermute | solution.py:497
  90.0 10.5 %collective-permute-start.21 = (bf16[512,128]{1,0:T(8,128)(2,1)S(1)}, bf16[512,128]{1,0:T(8,128)(2,1)S(1)}, u32[]{:S(2)}, u32[]{:S(2)}) collective-permute-start(bf16[512,128]{1,0:T(8,128)(2,1)S(1)} %get-tuple-element.80.refs_6_), channel_id=1, source_target_pairs={{0,1},{1,0},{2,3},{3,2},{4,5},{5,4},{6,7},{7,6},{8,9},{9,8},{10,11... | collective-permute-start | bytes 393224 | tf_op jit(solution)/shard_map/ppermute | solution.py:497
  97.4 13.2 %collective-permute-start.24 = (bf16[2,672,128]{2,1,0:T(8,128)(2,1)S(1)}, bf16[2,672,128]{2,1,0:T(8,128)(2,1)S(1)}, u32[]{:S(2)}, u32[]{:S(2)}) collective-permute-start(bf16[2,672,128]{2,1,0:T(8,128)(2,1)S(1)} %pad_maximum_fusion.refs_6_.refs_0_), channel_id=1, source_target_pairs={{0,8},{4,12},{8,0},{12,4},{16,24},{20,28},{24,16},{28,20},{1,9},{5... | collective-permute-start | bytes 1032200 | tf_op jit(solution)/shard_map/ppermute | solution.py:494
  97.4 9.6 %collective-permute-start.27 = (bf16[1,432,128]{2,1,0:T(8,128)(2,1)S(1)}, bf16[1,432,128]{2,1,0:T(8,128)(2,1)S(1)}, u32[]{:S(2)}, u32[]{:S(2)}) collective-permute-start(bf16[1,432,128]{2,1,0:T(8,128)(2,1)S(1)} %sums.19), channel_id=1, source_target_pairs={{0,16},{4,20},{8,24},{12,28},{16,0},{20,4},{24,8},{28,12},{1,17},{... | collective-permute-start | bytes 331784 | tf_op jit(solution)/shard_map/ppermute | solution.py:494
  107.0 7.6 %collective-permute-start.28 = (bf16[2,432,128]{2,1,0:T(8,128)(2,1)S(1)}, bf16[2,432,128]{2,1,0:T(8,128)(2,1)S(1)}, u32[]{:S(2)}, u32[]{:S(2)}) collective-permute-start(bf16[2,432,128]{2,1,0:T(8,128)(2,1)S(1)} %pad_maximum_fusion.1.refs_4_), channel_id=1, source_target_pairs={{0,8},{4,12},{8,0},{12,4},{16,24},{20,28},{24,16},{28,20},{1,9},{5... | collective-permute-start | bytes 663560 | tf_op jit(solution)/shard_map/ppermute | solution.py:494
  110.6 4.1 %collective-permute-start.25 = (bf16[2,672,128]{2,1,0:T(8,128)(2,1)S(1)}, bf16[2,672,128]{2,1,0:T(8,128)(2,1)S(1)}, u32[]{:S(2)}, u32[]{:S(2)}) collective-permute-start(bf16[2,672,128]{2,1,0:T(8,128)(2,1)S(1)} %pad_maximum_fusion.refs_6_.refs_0_), channel_id=1, source_target_pairs={{0,4},{4,0},{8,12},{12,8},{16,20},{20,16},{24,28},{28,24},{1,5},{5... | collective-permute-start | bytes 1032200 | tf_op jit(solution)/shard_map/ppermute | solution.py:491
  110.6 5.6 %collective-permute-start.26 = (bf16[2,672,128]{2,1,0:T(8,128)(2,1)S(1)}, bf16[2,672,128]{2,1,0:T(8,128)(2,1)S(1)}, u32[]{:S(2)}, u32[]{:S(2)}) collective-permute-start(bf16[2,672,128]{2,1,0:T(8,128)(2,1)S(1)} %collective-permute-done.24.refs_1_), channel_id=1, source_target_pairs={{0,4},{4,0},{8,12},{12,8},{16,20},{20,16},{24,28},{28,24},{1,5},{5... | collective-permute-start | bytes 1032200 | tf_op jit(solution)/shard_map/ppermute | solution.py:491
  111.1 3.6 %collective-permute-start.29 = (bf16[2,432,128]{2,1,0:T(8,128)(2,1)S(1)}, bf16[2,432,128]{2,1,0:T(8,128)(2,1)S(1)}, u32[]{:S(2)}, u32[]{:S(2)}) collective-permute-start(bf16[2,432,128]{2,1,0:T(8,128)(2,1)S(1)} %pad_maximum_fusion.1.refs_4_), channel_id=1, source_target_pairs={{0,4},{4,0},{8,12},{12,8},{16,20},{20,16},{24,28},{28,24},{1,5},{5... | collective-permute-start | bytes 663560 | tf_op jit(solution)/shard_map/ppermute | solution.py:491
  114.7 1.5 %collective-permute-start.30 = (bf16[2,432,128]{2,1,0:T(8,128)(2,1)S(1)}, bf16[2,432,128]{2,1,0:T(8,128)(2,1)S(1)}, u32[]{:S(2)}, u32[]{:S(2)}) collective-permute-start(bf16[2,432,128]{2,1,0:T(8,128)(2,1)S(1)} %collective-permute-done.28.refs_5_), channel_id=1, source_target_pairs={{0,4},{4,0},{8,12},{12,8},{16,20},{20,16},{24,28},{28,24},{1,5},{5... | collective-permute-start | bytes 663560 | tf_op jit(solution)/shard_map/ppermute | solution.py:491

commit v13 on v9

--- a/solution.py
+++ b/solution.py
@@ -646,13 +646,12 @@
     for which in [half, *range(1, half)]:
         values[which] = swap_z(pooled_out[which], which)
     for which in range(half + 1, n_z):
-        (moved,) = after([pooled_out[which]], [values[half], values[which - half]])
-        values[which] = swap_z(moved, which)
+        values[which] = swap_z(pooled_out[which], which)
     one.settle([values[1]])
-    last = [values[which] for which in range(1, half + 1)]
+    last = [values[1]]
     for at in range(1, row_bits):
         last = one.row_step(at, last)
-    last = two.first_step(last)
+    last = two.first_step([*last, *[values[which] for which in range(1, n_z)]])
     last = one.z_step(0, last)
     two.settle(last)
     values = [values[which] for which in range(n_z)]

time: 119 us -> 118 us (level)
  starting transfers between devices: 41.7 us -> 36.7 us
  waiting for transfers between devices: 34.7 us -> 39.5 us
    ppermute x12, waiting for transfers between devices: 6.89 us -> 10.5 us  [swap_row(): lax.ppermute(value, 'row', [(at, at ^ 1 << bit) for at in range(n_row)])]
    ppermute x12, starting transfers between devices: 15.8 us -> 12.6 us  [swap_row(): lax.ppermute(value, 'row', [(at, at ^ 1 << bit) for at in range(n_row)])]
    ppermute x11, starting transfers between devices: 24.2 us -> 22.4 us  [swap_z(): lax.ppermute(value, 'table', [(at, at ^ 2 * which) for at in range(n_tabl...]
  transfers between devices with their start and end apart: 31 -> 31, of which waited for: 13 -> 16; matrix products, arithmetic and copies ran while one was open for 0% -> 0% of each run, Pallas kernels for 23% -> 23%
where the time goes in v13:
time: 118 us
  Pallas kernels  41 us (35%)
  waiting for transfers between devices  39.5 us (33%)
  starting transfers between devices  36.7 us (31%)
    ppermute x11, waiting for transfers between devices, swap_z(): lax.ppermute(value, 'table', [(at, at ^ 2 * which) for at in range(n_tabl...  27.4 us
    ppermute x11, starting transfers between devices, swap_z(): lax.ppermute(value, 'table', [(at, at ^ 2 * which) for at in range(n_tabl...  22.4 us
    ppermute x12, starting transfers between devices, swap_row(): lax.ppermute(value, 'row', [(at, at ^ 1 << bit) for at in range(n_row)])  12.6 us
    pallas_call x1, Pallas kernels, local(): call(front_kernel, [packed(rows_front)] * 2 + [wide(feat, batch), wide(ba...  11.9 us
    ppermute x12, waiting for transfers between devices, swap_row(): lax.ppermute(value, 'row', [(at, at ^ 1 << bit) for at in range(n_row)])  10.5 us
    pallas_call x1, Pallas kernels, local(): call(functools.partial(middle_kernel, n_z), [packed(rows_back)] * 2 + [wi...  10.1 us
    pallas_call x2, Pallas kernels, local(): pl.pallas_call(functools.partial(count_kernel, n_row, table, hot, n_z), o...  8.03 us
    pallas_call x4, Pallas kernels, fetch_sums(): call(functools.partial(fetch_sum_kernel, plan, n_in), shapes, scratch + [...  6 us
  transfers between devices with their start and end apart: 31, of which 16 were waited for; matrix products, arithmetic and copies ran while one was open for 0% of the time, Pallas kernels for 23%

profile of v13, /device:TPU:0, one launch (start us, length us, event | category | flops | bytes accessed | tf_op | source)
XLA Modules:
  0.0 118.2 jit_solution(9365091532795568575)
XLA Ops:
  0.6 11.9 %front.1 = (bf16[2,4,2,672,128]{4,3,2,1,0:T(8,128)(2,1)}, bf16[2,4,2,672,128]{4,3,2,1,0:T(8,128)(2,1)}, bf16[2176,256]{1,0:T(8,128)(2,1)}, bf16[256,1024]{1,0:T(8,128)(2,1)}, f32[24,128]{1,0:T(8,128)}) custom-call(bf16[256,128]{1,0:T(8,128)(2,1)} %refs_0_.3, bf16[256,2048]{1,0:T(8,128)(2,1)} %refs_1_.3, bf16[2176,256]{1,0:T(8,128)(2,1)} %refs_2_.3, ...), custom_call_target="tpu_custom_call" | custom-call | tf_op jit(solution)/shard_map/front/pallas_call | solution.py:504
  12.5 0.5 collective-permute-start.3
  13.1 10.1 %middle.1 = (bf16[2,4,2,432,128]{4,3,2,1,0:T(8,128)(2,1)}, bf16[2,4,2,432,128]{4,3,2,1,0:T(8,128)(2,1)}, bf16[2,2,256,128]{3,2,1,0:T(8,128)(2,1)}, bf16[2,2,256,...) custom-call(bf16[256,128]{1,0:T(8,128)(2,1)} %refs_0_.3, ...), custom_call_target="tpu_custom_call" | custom-call | tf_op jit(solution)/shard_map/middle/pallas_call | solution.py:531
  23.4 2.0 %first_sums.5 = (bf16[2,2,672,128]{3,2,1,0:T(8,128)(2,1)S(1)}, bf16[2,2,672,128]{3,2,1,0:T(8,128)(2,1)S(1)}) custom-call(bf16[2,2,2,2,672,128]{5,4,3,2,1,0:T(8,128)(2,1)S(1)} %bitcast.7, bf16[2,2,2,2,672,128]{5,4,3,2,1,0:T(8,128)(2,1)} %bitcast.2.refs_1_.refs_3_, bf16[2,2,2,2,672,128]{5,4,3,2,1,0:T(8,128)(2,1)S(1)} %bitcast.8, ...), custom_call_target="tpu_custom_call" | custom-call | tf_op jit(solution)/shard_map/first_sums/pallas_call | solution.py:408
  25.4 3.0 %collective-permute-start.4 = (bf16[2,2,672,128]{3,2,1,0:T(8,128)(2,1)S(1)}, bf16[2,2,672,128]{3,2,1,0:T(8,128)(2,1)S(1)}, u32[]{:S(2)}, u32[]{:S(2)}) collective-permute-start(bf16[2,2,672,128]{3,2,1,0:T(8,128)(2,1)S(1)} %get-tuple-element.60), channel_id=1, source_target_pairs={{0,2},{1,3},{2,0},{3,1},{4,6},{5,7},{6,4},{7,5},{8,10},{9,11},{10,... | collective-permute-start | bytes 2064392 | tf_op jit(solution)/shard_map/ppermute | solution.py:472
  28.4 1.5 %collective-permute-start.5 = (bf16[2,2,672,128]{3,2,1,0:T(8,128)(2,1)S(1)}, bf16[2,2,672,128]{3,2,1,0:T(8,128)(2,1)S(1)}, u32[]{:S(2)}, u32[]{:S(2)}) collective-permute-start(bf16[2,2,672,128]{3,2,1,0:T(8,128)(2,1)S(1)} %get-tuple-element.62), channel_id=1, source_target_pairs={{0,1},{1,0},{2,3},{3,2},{4,5},{5,4},{6,7},{7,6},{8,9},{9,8},{10,11... | collective-permute-start | bytes 2064392 | tf_op jit(solution)/shard_map/ppermute | solution.py:472
  29.9 1.6 %collective-permute-start = (bf16[2,2,256,128]{3,2,1,0:T(8,128)(2,1)S(1)}, bf16[2,2,256,128]{3,2,1,0:T(8,128)(2,1)S(1)}, u32[]{:S(2)}, u32[]{:S(2)}) collective-permute-start(bf16[2,2,256,128]{3,2,1,0:T(8,128)(2,1)S(1)} %copy-done.6), channel_id=1, source_target_pairs={{0,8},{4,12},{8,0},{12,4},{16,24},{20,28},{24,16},{28,20},{1,9},{5... | collective-permute-start | bytes 786440 | tf_op jit(solution)/shard_map/ppermute | solution.py:469
  31.5 2.6 %collective-permute-start.1 = (bf16[2,2,256,128]{3,2,1,0:T(8,128)(2,1)S(1)}, bf16[2,2,256,128]{3,2,1,0:T(8,128)(2,1)S(1)}, u32[]{:S(2)}, u32[]{:S(2)}) collective-permute-start(bf16[2,2,256,128]{3,2,1,0:T(8,128)(2,1)S(1)} %copy-done.5), channel_id=1, source_target_pairs={{0,16},{4,20},{8,24},{12,28},{16,0},{20,4},{24,8},{28,12},{1,17},{... | collective-permute-start | bytes 786440 | tf_op jit(solution)/shard_map/ppermute | solution.py:469
  34.1 9.0 %collective-permute-done.refs_4_.refs_6_.refs_1_.rest_1_ = bf16[2,2,256,128]{3,2,1,0:T(8,128)(2,1)S(1)} collective-permute-done((bf16[2,2,256,128]{3,2,1,0:T(8,128)(2,1)S(1)}, bf16[2,2,256,128]{3,2,1,0:T(8,128)(2,1)S(1)}, u32[]{:S(2)}, u32[]{:S(2)}) %collective-permute-start) | collective-permute-done | bytes 262176 | tf_op jit(solution)/shard_map/ppermute | solution.py:469
  43.1 2.5 %collective-permute-start.2 = (bf16[2,2,256,128]{3,2,1,0:T(8,128)(2,1)S(1)}, bf16[2,2,256,128]{3,2,1,0:T(8,128)(2,1)S(1)}, u32[]{:S(2)}, u32[]{:S(2)}) collective-permute-start(bf16[2,2,256,128]{3,2,1,0:T(8,128)(2,1)S(1)} %copy-done.4), channel_id=1, source_target_pairs={{0,24},{4,28},{8,16},{12,20},{16,8},{20,12},{24,0},{28,4},{1,25},{... | collective-permute-start | bytes 786440 | tf_op jit(solution)/shard_map/ppermute | solution.py:469
  45.6 1.8 %first_sums.4 = (bf16[2,2,672,128]{3,2,1,0:T(8,128)(2,1)S(1)}, bf16[2,2,672,128]{3,2,1,0:T(8,128)(2,1)S(1)}) custom-call(bf16[2,2,2,2,672,128]{5,4,3,2,1,0:T(8,128)(2,1)S(1)} %bitcast.9, bf16[2,2,2,2,672,128]{5,4,3,2,1,0:T(8,128)(2,1)} %bitcast.2.refs_1_.refs_3_, bf16[2,2,2,2,672,128]{5,4,3,2,1,0:T(8,128)(2,1)S(1)} %bitcast.10, ...), custom_call_target="tpu_custom_call" | custom-call | tf_op jit(solution)/shard_map/first_sums/pallas_call | solution.py:408
  47.4 0.3 sums.10
  47.7 0.6 collective-permute-start.6
  48.3 0.5 collective-permute-start.8
  48.8 2.9 %collective-permute-done.2.refs_8_.refs_3_.rest_3_ = bf16[2,2,256,128]{3,2,1,0:T(8,128)(2,1)S(1)} collective-permute-done((bf16[2,2,256,128]{3,2,1,0:T(8,128)(2,1)S(1)}, bf16[2,2,256,128]{3,2,1,0:T(8,128)(2,1)S(1)}, u32[]{:S(2)}, u32[]{:S(2)}) %collective-permute-start.2) | collective-permute-done | bytes 262176 | tf_op jit(solution)/shard_map/ppermute | solution.py:469
  51.8 1.1 first_sums.6
  52.9 0.6 collective-permute-start.12
  53.5 0.7 collective-permute-start.11
  54.2 4.6 %collective-permute-done.6.refs_2_ = bf16[2,672,128]{2,1,0:T(8,128)(2,1)S(1)} collective-permute-done((bf16[2,672,128]{2,1,0:T(8,128)(2,1)S(1)}, bf16[2,672,128]{2,1,0:T(8,128)(2,1)S(1)}, u32[]{:S(2)}, u32[]{:S(2)}) %collective-permute-start.6) | collective-permute-done | bytes 344096 | tf_op jit(solution)/shard_map/ppermute | solution.py:472
  58.8 0.5 collective-permute-done.8.refs_5_.refs_2_
  59.7 0.5 collective-permute-start.9
  60.3 1.1 first_sums.7
  61.6 4.0 %counts.2.refs_4_ = bf16[4,512,128]{2,1,0:T(8,128)(2,1)S(1)} custom-call(s32[2,4,8192]{2,1,0:T(4,128)S(1)} %bitcast.25, bf16[2,2,256,128]{3,2,1,0:T(8,128)(2,1)S(1)} %copy-done.2, bf16[2,2,256,128]{3,2,1,0:T(8,128)(2,1)S(1)} %collective-permute-done.refs_4_.refs_6_.refs_1_.rest_1_, ...), custom_call_target="tpu_custom_call" | custom-call | tf_op jit(solution)/shard_map/counts/pallas_call | solution.py:670
  65.6 0.3 collective-permute-done.12.refs_1_.refs_5_
  65.8 0.2 collective-permute-done.11.refs_3_.refs_6_.refs_1_
  66.3 1.6 %collective-permute-start.13 = (bf16[2,432,128]{2,1,0:T(8,128)(2,1)S(1)}, bf16[2,432,128]{2,1,0:T(8,128)(2,1)S(1)}, u32[]{:S(2)}, u32[]{:S(2)}) collective-permute-start(bf16[2,432,128]{2,1,0:T(8,128)(2,1)S(1)} %get-tuple-element.73.refs_5_), channel_id=1, source_target_pairs={{0,1},{1,0},{2,3},{3,2},{4,5},{5,4},{6,7},{7,6},{8,9},{9,8},{10,11... | collective-permute-start | bytes 663560 | tf_op jit(solution)/shard_map/ppermute | solution.py:472
  67.9 1.0 collective-permute-start.15
  68.8 1.4 %collective-permute-done.14.refs_3_.refs_6_ = bf16[2,672,128]{2,1,0:T(8,128)(2,1)S(1)} collective-permute-done((bf16[2,672,128]{2,1,0:T(8,128)(2,1)S(1)}, bf16[2,672,128]{2,1,0:T(8,128)(2,1)S(1)}, u32[]{:S(2)}, u32[]{:S(2)}) %collective-permute-start.14) | collective-permute-done | bytes 344096 | tf_op jit(solution)/shard_map/ppermute | solution.py:469
  70.4 2.8 %collective-permute-start.19 = (bf16[1,672,128]{2,1,0:T(8,128)(2,1)S(1)}, bf16[1,672,128]{2,1,0:T(8,128)(2,1)S(1)}, u32[]{:S(2)}, u32[]{:S(2)}) collective-permute-start(bf16[1,672,128]{2,1,0:T(8,128)(2,1)S(1)} %sums.13.refs_3_), channel_id=1, source_target_pairs={{0,16},{4,20},{8,24},{12,28},{16,0},{20,4},{24,8},{28,12},{1,17},{... | collective-permute-start | bytes 516104 | tf_op jit(solution)/shard_map/ppermute | solution.py:469
  73.4 1.2 %collective-permute-done.15.refs_4_.refs_2_ = bf16[2,432,128]{2,1,0:T(8,128)(2,1)S(1)} collective-permute-done((bf16[2,432,128]{2,1,0:T(8,128)(2,1)S(1)}, bf16[2,432,128]{2,1,0:T(8,128)(2,1)S(1)}, u32[]{:S(2)}, u32[]{:S(2)}) %collective-permute-start.15) | collective-permute-done | bytes 221216 | tf_op jit(solution)/shard_map/ppermute | solution.py:472
  74.7 3.9 %collective-permute-start.18 = (bf16[2,432,128]{2,1,0:T(8,128)(2,1)S(1)}, bf16[2,432,128]{2,1,0:T(8,128)(2,1)S(1)}, u32[]{:S(2)}, u32[]{:S(2)}) collective-permute-start(bf16[2,432,128]{2,1,0:T(8,128)(2,1)S(1)} %sums.14.rest_6_), channel_id=1, source_target_pairs={{0,8},{4,12},{8,0},{12,4},{16,24},{20,28},{24,16},{28,20},{1,9},{5... | collective-permute-start | bytes 663560 | tf_op jit(solution)/shard_map/ppermute | solution.py:469
  78.6 4.0 %counts.3.refs_2_ = bf16[4,512,128]{2,1,0:T(8,128)(2,1)S(1)} custom-call(s32[2,4,8192]{2,1,0:T(4,128)S(1)} %bitcast.26, bf16[2,2,256,128]{3,2,1,0:T(8,128)(2,1)S(1)} %copy-done.2, bf16[2,2,256,128]{3,2,1,0:T(8,128)(2,1)S(1)} %collective-permute-done.refs_4_.refs_6_.refs_1_.rest_1_, ...), custom_call_target="tpu_custom_call" | custom-call | tf_op jit(solution)/shard_map/counts/pallas_call | solution.py:670
  82.8 0.6 collective-permute-start.16
  83.4 0.7 collective-permute-start.17
  84.5 3.0 %collective-permute-start.23 = (bf16[1,432,128]{2,1,0:T(8,128)(2,1)S(1)}, bf16[1,432,128]{2,1,0:T(8,128)(2,1)S(1)}, u32[]{:S(2)}, u32[]{:S(2)}) collective-permute-start(bf16[1,432,128]{2,1,0:T(8,128)(2,1)S(1)} %sums.17.refs_4_), channel_id=1, source_target_pairs={{0,16},{4,20},{8,24},{12,28},{16,0},{20,4},{24,8},{28,12},{1,17},{... | collective-permute-start | bytes 331784 | tf_op jit(solution)/shard_map/ppermute | solution.py:469
  87.4 2.0 %collective-permute-done.16.refs_1_ = bf16[2,512,128]{2,1,0:T(8,128)(2,1)S(1)} collective-permute-done((bf16[2,512,128]{2,1,0:T(8,128)(2,1)S(1)}, bf16[2,512,128]{2,1,0:T(8,128)(2,1)S(1)}, u32[]{:S(2)}, u32[]{:S(2)}) %collective-permute-start.16) | collective-permute-done | bytes 262176 | tf_op jit(solution)/shard_map/ppermute | solution.py:472
  89.4 1.5 %collective-permute-done.17.refs_3_.refs_4_ = bf16[2,512,128]{2,1,0:T(8,128)(2,1)S(1)} collective-permute-done((bf16[2,512,128]{2,1,0:T(8,128)(2,1)S(1)}, bf16[2,512,128]{2,1,0:T(8,128)(2,1)S(1)}, u32[]{:S(2)}, u32[]{:S(2)}) %collective-permute-start.17) | collective-permute-done | bytes 262176 | tf_op jit(solution)/shard_map/ppermute | solution.py:472
  91.1 0.7 collective-permute-start.20
  91.7 1.2 collective-permute-start.21
  92.9 3.7 %collective-permute-done.23.refs_4_ = bf16[1,432,128]{2,1,0:T(8,128)(2,1)S(1)} collective-permute-done((bf16[1,432,128]{2,1,0:T(8,128)(2,1)S(1)}, bf16[1,432,128]{2,1,0:T(8,128)(2,1)S(1)}, u32[]{:S(2)}, u32[]{:S(2)}) %collective-permute-start.23) | collective-permute-done | bytes 110624 | tf_op jit(solution)/shard_map/ppermute | solution.py:469
  96.9 2.4 %collective-permute-start.27 = (bf16[1,432,128]{2,1,0:T(8,128)(2,1)S(1)}, bf16[1,432,128]{2,1,0:T(8,128)(2,1)S(1)}, u32[]{:S(2)}, u32[]{:S(2)}) collective-permute-start(bf16[1,432,128]{2,1,0:T(8,128)(2,1)S(1)} %sums.19), channel_id=1, source_target_pairs={{0,16},{4,20},{8,24},{12,28},{16,0},{20,4},{24,8},{28,12},{1,17},{... | collective-permute-start | bytes 331784 | tf_op jit(solution)/shard_map/ppermute | solution.py:469
  99.3 0.9 rows.1
  100.2 6.1 %collective-permute-done.27 = bf16[1,432,128]{2,1,0:T(8,128)(2,1)S(1)} collective-permute-done((bf16[1,432,128]{2,1,0:T(8,128)(2,1)S(1)}, bf16[1,432,128]{2,1,0:T(8,128)(2,1)S(1)}, u32[]{:S(2)}, u32[]{:S(2)}) %collective-permute-start.27) | collective-permute-done | bytes 110624 | tf_op jit(solution)/shard_map/ppermute | solution.py:469
  106.3 3.4 %collective-permute-start.28 = (bf16[2,432,128]{2,1,0:T(8,128)(2,1)S(1)}, bf16[2,432,128]{2,1,0:T(8,128)(2,1)S(1)}, u32[]{:S(2)}, u32[]{:S(2)}) collective-permute-start(bf16[2,432,128]{2,1,0:T(8,128)(2,1)S(1)} %pad_maximum_fusion.1.refs_4_), channel_id=1, source_target_pairs={{0,8},{4,12},{8,0},{12,4},{16,24},{20,28},{24,16},{28,20},{1,9},{5... | collective-permute-start | bytes 663560 | tf_op jit(solution)/shard_map/ppermute | solution.py:469
  109.7 0.5 collective-permute-start.26
  110.2 4.3 %collective-permute-done.28.refs_5_ = bf16[2,432,128]{2,1,0:T(8,128)(2,1)S(1)} collective-permute-done((bf16[2,432,128]{2,1,0:T(8,128)(2,1)S(1)}, bf16[2,432,128]{2,1,0:T(8,128)(2,1)S(1)}, u32[]{:S(2)}, u32[]{:S(2)}) %collective-permute-start.28) | collective-permute-done | bytes 221216 | tf_op jit(solution)/shard_map/ppermute | solution.py:469
  114.5 1.5 %collective-permute-done.30.refs_7_ = bf16[2,432,128]{2,1,0:T(8,128)(2,1)S(1)} collective-permute-done((bf16[2,432,128]{2,1,0:T(8,128)(2,1)S(1)}, bf16[2,432,128]{2,1,0:T(8,128)(2,1)S(1)}, u32[]{:S(2)}, u32[]{:S(2)}) %collective-permute-start.30) | collective-permute-done | bytes 221216 | tf_op jit(solution)/shard_map/ppermute | solution.py:466
  116.0 2.2 %unpack.1 = (f32[544,256]{1,0:T(8,128)}, f32[64,2176]{1,0:T(8,128)}, f32[544,1024]{1,0:T(8,128)}, f32[256,1024]{1,0:T(8,128)}, f32[544]{0:T(1024)}, /*index=5*/f32[256]{0:T(256)}, f32[256]{0:T(256)}, f32[256]{0:T(256)}) custom-call(bf16[2,672,128]{2,1,0:T(8,128)(2,1)S(1)} %pad_maximum_fusion.refs_6_.refs_0_, ...), custom_call_target="tpu_custom_call" | custom-call | tf_op jit(solution)/shard_map/unpack/pallas_call | solution.py:699
  (51 shorter events, 2.4 us)
Async XLA Ops:
  12.5 10.8 %collective-permute-start.3 = (bf16[2,4,2,672,128]{4,3,2,1,0:T(8,128)(2,1)}, bf16[2,4,2,672,128]{4,3,2,1,0:T(8,128)(2,1)}, u32[]{:S(2)}, u32[]{:S(2)}) collective-permute-start(bf16[2,4,2,672,128]{4,3,2,1,0:T(8,128)(2,1)} %get-tuple-element.57), channel_id=1, source_target_pairs={{0,4},{4,0},{8,12},{12,8},{16,20},{20,16},{24,28},{28,24},{1,5},{5... | collective-permute-start | bytes 8257544 | tf_op jit(solution)/shard_map/ppermute | solution.py:466
  13.1 10.3 %copy-start = (bf16[2,4,2,672,128]{4,3,2,1,0:T(8,128)(2,1)S(1)}, bf16[2,4,2,672,128]{4,3,2,1,0:T(8,128)(2,1)}, u32[]{:S(2)}) copy-start(bf16[2,4,2,672,128]{4,3,2,1,0:T(8,128)(2,1)} %get-tuple-element.56) | copy-start | bytes 8257540
  23.2 28.6 %collective-permute-start.7 = (bf16[2,4,2,432,128]{4,3,2,1,0:T(8,128)(2,1)}, bf16[2,4,2,432,128]{4,3,2,1,0:T(8,128)(2,1)S(1)}, u32[]{:S(2)}, u32[]{:S(2)}) collective-permute-start(bf16[2,4,2,432,128]{4,3,2,1,0:T(8,128)(2,1)} %get-tuple-element.65), channel_id=1, source_target_pairs={{0,4},{4,0},{8,12},{12,8},{16,20},{20,16},{24,28},{28,24},{1,5},{5... | collective-permute-start | bytes 5308424 | tf_op jit(solution)/shard_map/ppermute | solution.py:466
  23.4 6.5 %copy-start.6 = (bf16[2,2,256,128]{3,2,1,0:T(8,128)(2,1)S(1)}, bf16[2,2,256,128]{3,2,1,0:T(8,128)(2,1)}, u32[]{:S(2)}) copy-start(bf16[2,2,256,128]{3,2,1,0:T(8,128)(2,1)} %get-tuple-element.53) | copy-start | bytes 786436
  23.4 8.1 %copy-start.5 = (bf16[2,2,256,128]{3,2,1,0:T(8,128)(2,1)S(1)}, bf16[2,2,256,128]{3,2,1,0:T(8,128)(2,1)}, u32[]{:S(2)}) copy-start(bf16[2,2,256,128]{3,2,1,0:T(8,128)(2,1)} %get-tuple-element.54) | copy-start | bytes 786436
  23.4 19.7 %copy-start.4 = (bf16[2,2,256,128]{3,2,1,0:T(8,128)(2,1)S(1)}, bf16[2,2,256,128]{3,2,1,0:T(8,128)(2,1)}, u32[]{:S(2)}) copy-start(bf16[2,2,256,128]{3,2,1,0:T(8,128)(2,1)} %get-tuple-element.55) | copy-start | bytes 786436
  25.4 22.0 %collective-permute-start.4 = (bf16[2,2,672,128]{3,2,1,0:T(8,128)(2,1)S(1)}, bf16[2,2,672,128]{3,2,1,0:T(8,128)(2,1)S(1)}, u32[]{:S(2)}, u32[]{:S(2)}) collective-permute-start(bf16[2,2,672,128]{3,2,1,0:T(8,128)(2,1)S(1)} %get-tuple-element.60), channel_id=1, source_target_pairs={{0,2},{1,3},{2,0},{3,1},{4,6},{5,7},{6,4},{7,5},{8,10},{9,11},{10,... | collective-permute-start | bytes 2064392 | tf_op jit(solution)/shard_map/ppermute | solution.py:472
  28.4 19.0 %collective-permute-start.5 = (bf16[2,2,672,128]{3,2,1,0:T(8,128)(2,1)S(1)}, bf16[2,2,672,128]{3,2,1,0:T(8,128)(2,1)S(1)}, u32[]{:S(2)}, u32[]{:S(2)}) collective-permute-start(bf16[2,2,672,128]{3,2,1,0:T(8,128)(2,1)S(1)} %get-tuple-element.62), channel_id=1, source_target_pairs={{0,1},{1,0},{2,3},{3,2},{4,5},{5,4},{6,7},{7,6},{8,9},{9,8},{10,11... | collective-permute-start | bytes 2064392 | tf_op jit(solution)/shard_map/ppermute | solution.py:472
  29.9 13.2 %collective-permute-start = (bf16[2,2,256,128]{3,2,1,0:T(8,128)(2,1)S(1)}, bf16[2,2,256,128]{3,2,1,0:T(8,128)(2,1)S(1)}, u32[]{:S(2)}, u32[]{:S(2)}) collective-permute-start(bf16[2,2,256,128]{3,2,1,0:T(8,128)(2,1)S(1)} %copy-done.6), channel_id=1, source_target_pairs={{0,8},{4,12},{8,0},{12,4},{16,24},{20,28},{24,16},{28,20},{1,9},{5... | collective-permute-start | bytes 786440 | tf_op jit(solution)/shard_map/ppermute | solution.py:469
  31.5 17.4 %collective-permute-start.1 = (bf16[2,2,256,128]{3,2,1,0:T(8,128)(2,1)S(1)}, bf16[2,2,256,128]{3,2,1,0:T(8,128)(2,1)S(1)}, u32[]{:S(2)}, u32[]{:S(2)}) collective-permute-start(bf16[2,2,256,128]{3,2,1,0:T(8,128)(2,1)S(1)} %copy-done.5), channel_id=1, source_target_pairs={{0,16},{4,20},{8,24},{12,28},{16,0},{20,4},{24,8},{28,12},{1,17},{... | collective-permute-start | bytes 786440 | tf_op jit(solution)/shard_map/ppermute | solution.py:469
  43.1 8.7 %collective-permute-start.2 = (bf16[2,2,256,128]{3,2,1,0:T(8,128)(2,1)S(1)}, bf16[2,2,256,128]{3,2,1,0:T(8,128)(2,1)S(1)}, u32[]{:S(2)}, u32[]{:S(2)}) collective-permute-start(bf16[2,2,256,128]{3,2,1,0:T(8,128)(2,1)S(1)} %copy-done.4), channel_id=1, source_target_pairs={{0,24},{4,28},{8,16},{12,20},{16,8},{20,12},{24,0},{28,4},{1,25},{... | collective-permute-start | bytes 786440 | tf_op jit(solution)/shard_map/ppermute | solution.py:469
  47.4 4.4 %copy-start.1 = (bf16[2,4,2,432,128]{4,3,2,1,0:T(8,128)(2,1)S(1)}, bf16[2,4,2,432,128]{4,3,2,1,0:T(8,128)(2,1)}, u32[]{:S(2)}) copy-start(bf16[2,4,2,432,128]{4,3,2,1,0:T(8,128)(2,1)} %get-tuple-element.64) | copy-start | bytes 5308420
  47.7 11.1 %collective-permute-start.6 = (bf16[2,672,128]{2,1,0:T(8,128)(2,1)S(1)}, bf16[2,672,128]{2,1,0:T(8,128)(2,1)S(1)}, u32[]{:S(2)}, u32[]{:S(2)}) collective-permute-start(bf16[2,672,128]{2,1,0:T(8,128)(2,1)S(1)} %get-tuple-element.63.refs_5_), channel_id=1, source_target_pairs={{0,1},{1,0},{2,3},{3,2},{4,5},{5,4},{6,7},{7,6},{8,9},{9,8},{10,11... | collective-permute-start | bytes 1032200 | tf_op jit(solution)/shard_map/ppermute | solution.py:472
  48.3 11.0 %collective-permute-start.8 = (bf16[2,672,128]{2,1,0:T(8,128)(2,1)S(1)}, bf16[2,672,128]{2,1,0:T(8,128)(2,1)S(1)}, u32[]{:S(2)}, u32[]{:S(2)}) collective-permute-start(bf16[2,672,128]{2,1,0:T(8,128)(2,1)S(1)} %get-tuple-element.66.refs_4_), channel_id=1, source_target_pairs={{0,2},{1,3},{2,0},{3,1},{4,6},{5,7},{6,4},{7,5},{8,10},{9,11},{10,... | collective-permute-start | bytes 1032200 | tf_op jit(solution)/shard_map/ppermute | solution.py:472
  52.9 6.6 %copy-start.2 = (bf16[2,2,256,128]{3,2,1,0:T(8,128)(2,1)S(1)}, bf16[2,2,256,128]{3,2,1,0:T(8,128)(2,1)}, u32[]{:S(2)}) copy-start(bf16[2,2,256,128]{3,2,1,0:T(8,128)(2,1)} %get-tuple-element.52.refs_0_.rest_0_) | copy-start | bytes 786436
  52.9 12.9 %collective-permute-start.12 = (bf16[2,2,432,128]{3,2,1,0:T(8,128)(2,1)S(1)}, bf16[2,2,432,128]{3,2,1,0:T(8,128)(2,1)S(1)}, u32[]{:S(2)}, u32[]{:S(2)}) collective-permute-start(bf16[2,2,432,128]{3,2,1,0:T(8,128)(2,1)S(1)} %get-tuple-element.67.refs_3_), channel_id=1, source_target_pairs={{0,1},{1,0},{2,3},{3,2},{4,5},{5,4},{6,7},{7,6},{8,9},{9,8},{10,11... | collective-permute-start | bytes 1327112 | tf_op jit(solution)/shard_map/ppermute | solution.py:472
  53.5 12.6 %collective-permute-start.11 = (bf16[2,2,432,128]{3,2,1,0:T(8,128)(2,1)S(1)}, bf16[2,2,432,128]{3,2,1,0:T(8,128)(2,1)S(1)}, u32[]{:S(2)}, u32[]{:S(2)}) collective-permute-start(bf16[2,2,432,128]{3,2,1,0:T(8,128)(2,1)S(1)} %get-tuple-element.68.refs_4_), channel_id=1, source_target_pairs={{0,2},{1,3},{2,0},{3,1},{4,6},{5,7},{6,4},{7,5},{8,10},{9,11},{10,... | collective-permute-start | bytes 1327112 | tf_op jit(solution)/shard_map/ppermute | solution.py:472
  59.6 1.9 %collective-permute-start.10 = (bf16[2,2,256,128]{3,2,1,0:T(8,128)(2,1)S(1)}, bf16[2,2,256,128]{3,2,1,0:T(8,128)(2,1)S(1)}, u32[]{:S(2)}, u32[]{:S(2)}) collective-permute-start(bf16[2,2,256,128]{3,2,1,0:T(8,128)(2,1)S(1)} %get-tuple-element.70), channel_id=1, source_target_pairs={{0,4},{4,0},{8,12},{12,8},{16,20},{20,16},{24,28},{28,24},{1,5},{5... | collective-permute-start | bytes 786440 | tf_op jit(solution)/shard_map/ppermute | solution.py:466
  59.7 1.9 %copy-start.3 = (s32[2,8192,4]{1,2,0:T(4,128)S(1)}, s32[2,8192,4]{1,2,0:T(4,128)}, u32[]{:S(2)}) copy-start(s32[2,8192,4]{1,2,0:T(4,128)} %param.23) | copy-start | bytes 786436
  59.7 1.9 %collective-permute-start.9 = (bf16[2,2,256,128]{3,2,1,0:T(8,128)(2,1)S(1)}, bf16[2,2,256,128]{3,2,1,0:T(8,128)(2,1)S(1)}, u32[]{:S(2)}, u32[]{:S(2)}) collective-permute-start(bf16[2,2,256,128]{3,2,1,0:T(8,128)(2,1)S(1)} %get-tuple-element.69.rest_6_), channel_id=1, source_target_pairs={{0,4},{4,0},{8,12},{12,8},{16,20},{20,16},{24,28},{28,24},{1,5},{5... | collective-permute-start | bytes 786440 | tf_op jit(solution)/shard_map/ppermute | solution.py:466
  60.2 10.1 %collective-permute-start.14 = (bf16[2,672,128]{2,1,0:T(8,128)(2,1)S(1)}, bf16[2,672,128]{2,1,0:T(8,128)(2,1)S(1)}, u32[]{:S(2)}, u32[]{:S(2)}) collective-permute-start(bf16[2,672,128]{2,1,0:T(8,128)(2,1)S(1)} %sums.11.refs_4_), channel_id=1, source_target_pairs={{0,8},{4,12},{8,0},{12,4},{16,24},{20,28},{24,16},{28,20},{1,9},{5... | collective-permute-start | bytes 1032200 | tf_op jit(solution)/shard_map/ppermute | solution.py:469
  66.3 7.1 %collective-permute-start.13 = (bf16[2,432,128]{2,1,0:T(8,128)(2,1)S(1)}, bf16[2,432,128]{2,1,0:T(8,128)(2,1)S(1)}, u32[]{:S(2)}, u32[]{:S(2)}) collective-permute-start(bf16[2,432,128]{2,1,0:T(8,128)(2,1)S(1)} %get-tuple-element.73.refs_5_), channel_id=1, source_target_pairs={{0,1},{1,0},{2,3},{3,2},{4,5},{5,4},{6,7},{7,6},{8,9},{9,8},{10,11... | collective-permute-start | bytes 663560 | tf_op jit(solution)/shard_map/ppermute | solution.py:472
  67.9 6.7 %collective-permute-start.15 = (bf16[2,432,128]{2,1,0:T(8,128)(2,1)S(1)}, bf16[2,432,128]{2,1,0:T(8,128)(2,1)S(1)}, u32[]{:S(2)}, u32[]{:S(2)}) collective-permute-start(bf16[2,432,128]{2,1,0:T(8,128)(2,1)S(1)} %get-tuple-element.74.refs_4_), channel_id=1, source_target_pairs={{0,2},{1,3},{2,0},{3,1},{4,6},{5,7},{6,4},{7,5},{8,10},{9,11},{10,... | collective-permute-start | bytes 663560 | tf_op jit(solution)/shard_map/ppermute | solution.py:472
  70.4 13.7 %collective-permute-start.19 = (bf16[1,672,128]{2,1,0:T(8,128)(2,1)S(1)}, bf16[1,672,128]{2,1,0:T(8,128)(2,1)S(1)}, u32[]{:S(2)}, u32[]{:S(2)}) collective-permute-start(bf16[1,672,128]{2,1,0:T(8,128)(2,1)S(1)} %sums.13.refs_3_), channel_id=1, source_target_pairs={{0,16},{4,20},{8,24},{12,28},{16,0},{20,4},{24,8},{28,12},{1,17},{... | collective-permute-start | bytes 516104 | tf_op jit(solution)/shard_map/ppermute | solution.py:469
  74.7 9.6 %collective-permute-start.18 = (bf16[2,432,128]{2,1,0:T(8,128)(2,1)S(1)}, bf16[2,432,128]{2,1,0:T(8,128)(2,1)S(1)}, u32[]{:S(2)}, u32[]{:S(2)}) collective-permute-start(bf16[2,432,128]{2,1,0:T(8,128)(2,1)S(1)} %sums.14.rest_6_), channel_id=1, source_target_pairs={{0,8},{4,12},{8,0},{12,4},{16,24},{20,28},{24,16},{28,20},{1,9},{5... | collective-permute-start | bytes 663560 | tf_op jit(solution)/shard_map/ppermute | solution.py:469
  82.8 6.6 %collective-permute-start.16 = (bf16[2,512,128]{2,1,0:T(8,128)(2,1)S(1)}, bf16[2,512,128]{2,1,0:T(8,128)(2,1)S(1)}, u32[]{:S(2)}, u32[]{:S(2)}) collective-permute-start(bf16[2,512,128]{2,1,0:T(8,128)(2,1)S(1)} %get-tuple-element.75.refs_5_), channel_id=1, source_target_pairs={{0,1},{1,0},{2,3},{3,2},{4,5},{5,4},{6,7},{7,6},{8,9},{9,8},{10,11... | collective-permute-start | bytes 786440 | tf_op jit(solution)/shard_map/ppermute | solution.py:472
  83.4 7.5 %collective-permute-start.17 = (bf16[2,512,128]{2,1,0:T(8,128)(2,1)S(1)}, bf16[2,512,128]{2,1,0:T(8,128)(2,1)S(1)}, u32[]{:S(2)}, u32[]{:S(2)}) collective-permute-start(bf16[2,512,128]{2,1,0:T(8,128)(2,1)S(1)} %get-tuple-element.76.refs_6_), channel_id=1, source_target_pairs={{0,2},{1,3},{2,0},{3,1},{4,6},{5,7},{6,4},{7,5},{8,10},{9,11},{10,... | collective-permute-start | bytes 786440 | tf_op jit(solution)/shard_map/ppermute | solution.py:472
  84.3 12.5 %collective-permute-start.22 = (bf16[1,672,128]{2,1,0:T(8,128)(2,1)S(1)}, bf16[1,672,128]{2,1,0:T(8,128)(2,1)S(1)}, u32[]{:S(2)}, u32[]{:S(2)}) collective-permute-start(bf16[1,672,128]{2,1,0:T(8,128)(2,1)S(1)} %sums.16.refs_4_), channel_id=1, source_target_pairs={{0,16},{4,20},{8,24},{12,28},{16,0},{20,4},{24,8},{28,12},{1,17},{... | collective-permute-start | bytes 516104 | tf_op jit(solution)/shard_map/ppermute | solution.py:469
  84.5 12.1 %collective-permute-start.23 = (bf16[1,432,128]{2,1,0:T(8,128)(2,1)S(1)}, bf16[1,432,128]{2,1,0:T(8,128)(2,1)S(1)}, u32[]{:S(2)}, u32[]{:S(2)}) collective-permute-start(bf16[1,432,128]{2,1,0:T(8,128)(2,1)S(1)} %sums.17.refs_4_), channel_id=1, source_target_pairs={{0,16},{4,20},{8,24},{12,28},{16,0},{20,4},{24,8},{28,12},{1,17},{... | collective-permute-start | bytes 331784 | tf_op jit(solution)/shard_map/ppermute | solution.py:469
  91.1 8.2 %collective-permute-start.20 = (bf16[512,128]{1,0:T(8,128)(2,1)S(1)}, bf16[512,128]{1,0:T(8,128)(2,1)S(1)}, u32[]{:S(2)}, u32[]{:S(2)}) collective-permute-start(bf16[512,128]{1,0:T(8,128)(2,1)S(1)} %get-tuple-element.77.refs_5_), channel_id=1, source_target_pairs={{0,2},{1,3},{2,0},{3,1},{4,6},{5,7},{6,4},{7,5},{8,10},{9,11},{10,... | collective-permute-start | bytes 393224 | tf_op jit(solution)/shard_map/ppermute | solution.py:472
  91.7 7.5 %collective-permute-start.21 = (bf16[512,128]{1,0:T(8,128)(2,1)S(1)}, bf16[512,128]{1,0:T(8,128)(2,1)S(1)}, u32[]{:S(2)}, u32[]{:S(2)}) collective-permute-start(bf16[512,128]{1,0:T(8,128)(2,1)S(1)} %get-tuple-element.78.refs_6_), channel_id=1, source_target_pairs={{0,1},{1,0},{2,3},{3,2},{4,5},{5,4},{6,7},{7,6},{8,9},{9,8},{10,11... | collective-permute-start | bytes 393224 | tf_op jit(solution)/shard_map/ppermute | solution.py:472
  96.8 12.9 %collective-permute-start.24 = (bf16[2,672,128]{2,1,0:T(8,128)(2,1)S(1)}, bf16[2,672,128]{2,1,0:T(8,128)(2,1)S(1)}, u32[]{:S(2)}, u32[]{:S(2)}) collective-permute-start(bf16[2,672,128]{2,1,0:T(8,128)(2,1)S(1)} %pad_maximum_fusion.refs_6_.refs_0_), channel_id=1, source_target_pairs={{0,8},{4,12},{8,0},{12,4},{16,24},{20,28},{24,16},{28,20},{1,9},{5... | collective-permute-start | bytes 1032200 | tf_op jit(solution)/shard_map/ppermute | solution.py:469
  96.9 9.4 %collective-permute-start.27 = (bf16[1,432,128]{2,1,0:T(8,128)(2,1)S(1)}, bf16[1,432,128]{2,1,0:T(8,128)(2,1)S(1)}, u32[]{:S(2)}, u32[]{:S(2)}) collective-permute-start(bf16[1,432,128]{2,1,0:T(8,128)(2,1)S(1)} %sums.19), channel_id=1, source_target_pairs={{0,16},{4,20},{8,24},{12,28},{16,0},{20,4},{24,8},{28,12},{1,17},{... | collective-permute-start | bytes 331784 | tf_op jit(solution)/shard_map/ppermute | solution.py:469
  106.3 8.2 %collective-permute-start.28 = (bf16[2,432,128]{2,1,0:T(8,128)(2,1)S(1)}, bf16[2,432,128]{2,1,0:T(8,128)(2,1)S(1)}, u32[]{:S(2)}, u32[]{:S(2)}) collective-permute-start(bf16[2,432,128]{2,1,0:T(8,128)(2,1)S(1)} %pad_maximum_fusion.1.refs_4_), channel_id=1, source_target_pairs={{0,8},{4,12},{8,0},{12,4},{16,24},{20,28},{24,16},{28,20},{1,9},{5... | collective-permute-start | bytes 663560 | tf_op jit(solution)/shard_map/ppermute | solution.py:469
  109.7 4.8 %collective-permute-start.25 = (bf16[2,672,128]{2,1,0:T(8,128)(2,1)S(1)}, bf16[2,672,128]{2,1,0:T(8,128)(2,1)S(1)}, u32[]{:S(2)}, u32[]{:S(2)}) collective-permute-start(bf16[2,672,128]{2,1,0:T(8,128)(2,1)S(1)} %pad_maximum_fusion.refs_6_.refs_0_), channel_id=1, source_target_pairs={{0,4},{4,0},{8,12},{12,8},{16,20},{20,16},{24,28},{28,24},{1,5},{5... | collective-permute-start | bytes 1032200 | tf_op jit(solution)/shard_map/ppermute | solution.py:466
  109.7 6.3 %collective-permute-start.26 = (bf16[2,672,128]{2,1,0:T(8,128)(2,1)S(1)}, bf16[2,672,128]{2,1,0:T(8,128)(2,1)S(1)}, u32[]{:S(2)}, u32[]{:S(2)}) collective-permute-start(bf16[2,672,128]{2,1,0:T(8,128)(2,1)S(1)} %collective-permute-done.24.refs_1_), channel_id=1, source_target_pairs={{0,4},{4,0},{8,12},{12,8},{16,20},{20,16},{24,28},{28,24},{1,5},{5... | collective-permute-start | bytes 1032200 | tf_op jit(solution)/shard_map/ppermute | solution.py:466
  110.2 4.3 %collective-permute-start.29 = (bf16[2,432,128]{2,1,0:T(8,128)(2,1)S(1)}, bf16[2,432,128]{2,1,0:T(8,128)(2,1)S(1)}, u32[]{:S(2)}, u32[]{:S(2)}) collective-permute-start(bf16[2,432,128]{2,1,0:T(8,128)(2,1)S(1)} %pad_maximum_fusion.1.refs_4_), channel_id=1, source_target_pairs={{0,4},{4,0},{8,12},{12,8},{16,20},{20,16},{24,28},{28,24},{1,5},{5... | collective-permute-start | bytes 663560 | tf_op jit(solution)/shard_map/ppermute | solution.py:466
  114.5 1.5 %collective-permute-start.30 = (bf16[2,432,128]{2,1,0:T(8,128)(2,1)S(1)}, bf16[2,432,128]{2,1,0:T(8,128)(2,1)S(1)}, u32[]{:S(2)}, u32[]{:S(2)}) collective-permute-start(bf16[2,432,128]{2,1,0:T(8,128)(2,1)S(1)} %collective-permute-done.28.refs_5_), channel_id=1, source_target_pairs={{0,4},{4,0},{8,12},{12,8},{16,20},{20,16},{24,28},{28,24},{1,5},{5... | collective-permute-start | bytes 663560 | tf_op jit(solution)/shard_map/ppermute | solution.py:466
